TPU v7x, 32 devices: a whole 2x2x4 slice. The times are simulated.
32 devices in a mesh: gx: 4 (over y, x), gy: 4 (over z), gz: 2 (over core).
Axes of the slice: x: 2, y: 2, z: 4, core: 2. Of those that a mesh axis runs over, the one named last changes fastest.
Arguments:
- initial: float32 [32, 32, 256], P('gx', 'gy', 'gz'), may hold values from -6 to 6
- source: float32 [32, 32, 256], P('gx', 'gy', 'gz'), may hold values from -6 to 6
- metric: float32 [3, 32, 32, 256], P(None, 'gx', 'gy', 'gz'), may hold values from 0.005 to 0.05
- eigenvectors: float32 [3, 10, 10, 4, 4, 32], P(None, None, None, 'gx', 'gy', 'gz'), may hold values from -2 to 2
- eigenvalues: float32 [3, 10, 4, 4, 32], P(None, None, 'gx', 'gy', 'gz'), may hold values from 1 to 8
Outputs:
- solution: float32 [32, 32, 256], P('gx', 'gy', 'gz')
All inputs are finite; a program needn't handle non-finite values.
Results may differ from a plain program's by a relative error of at most 0.0001.
Values sent between devices are 32-bit elements; how exact they have to be, the bound alone decides.
No kernel may reach another device: no remote copies, remote signals or barrier semaphores. Data moves between devices by JAX's collectives and lax.ppermute only.
A program may use at most 64 MiB of HBM per device.

v0:
```python
import jax
import jax.numpy as jnp
import numpy as np
from jax import lax
from jax.sharding import PartitionSpec as P

gll_points = np.array(
    [
        -1.0,
        -0.8717401485096066,
        -0.5917001814331423,
        -0.2092992179024789,
        0.2092992179024789,
        0.5917001814331423,
        0.8717401485096066,
        1.0,
    ]
)


def extended_2(value, sides, width):
    for axis, dim in sides:
        size, length = (lax.axis_size(axis), value.shape[dim])
        up = [(i, (i + 1) % size) for i in range(size - 1)]
        down = [(j, i) for i, j in up]
        last = lax.slice_in_dim(value, length - width, length, axis=dim)
        first = lax.slice_in_dim(value, 0, width, axis=dim)
        before = lax.ppermute(last, axis, up)
        after = lax.ppermute(first, axis, down)
        value = jnp.concatenate([before, value, after], axis=dim)
    return value


def derivative_table():
    number = gll_points.shape[0]
    products = np.array(
        [
            np.prod(
                [
                    gll_points[row_index] - gll_points[other]
                    for other in range(number)
                    if other != row_index
                ]
            )
            for row_index in range(number)
        ]
    )
    matrix_out = np.zeros((number, number))
    for row_index in range(number):
        for col_index in range(number):
            if row_index != col_index:
                matrix_out[row_index, col_index] = (
                    products[row_index]
                    / products[col_index]
                    / (gll_points[row_index] - gll_points[col_index])
                )
        matrix_out[row_index, row_index] = -np.sum(matrix_out[row_index])
    return matrix_out


def apply_along(values, matrix, direction):
    block_size = matrix.shape[1]
    old_shape = values.shape
    pieces_shape = (
        old_shape[:direction]
        + (old_shape[direction] // block_size, block_size)
        + old_shape[direction + 1 :]
    )
    result = jnp.tensordot(
        values.reshape(pieces_shape),
        matrix,
        axes=((direction + 1,), (1,)),
        precision=lax.Precision.HIGHEST,
    )
    result = jnp.moveaxis(result, -1, direction + 1)
    return result.reshape(
        old_shape[:direction]
        + (old_shape[direction] // block_size * matrix.shape[0],)
        + old_shape[direction + 1 :]
    )


def apply_operator(values, metric):
    deriv_table = jnp.asarray(derivative_table(), jnp.float32)
    summed = jnp.zeros_like(values)
    for direction in range(3):
        gradient = apply_along(values, deriv_table, direction)
        summed = summed + apply_along(metric[direction] * gradient, deriv_table.T, direction)
    return summed


def assemble(padded, offset):
    result = padded
    for direction in range(3):
        length = result.shape[direction]
        view_shape = [1, 1, 1]
        view_shape[direction] = length
        node_index = ((jnp.arange(length) - offset) % 8).reshape(view_shape)
        edge_zero = jnp.zeros_like(lax.slice_in_dim(result, 0, 1, axis=direction))
        upward = jnp.concatenate(
            [lax.slice_in_dim(result, 1, length, axis=direction), edge_zero], axis=direction
        )
        downward = jnp.concatenate(
            [edge_zero, lax.slice_in_dim(result, 0, length - 1, axis=direction)], axis=direction
        )
        result = (
            result
            + jnp.where(node_index == 7, upward, 0.0)
            + jnp.where(node_index == 0, downward, 0.0)
        )
    return result


def extend_axis(padded, direction):
    shifted = jnp.moveaxis(padded, direction, 0)
    blocks = (shifted.shape[0] - 4) // 8
    trailing = shifted.shape[1:]
    middle = shifted[2:-2].reshape((blocks, 8) + trailing)
    lowest = shifted[0 : 8 * blocks : 8][:, None]
    beyond = shifted[11::8][:, None]
    joined = jnp.concatenate([lowest, middle, beyond], axis=1).reshape((blocks * 10,) + trailing)
    return jnp.moveaxis(joined, 0, direction)


def widen(padded):
    return extend_axis(extend_axis(extend_axis(padded, 0), 1), 2)


def fast_solve(extended, eigenvectors, eigenvalues):
    count_x, count_y, count_z = eigenvectors.shape[3:]
    precise = lax.Precision.HIGHEST
    spectral = extended.reshape(count_x, 10, count_y, 10, count_z, 10)
    spectral = jnp.einsum("apxyz,xaybzc->xpybzc", eigenvectors[0], spectral, precision=precise)
    spectral = jnp.einsum("bqxyz,xpybzc->xpyqzc", eigenvectors[1], spectral, precision=precise)
    spectral = jnp.einsum("csxyz,xpyqzc->xpyqzs", eigenvectors[2], spectral, precision=precise)
    rate_x = jnp.transpose(eigenvalues[0], (1, 0, 2, 3))[:, :, :, None, :, None]
    rate_y = jnp.transpose(eigenvalues[1], (1, 2, 0, 3))[:, None, :, :, :, None]
    rate_z = jnp.transpose(eigenvalues[2], (1, 2, 3, 0))[:, None, :, None, :, :]
    spectral = spectral / (rate_x + rate_y + rate_z)
    spectral = jnp.einsum("csxyz,xpyqzs->xpyqzc", eigenvectors[2], spectral, precision=precise)
    spectral = jnp.einsum("bqxyz,xpyqzc->xpybzc", eigenvectors[1], spectral, precision=precise)
    spectral = jnp.einsum("apxyz,xpybzc->xaybzc", eigenvectors[0], spectral, precision=precise)
    return spectral.reshape(count_x * 10, count_y * 10, count_z * 10)


def return_axis(padded, direction):
    shifted = jnp.moveaxis(padded, direction, 0)
    blocks = (shifted.shape[0] - 4) // 10
    trailing = shifted.shape[1:]
    owned = shifted[2:-2].reshape((blocks, 10) + trailing)[:, 1:9]
    before = shifted[0 : 10 * blocks].reshape((blocks, 10) + trailing)[:, 0:2]
    following = shifted[4:].reshape((blocks, 10) + trailing)[:, 8:10]
    middle = jnp.zeros((blocks, 4) + trailing, shifted.dtype)
    summed = owned + jnp.concatenate([before, middle, following], axis=1)
    return jnp.moveaxis(summed.reshape((blocks * 8,) + trailing), 0, direction)


def body(initial, source, metric, eigenvectors, eigenvalues):
    solution = initial
    local_res = source - apply_operator(solution, metric)
    deeper = extended_2(local_res, (("gx", 0), ("gy", 1), ("gz", 2)), 2)
    widened = assemble(deeper, 2)
    extended = widen(widened)
    corrected = fast_solve(extended, eigenvectors, eigenvalues)
    padded = extended_2(corrected, (("gx", 0), ("gy", 1), ("gz", 2)), 2)
    correction = return_axis(return_axis(return_axis(padded, 0), 1), 2)
    solution = solution + correction
    return solution


def solution(mesh):
    placed = (
        P("gx", "gy", "gz"),
        P("gx", "gy", "gz"),
        P(None, "gx", "gy", "gz"),
        P(None, None, None, "gx", "gy", "gz"),
        P(None, None, "gx", "gy", "gz"),
    )
    return jax.shard_map(
        body, mesh=mesh, in_specs=placed, out_specs=P("gx", "gy", "gz"), check_vma=False
    )
```

profile of v0, /device:TPU:0, one launch (start us, length us, event | category | flops | bytes accessed | tf_op | source)
XLA Modules:
  0.0 78.2 jit_solution(9911344767102657591)
XLA Ops:
  0.0 0.8 fusion.33
  0.8 0.3 squeeze.7
  1.1 1.1 %reshape.226 = f32[8,8,16,8]{3,2,1,0:T(8,128)S(1)} reshape(f32[8,8,128]{2,1,0:T(8,128)} %param.6) | data formatting | bytes 65536 | tf_op jit(solution)/shard_map/reshape | solution.py:70
  2.2 1.2 %fusion.4 = f32[8,8,16,8]{3,2,1,0:T(8,128)S(1)} fusion(f32[8,8,16,8]{3,2,1,0:T(8,128)S(1)} %squeeze.7, f32[8,8,1,1]{1,0,3,2:T(8,128)} %constant.65, f32[8,8,16,8]{3,2,1,0:T(8,128)S(1)} %reshape.226), kind=kOutput, calls=%fused_computation.11 | convolution fusion | flops 794624 | bytes 98560 | tf_op jit(solution)/shard_map/dot_general | solution.py:69
  3.5 0.5 fusion.38
  4.0 0.3 reshape.227
  4.3 0.9 %fusion.11 = f32[8,8,128]{2,1,0:T(8,128)S(1)} fusion(f32[8,8,1]{1,0,2:T(8,128)S(1)} %copy-done.8, f32[8,8,128]{2,1,0:T(8,128)S(1)} %copy-done.4, f32[3,8,8,128]{3,2,1,0:T(8,128)} %param.8), kind=kOutput, calls=%fused_computation.21 | convolution fusion | flops 794624 | bytes 98560 | tf_op jit(solution)/shard_map/dot_general | solution.py:69
  5.2 0.2 fusion.9
  5.4 0.2 fusion.37
  5.6 0.2 fusion.7
  5.9 4.8 %collective-permute-start = (f32[2,8,128]{2,0,1:T(2,128)S(1)}, f32[2,8,128]{2,0,1:T(2,128)S(1)}, u32[]{:S(2)}, u32[]{:S(2)}) collective-permute-start(f32[2,8,128]{2,0,1:T(2,128)S(1)} %get-tuple-element.39), channel_id=1, source_target_pairs={{0,8},{8,16},{16,24},{1,9},{9,17},{17,25},{2,10},{10,18},{18,26},{... | collective-permute-start | bytes 24584 | tf_op jit(solution)/shard_map/ppermute | solution.py:28
  10.7 1.3 %collective-permute-start.1 = (f32[2,8,128]{2,0,1:T(2,128)S(1)}, f32[2,8,128]{2,0,1:T(2,128)S(1)}, u32[]{:S(2)}, u32[]{:S(2)}) collective-permute-start(f32[2,8,128]{2,0,1:T(2,128)S(1)} %get-tuple-element.40), channel_id=1, source_target_pairs={{8,0},{16,8},{24,16},{9,1},{17,9},{25,17},{10,2},{18,10},{26,18},{... | collective-permute-start | bytes 24584 | tf_op jit(solution)/shard_map/ppermute | solution.py:29
  12.2 0.7 broadcast_add_fusion
  13.0 3.3 %collective-permute-done.1 = f32[2,8,128]{2,0,1:T(2,128)S(1)} collective-permute-done((f32[2,8,128]{2,0,1:T(2,128)S(1)}, f32[2,8,128]{2,0,1:T(2,128)S(1)}, u32[]{:S(2)}, u32[]{:S(2)}) %collective-permute-start.1) | collective-permute-done | bytes 8224 | tf_op jit(solution)/shard_map/ppermute | solution.py:29
  16.3 3.5 %collective-permute-start.2 = (f32[12,2,128]{2,0,1:T(8,128)S(1)}, f32[12,2,128]{2,0,1:T(8,128)S(1)}, u32[]{:S(2)}, u32[]{:S(2)}) collective-permute-start(f32[12,2,128]{2,0,1:T(8,128)S(1)} %get-tuple-element.37), channel_id=1, source_target_pairs={{0,2},{2,4},{4,6},{1,3},{3,5},{5,7},{8,10},{10,12},{12,14},{9,11},... | collective-permute-start | bytes 36872 | tf_op jit(solution)/shard_map/ppermute | solution.py:28
  19.8 1.3 %collective-permute-start.3 = (f32[12,2,128]{2,0,1:T(8,128)S(1)}, f32[12,2,128]{2,0,1:T(8,128)S(1)}, u32[]{:S(2)}, u32[]{:S(2)}) collective-permute-start(f32[12,2,128]{2,0,1:T(8,128)S(1)} %get-tuple-element.38), channel_id=1, source_target_pairs={{2,0},{4,2},{6,4},{3,1},{5,3},{7,5},{10,8},{12,10},{14,12},{11,9},... | collective-permute-start | bytes 36872 | tf_op jit(solution)/shard_map/ppermute | solution.py:29
  21.2 4.2 %collective-permute-done.3 = f32[12,2,128]{2,0,1:T(8,128)S(1)} collective-permute-done((f32[12,2,128]{2,0,1:T(8,128)S(1)}, f32[12,2,128]{2,0,1:T(8,128)S(1)}, u32[]{:S(2)}, u32[]{:S(2)}) %collective-permute-start.3) | collective-permute-done | bytes 12320 | tf_op jit(solution)/shard_map/ppermute | solution.py:29
  25.5 1.3 %collective-permute-start.4 = (f32[12,12,2]{2,0,1:T(8,128)S(1)}, f32[12,12,2]{2,0,1:T(8,128)S(1)}, u32[]{:S(2)}, u32[]{:S(2)}) collective-permute-start(f32[12,12,2]{2,0,1:T(8,128)S(1)} %get-tuple-element.30), channel_id=1, source_target_pairs={{0,1},{2,3},{4,5},{6,7},{8,9},{10,11},{12,13},{14,15},{16,17},{18,... | collective-permute-start | bytes 3464 | tf_op jit(solution)/shard_map/ppermute | solution.py:28
  26.8 1.5 %collective-permute-start.5 = (f32[12,12,2]{2,0,1:T(8,128)S(1)}, f32[12,12,2]{2,0,1:T(8,128)S(1)}, u32[]{:S(2)}, u32[]{:S(2)}) collective-permute-start(f32[12,12,2]{2,0,1:T(8,128)S(1)} %get-tuple-element.31), channel_id=1, source_target_pairs={{1,0},{3,2},{5,4},{7,6},{9,8},{11,10},{13,12},{15,14},{17,16},{19,... | collective-permute-start | bytes 3464 | tf_op jit(solution)/shard_map/ppermute | solution.py:29
  28.3 0.2 copy.79
  28.5 0.8 %copy.80 = f32[1,10,10,1,1,16]{2,1,5,4,3,0:T(8,128)} copy(f32[1,10,10,1,1,16]{5,4,3,2,1,0:T(1,128)S(1)} %get-tuple-element.25) | data formatting | bytes 12800
  29.3 0.8 %copy.81 = f32[1,10,10,1,1,16]{2,1,5,4,3,0:T(8,128)} copy(f32[1,10,10,1,1,16]{5,4,3,2,1,0:T(1,128)S(1)} %get-tuple-element.24) | data formatting | bytes 12800
  30.2 0.2 pad_maximum_fusion.3
  30.4 0.2 select_add_fusion.2
  30.7 0.1 fusion.28
  30.8 0.1 select_add_fusion
  31.2 0.3 slice.196
  31.5 0.3 slice.198
  31.9 0.4 reshape.232
  32.3 0.7 copy.41
  33.0 0.7 copy.42
  33.6 0.5 pad_maximum_fusion
  34.1 0.4 reshape.233
  34.5 0.5 reshape.234
  35.0 2.6 %convolution_bitcast_fusion.5 = f32[10,10,16,10]{0,3,1,2:T(8,128)S(1)} fusion(f32[10,10,16,10]{3,2,1,0:T(8,128)S(1)} %reshape.234, f32[1,10,10,1,1,16]{2,1,5,4,3,0:T(8,128)S(1)} %copy.79), kind=kOutput, calls=%fused_computation.5 | convolution fusion | flops 1920000 | bytes 134400 | tf_op jit(solution)/shard_map/apxyz,xaybzc->xpybzc/dot_general | solution.py:133
  37.6 1.6 %copy.46 = f32[10,10,16,10]{1,3,0,2:T(8,128)S(1)} copy(f32[10,10,16,10]{0,3,1,2:T(8,128)S(1)} %convolution_bitcast_fusion.5) | data formatting | bytes 128000 | tf_op jit(solution)/shard_map/reshape.11
  39.3 1.2 %convolution_bitcast_fusion.4 = f32[10,10,16,10]{1,3,0,2:T(8,128)S(1)} fusion(f32[10,10,16,10]{1,3,0,2:T(8,128)S(1)} %copy.46, f32[1,10,10,1,1,16]{2,1,5,4,3,0:T(8,128)S(1)} %copy-done.2), kind=kOutput, calls=%fused_computation.4 | convolution fusion | flops 1920000 | bytes 134400 | tf_op jit(solution)/shard_map/bqxyz,xpybzc->xpyqzc/dot_general | solution.py:134
  40.5 2.2 %convolution_bitcast_fusion.3 = f32[1,10,1,10,16,10]{5,3,1,4,2,0:T(8,128)S(1)} fusion(f32[10,10,16,10]{1,3,0,2:T(8,128)S(1)} %convolution_bitcast_fusion.4, f32[1,10,10,1,1,16]{2,1,5,4,3,0:T(8,128)S(1)} %copy-done.5), kind=kOutput, calls=%fused_computation.3 | convolution fusion | flops 1920000 | bytes 134400 | tf_op jit(solution)/shard_map/csxyz,xpyqzc->xpyqzs/dot_general | solution.py:135
  42.8 1.7 %convolution_bitcast_fusion.2 = f32[10,10,16,10]{3,1,0,2:T(8,128)S(1)} fusion(f32[1,10,1,10,16,10]{5,3,1,4,2,0:T(8,128)S(1)} %convolution_bitcast_fusion.3, f32[16,10]{1,0:T(8,128)S(1)} %bitcast.225, f32[10,10,16]{1,0,2:T(8,128)S(1)} %copy-done.7, f32[1,10,10,1,1,16]{2,1,5,4,3,0:T(8,128)S(1)} %copy-done.5), kind=kOutput, calls=%fused_computation.2 | convolution fusion | flops 1952000 | bytes 141440 | tf_op jit(solution)/shard_map/csxyz,xpyqzs->xpyqzc/dot_general | solution.py:140
  44.5 2.2 %convolution_bitcast_fusion.1 = f32[10,10,16,10]{1,3,0,2:T(8,128)S(1)} fusion(f32[10,10,16,10]{3,1,0,2:T(8,128)S(1)} %convolution_bitcast_fusion.2, f32[1,10,10,1,1,16]{2,1,5,4,3,0:T(8,128)S(1)} %copy-done.3), kind=kOutput, calls=%fused_computation.1 | convolution fusion | flops 1920000 | bytes 134400 | tf_op jit(solution)/shard_map/bqxyz,xpyqzc->xpybzc/dot_general | solution.py:141
  46.7 1.6 %copy.53 = f32[10,10,16,10]{3,0,1,2:T(8,128)S(1)} copy(f32[10,10,16,10]{1,3,0,2:T(8,128)S(1)} %convolution_bitcast_fusion.1) | data formatting | bytes 128000 | tf_op jit(solution)/shard_map/reshape.27
  48.4 1.2 %convolution_bitcast_fusion = f32[1,10,1,10,16,10]{5,1,3,4,2,0:T(8,128)S(1)} fusion(f32[10,10,16,10]{3,0,1,2:T(8,128)S(1)} %copy.53, f32[1,10,10,1,1,16]{2,1,5,4,3,0:T(8,128)S(1)} %copy-done.1), kind=kOutput, calls=%fused_computation | convolution fusion | flops 1920000 | bytes 134400 | tf_op jit(solution)/shard_map/apxyz,xpybzc->xaybzc/dot_general | solution.py:142
  49.7 0.1 slice.206
  49.8 4.3 %collective-permute-start.6 = (f32[2,10,160]{2,0,1:T(2,128)S(1)}, f32[2,10,160]{2,0,1:T(2,128)S(1)}, u32[]{:S(2)}, u32[]{:S(2)}) collective-permute-start(f32[2,10,160]{2,0,1:T(2,128)S(1)} %slice.206), channel_id=1, source_target_pairs={{0,8},{8,16},{16,24},{1,9},{9,17},{17,25},{2,10},{10,18},{18,26},{... | collective-permute-start | bytes 38408 | tf_op jit(solution)/shard_map/ppermute | solution.py:28
  54.2 0.5 copy.55
  54.6 0.4 reshape.243
  55.1 0.1 reshape.264
  55.2 1.3 %collective-permute-start.7 = (f32[2,10,160]{2,1,0:T(8,128)S(1)}, f32[2,10,160]{2,1,0:T(8,128)S(1)}, u32[]{:S(2)}, u32[]{:S(2)}) collective-permute-start(f32[2,10,160]{2,1,0:T(8,128)S(1)} %reshape.264), channel_id=1, source_target_pairs={{8,0},{16,8},{24,16},{9,1},{17,9},{25,17},{10,2},{18,10},{26,18},{... | collective-permute-start | bytes 38408 | tf_op jit(solution)/shard_map/ppermute | solution.py:29
  56.5 4.7 %collective-permute-done.7 = f32[2,10,160]{2,1,0:T(8,128)S(1)} collective-permute-done((f32[2,10,160]{2,1,0:T(8,128)S(1)}, f32[2,10,160]{2,1,0:T(8,128)S(1)}, u32[]{:S(2)}, u32[]{:S(2)}) %collective-permute-start.7) | collective-permute-done | bytes 12832 | tf_op jit(solution)/shard_map/ppermute | solution.py:29
  61.2 3.5 %collective-permute-start.8 = (f32[14,2,160]{2,1,0:T(2,128)S(1)}, f32[14,2,160]{2,1,0:T(2,128)S(1)}, u32[]{:S(2)}, u32[]{:S(2)}) collective-permute-start(f32[14,2,160]{2,1,0:T(2,128)S(1)} %get-tuple-element.12), channel_id=1, source_target_pairs={{0,2},{2,4},{4,6},{1,3},{3,5},{5,7},{8,10},{10,12},{12,14},{9,11},... | collective-permute-start | bytes 53768 | tf_op jit(solution)/shard_map/ppermute | solution.py:28
  64.7 1.3 %collective-permute-start.9 = (f32[14,2,160]{2,1,0:T(2,128)S(1)}, f32[14,2,160]{2,1,0:T(2,128)S(1)}, u32[]{:S(2)}, u32[]{:S(2)}) collective-permute-start(f32[14,2,160]{2,1,0:T(2,128)S(1)} %get-tuple-element.13), channel_id=1, source_target_pairs={{2,0},{4,2},{6,4},{3,1},{5,3},{7,5},{10,8},{12,10},{14,12},{11,9},... | collective-permute-start | bytes 53768 | tf_op jit(solution)/shard_map/ppermute | solution.py:29
  66.0 0.2 collective-permute-done.8
  66.3 4.2 %collective-permute-done.9 = f32[14,2,160]{2,1,0:T(2,128)S(1)} collective-permute-done((f32[14,2,160]{2,1,0:T(2,128)S(1)}, f32[14,2,160]{2,1,0:T(2,128)S(1)}, u32[]{:S(2)}, u32[]{:S(2)}) %collective-permute-start.9) | collective-permute-done | bytes 17952 | tf_op jit(solution)/shard_map/ppermute | solution.py:29
  70.7 1.3 %collective-permute-start.10 = (f32[14,14,2]{2,1,0:T(8,128)S(1)}, f32[14,14,2]{2,1,0:T(8,128)S(1)}, u32[]{:S(2)}, u32[]{:S(2)}) collective-permute-start(f32[14,14,2]{2,1,0:T(8,128)S(1)} %get-tuple-element.10), channel_id=1, source_target_pairs={{0,1},{2,3},{4,5},{6,7},{8,9},{10,11},{12,13},{14,15},{16,17},{18,... | collective-permute-start | bytes 4712 | tf_op jit(solution)/shard_map/ppermute | solution.py:28
  72.0 1.3 %collective-permute-start.11 = (f32[14,14,2]{2,1,0:T(8,128)S(1)}, f32[14,14,2]{2,1,0:T(8,128)S(1)}, u32[]{:S(2)}, u32[]{:S(2)}) collective-permute-start(f32[14,14,2]{2,1,0:T(8,128)S(1)} %get-tuple-element.11), channel_id=1, source_target_pairs={{1,0},{3,2},{5,4},{7,6},{9,8},{11,10},{13,12},{15,14},{17,16},{19,... | collective-permute-start | bytes 4712 | tf_op jit(solution)/shard_map/ppermute | solution.py:29
  73.3 1.8 %collective-permute-done.11 = f32[14,14,2]{2,1,0:T(8,128)S(1)} collective-permute-done((f32[14,14,2]{2,1,0:T(8,128)S(1)}, f32[14,14,2]{2,1,0:T(8,128)S(1)}, u32[]{:S(2)}, u32[]{:S(2)}) %collective-permute-start.11) | collective-permute-done | bytes 1600 | tf_op jit(solution)/shard_map/ppermute | solution.py:29
  75.2 0.2 pad_maximum_fusion.2
  75.8 0.3 reshape.254
  76.1 0.2 slice.271
  76.3 0.3 reshape.253
  76.7 0.3 reshape.252
  77.0 0.3 slice_add_fusion
  77.3 0.3 reshape.255
  77.6 0.6 bitcast_add_fusion
  (72 shorter events, 1.7 us)
Async XLA Ops:
  0.8 2.6 %copy-start.10 = (f32[8,8,1,1]{1,0,3,2:T(8,128)S(1)}, f32[8,8,1,1]{1,0,3,2:T(8,128)}, u32[]{:S(2)}) copy-start(f32[8,8,1,1]{1,0,3,2:T(8,128)} %constant.65) | copy-start | bytes 772
  2.1 2.1 %copy-start.4 = (f32[8,8,128]{2,1,0:T(8,128)S(1)}, f32[8,8,128]{2,1,0:T(8,128)}, u32[]{:S(2)}) copy-start(f32[8,8,128]{2,1,0:T(8,128)} %param.6) | copy-start | bytes 98308
  2.2 2.1 %copy-start.8 = (f32[8,8,1]{1,0,2:T(8,128)S(1)}, f32[8,8,1]{1,0,2:T(8,128)}, u32[]{:S(2)}) copy-start(f32[8,8,1]{1,0,2:T(8,128)} %constant.64) | copy-start | bytes 772
  3.4 2.2 %copy-start.9 = (f32[8,8,128]{2,1,0:T(8,128)S(1)}, f32[8,8,128]{2,1,0:T(8,128)}, u32[]{:S(2)}) copy-start(f32[8,8,128]{2,1,0:T(8,128)} %param.7) | copy-start | bytes 98308
  3.4 8.6 %copy-start.6 = (f32[3,10,10,1,1,16]{5,4,3,2,1,0:T(1,128)S(1)}, f32[3,10,10,1,1,16]{5,4,3,2,1,0:T(1,128)}, u32[]{:S(2)}) copy-start(f32[3,10,10,1,1,16]{5,4,3,2,1,0:T(1,128)} %param.9) | copy-start | bytes 57604
  3.5 8.6 %copy-start.11 = (f32[3,10,1,1,16]{4,3,2,1,0:T(1,128)S(1)}, f32[3,10,1,1,16]{4,3,2,1,0:T(1,128)}, u32[]{:S(2)}) copy-start(f32[3,10,1,1,16]{4,3,2,1,0:T(1,128)} %param.10) | copy-start | bytes 5764
  5.9 7.1 %collective-permute-start = (f32[2,8,128]{2,0,1:T(2,128)S(1)}, f32[2,8,128]{2,0,1:T(2,128)S(1)}, u32[]{:S(2)}, u32[]{:S(2)}) collective-permute-start(f32[2,8,128]{2,0,1:T(2,128)S(1)} %get-tuple-element.39), channel_id=1, source_target_pairs={{0,8},{8,16},{16,24},{1,9},{9,17},{17,25},{2,10},{10,18},{18,26},{... | collective-permute-start | bytes 24584 | tf_op jit(solution)/shard_map/ppermute | solution.py:28
  10.7 5.5 %collective-permute-start.1 = (f32[2,8,128]{2,0,1:T(2,128)S(1)}, f32[2,8,128]{2,0,1:T(2,128)S(1)}, u32[]{:S(2)}, u32[]{:S(2)}) collective-permute-start(f32[2,8,128]{2,0,1:T(2,128)S(1)} %get-tuple-element.40), channel_id=1, source_target_pairs={{8,0},{16,8},{24,16},{9,1},{17,9},{25,17},{10,2},{18,10},{26,18},{... | collective-permute-start | bytes 24584 | tf_op jit(solution)/shard_map/ppermute | solution.py:29
  16.3 4.9 %collective-permute-start.2 = (f32[12,2,128]{2,0,1:T(8,128)S(1)}, f32[12,2,128]{2,0,1:T(8,128)S(1)}, u32[]{:S(2)}, u32[]{:S(2)}) collective-permute-start(f32[12,2,128]{2,0,1:T(8,128)S(1)} %get-tuple-element.37), channel_id=1, source_target_pairs={{0,2},{2,4},{4,6},{1,3},{3,5},{5,7},{8,10},{10,12},{12,14},{9,11},... | collective-permute-start | bytes 36872 | tf_op jit(solution)/shard_map/ppermute | solution.py:28
  19.8 5.6 %collective-permute-start.3 = (f32[12,2,128]{2,0,1:T(8,128)S(1)}, f32[12,2,128]{2,0,1:T(8,128)S(1)}, u32[]{:S(2)}, u32[]{:S(2)}) collective-permute-start(f32[12,2,128]{2,0,1:T(8,128)S(1)} %get-tuple-element.38), channel_id=1, source_target_pairs={{2,0},{4,2},{6,4},{3,1},{5,3},{7,5},{10,8},{12,10},{14,12},{11,9},... | collective-permute-start | bytes 36872 | tf_op jit(solution)/shard_map/ppermute | solution.py:29
  25.5 4.7 %collective-permute-start.4 = (f32[12,12,2]{2,0,1:T(8,128)S(1)}, f32[12,12,2]{2,0,1:T(8,128)S(1)}, u32[]{:S(2)}, u32[]{:S(2)}) collective-permute-start(f32[12,12,2]{2,0,1:T(8,128)S(1)} %get-tuple-element.30), channel_id=1, source_target_pairs={{0,1},{2,3},{4,5},{6,7},{8,9},{10,11},{12,13},{14,15},{16,17},{18,... | collective-permute-start | bytes 3464 | tf_op jit(solution)/shard_map/ppermute | solution.py:28
  26.8 3.4 %collective-permute-start.5 = (f32[12,12,2]{2,0,1:T(8,128)S(1)}, f32[12,12,2]{2,0,1:T(8,128)S(1)}, u32[]{:S(2)}, u32[]{:S(2)}) collective-permute-start(f32[12,12,2]{2,0,1:T(8,128)S(1)} %get-tuple-element.31), channel_id=1, source_target_pairs={{1,0},{3,2},{5,4},{7,6},{9,8},{11,10},{13,12},{15,14},{17,16},{19,... | collective-permute-start | bytes 3464 | tf_op jit(solution)/shard_map/ppermute | solution.py:29
  28.5 6.5 %copy-start = (f32[1,10,10,1,1,16]{2,1,5,4,3,0:T(8,128)}, f32[1,10,10,1,1,16]{2,1,5,4,3,0:T(8,128)S(1)}, u32[]{:S(2)}) copy-start(f32[1,10,10,1,1,16]{2,1,5,4,3,0:T(8,128)S(1)} %copy.79) | copy-start | bytes 19204
  37.6 1.7 %copy-start.2 = (f32[1,10,10,1,1,16]{2,1,5,4,3,0:T(8,128)S(1)}, f32[1,10,10,1,1,16]{2,1,5,4,3,0:T(8,128)}, u32[]{:S(2)}) copy-start(f32[1,10,10,1,1,16]{2,1,5,4,3,0:T(8,128)} %copy.80) | copy-start | bytes 19204
  39.3 1.3 %copy-start.5 = (f32[1,10,10,1,1,16]{2,1,5,4,3,0:T(8,128)S(1)}, f32[1,10,10,1,1,16]{2,1,5,4,3,0:T(8,128)}, u32[]{:S(2)}) copy-start(f32[1,10,10,1,1,16]{2,1,5,4,3,0:T(8,128)} %copy.81) | copy-start | bytes 19204
  40.5 2.2 %copy-start.7 = (f32[10,10,16]{1,0,2:T(8,128)S(1)}, f32[10,10,16]{1,0,2:T(8,128)}, u32[]{:S(2)}) copy-start(f32[10,10,16]{1,0,2:T(8,128)} %broadcast_add_fusion) | copy-start | bytes 19204
  42.8 1.7 %copy-start.3 = (f32[1,10,10,1,1,16]{2,1,5,4,3,0:T(8,128)S(1)}, f32[1,10,10,1,1,16]{2,1,5,4,3,0:T(8,128)}, u32[]{:S(2)}) copy-start(f32[1,10,10,1,1,16]{2,1,5,4,3,0:T(8,128)} %copy.80) | copy-start | bytes 19204
  46.7 1.6 %copy-start.1 = (f32[1,10,10,1,1,16]{2,1,5,4,3,0:T(8,128)S(1)}, f32[1,10,10,1,1,16]{2,1,5,4,3,0:T(8,128)}, u32[]{:S(2)}) copy-start(f32[1,10,10,1,1,16]{2,1,5,4,3,0:T(8,128)} %copy-done) | copy-start | bytes 19204
  49.8 6.6 %collective-permute-start.6 = (f32[2,10,160]{2,0,1:T(2,128)S(1)}, f32[2,10,160]{2,0,1:T(2,128)S(1)}, u32[]{:S(2)}, u32[]{:S(2)}) collective-permute-start(f32[2,10,160]{2,0,1:T(2,128)S(1)} %slice.206), channel_id=1, source_target_pairs={{0,8},{8,16},{16,24},{1,9},{9,17},{17,25},{2,10},{10,18},{18,26},{... | collective-permute-start | bytes 38408 | tf_op jit(solution)/shard_map/ppermute | solution.py:28
  55.2 6.0 %collective-permute-start.7 = (f32[2,10,160]{2,1,0:T(8,128)S(1)}, f32[2,10,160]{2,1,0:T(8,128)S(1)}, u32[]{:S(2)}, u32[]{:S(2)}) collective-permute-start(f32[2,10,160]{2,1,0:T(8,128)S(1)} %reshape.264), channel_id=1, source_target_pairs={{8,0},{16,8},{24,16},{9,1},{17,9},{25,17},{10,2},{18,10},{26,18},{... | collective-permute-start | bytes 38408 | tf_op jit(solution)/shard_map/ppermute | solution.py:29
  61.2 5.0 %collective-permute-start.8 = (f32[14,2,160]{2,1,0:T(2,128)S(1)}, f32[14,2,160]{2,1,0:T(2,128)S(1)}, u32[]{:S(2)}, u32[]{:S(2)}) collective-permute-start(f32[14,2,160]{2,1,0:T(2,128)S(1)} %get-tuple-element.12), channel_id=1, source_target_pairs={{0,2},{2,4},{4,6},{1,3},{3,5},{5,7},{8,10},{10,12},{12,14},{9,11},... | collective-permute-start | bytes 53768 | tf_op jit(solution)/shard_map/ppermute | solution.py:28
  64.7 5.8 %collective-permute-start.9 = (f32[14,2,160]{2,1,0:T(2,128)S(1)}, f32[14,2,160]{2,1,0:T(2,128)S(1)}, u32[]{:S(2)}, u32[]{:S(2)}) collective-permute-start(f32[14,2,160]{2,1,0:T(2,128)S(1)} %get-tuple-element.13), channel_id=1, source_target_pairs={{2,0},{4,2},{6,4},{3,1},{5,3},{7,5},{10,8},{12,10},{14,12},{11,9},... | collective-permute-start | bytes 53768 | tf_op jit(solution)/shard_map/ppermute | solution.py:29
  70.7 2.7 %collective-permute-start.10 = (f32[14,14,2]{2,1,0:T(8,128)S(1)}, f32[14,14,2]{2,1,0:T(8,128)S(1)}, u32[]{:S(2)}, u32[]{:S(2)}) collective-permute-start(f32[14,14,2]{2,1,0:T(8,128)S(1)} %get-tuple-element.10), channel_id=1, source_target_pairs={{0,1},{2,3},{4,5},{6,7},{8,9},{10,11},{12,13},{14,15},{16,17},{18,... | collective-permute-start | bytes 4712 | tf_op jit(solution)/shard_map/ppermute | solution.py:28
  72.0 3.2 %collective-permute-start.11 = (f32[14,14,2]{2,1,0:T(8,128)S(1)}, f32[14,14,2]{2,1,0:T(8,128)S(1)}, u32[]{:S(2)}, u32[]{:S(2)}) collective-permute-start(f32[14,14,2]{2,1,0:T(8,128)S(1)} %get-tuple-element.11), channel_id=1, source_target_pairs={{1,0},{3,2},{5,4},{7,6},{9,8},{11,10},{13,12},{15,14},{17,16},{19,... | collective-permute-start | bytes 4712 | tf_op jit(solution)/shard_map/ppermute | solution.py:29
where the time goes:
time: 78.8 us; the launch traced here: 78.2 us
  starting transfers between devices  26.6 us (34%)
  waiting for transfers between devices  18.6 us (24%)
  matrix products  14.5 us (18%)
  local copies, waits for them, and re-layouts  14.4 us (18%)
  other arithmetic  3.36 us (4%)
    ppermute x6, starting transfers between devices, extended_2(): before = lax.ppermute(last, axis, up)  18.7 us
    ppermute x6, waiting for transfers between devices, extended_2(): after = lax.ppermute(first, axis, down)  18.2 us
    ppermute x6, starting transfers between devices, extended_2(): after = lax.ppermute(first, axis, down)  7.93 us
    another operation x3, local copies, waits for them, and re-layouts  3.76 us
    dot_general x6, matrix products, apply_along(): jnp.tensordot(values.reshape(pieces_shape), matrix, axes=((direction + 1,...  3.32 us
    dot_general x1, matrix products, fast_solve(): jnp.einsum('apxyz,xaybzc->xpybzc', eigenvectors[0], spectral, precision=p...  2.6 us
    dot_general x1, matrix products, fast_solve(): jnp.einsum('bqxyz,xpyqzc->xpybzc', eigenvectors[1], spectral, precision=p...  2.23 us
    dot_general x1, matrix products, fast_solve(): jnp.einsum('csxyz,xpyqzc->xpyqzs', eigenvectors[2], spectral, precision=p...  2.21 us
  transfers between devices with their start and end apart: 12, of which 7 were waited for; matrix products, arithmetic and copies ran while one was open for 5% of the time, Pallas kernels for 0%

commit v1 on v0

--- a/solution.py
+++ b/solution.py
@@ -1,7 +1,12 @@
+import functools
+
 import jax
 import jax.numpy as jnp
+import ml_dtypes
 import numpy as np
 from jax import lax
+from jax.experimental import pallas as pl
+from jax.experimental.pallas import tpu as pltpu
 from jax.sharding import PartitionSpec as P
 
 gll_points = np.array(
@@ -155,7 +160,7 @@
     return jnp.moveaxis(summed.reshape((blocks * 8,) + trailing), 0, direction)
 
 
-def body(initial, source, metric, eigenvectors, eigenvalues):
+def general_body(initial, source, metric, eigenvectors, eigenvalues):
     solution = initial
     local_res = source - apply_operator(solution, metric)
     deeper = extended_2(local_res, (("gx", 0), ("gy", 1), ("gz", 2)), 2)
@@ -168,6 +173,426 @@
     return solution
 
 
+AXES = ("gx", "gy", "gz")
+VMEM = pl.BlockSpec(memory_space=pltpu.VMEM)
+VMEM_LIMIT = 16 * 2**20
+f32 = jnp.float32
+bf16 = jnp.bfloat16
+
+
+def call(kernel, outs, args, flops=0, scratch=()):
+    moved = sum(int(np.prod(a.shape)) * a.dtype.itemsize for a in (*args, *outs))
+    return pl.pallas_call(
+        kernel,
+        out_shape=outs,
+        in_specs=[VMEM] * len(args),
+        out_specs=[VMEM] * len(outs),
+        scratch_shapes=scratch,
+        compiler_params=pltpu.CompilerParams(vmem_limit_bytes=VMEM_LIMIT),
+        cost_estimate=pl.CostEstimate(flops=flops, bytes_accessed=moved, transcendentals=0),
+    )(*args)
+
+
+def shaped(shape, dtype=f32):
+    return jax.ShapeDtypeStruct(shape, dtype)
+
+
+def split2(value):
+    high = value.astype(bf16)
+    return high, (value - high.astype(f32)).astype(bf16)
+
+
+def split3(value):
+    high = value.astype(bf16)
+    rest = value - high.astype(f32)
+    middle = rest.astype(bf16)
+    return high, middle, (rest - middle.astype(f32)).astype(bf16)
+
+
+def table_split2(table):
+    table = np.asarray(table, np.float32)
+    high = table.astype(ml_dtypes.bfloat16)
+    return high, (table - high.astype(np.float32)).astype(ml_dtypes.bfloat16)
+
+
+def dot(left, right, transposed=False):
+    dims = (((1,), (1 if transposed else 0,)), ((), ()))
+    return lax.dot_general(left, right, dims, preferred_element_type=f32)
+
+
+def operator_tables(count_y, length_z):
+    table = np.asarray(derivative_table(), np.float32)
+    nodes = table.shape[0]
+    along_y = np.kron(np.eye(nodes), table)
+    along_z = np.kron(np.eye(length_z // nodes), table.T)
+    tables = []
+    for matrix in (along_y, along_y.T):
+        high, low = table_split2(matrix)
+        tables.append(np.concatenate([high, high, low], axis=1))
+    for matrix in (along_z, along_z.T):
+        high, low = table_split2(matrix)
+        tables.append(np.concatenate([high, high, low], axis=0))
+    return [jnp.asarray(t) for t in tables]
+
+
+def residual_kernel(u_ref, source_ref, metric_ref, ay, ayt, bz, bzt, out_ref):
+    nodes, rows, width = u_ref.shape
+    table = np.asarray(derivative_table(), np.float32)
+
+    def stacked(value, axis):
+        high, low = split2(value)
+        return jnp.concatenate([high, low, high], axis=axis)
+
+    flat = u_ref[...].reshape(nodes * rows, width)
+    along_y = dot(ay[...], stacked(flat, 0)) * metric_ref[1].reshape(flat.shape)
+    along_z = dot(stacked(flat, 1), bz[...]) * metric_ref[2].reshape(flat.shape)
+    total = dot(ayt[...], stacked(along_y, 0)) + dot(stacked(along_z, 1), bzt[...])
+    total = total.reshape(nodes, rows, width)
+    layers = [u_ref[j] for j in range(nodes)]
+    fluxes = []
+    for i in range(nodes):
+        gradient = sum(float(table[i, j]) * layers[j] for j in range(nodes))
+        fluxes.append(metric_ref[0, i] * gradient)
+    for j in range(nodes):
+        applied = sum(float(table[i, j]) * fluxes[i] for i in range(nodes))
+        out_ref[j] = source_ref[j] - (applied + total[j])
+
+
+def spread_tables(blocks, ext):
+    lanes = np.arange(blocks * ext)
+    repeat = (lanes[None, :] // ext == np.arange(blocks)[:, None]).astype(np.float32)
+    repeat = np.concatenate([repeat] * 3, axis=0)
+    rows = np.arange(ext * ext)
+    mask = (rows[:, None] % ext == lanes[None, :] % ext).astype(np.float32)
+    gather = (rows[None, :] // ext == np.arange(ext)[:, None]).astype(np.float32)
+    gather = np.concatenate([gather] * 3, axis=1)
+    padded = 2 * (ext - 2)
+    order = list(range(1, ext - 1)) + [0, ext - 1]
+    forward = np.zeros((ext, padded, ext * ext), np.float32)
+    backward = np.zeros((ext, padded, ext * ext), np.float32)
+    for first in range(ext):
+        for second in range(ext):
+            forward[first, second, first * ext + second] = 1
+            backward[first, second, order[second] * ext + first] = 1
+    both = np.concatenate([forward.reshape(-1, ext * ext), backward.reshape(-1, ext * ext)])
+    both = np.concatenate([both] * 3, axis=1)
+    return [
+        jnp.asarray(repeat, bf16),
+        jnp.asarray(mask),
+        jnp.asarray(gather, bf16),
+        jnp.asarray(both, bf16),
+    ]
+
+
+def coefficients_kernel(
+    vec_ref, val_ref, repeat, mask, gather, both, after_ref, cx_ref, cy_ref, rate_ref, mz_ref
+):
+    ext = rate_ref.shape[0]
+    square = ext * ext
+    padded, lanes = rate_ref.shape[1:]
+    blocks = lanes // ext
+    nodes = ext - 2
+    core = lax.axis_index("gz")
+
+    def spread(ref, first, count):
+        value = ref[first : first + count].reshape(count, blocks)
+        return dot(jnp.concatenate(split3(value), axis=1), repeat[...])
+
+    cx_ref[...] = spread(vec_ref, 0, square)
+    along_y = spread(vec_ref, square, square)
+    cy_ref[...] = dot(both[...], jnp.concatenate(split3(along_y), axis=0)).reshape(cy_ref.shape)
+    along_z = spread(vec_ref, 2 * square, square) * mask[...]
+    along_z = dot(gather[...], jnp.concatenate(split3(along_z), axis=0))
+
+    rate_x = spread(val_ref, 0, ext)
+    rate_y = spread(val_ref, ext, ext)
+    rate_z = jnp.sum(spread(val_ref, 2 * ext, ext) * mask[0:ext, :], axis=0, keepdims=True)
+    rate_y = jnp.concatenate([rate_y, jnp.ones((padded - ext, lanes), f32)], axis=0)
+    for p in range(ext):
+        rate_ref[p] = 1.0 / (rate_x[p : p + 1] + rate_y + rate_z)
+
+    zeros = jnp.zeros((nodes - 2, lanes), f32)
+    own = along_z[1 : nodes + 1]
+    below = jnp.concatenate([zeros, along_z[0:2]], axis=0)
+    above = jnp.concatenate([along_z[nodes : nodes + 2], zeros], axis=0)
+    element = lax.broadcasted_iota(jnp.int32, (nodes, lanes), 1) // ext
+    zero = jnp.zeros_like(own)
+    for half in range(2):
+        shift = 0 if half == 0 else jnp.where(core == 0, blocks, -blocks)
+        for first in range(0, blocks, 2):
+            pair = []
+            for block in (first + shift, first + 1 + shift):
+                value = jnp.where(element == block, own, zero)
+                value = value + jnp.where(element == block + 1, below, zero)
+                pair.append(value + jnp.where(element == block - 1, above, zero))
+            high, low = split2(jnp.concatenate(pair, axis=0))
+            start = (half * blocks + first) * nodes
+            mz_ref[0, start : start + 2 * nodes, :] = high
+            mz_ref[1, start : start + 2 * nodes, :] = low
+
+
+def both_sides(core, direct, passed):
+    low = [jnp.where(core == 0, direct[h], passed[1 - h]) for h in range(2)]
+    high = [jnp.where(core == 0, passed[1 - h], direct[h]) for h in range(2)]
+    return low, high
+
+
+def edges(axis):
+    place, size = lax.axis_index(axis), lax.axis_size(axis)
+    return place > 0, place < size - 1
+
+
+def layers_kernel(own_ref, partner_ref, out_ref):
+    start = lax.axis_index("gz") * (own_ref.shape[0] - 2)
+    for half, ref in enumerate((partner_ref, own_ref)):
+        for layer in range(2):
+            out_ref[half, layer] = ref[start + layer]
+
+
+def x_layers(core, own_ref, partner_ref, direct_ref, passed_ref):
+    has_low, has_high = edges("gx")
+    length = own_ref.shape[0]
+
+    def at(layer):
+        if 2 <= layer < length + 2:
+            return own_ref[layer - 2], partner_ref[layer - 2]
+        slot = layer if layer < 2 else layer - length - 2
+        direct = [direct_ref[h, slot] for h in range(2)]
+        passed = [passed_ref[h, slot] for h in range(2)]
+        low, high = both_sides(core, direct, passed)
+        side, valid = (low, has_low) if layer < 2 else (high, has_high)
+        return [jnp.where(valid, v, jnp.zeros_like(v)) for v in side]
+
+    return at
+
+
+def rows_kernel(own_ref, partner_ref, direct_ref, passed_ref, out_ref):
+    core = lax.axis_index("gz")
+    length, rows, _ = own_ref.shape
+    at = x_layers(core, own_ref, partner_ref, direct_ref, passed_ref)
+    for layer in range(length + 4):
+        own, partner = at(layer)
+        for half, value in enumerate((partner, own)):
+            row = layer * 4 + half * 2
+            out_ref[row // 8, row % 8 : row % 8 + 2, :] = jnp.where(
+                core == 0, value[0:2], value[rows - 2 : rows]
+            )
+
+
+def solve_kernel(
+    own_ref, partner_ref, xd_ref, xp_ref, yd_ref, yp_ref, cx, cy, rate, mz, out_ref, grid, spectral
+):
+    core = lax.axis_index("gz")
+    length, rows, width = own_ref.shape
+    ext, padded, lanes = rate.shape
+    has_low, has_high = edges("gy")
+    at = x_layers(core, own_ref, partner_ref, xd_ref, xp_ref)
+    nothing = jnp.zeros((padded - rows - 4, width), f32)
+    for layer in range(length + 4):
+        place, row = divmod(layer * 4, 8)
+        direct = [yd_ref[place, row + 2 * h : row + 2 * h + 2, :] for h in range(2)]
+        passed = [yp_ref[place, row + 2 * h : row + 2 * h + 2, :] for h in range(2)]
+        low, high = both_sides(core, direct, passed)
+        for half, value in enumerate(at(layer)):
+            before = jnp.where(has_low, low[half], jnp.zeros_like(low[half]))
+            after = jnp.where(has_high, high[half], jnp.zeros_like(high[half]))
+            at_lanes = slice(half * width, (half + 1) * width)
+            grid[layer, 0:rows, at_lanes] = value
+            grid[layer, rows:padded, at_lanes] = jnp.concatenate([before, after, nothing], axis=0)
+
+    high, low = split2(grid[...].reshape((length + 4) * padded, 2 * width))
+    along_z = dot(high, mz[0]) + (dot(low, mz[0]) + dot(high, mz[1]))
+    along_z = along_z.reshape(length + 4, padded, lanes)
+    block = [along_z[0], along_z[1] + along_z[2]]
+    block += [along_z[k] for k in range(3, length + 1)]
+    block += [along_z[length + 1] + along_z[length + 2], along_z[length + 3]]
+
+    places = [(rows,), (rows + 1, 0)] + [(k,) for k in range(1, rows - 1)]
+    places += [(rows - 1, rows + 2), (rows + 3,)]
+    for p in range(ext):
+        value = sum(cx[a * ext + p : a * ext + p + 1, :] * block[a] for a in range(ext))
+        total = None
+        for b in range(ext):
+            row = sum(value[k : k + 1] for k in places[b])
+            term = cy[0, b] * row
+            total = term if total is None else total + term
+        total = total * rate[p]
+        spectral[p] = sum(cy[1, q] * total[q : q + 1] for q in range(ext))
+    back = []
+    for a in range(ext):
+        back.append(sum(cx[a * ext + p : a * ext + p + 1, :] * spectral[p] for p in range(ext)))
+    high, low = split2(jnp.concatenate(back, axis=0))
+    result = dot(high, mz[0], True) + (dot(low, mz[0], True) + dot(high, mz[1], True))
+    out_ref[...] = result.reshape(out_ref.shape)
+
+
+def totals(layer, mine_ref, other_ref, width, rows=slice(None)):
+    own = mine_ref[layer, rows, 0:width] + other_ref[layer, rows, width:]
+    partner = mine_ref[layer, rows, width:] + other_ref[layer, rows, 0:width]
+    return own, partner
+
+
+def return_layers_kernel(mine_ref, other_ref, out_ref):
+    ext, padded, width = mine_ref.shape
+    nodes, width = ext - 2, width // 2
+    start = lax.axis_index("gz") * nodes
+    for layer in range(2):
+        own, partner = totals(start + layer, mine_ref, other_ref, width)
+        for half, value in enumerate((partner, own)):
+            place = half * 2 + layer
+            out_ref[place] = value[0:nodes]
+            out_ref[4, 2 * place : 2 * place + 2, :] = value[nodes : nodes + 2]
+
+
+def interior_kernel(mine_ref, other_ref, after_ref, out_ref):
+    ext, padded, width = mine_ref.shape
+    for layer in range(1, ext - 1):
+        own, partner = totals(layer, mine_ref, other_ref, width // 2)
+        out_ref[0, layer - 1] = own
+        out_ref[1, layer - 1] = partner
+
+
+def return_rows_kernel(initial_ref, inner_ref, direct_ref, passed_ref, out_ref, base_ref):
+    core = lax.axis_index("gz")
+    has_low, has_high = edges("gx")
+    nodes, rows, _ = initial_ref.shape
+    for layer in range(nodes):
+        values = [inner_ref[h, layer] for h in range(2)]
+        outer = [values[h][rows : rows + 2] for h in range(2)]
+        values = [values[h][0:rows] for h in range(2)]
+        if layer < 2 or layer >= nodes - 2:
+            slot = layer if layer < 2 else layer - (nodes - 2)
+
+            def parts(ref, h, slot=slot):
+                place = 2 * h + slot
+                return ref[place], ref[4, 2 * place : 2 * place + 2, :]
+
+            direct = [parts(direct_ref, h) for h in range(2)]
+            passed = [parts(passed_ref, h) for h in range(2)]
+            side = 0 if layer < 2 else 1
+            valid = (has_low, has_high)[side]
+            for k, target in enumerate((values, outer)):
+                both = both_sides(core, [d[k] for d in direct], [d[k] for d in passed])[side]
+                for h in range(2):
+                    target[h] = target[h] + jnp.where(valid, both[h], jnp.zeros_like(both[h]))
+        base_ref[layer] = initial_ref[layer] + values[0]
+        for place, h in enumerate((1, 0)):
+            row = layer * 4 + place * 2
+            first = jnp.where(core == 0, outer[h][0:1], values[h][rows - 1 : rows])
+            second = jnp.where(core == 0, values[h][0:1], outer[h][1:2])
+            out_ref[row // 8, row % 8 : row % 8 + 1, :] = first
+            out_ref[row // 8, row % 8 + 1 : row % 8 + 2, :] = second
+
+
+def result_kernel(base_ref, direct_ref, passed_ref, out_ref):
+    core = lax.axis_index("gz")
+    has_low, has_high = edges("gy")
+    nodes, rows, _ = base_ref.shape
+    for layer in range(nodes):
+        place, row = divmod(layer * 4, 8)
+        direct = direct_ref[place, row : row + 2, :]
+        passed = passed_ref[place, row + 2 : row + 4, :]
+        low = jnp.where(core == 0, direct, passed)
+        high = jnp.where(core == 0, passed, direct)
+        low = jnp.where(has_low, low, jnp.zeros_like(low))
+        high = jnp.where(has_high, high, jnp.zeros_like(high))
+        between = jnp.zeros((rows - 4, low.shape[1]), f32)
+        out_ref[layer] = base_ref[layer] + jnp.concatenate([low, between, high], axis=0)
+
+
+def swap_pairs(axis):
+    sizes = [lax.axis_size(name) for name in AXES]
+    along, across = (0, 1) if axis == "gx" else (1, 0)
+
+    def number(place, other, core):
+        spot = (place, other) if along == 0 else (other, place)
+        return (spot[0] * sizes[1] + spot[1]) * 2 + core
+
+    pairs = []
+    for other in range(sizes[across]):
+        for place in range(sizes[along] - 1):
+            here, there = number(place, other, 1), number(place + 1, other, 0)
+            pairs += [(here, there), (there, here)]
+        if other ^ 1 < sizes[across]:
+            for place, core in ((0, 0), (sizes[along] - 1, 1)):
+                pairs.append((number(place, other, core), number(place, other ^ 1, core)))
+    return pairs
+
+
+def swap(value, axis):
+    if axis == "gz":
+        return lax.ppermute(value, "gz", [(0, 1), (1, 0)])
+    return lax.ppermute(value, AXES, swap_pairs(axis))
+
+
+def paired_body(initial, source, metric, eigenvectors, eigenvalues):
+    nodes, rows, width = initial.shape
+    ext = eigenvectors.shape[1]
+    blocks = width // nodes
+    lanes = blocks * ext
+    padded = 2 * rows
+
+    own = call(
+        residual_kernel,
+        [shaped(initial.shape)],
+        [initial, source, metric, *operator_tables(rows, width)],
+    )[0]
+    vectors = eigenvectors.reshape(3 * ext * ext, 1, blocks)
+    values = eigenvalues.reshape(3 * ext, 1, blocks)
+    cx, cy, rate, mz = call(
+        coefficients_kernel,
+        [
+            shaped((ext * ext, lanes)),
+            shaped((2, ext, padded, lanes)),
+            shaped((ext, padded, lanes)),
+            shaped((2, 2 * width, lanes), bf16),
+        ],
+        [vectors, values, *spread_tables(blocks, ext), own],
+    )
+    partner = swap(own, "gz")
+    sent = call(layers_kernel, [shaped((2, 2, rows, width))], [own, partner])[0]
+    x_direct = swap(sent, "gx")
+    x_passed = swap(x_direct, "gz")
+    sent = call(
+        rows_kernel,
+        [shaped(((nodes + 4) * 4 // 8, 8, width))],
+        [own, partner, x_direct, x_passed],
+    )[0]
+    y_direct = swap(sent, "gy")
+    y_passed = swap(y_direct, "gz")
+    mine = call(
+        solve_kernel,
+        [shaped((ext, padded, 2 * width))],
+        [own, partner, x_direct, x_passed, y_direct, y_passed, cx, cy, rate, mz],
+        scratch=[
+            pltpu.VMEM((nodes + 4, padded, 2 * width), f32),
+            pltpu.VMEM((ext, padded, lanes), f32),
+        ],
+    )[0]
+
+    other = swap(mine, "gz")
+    sent = call(return_layers_kernel, [shaped((5, rows, width))], [mine, other])[0]
+    inner = call(interior_kernel, [shaped((2, nodes, padded, width))], [mine, other, sent])[0]
+    x_direct = swap(sent, "gx")
+    x_passed = swap(x_direct, "gz")
+    sent, base = call(
+        return_rows_kernel,
+        [shaped((nodes * 4 // 8, 8, width)), shaped(initial.shape)],
+        [initial, inner, x_direct, x_passed],
+    )
+    y_direct = swap(sent, "gy")
+    y_passed = swap(y_direct, "gz")
+    return call(result_kernel, [shaped(initial.shape)], [base, y_direct, y_passed])[0]
+
+
+def body(initial, source, metric, eigenvectors, eigenvalues):
+    nodes = gll_points.shape[0]
+    one_element = initial.shape[0] == nodes and initial.shape[1] == nodes
+    if lax.axis_size("gz") == 2 and one_element and initial.shape[2] % 128 == 0:
+        return paired_body(initial, source, metric, eigenvectors, eigenvalues)
+    return general_body(initial, source, metric, eigenvectors, eigenvalues)
+
+
 def solution(mesh):
     placed = (
         P("gx", "gy", "gz"),

time: 78.8 us -> 32.6 us (0.41)
  starting transfers between devices: 26.6 us -> 10.2 us
  matrix products: 14.5 us -> 0 us
  local copies, waits for them, and re-layouts: 14.4 us -> 5.78 us
  waiting for transfers between devices: 18.6 us -> 12.9 us
  other arithmetic: 3.36 us -> 0 us
  Pallas kernels: 0 us -> 3.19 us
    ppermute x12 -> x10, starting transfers between devices: 26.6 us -> 10.2 us  [the longest x4 9 us: swap(): return lax.ppermute(value, AXES, swap_pairs(axis))]
    dot_general x12 -> x0, matrix products: 14.5 us -> none  [the longest x6 3.32 us: apply_along(): jnp.tensordot(values.reshape(pieces_shape), matrix, axes=((direction + 1,...]
    ppermute x12 -> x10, waiting for transfers between devices: 18.6 us -> 12.9 us  [the longest x4 7.58 us: swap(): return lax.ppermute(value, AXES, swap_pairs(axis))]
    unnamed x29 -> x28, local copies, waits for them, and re-layouts: 1.84 us -> 5.78 us
    reshape x13 -> x0, local copies, waits for them, and re-layouts: 3.8 us -> none  [the longest x1 1.05 us: apply_along(): values.reshape(pieces_shape)]
    another operation x3 -> x0, local copies, waits for them, and re-layouts: 3.76 us -> none
    pallas_call x0 -> x9, Pallas kernels: none -> 3.19 us  [call(): pl.pallas_call(kernel, out_shape=outs, in_specs=[VMEM] * len(args), out_s...]
    slice x25 -> x0, local copies, waits for them, and re-layouts: 2.55 us -> none  [the longest x1 0.78 us: apply_operator(): metric[direction] * gradient]
  transfers between devices with their start and end apart: 12 -> 10, of which waited for: 7 -> 9; matrix products, arithmetic and copies ran while one was open for 5% -> 0% of each run, Pallas kernels for 0% -> 4%
where the time goes in v1:
time: 32.6 us; the launch traced here: 32.2 us
  waiting for transfers between devices  12.9 us (40%)
  starting transfers between devices  10.2 us (31%)
  local copies, waits for them, and re-layouts  5.78 us (18%)
  Pallas kernels  3.19 us (10%)
    ppermute x4, starting transfers between devices, swap(): return lax.ppermute(value, AXES, swap_pairs(axis))  9 us
    ppermute x4, waiting for transfers between devices, swap(): return lax.ppermute(value, AXES, swap_pairs(axis))  7.58 us
    unnamed x28, local copies, waits for them, and re-layouts  5.78 us
    ppermute x6, waiting for transfers between devices, swap(): return lax.ppermute(value, 'gz', [(0, 1), (1, 0)])  5.28 us
    pallas_call x9, Pallas kernels, call(): pl.pallas_call(kernel, out_shape=outs, in_specs=[VMEM] * len(args), out_s...  3.19 us
    ppermute x6, starting transfers between devices, swap(): return lax.ppermute(value, 'gz', [(0, 1), (1, 0)])  1.24 us
  transfers between devices with their start and end apart: 10, of which 9 were waited for; matrix products, arithmetic and copies ran while one was open for 0% of the time, Pallas kernels for 4%

profile of v1, /device:TPU:0, one launch (start us, length us, event | category | flops | bytes accessed | tf_op | source)
XLA Modules:
  0.0 32.2 jit_solution(18225209945254866700)
XLA Ops:
  0.0 0.0 copy-start
  0.0 0.0 copy-start.2
  0.0 0.8 %copy-done.2 = f32[8,8,128]{2,1,0:T(8,128)S(1)} copy-done((f32[8,8,128]{2,1,0:T(8,128)S(1)}, f32[8,8,128]{2,1,0:T(8,128)}, u32[]{:S(2)}) %copy-start.2) | copy-done | bytes 32792
  0.8 0.0 copy-start.5
  0.8 0.9 %copy-done.5 = f32[3,8,8,128]{3,2,1,0:T(8,128)S(1)} copy-done((f32[3,8,8,128]{3,2,1,0:T(8,128)S(1)}, f32[3,8,8,128]{3,2,1,0:T(8,128)}, u32[]{:S(2)}) %copy-start.5) | copy-done | bytes 98328
  1.7 0.0 copy-start.6
  1.7 0.9 %copy-done.6 = bf16[384,128]{1,0:T(8,128)(2,1)S(1)} copy-done((bf16[384,128]{1,0:T(8,128)(2,1)S(1)}, bf16[384,128]{1,0:T(8,128)(2,1)}, u32[]{:S(2)}) %copy-start.6) | copy-done | bytes 98328
  2.6 0.0 copy-start.7
  2.6 0.9 %copy-done.7 = bf16[384,128]{1,0:T(8,128)(2,1)S(1)} copy-done((bf16[384,128]{1,0:T(8,128)(2,1)S(1)}, bf16[384,128]{1,0:T(8,128)(2,1)}, u32[]{:S(2)}) %copy-start.7) | copy-done | bytes 98328
  3.5 0.0 copy-start.8
  3.5 0.8 %copy-done.8 = f32[8,8,128]{2,1,0:T(8,128)S(1)} copy-done((f32[8,8,128]{2,1,0:T(8,128)S(1)}, f32[8,8,128]{2,1,0:T(8,128)}, u32[]{:S(2)}) %copy-start.8) | copy-done | bytes 32792
  4.2 0.0 copy-start.9
  4.2 0.8 %copy-done.9 = bf16[64,192]{1,0:T(8,128)(2,1)S(1)} copy-done((bf16[64,192]{1,0:T(8,128)(2,1)S(1)}, bf16[64,192]{1,0:T(8,128)(2,1)}, u32[]{:S(2)}) %copy-start.9) | copy-done | bytes 24600
  5.0 0.0 copy-start.10
  5.0 0.8 %copy-done.10 = bf16[64,192]{1,0:T(8,128)(2,1)S(1)} copy-done((bf16[64,192]{1,0:T(8,128)(2,1)S(1)}, bf16[64,192]{1,0:T(8,128)(2,1)}, u32[]{:S(2)}) %copy-start.10) | copy-done | bytes 24600
  5.8 0.0 copy-start.4
  5.8 0.3 %shard_map.127.own_ref.after_ref = f32[8,8,128]{2,1,0:T(8,128)S(1)} custom-call(f32[8,8,128]{2,1,0:T(8,128)S(1)} %copy-done.2, f32[8,8,128]{2,1,0:T(8,128)S(1)} %copy-done.8, f32[3,8,8,128]{3,2,1,0:T(8,128)S(1)} %copy-done.5, bf16[64,192]{1,0:T(8,128)(2,1)S(1)} %copy-done.10, bf16[64,192]{1,0:T(8,128)(2,1)S(1)} %copy-done.9, bf16[384,128]{1,0:T(8,128)(2,1)S(1)} %copy-done.7, ...), custom_call_target="tpu_custom_call" | custom-call | bytes 442368 | tf_op jit(solution)/shard_map/pallas_call | solution.py:185
  6.1 0.0 copy-start.1
  6.1 0.5 %collective-permute-start = (f32[8,8,128]{2,1,0:T(8,128)S(1)}, f32[8,8,128]{2,1,0:T(8,128)S(1)}, u32[]{:S(2)}, u32[]{:S(2)}) collective-permute-start(f32[8,8,128]{2,1,0:T(8,128)S(1)} %shard_map.127.own_ref.after_ref), channel_id=1, source_target_pairs={{0,1},{1,0},{2,3},{3,2},{4,5},{5,4},{6,7},{7,6},{8,9},{9,8},{10,11... | collective-permute-start | bytes 98312 | tf_op jit(solution)/shard_map/ppermute | solution.py:524
  6.6 0.9 %collective-permute-done.partner_ref = f32[8,8,128]{2,1,0:T(8,128)S(1)} collective-permute-done((f32[8,8,128]{2,1,0:T(8,128)S(1)}, f32[8,8,128]{2,1,0:T(8,128)S(1)}, u32[]{:S(2)}, u32[]{:S(2)}) %collective-permute-start) | collective-permute-done | bytes 32800 | tf_op jit(solution)/shard_map/ppermute | solution.py:524
  7.5 0.0 copy-start.11
  7.5 0.0 copy-start.12
  7.5 2.9 %collective-permute-start.1 = (f32[2,2,8,128]{3,2,1,0:T(8,128)S(1)}, f32[2,2,8,128]{3,2,1,0:T(8,128)S(1)}, u32[]{:S(2)}, u32[]{:S(2)}) collective-permute-start(f32[2,2,8,128]{3,2,1,0:T(8,128)S(1)} %shard_map.128), channel_id=1, source_target_pairs={{1,8},{8,1},{9,16},{16,9},{17,24},{24,17},{0,2},{25,27},{3,10},{10... | collective-permute-start | bytes 49160 | tf_op jit(solution)/shard_map/ppermute | solution.py:525
  10.4 1.7 %collective-permute-done.1.direct_ref.xd_ref = f32[2,2,8,128]{3,2,1,0:T(8,128)S(1)} collective-permute-done((f32[2,2,8,128]{3,2,1,0:T(8,128)S(1)}, f32[2,2,8,128]{3,2,1,0:T(8,128)S(1)}, u32[]{:S(2)}, u32[]{:S(2)}) %collective-permute-start.1) | collective-permute-done | bytes 16416 | tf_op jit(solution)/shard_map/ppermute | solution.py:525
  12.1 0.0 collective-permute-start.2
  12.2 1.2 %collective-permute-done.2.passed_ref.xp_ref = f32[2,2,8,128]{3,2,1,0:T(8,128)S(1)} collective-permute-done((f32[2,2,8,128]{3,2,1,0:T(8,128)S(1)}, f32[2,2,8,128]{3,2,1,0:T(8,128)S(1)}, u32[]{:S(2)}, u32[]{:S(2)}) %collective-permute-start.2) | collective-permute-done | bytes 16416 | tf_op jit(solution)/shard_map/ppermute | solution.py:524
  13.3 0.0 copy-start.13
  13.3 2.1 %collective-permute-start.3 = (f32[6,8,128]{2,1,0:T(8,128)S(1)}, f32[6,8,128]{2,1,0:T(8,128)S(1)}, u32[]{:S(2)}, u32[]{:S(2)}) collective-permute-start(f32[6,8,128]{2,1,0:T(8,128)S(1)} %shard_map.129), channel_id=1, source_target_pairs={{1,2},{2,1},{3,4},{4,3},{5,6},{6,5},{0,8},{7,15},{9,10},{10,9},{11... | collective-permute-start | bytes 73736 | tf_op jit(solution)/shard_map/ppermute | solution.py:525
  15.5 1.8 %collective-permute-done.3.yd_ref = f32[6,8,128]{2,1,0:T(8,128)S(1)} collective-permute-done((f32[6,8,128]{2,1,0:T(8,128)S(1)}, f32[6,8,128]{2,1,0:T(8,128)S(1)}, u32[]{:S(2)}, u32[]{:S(2)}) %collective-permute-start.3) | collective-permute-done | bytes 24608 | tf_op jit(solution)/shard_map/ppermute | solution.py:525
  17.3 0.1 collective-permute-start.4
  17.3 0.0 copy-done
  17.3 0.0 copy-done.4
  17.3 0.0 copy-done.1
  17.3 0.0 copy-done.11
  17.4 0.0 copy-done.12
  17.4 0.0 copy-done.13
  17.4 1.2 %shard_map.130 = (f32[100,160]{1,0:T(8,128)S(1)}, f32[2,10,16,160]{3,2,1,0:T(8,128)S(1)}, f32[10,16,160]{2,1,0:T(8,128)S(1)}, bf16[2,256,160]{2,1,0:T(8,128)(2,1)S(1)}) custom-call(f32[300,1,16]{2,1,0:T(1,128)S(1)} %bitcast.2, f32[30,1,16]{2,1,0:T(1,128)S(1)} %bitcast.3, bf16[48,160]{1,0:T(8,128)(2,1)S(1)} %copy-done.11, f32[100,160]{1,0:T(8,128)S(1)} %copy-done.4, ...), custom_call_target="tpu_custom_call" | custom-call | bytes 866288 | tf_op jit(solution)/shard_map/pallas_call | solution.py:185
  18.5 0.0 collective-permute-done.4.yp_ref
  18.6 1.0 %shard_map.131.mine_ref = f32[10,16,256]{2,1,0:T(8,128)S(1)} custom-call(f32[8,8,128]{2,1,0:T(8,128)S(1)} %shard_map.127.own_ref.after_ref, f32[8,8,128]{2,1,0:T(8,128)S(1)} %collective-permute-done.partner_ref, f32[2,2,8,128]{3,2,1,0:T(8,128)S(1)} %collective-permute-done.1.direct_ref.xd_ref, f32[2,2,8,128]{3,2,1,0:T(8,128)S(1)} %collective-permute-done.2.passed_ref.xp_ref, ...), custom_call_target="tpu_custom_call" | custom-call | bytes 846336 | tf_op jit(solution)/shard_map/pallas_call | solution.py:185
  19.6 0.5 %collective-permute-start.5 = (f32[10,16,256]{2,1,0:T(8,128)S(1)}, f32[10,16,256]{2,1,0:T(8,128)S(1)}, u32[]{:S(2)}, u32[]{:S(2)}) collective-permute-start(f32[10,16,256]{2,1,0:T(8,128)S(1)} %shard_map.131.mine_ref), channel_id=1, source_target_pairs={{0,1},{1,0},{2,3},{3,2},{4,5},{5,4},{6,7},{7,6},{8,9},{9,8},{10,11... | collective-permute-start | bytes 491528 | tf_op jit(solution)/shard_map/ppermute | solution.py:524
  20.1 1.0 %collective-permute-done.5.other_ref = f32[10,16,256]{2,1,0:T(8,128)S(1)} collective-permute-done((f32[10,16,256]{2,1,0:T(8,128)S(1)}, f32[10,16,256]{2,1,0:T(8,128)S(1)}, u32[]{:S(2)}, u32[]{:S(2)}) %collective-permute-start.5) | collective-permute-done | bytes 163872 | tf_op jit(solution)/shard_map/ppermute | solution.py:524
  21.1 0.0 copy-start.3
  21.1 1.5 %collective-permute-start.6 = (f32[5,8,128]{2,1,0:T(8,128)S(1)}, f32[5,8,128]{2,1,0:T(8,128)S(1)}, u32[]{:S(2)}, u32[]{:S(2)}) collective-permute-start(f32[5,8,128]{2,1,0:T(8,128)S(1)} %shard_map.132.after_ref), channel_id=1, source_target_pairs={{1,8},{8,1},{9,16},{16,9},{17,24},{24,17},{0,2},{25,27},{3,10},{10... | collective-permute-start | bytes 61448 | tf_op jit(solution)/shard_map/ppermute | solution.py:525
  22.6 2.3 %collective-permute-done.6.direct_ref = f32[5,8,128]{2,1,0:T(8,128)S(1)} collective-permute-done((f32[5,8,128]{2,1,0:T(8,128)S(1)}, f32[5,8,128]{2,1,0:T(8,128)S(1)}, u32[]{:S(2)}, u32[]{:S(2)}) %collective-permute-start.6) | collective-permute-done | bytes 20512 | tf_op jit(solution)/shard_map/ppermute | solution.py:525
  24.9 0.1 collective-permute-start.7
  25.1 1.1 %collective-permute-done.7.passed_ref = f32[5,8,128]{2,1,0:T(8,128)S(1)} collective-permute-done((f32[5,8,128]{2,1,0:T(8,128)S(1)}, f32[5,8,128]{2,1,0:T(8,128)S(1)}, u32[]{:S(2)}, u32[]{:S(2)}) %collective-permute-start.7) | collective-permute-done | bytes 20512 | tf_op jit(solution)/shard_map/ppermute | solution.py:524
  26.1 0.0 copy-done.3
  26.2 2.5 %collective-permute-start.8 = (f32[4,8,128]{2,1,0:T(8,128)S(1)}, f32[4,8,128]{2,1,0:T(8,128)S(1)}, u32[]{:S(2)}, u32[]{:S(2)}) collective-permute-start(f32[4,8,128]{2,1,0:T(8,128)S(1)} %get-tuple-element.16), channel_id=1, source_target_pairs={{1,2},{2,1},{3,4},{4,3},{5,6},{6,5},{0,8},{7,15},{9,10},{10,9},{11... | collective-permute-start | bytes 49160 | tf_op jit(solution)/shard_map/ppermute | solution.py:525
  28.6 1.7 %collective-permute-done.8.direct_ref = f32[4,8,128]{2,1,0:T(8,128)S(1)} collective-permute-done((f32[4,8,128]{2,1,0:T(8,128)S(1)}, f32[4,8,128]{2,1,0:T(8,128)S(1)}, u32[]{:S(2)}, u32[]{:S(2)}) %collective-permute-start.8) | collective-permute-done | bytes 16416 | tf_op jit(solution)/shard_map/ppermute | solution.py:525
  30.3 0.0 collective-permute-start.9
  30.3 1.2 %collective-permute-done.9.passed_ref = f32[4,8,128]{2,1,0:T(8,128)S(1)} collective-permute-done((f32[4,8,128]{2,1,0:T(8,128)S(1)}, f32[4,8,128]{2,1,0:T(8,128)S(1)}, u32[]{:S(2)}, u32[]{:S(2)}) %collective-permute-start.9) | collective-permute-done | bytes 16416 | tf_op jit(solution)/shard_map/ppermute | solution.py:524
  31.5 0.6 %shard_map.135 = f32[8,8,128]{2,1,0:T(8,128)} custom-call(f32[8,8,128]{2,1,0:T(8,128)S(1)} %get-tuple-element.15.base_ref, f32[4,8,128]{2,1,0:T(8,128)S(1)} %collective-permute-done.8.direct_ref, f32[4,8,128]{2,1,0:T(8,128)S(1)} %collective-permute-done.9.passed_ref), custom_call_target="tpu_custom_call" | custom-call | bytes 98304 | tf_op jit(solution)/shard_map/pallas_call | solution.py:185
  (5 shorter events, 0.1 us)
Async XLA Ops:
  0.0 17.3 %copy-start = (bf16[320,300]{1,0:T(8,128)(2,1)S(1)}, bf16[320,300]{1,0:T(8,128)(2,1)}, u32[]{:S(2)}) copy-start(bf16[320,300]{1,0:T(8,128)(2,1)} %constant.23.clone.both) | copy-start | bytes 576004
  0.0 0.8 %copy-start.2 = (f32[8,8,128]{2,1,0:T(8,128)S(1)}, f32[8,8,128]{2,1,0:T(8,128)}, u32[]{:S(2)}) copy-start(f32[8,8,128]{2,1,0:T(8,128)} %initial_ref.1) | copy-start | bytes 98308
  0.8 0.9 %copy-start.5 = (f32[3,8,8,128]{3,2,1,0:T(8,128)S(1)}, f32[3,8,8,128]{3,2,1,0:T(8,128)}, u32[]{:S(2)}) copy-start(f32[3,8,8,128]{3,2,1,0:T(8,128)} %metric_ref.1) | copy-start | bytes 294916
  1.7 0.9 %copy-start.6 = (bf16[384,128]{1,0:T(8,128)(2,1)S(1)}, bf16[384,128]{1,0:T(8,128)(2,1)}, u32[]{:S(2)}) copy-start(bf16[384,128]{1,0:T(8,128)(2,1)} %constant.19.clone.bzt) | copy-start | bytes 294916
  2.6 0.9 %copy-start.7 = (bf16[384,128]{1,0:T(8,128)(2,1)S(1)}, bf16[384,128]{1,0:T(8,128)(2,1)}, u32[]{:S(2)}) copy-start(bf16[384,128]{1,0:T(8,128)(2,1)} %constant.18.clone.bz) | copy-start | bytes 294916
  3.5 0.8 %copy-start.8 = (f32[8,8,128]{2,1,0:T(8,128)S(1)}, f32[8,8,128]{2,1,0:T(8,128)}, u32[]{:S(2)}) copy-start(f32[8,8,128]{2,1,0:T(8,128)} %source_ref.1) | copy-start | bytes 98308
  4.2 0.8 %copy-start.9 = (bf16[64,192]{1,0:T(8,128)(2,1)S(1)}, bf16[64,192]{1,0:T(8,128)(2,1)}, u32[]{:S(2)}) copy-start(bf16[64,192]{1,0:T(8,128)(2,1)} %constant.17.clone.ayt) | copy-start | bytes 73732
  5.0 0.8 %copy-start.10 = (bf16[64,192]{1,0:T(8,128)(2,1)S(1)}, bf16[64,192]{1,0:T(8,128)(2,1)}, u32[]{:S(2)}) copy-start(bf16[64,192]{1,0:T(8,128)(2,1)} %constant.16.clone.ay) | copy-start | bytes 73732
  5.8 11.6 %copy-start.4 = (f32[100,160]{1,0:T(8,128)S(1)}, f32[100,160]{1,0:T(8,128)}, u32[]{:S(2)}) copy-start(f32[100,160]{1,0:T(8,128)} %constant.21.clone.mask) | copy-start | bytes 192004
  6.1 11.3 %copy-start.1 = (f32[3,10,10,1,1,16]{5,4,3,2,1,0:T(1,128)S(1)}, f32[3,10,10,1,1,16]{5,4,3,2,1,0:T(1,128)}, u32[]{:S(2)}) copy-start(f32[3,10,10,1,1,16]{5,4,3,2,1,0:T(1,128)} %param.16) | copy-start | bytes 57604
  6.1 1.4 %collective-permute-start = (f32[8,8,128]{2,1,0:T(8,128)S(1)}, f32[8,8,128]{2,1,0:T(8,128)S(1)}, u32[]{:S(2)}, u32[]{:S(2)}) collective-permute-start(f32[8,8,128]{2,1,0:T(8,128)S(1)} %shard_map.127.own_ref.after_ref), channel_id=1, source_target_pairs={{0,1},{1,0},{2,3},{3,2},{4,5},{5,4},{6,7},{7,6},{8,9},{9,8},{10,11... | collective-permute-start | bytes 98312 | tf_op jit(solution)/shard_map/ppermute | solution.py:524
  7.5 9.9 %copy-start.11 = (bf16[48,160]{1,0:T(8,128)(2,1)S(1)}, bf16[48,160]{1,0:T(8,128)(2,1)}, u32[]{:S(2)}) copy-start(bf16[48,160]{1,0:T(8,128)(2,1)} %constant.20.clone.repeat) | copy-start | bytes 46084
  7.5 9.9 %copy-start.12 = (f32[3,10,1,1,16]{4,3,2,1,0:T(1,128)S(1)}, f32[3,10,1,1,16]{4,3,2,1,0:T(1,128)}, u32[]{:S(2)}) copy-start(f32[3,10,1,1,16]{4,3,2,1,0:T(1,128)} %param.17) | copy-start | bytes 5764
  7.5 4.6 %collective-permute-start.1 = (f32[2,2,8,128]{3,2,1,0:T(8,128)S(1)}, f32[2,2,8,128]{3,2,1,0:T(8,128)S(1)}, u32[]{:S(2)}, u32[]{:S(2)}) collective-permute-start(f32[2,2,8,128]{3,2,1,0:T(8,128)S(1)} %shard_map.128), channel_id=1, source_target_pairs={{1,8},{8,1},{9,16},{16,9},{17,24},{24,17},{0,2},{25,27},{3,10},{10... | collective-permute-start | bytes 49160 | tf_op jit(solution)/shard_map/ppermute | solution.py:525
  12.1 1.2 %collective-permute-start.2 = (f32[2,2,8,128]{3,2,1,0:T(8,128)S(1)}, f32[2,2,8,128]{3,2,1,0:T(8,128)S(1)}, u32[]{:S(2)}, u32[]{:S(2)}) collective-permute-start(f32[2,2,8,128]{3,2,1,0:T(8,128)S(1)} %collective-permute-done.1.direct_ref.xd_ref), channel_id=1, source_target_pairs={{0,1},{1,0},{2,3},{3,2},{4,5},{5,4},{6,7},{7,6},{8,9},{9,8},{10,11... | collective-permute-start | bytes 49160 | tf_op jit(solution)/shard_map/ppermute | solution.py:524
  13.3 4.1 %copy-start.13 = (bf16[10,300]{1,0:T(8,128)(2,1)S(1)}, bf16[10,300]{1,0:T(8,128)(2,1)}, u32[]{:S(2)}) copy-start(bf16[10,300]{1,0:T(8,128)(2,1)} %constant.22.clone.gather) | copy-start | bytes 18004
  13.3 4.0 %collective-permute-start.3 = (f32[6,8,128]{2,1,0:T(8,128)S(1)}, f32[6,8,128]{2,1,0:T(8,128)S(1)}, u32[]{:S(2)}, u32[]{:S(2)}) collective-permute-start(f32[6,8,128]{2,1,0:T(8,128)S(1)} %shard_map.129), channel_id=1, source_target_pairs={{1,2},{2,1},{3,4},{4,3},{5,6},{6,5},{0,8},{7,15},{9,10},{10,9},{11... | collective-permute-start | bytes 73736 | tf_op jit(solution)/shard_map/ppermute | solution.py:525
  17.3 1.3 %collective-permute-start.4 = (f32[6,8,128]{2,1,0:T(8,128)S(1)}, f32[6,8,128]{2,1,0:T(8,128)S(1)}, u32[]{:S(2)}, u32[]{:S(2)}) collective-permute-start(f32[6,8,128]{2,1,0:T(8,128)S(1)} %collective-permute-done.3.yd_ref), channel_id=1, source_target_pairs={{0,1},{1,0},{2,3},{3,2},{4,5},{5,4},{6,7},{7,6},{8,9},{9,8},{10,11... | collective-permute-start | bytes 73736 | tf_op jit(solution)/shard_map/ppermute | solution.py:524
  19.6 1.5 %collective-permute-start.5 = (f32[10,16,256]{2,1,0:T(8,128)S(1)}, f32[10,16,256]{2,1,0:T(8,128)S(1)}, u32[]{:S(2)}, u32[]{:S(2)}) collective-permute-start(f32[10,16,256]{2,1,0:T(8,128)S(1)} %shard_map.131.mine_ref), channel_id=1, source_target_pairs={{0,1},{1,0},{2,3},{3,2},{4,5},{5,4},{6,7},{7,6},{8,9},{9,8},{10,11... | collective-permute-start | bytes 491528 | tf_op jit(solution)/shard_map/ppermute | solution.py:524
  21.1 5.0 %copy-start.3 = (f32[8,8,128]{2,1,0:T(8,128)S(1)}, f32[8,8,128]{2,1,0:T(8,128)}, u32[]{:S(2)}) copy-start(f32[8,8,128]{2,1,0:T(8,128)} %initial_ref.1) | copy-start | bytes 98308
  21.1 3.8 %collective-permute-start.6 = (f32[5,8,128]{2,1,0:T(8,128)S(1)}, f32[5,8,128]{2,1,0:T(8,128)S(1)}, u32[]{:S(2)}, u32[]{:S(2)}) collective-permute-start(f32[5,8,128]{2,1,0:T(8,128)S(1)} %shard_map.132.after_ref), channel_id=1, source_target_pairs={{1,8},{8,1},{9,16},{16,9},{17,24},{24,17},{0,2},{25,27},{3,10},{10... | collective-permute-start | bytes 61448 | tf_op jit(solution)/shard_map/ppermute | solution.py:525
  24.9 1.2 %collective-permute-start.7 = (f32[5,8,128]{2,1,0:T(8,128)S(1)}, f32[5,8,128]{2,1,0:T(8,128)S(1)}, u32[]{:S(2)}, u32[]{:S(2)}) collective-permute-start(f32[5,8,128]{2,1,0:T(8,128)S(1)} %collective-permute-done.6.direct_ref), channel_id=1, source_target_pairs={{0,1},{1,0},{2,3},{3,2},{4,5},{5,4},{6,7},{7,6},{8,9},{9,8},{10,11... | collective-permute-start | bytes 61448 | tf_op jit(solution)/shard_map/ppermute | solution.py:524
  26.2 4.2 %collective-permute-start.8 = (f32[4,8,128]{2,1,0:T(8,128)S(1)}, f32[4,8,128]{2,1,0:T(8,128)S(1)}, u32[]{:S(2)}, u32[]{:S(2)}) collective-permute-start(f32[4,8,128]{2,1,0:T(8,128)S(1)} %get-tuple-element.16), channel_id=1, source_target_pairs={{1,2},{2,1},{3,4},{4,3},{5,6},{6,5},{0,8},{7,15},{9,10},{10,9},{11... | collective-permute-start | bytes 49160 | tf_op jit(solution)/shard_map/ppermute | solution.py:525
  30.3 1.2 %collective-permute-start.9 = (f32[4,8,128]{2,1,0:T(8,128)S(1)}, f32[4,8,128]{2,1,0:T(8,128)S(1)}, u32[]{:S(2)}, u32[]{:S(2)}) collective-permute-start(f32[4,8,128]{2,1,0:T(8,128)S(1)} %collective-permute-done.8.direct_ref), channel_id=1, source_target_pairs={{0,1},{1,0},{2,3},{3,2},{4,5},{5,4},{6,7},{7,6},{8,9},{9,8},{10,11... | collective-permute-start | bytes 49160 | tf_op jit(solution)/shard_map/ppermute | solution.py:524

commit v2 on v1

--- a/solution.py
+++ b/solution.py
@@ -175,17 +175,18 @@
 
 AXES = ("gx", "gy", "gz")
 VMEM = pl.BlockSpec(memory_space=pltpu.VMEM)
+HBM = pl.BlockSpec(memory_space=pltpu.HBM)
 VMEM_LIMIT = 16 * 2**20
 f32 = jnp.float32
 bf16 = jnp.bfloat16
 
 
-def call(kernel, outs, args, flops=0, scratch=()):
+def call(kernel, outs, args, flops=0, scratch=(), where=VMEM):
     moved = sum(int(np.prod(a.shape)) * a.dtype.itemsize for a in (*args, *outs))
     return pl.pallas_call(
         kernel,
         out_shape=outs,
-        in_specs=[VMEM] * len(args),
+        in_specs=[where] * len(args),
         out_specs=[VMEM] * len(outs),
         scratch_shapes=scratch,
         compiler_params=pltpu.CompilerParams(vmem_limit_bytes=VMEM_LIMIT),
@@ -235,7 +236,17 @@
     return [jnp.asarray(t) for t in tables]
 
 
-def residual_kernel(u_ref, source_ref, metric_ref, ay, ayt, bz, bzt, out_ref):
+def residual_kernel(*refs):
+    count = (len(refs) - 2) // 2
+    copies = [
+        pltpu.make_async_copy(refs[k], refs[count + 1 + k], refs[-1].at[k]) for k in range(count)
+    ]
+    out_ref = refs[count]
+    u_ref, source_ref, metric_ref, ay, ayt, bz, bzt = refs[count + 1 : -1]
+    for copy in copies:
+        copy.start()
+    for copy in copies:
+        copy.wait()
     nodes, rows, width = u_ref.shape
     table = np.asarray(derivative_table(), np.float32)
 
@@ -532,10 +543,16 @@
     lanes = blocks * ext
     padded = 2 * rows
 
+    inputs = [initial, source, metric, *operator_tables(rows, width)]
     own = call(
         residual_kernel,
         [shaped(initial.shape)],
-        [initial, source, metric, *operator_tables(rows, width)],
+        inputs,
+        scratch=[
+            *(pltpu.VMEM(value.shape, value.dtype) for value in inputs),
+            pltpu.SemaphoreType.DMA((len(inputs),)),
+        ],
+        where=HBM,
     )[0]
     vectors = eigenvectors.reshape(3 * ext * ext, 1, blocks)
     values = eigenvalues.reshape(3 * ext, 1, blocks)

time: 32.6 us -> 33.2 us (1.018)
  Pallas kernels: 3.19 us -> 3.79 us
    pallas_call x9, Pallas kernels: 3.19 us -> 3.79 us  [call(): pl.pallas_call(kernel, out_shape=outs, in_specs=[where] * len(args), out_...]
where the time goes in v2:
time: 33.2 us; the launch traced here: 32.8 us
  waiting for transfers between devices  12.9 us (39%)
  starting transfers between devices  10.2 us (31%)
  local copies, waits for them, and re-layouts  5.78 us (17%)
  Pallas kernels  3.79 us (11%)
    ppermute x4, starting transfers between devices, swap(): return lax.ppermute(value, AXES, swap_pairs(axis))  9 us
    ppermute x4, waiting for transfers between devices, swap(): return lax.ppermute(value, AXES, swap_pairs(axis))  7.58 us
    unnamed x28, local copies, waits for them, and re-layouts  5.78 us
    ppermute x6, waiting for transfers between devices, swap(): return lax.ppermute(value, 'gz', [(0, 1), (1, 0)])  5.28 us
    pallas_call x9, Pallas kernels, call(): pl.pallas_call(kernel, out_shape=outs, in_specs=[where] * len(args), out_...  3.79 us
    ppermute x6, starting transfers between devices, swap(): return lax.ppermute(value, 'gz', [(0, 1), (1, 0)])  1.24 us
  transfers between devices with their start and end apart: 10, of which 9 were waited for; matrix products, arithmetic and copies ran while one was open for 0% of the time, Pallas kernels for 4%

profile of v2, /device:TPU:0, one launch (start us, length us, event | category | flops | bytes accessed | tf_op | source)
XLA Modules:
  0.0 32.8 jit_solution(6908688752247979913)
XLA Ops:
  0.0 0.0 copy-start
  0.0 0.0 copy-start.2
  0.0 0.8 %copy-done.2 = f32[8,8,128]{2,1,0:T(8,128)S(1)} copy-done((f32[8,8,128]{2,1,0:T(8,128)S(1)}, f32[8,8,128]{2,1,0:T(8,128)}, u32[]{:S(2)}) %copy-start.2) | copy-done | bytes 32792
  0.8 0.0 copy-start.5
  0.8 0.9 %copy-done.5 = f32[3,8,8,128]{3,2,1,0:T(8,128)S(1)} copy-done((f32[3,8,8,128]{3,2,1,0:T(8,128)S(1)}, f32[3,8,8,128]{3,2,1,0:T(8,128)}, u32[]{:S(2)}) %copy-start.5) | copy-done | bytes 98328
  1.7 0.0 copy-start.6
  1.7 0.9 %copy-done.6 = bf16[384,128]{1,0:T(8,128)(2,1)S(1)} copy-done((bf16[384,128]{1,0:T(8,128)(2,1)S(1)}, bf16[384,128]{1,0:T(8,128)(2,1)}, u32[]{:S(2)}) %copy-start.6) | copy-done | bytes 98328
  2.6 0.0 copy-start.7
  2.6 0.9 %copy-done.7 = bf16[384,128]{1,0:T(8,128)(2,1)S(1)} copy-done((bf16[384,128]{1,0:T(8,128)(2,1)S(1)}, bf16[384,128]{1,0:T(8,128)(2,1)}, u32[]{:S(2)}) %copy-start.7) | copy-done | bytes 98328
  3.5 0.0 copy-start.8
  3.5 0.8 %copy-done.8 = f32[8,8,128]{2,1,0:T(8,128)S(1)} copy-done((f32[8,8,128]{2,1,0:T(8,128)S(1)}, f32[8,8,128]{2,1,0:T(8,128)}, u32[]{:S(2)}) %copy-start.8) | copy-done | bytes 32792
  4.2 0.0 copy-start.9
  4.2 0.8 %copy-done.9 = bf16[64,192]{1,0:T(8,128)(2,1)S(1)} copy-done((bf16[64,192]{1,0:T(8,128)(2,1)S(1)}, bf16[64,192]{1,0:T(8,128)(2,1)}, u32[]{:S(2)}) %copy-start.9) | copy-done | bytes 24600
  5.0 0.0 copy-start.10
  5.0 0.8 %copy-done.10 = bf16[64,192]{1,0:T(8,128)(2,1)S(1)} copy-done((bf16[64,192]{1,0:T(8,128)(2,1)S(1)}, bf16[64,192]{1,0:T(8,128)(2,1)}, u32[]{:S(2)}) %copy-start.10) | copy-done | bytes 24600
  5.8 0.0 copy-start.4
  5.8 0.9 %shard_map.127.own_ref.after_ref = f32[8,8,128]{2,1,0:T(8,128)S(1)} custom-call(f32[8,8,128]{2,1,0:T(8,128)S(1)} %copy-done.2, f32[8,8,128]{2,1,0:T(8,128)S(1)} %copy-done.8, f32[3,8,8,128]{3,2,1,0:T(8,128)S(1)} %copy-done.5, bf16[64,192]{1,0:T(8,128)(2,1)S(1)} %copy-done.10, bf16[64,192]{1,0:T(8,128)(2,1)S(1)} %copy-done.9, bf16[384,128]{1,0:T(8,128)(2,1)S(1)} %copy-done.7, ...), custom_call_target="tpu_custom_call" | custom-call | bytes 442368 | tf_op jit(solution)/shard_map/pallas_call | solution.py:186
  6.7 0.0 copy-start.1
  6.7 0.5 %collective-permute-start = (f32[8,8,128]{2,1,0:T(8,128)S(1)}, f32[8,8,128]{2,1,0:T(8,128)S(1)}, u32[]{:S(2)}, u32[]{:S(2)}) collective-permute-start(f32[8,8,128]{2,1,0:T(8,128)S(1)} %shard_map.127.own_ref.after_ref), channel_id=1, source_target_pairs={{0,1},{1,0},{2,3},{3,2},{4,5},{5,4},{6,7},{7,6},{8,9},{9,8},{10,11... | collective-permute-start | bytes 98312 | tf_op jit(solution)/shard_map/ppermute | solution.py:535
  7.2 0.9 %collective-permute-done.partner_ref = f32[8,8,128]{2,1,0:T(8,128)S(1)} collective-permute-done((f32[8,8,128]{2,1,0:T(8,128)S(1)}, f32[8,8,128]{2,1,0:T(8,128)S(1)}, u32[]{:S(2)}, u32[]{:S(2)}) %collective-permute-start) | collective-permute-done | bytes 32800 | tf_op jit(solution)/shard_map/ppermute | solution.py:535
  8.1 0.0 copy-start.11
  8.1 0.0 copy-start.12
  8.1 2.9 %collective-permute-start.1 = (f32[2,2,8,128]{3,2,1,0:T(8,128)S(1)}, f32[2,2,8,128]{3,2,1,0:T(8,128)S(1)}, u32[]{:S(2)}, u32[]{:S(2)}) collective-permute-start(f32[2,2,8,128]{3,2,1,0:T(8,128)S(1)} %shard_map.128), channel_id=1, source_target_pairs={{1,8},{8,1},{9,16},{16,9},{17,24},{24,17},{0,2},{25,27},{3,10},{10... | collective-permute-start | bytes 49160 | tf_op jit(solution)/shard_map/ppermute | solution.py:536
  11.0 1.7 %collective-permute-done.1.direct_ref.xd_ref = f32[2,2,8,128]{3,2,1,0:T(8,128)S(1)} collective-permute-done((f32[2,2,8,128]{3,2,1,0:T(8,128)S(1)}, f32[2,2,8,128]{3,2,1,0:T(8,128)S(1)}, u32[]{:S(2)}, u32[]{:S(2)}) %collective-permute-start.1) | collective-permute-done | bytes 16416 | tf_op jit(solution)/shard_map/ppermute | solution.py:536
  12.7 0.0 collective-permute-start.2
  12.7 1.2 %collective-permute-done.2.passed_ref.xp_ref = f32[2,2,8,128]{3,2,1,0:T(8,128)S(1)} collective-permute-done((f32[2,2,8,128]{3,2,1,0:T(8,128)S(1)}, f32[2,2,8,128]{3,2,1,0:T(8,128)S(1)}, u32[]{:S(2)}, u32[]{:S(2)}) %collective-permute-start.2) | collective-permute-done | bytes 16416 | tf_op jit(solution)/shard_map/ppermute | solution.py:535
  13.9 0.0 copy-start.13
  13.9 2.1 %collective-permute-start.3 = (f32[6,8,128]{2,1,0:T(8,128)S(1)}, f32[6,8,128]{2,1,0:T(8,128)S(1)}, u32[]{:S(2)}, u32[]{:S(2)}) collective-permute-start(f32[6,8,128]{2,1,0:T(8,128)S(1)} %shard_map.129), channel_id=1, source_target_pairs={{1,2},{2,1},{3,4},{4,3},{5,6},{6,5},{0,8},{7,15},{9,10},{10,9},{11... | collective-permute-start | bytes 73736 | tf_op jit(solution)/shard_map/ppermute | solution.py:536
  16.1 1.8 %collective-permute-done.3.yd_ref = f32[6,8,128]{2,1,0:T(8,128)S(1)} collective-permute-done((f32[6,8,128]{2,1,0:T(8,128)S(1)}, f32[6,8,128]{2,1,0:T(8,128)S(1)}, u32[]{:S(2)}, u32[]{:S(2)}) %collective-permute-start.3) | collective-permute-done | bytes 24608 | tf_op jit(solution)/shard_map/ppermute | solution.py:536
  17.9 0.1 collective-permute-start.4
  17.9 0.0 copy-done
  17.9 0.0 copy-done.4
  17.9 0.0 copy-done.1
  17.9 0.0 copy-done.11
  17.9 0.0 copy-done.12
  18.0 0.0 copy-done.13
  18.0 1.2 %shard_map.130 = (f32[100,160]{1,0:T(8,128)S(1)}, f32[2,10,16,160]{3,2,1,0:T(8,128)S(1)}, f32[10,16,160]{2,1,0:T(8,128)S(1)}, bf16[2,256,160]{2,1,0:T(8,128)(2,1)S(1)}) custom-call(f32[300,1,16]{2,1,0:T(1,128)S(1)} %bitcast.2, f32[30,1,16]{2,1,0:T(1,128)S(1)} %bitcast.3, bf16[48,160]{1,0:T(8,128)(2,1)S(1)} %copy-done.11, f32[100,160]{1,0:T(8,128)S(1)} %copy-done.4, ...), custom_call_target="tpu_custom_call" | custom-call | bytes 866288 | tf_op jit(solution)/shard_map/pallas_call | solution.py:186
  19.1 0.0 collective-permute-done.4.yp_ref
  19.2 1.0 %shard_map.131.mine_ref = f32[10,16,256]{2,1,0:T(8,128)S(1)} custom-call(f32[8,8,128]{2,1,0:T(8,128)S(1)} %shard_map.127.own_ref.after_ref, f32[8,8,128]{2,1,0:T(8,128)S(1)} %collective-permute-done.partner_ref, f32[2,2,8,128]{3,2,1,0:T(8,128)S(1)} %collective-permute-done.1.direct_ref.xd_ref, f32[2,2,8,128]{3,2,1,0:T(8,128)S(1)} %collective-permute-done.2.passed_ref.xp_ref, ...), custom_call_target="tpu_custom_call" | custom-call | bytes 846336 | tf_op jit(solution)/shard_map/pallas_call | solution.py:186
  20.2 0.5 %collective-permute-start.5 = (f32[10,16,256]{2,1,0:T(8,128)S(1)}, f32[10,16,256]{2,1,0:T(8,128)S(1)}, u32[]{:S(2)}, u32[]{:S(2)}) collective-permute-start(f32[10,16,256]{2,1,0:T(8,128)S(1)} %shard_map.131.mine_ref), channel_id=1, source_target_pairs={{0,1},{1,0},{2,3},{3,2},{4,5},{5,4},{6,7},{7,6},{8,9},{9,8},{10,11... | collective-permute-start | bytes 491528 | tf_op jit(solution)/shard_map/ppermute | solution.py:535
  20.7 1.0 %collective-permute-done.5.other_ref = f32[10,16,256]{2,1,0:T(8,128)S(1)} collective-permute-done((f32[10,16,256]{2,1,0:T(8,128)S(1)}, f32[10,16,256]{2,1,0:T(8,128)S(1)}, u32[]{:S(2)}, u32[]{:S(2)}) %collective-permute-start.5) | collective-permute-done | bytes 163872 | tf_op jit(solution)/shard_map/ppermute | solution.py:535
  21.7 0.0 copy-start.3
  21.7 1.5 %collective-permute-start.6 = (f32[5,8,128]{2,1,0:T(8,128)S(1)}, f32[5,8,128]{2,1,0:T(8,128)S(1)}, u32[]{:S(2)}, u32[]{:S(2)}) collective-permute-start(f32[5,8,128]{2,1,0:T(8,128)S(1)} %shard_map.132.after_ref), channel_id=1, source_target_pairs={{1,8},{8,1},{9,16},{16,9},{17,24},{24,17},{0,2},{25,27},{3,10},{10... | collective-permute-start | bytes 61448 | tf_op jit(solution)/shard_map/ppermute | solution.py:536
  23.2 2.3 %collective-permute-done.6.direct_ref = f32[5,8,128]{2,1,0:T(8,128)S(1)} collective-permute-done((f32[5,8,128]{2,1,0:T(8,128)S(1)}, f32[5,8,128]{2,1,0:T(8,128)S(1)}, u32[]{:S(2)}, u32[]{:S(2)}) %collective-permute-start.6) | collective-permute-done | bytes 20512 | tf_op jit(solution)/shard_map/ppermute | solution.py:536
  25.5 0.1 collective-permute-start.7
  25.7 1.1 %collective-permute-done.7.passed_ref = f32[5,8,128]{2,1,0:T(8,128)S(1)} collective-permute-done((f32[5,8,128]{2,1,0:T(8,128)S(1)}, f32[5,8,128]{2,1,0:T(8,128)S(1)}, u32[]{:S(2)}, u32[]{:S(2)}) %collective-permute-start.7) | collective-permute-done | bytes 20512 | tf_op jit(solution)/shard_map/ppermute | solution.py:535
  26.7 0.0 copy-done.3
  26.8 2.5 %collective-permute-start.8 = (f32[4,8,128]{2,1,0:T(8,128)S(1)}, f32[4,8,128]{2,1,0:T(8,128)S(1)}, u32[]{:S(2)}, u32[]{:S(2)}) collective-permute-start(f32[4,8,128]{2,1,0:T(8,128)S(1)} %get-tuple-element.16), channel_id=1, source_target_pairs={{1,2},{2,1},{3,4},{4,3},{5,6},{6,5},{0,8},{7,15},{9,10},{10,9},{11... | collective-permute-start | bytes 49160 | tf_op jit(solution)/shard_map/ppermute | solution.py:536
  29.2 1.7 %collective-permute-done.8.direct_ref = f32[4,8,128]{2,1,0:T(8,128)S(1)} collective-permute-done((f32[4,8,128]{2,1,0:T(8,128)S(1)}, f32[4,8,128]{2,1,0:T(8,128)S(1)}, u32[]{:S(2)}, u32[]{:S(2)}) %collective-permute-start.8) | collective-permute-done | bytes 16416 | tf_op jit(solution)/shard_map/ppermute | solution.py:536
  30.9 0.0 collective-permute-start.9
  30.9 1.2 %collective-permute-done.9.passed_ref = f32[4,8,128]{2,1,0:T(8,128)S(1)} collective-permute-done((f32[4,8,128]{2,1,0:T(8,128)S(1)}, f32[4,8,128]{2,1,0:T(8,128)S(1)}, u32[]{:S(2)}, u32[]{:S(2)}) %collective-permute-start.9) | collective-permute-done | bytes 16416 | tf_op jit(solution)/shard_map/ppermute | solution.py:535
  32.1 0.6 %shard_map.135 = f32[8,8,128]{2,1,0:T(8,128)} custom-call(f32[8,8,128]{2,1,0:T(8,128)S(1)} %get-tuple-element.15.base_ref, f32[4,8,128]{2,1,0:T(8,128)S(1)} %collective-permute-done.8.direct_ref, f32[4,8,128]{2,1,0:T(8,128)S(1)} %collective-permute-done.9.passed_ref), custom_call_target="tpu_custom_call" | custom-call | bytes 98304 | tf_op jit(solution)/shard_map/pallas_call | solution.py:186
  (5 shorter events, 0.1 us)
Async XLA Ops:
  0.0 17.9 %copy-start = (bf16[320,300]{1,0:T(8,128)(2,1)S(1)}, bf16[320,300]{1,0:T(8,128)(2,1)}, u32[]{:S(2)}) copy-start(bf16[320,300]{1,0:T(8,128)(2,1)} %constant.23.clone.both) | copy-start | bytes 576004
  0.0 0.8 %copy-start.2 = (f32[8,8,128]{2,1,0:T(8,128)S(1)}, f32[8,8,128]{2,1,0:T(8,128)}, u32[]{:S(2)}) copy-start(f32[8,8,128]{2,1,0:T(8,128)} %initial_ref.1) | copy-start | bytes 98308
  0.8 0.9 %copy-start.5 = (f32[3,8,8,128]{3,2,1,0:T(8,128)S(1)}, f32[3,8,8,128]{3,2,1,0:T(8,128)}, u32[]{:S(2)}) copy-start(f32[3,8,8,128]{3,2,1,0:T(8,128)} %refs_2_.1) | copy-start | bytes 294916
  1.7 0.9 %copy-start.6 = (bf16[384,128]{1,0:T(8,128)(2,1)S(1)}, bf16[384,128]{1,0:T(8,128)(2,1)}, u32[]{:S(2)}) copy-start(bf16[384,128]{1,0:T(8,128)(2,1)} %constant.19.clone.refs_6_) | copy-start | bytes 294916
  2.6 0.9 %copy-start.7 = (bf16[384,128]{1,0:T(8,128)(2,1)S(1)}, bf16[384,128]{1,0:T(8,128)(2,1)}, u32[]{:S(2)}) copy-start(bf16[384,128]{1,0:T(8,128)(2,1)} %constant.18.clone.refs_5_) | copy-start | bytes 294916
  3.5 0.8 %copy-start.8 = (f32[8,8,128]{2,1,0:T(8,128)S(1)}, f32[8,8,128]{2,1,0:T(8,128)}, u32[]{:S(2)}) copy-start(f32[8,8,128]{2,1,0:T(8,128)} %refs_1_.1) | copy-start | bytes 98308
  4.2 0.8 %copy-start.9 = (bf16[64,192]{1,0:T(8,128)(2,1)S(1)}, bf16[64,192]{1,0:T(8,128)(2,1)}, u32[]{:S(2)}) copy-start(bf16[64,192]{1,0:T(8,128)(2,1)} %constant.17.clone.refs_4_) | copy-start | bytes 73732
  5.0 0.8 %copy-start.10 = (bf16[64,192]{1,0:T(8,128)(2,1)S(1)}, bf16[64,192]{1,0:T(8,128)(2,1)}, u32[]{:S(2)}) copy-start(bf16[64,192]{1,0:T(8,128)(2,1)} %constant.16.clone.refs_3_) | copy-start | bytes 73732
  5.8 12.2 %copy-start.4 = (f32[100,160]{1,0:T(8,128)S(1)}, f32[100,160]{1,0:T(8,128)}, u32[]{:S(2)}) copy-start(f32[100,160]{1,0:T(8,128)} %constant.21.clone.mask) | copy-start | bytes 192004
  6.7 11.3 %copy-start.1 = (f32[3,10,10,1,1,16]{5,4,3,2,1,0:T(1,128)S(1)}, f32[3,10,10,1,1,16]{5,4,3,2,1,0:T(1,128)}, u32[]{:S(2)}) copy-start(f32[3,10,10,1,1,16]{5,4,3,2,1,0:T(1,128)} %param.16) | copy-start | bytes 57604
  6.7 1.4 %collective-permute-start = (f32[8,8,128]{2,1,0:T(8,128)S(1)}, f32[8,8,128]{2,1,0:T(8,128)S(1)}, u32[]{:S(2)}, u32[]{:S(2)}) collective-permute-start(f32[8,8,128]{2,1,0:T(8,128)S(1)} %shard_map.127.own_ref.after_ref), channel_id=1, source_target_pairs={{0,1},{1,0},{2,3},{3,2},{4,5},{5,4},{6,7},{7,6},{8,9},{9,8},{10,11... | collective-permute-start | bytes 98312 | tf_op jit(solution)/shard_map/ppermute | solution.py:535
  8.1 9.9 %copy-start.11 = (bf16[48,160]{1,0:T(8,128)(2,1)S(1)}, bf16[48,160]{1,0:T(8,128)(2,1)}, u32[]{:S(2)}) copy-start(bf16[48,160]{1,0:T(8,128)(2,1)} %constant.20.clone.repeat) | copy-start | bytes 46084
  8.1 9.9 %copy-start.12 = (f32[3,10,1,1,16]{4,3,2,1,0:T(1,128)S(1)}, f32[3,10,1,1,16]{4,3,2,1,0:T(1,128)}, u32[]{:S(2)}) copy-start(f32[3,10,1,1,16]{4,3,2,1,0:T(1,128)} %param.17) | copy-start | bytes 5764
  8.1 4.6 %collective-permute-start.1 = (f32[2,2,8,128]{3,2,1,0:T(8,128)S(1)}, f32[2,2,8,128]{3,2,1,0:T(8,128)S(1)}, u32[]{:S(2)}, u32[]{:S(2)}) collective-permute-start(f32[2,2,8,128]{3,2,1,0:T(8,128)S(1)} %shard_map.128), channel_id=1, source_target_pairs={{1,8},{8,1},{9,16},{16,9},{17,24},{24,17},{0,2},{25,27},{3,10},{10... | collective-permute-start | bytes 49160 | tf_op jit(solution)/shard_map/ppermute | solution.py:536
  12.7 1.2 %collective-permute-start.2 = (f32[2,2,8,128]{3,2,1,0:T(8,128)S(1)}, f32[2,2,8,128]{3,2,1,0:T(8,128)S(1)}, u32[]{:S(2)}, u32[]{:S(2)}) collective-permute-start(f32[2,2,8,128]{3,2,1,0:T(8,128)S(1)} %collective-permute-done.1.direct_ref.xd_ref), channel_id=1, source_target_pairs={{0,1},{1,0},{2,3},{3,2},{4,5},{5,4},{6,7},{7,6},{8,9},{9,8},{10,11... | collective-permute-start | bytes 49160 | tf_op jit(solution)/shard_map/ppermute | solution.py:535
  13.9 4.1 %copy-start.13 = (bf16[10,300]{1,0:T(8,128)(2,1)S(1)}, bf16[10,300]{1,0:T(8,128)(2,1)}, u32[]{:S(2)}) copy-start(bf16[10,300]{1,0:T(8,128)(2,1)} %constant.22.clone.gather) | copy-start | bytes 18004
  13.9 4.0 %collective-permute-start.3 = (f32[6,8,128]{2,1,0:T(8,128)S(1)}, f32[6,8,128]{2,1,0:T(8,128)S(1)}, u32[]{:S(2)}, u32[]{:S(2)}) collective-permute-start(f32[6,8,128]{2,1,0:T(8,128)S(1)} %shard_map.129), channel_id=1, source_target_pairs={{1,2},{2,1},{3,4},{4,3},{5,6},{6,5},{0,8},{7,15},{9,10},{10,9},{11... | collective-permute-start | bytes 73736 | tf_op jit(solution)/shard_map/ppermute | solution.py:536
  17.9 1.3 %collective-permute-start.4 = (f32[6,8,128]{2,1,0:T(8,128)S(1)}, f32[6,8,128]{2,1,0:T(8,128)S(1)}, u32[]{:S(2)}, u32[]{:S(2)}) collective-permute-start(f32[6,8,128]{2,1,0:T(8,128)S(1)} %collective-permute-done.3.yd_ref), channel_id=1, source_target_pairs={{0,1},{1,0},{2,3},{3,2},{4,5},{5,4},{6,7},{7,6},{8,9},{9,8},{10,11... | collective-permute-start | bytes 73736 | tf_op jit(solution)/shard_map/ppermute | solution.py:535
  20.2 1.5 %collective-permute-start.5 = (f32[10,16,256]{2,1,0:T(8,128)S(1)}, f32[10,16,256]{2,1,0:T(8,128)S(1)}, u32[]{:S(2)}, u32[]{:S(2)}) collective-permute-start(f32[10,16,256]{2,1,0:T(8,128)S(1)} %shard_map.131.mine_ref), channel_id=1, source_target_pairs={{0,1},{1,0},{2,3},{3,2},{4,5},{5,4},{6,7},{7,6},{8,9},{9,8},{10,11... | collective-permute-start | bytes 491528 | tf_op jit(solution)/shard_map/ppermute | solution.py:535
  21.7 5.0 %copy-start.3 = (f32[8,8,128]{2,1,0:T(8,128)S(1)}, f32[8,8,128]{2,1,0:T(8,128)}, u32[]{:S(2)}) copy-start(f32[8,8,128]{2,1,0:T(8,128)} %initial_ref.1) | copy-start | bytes 98308
  21.7 3.8 %collective-permute-start.6 = (f32[5,8,128]{2,1,0:T(8,128)S(1)}, f32[5,8,128]{2,1,0:T(8,128)S(1)}, u32[]{:S(2)}, u32[]{:S(2)}) collective-permute-start(f32[5,8,128]{2,1,0:T(8,128)S(1)} %shard_map.132.after_ref), channel_id=1, source_target_pairs={{1,8},{8,1},{9,16},{16,9},{17,24},{24,17},{0,2},{25,27},{3,10},{10... | collective-permute-start | bytes 61448 | tf_op jit(solution)/shard_map/ppermute | solution.py:536
  25.5 1.2 %collective-permute-start.7 = (f32[5,8,128]{2,1,0:T(8,128)S(1)}, f32[5,8,128]{2,1,0:T(8,128)S(1)}, u32[]{:S(2)}, u32[]{:S(2)}) collective-permute-start(f32[5,8,128]{2,1,0:T(8,128)S(1)} %collective-permute-done.6.direct_ref), channel_id=1, source_target_pairs={{0,1},{1,0},{2,3},{3,2},{4,5},{5,4},{6,7},{7,6},{8,9},{9,8},{10,11... | collective-permute-start | bytes 61448 | tf_op jit(solution)/shard_map/ppermute | solution.py:535
  26.8 4.2 %collective-permute-start.8 = (f32[4,8,128]{2,1,0:T(8,128)S(1)}, f32[4,8,128]{2,1,0:T(8,128)S(1)}, u32[]{:S(2)}, u32[]{:S(2)}) collective-permute-start(f32[4,8,128]{2,1,0:T(8,128)S(1)} %get-tuple-element.16), channel_id=1, source_target_pairs={{1,2},{2,1},{3,4},{4,3},{5,6},{6,5},{0,8},{7,15},{9,10},{10,9},{11... | collective-permute-start | bytes 49160 | tf_op jit(solution)/shard_map/ppermute | solution.py:536
  30.9 1.2 %collective-permute-start.9 = (f32[4,8,128]{2,1,0:T(8,128)S(1)}, f32[4,8,128]{2,1,0:T(8,128)S(1)}, u32[]{:S(2)}, u32[]{:S(2)}) collective-permute-start(f32[4,8,128]{2,1,0:T(8,128)S(1)} %collective-permute-done.8.direct_ref), channel_id=1, source_target_pairs={{0,1},{1,0},{2,3},{3,2},{4,5},{5,4},{6,7},{7,6},{8,9},{9,8},{10,11... | collective-permute-start | bytes 49160 | tf_op jit(solution)/shard_map/ppermute | solution.py:535

commit v3 on v2

--- a/solution.py
+++ b/solution.py
@@ -544,6 +544,7 @@
     padded = 2 * rows
 
     inputs = [initial, source, metric, *operator_tables(rows, width)]
+    inputs = [pltpu.with_memory_space_constraint(value, pltpu.HBM) for value in inputs]
     own = call(
         residual_kernel,
         [shaped(initial.shape)],

time: 33.2 us -> 27.7 us (0.83); the launches traced: 32.8 us -> 27.6 us
  local copies, waits for them, and re-layouts: 5.78 us -> 0.03 us
  Pallas kernels: 3.79 us -> 4.38 us
    unnamed x28 -> x14, local copies, waits for them, and re-layouts: 5.78 us -> 0.03 us
    pallas_call x9, Pallas kernels: 3.79 us -> 4.38 us  [call(): pl.pallas_call(kernel, out_shape=outs, in_specs=[where] * len(args), out_...]
where the time goes in v3:
time: 27.7 us; the launch traced here: 27.6 us
  waiting for transfers between devices  12.9 us (47%)
  starting transfers between devices  10.2 us (37%)
  Pallas kernels  4.38 us (16%)
    ppermute x4, starting transfers between devices, swap(): return lax.ppermute(value, AXES, swap_pairs(axis))  9 us
    ppermute x4, waiting for transfers between devices, swap(): return lax.ppermute(value, AXES, swap_pairs(axis))  7.58 us
    ppermute x6, waiting for transfers between devices, swap(): return lax.ppermute(value, 'gz', [(0, 1), (1, 0)])  5.28 us
    pallas_call x9, Pallas kernels, call(): pl.pallas_call(kernel, out_shape=outs, in_specs=[where] * len(args), out_...  4.38 us
    ppermute x6, starting transfers between devices, swap(): return lax.ppermute(value, 'gz', [(0, 1), (1, 0)])  1.24 us
  transfers between devices with their start and end apart: 10, of which 9 were waited for; matrix products, arithmetic and copies ran while one was open for 0% of the time, Pallas kernels for 4%

profile of v3, /device:TPU:0, one launch (start us, length us, event | category | flops | bytes accessed | tf_op | source)
XLA Modules:
  0.0 27.6 jit_solution(15236101799505503599)
XLA Ops:
  0.0 0.0 copy-start
  0.0 0.0 copy-start.3
  0.0 1.5 %shard_map.127.own_ref.after_ref = f32[8,8,128]{2,1,0:T(8,128)S(1)} custom-call(f32[8,8,128]{2,1,0:T(8,128)} %initial_ref.1, f32[8,8,128]{2,1,0:T(8,128)} %refs_1_.1, f32[3,8,8,128]{3,2,1,0:T(8,128)} %refs_2_.1, bf16[64,192]{1,0:T(8,128)(2,1)} %constant.16.clone.refs_3_, bf16[64,192]{1,0:T(8,128)(2,1)} %constant.17.clone.refs_4_, ...), custom_call_target="tpu_custom_call" | custom-call | bytes 442368 | tf_op jit(solution)/shard_map/pallas_call | solution.py:186
  1.5 0.0 copy-start.1
  1.5 0.5 %collective-permute-start = (f32[8,8,128]{2,1,0:T(8,128)S(1)}, f32[8,8,128]{2,1,0:T(8,128)S(1)}, u32[]{:S(2)}, u32[]{:S(2)}) collective-permute-start(f32[8,8,128]{2,1,0:T(8,128)S(1)} %shard_map.127.own_ref.after_ref), channel_id=1, source_target_pairs={{0,1},{1,0},{2,3},{3,2},{4,5},{5,4},{6,7},{7,6},{8,9},{9,8},{10,11... | collective-permute-start | bytes 98312 | tf_op jit(solution)/shard_map/ppermute | solution.py:535
  2.0 0.9 %collective-permute-done.partner_ref = f32[8,8,128]{2,1,0:T(8,128)S(1)} collective-permute-done((f32[8,8,128]{2,1,0:T(8,128)S(1)}, f32[8,8,128]{2,1,0:T(8,128)S(1)}, u32[]{:S(2)}, u32[]{:S(2)}) %collective-permute-start) | collective-permute-done | bytes 32800 | tf_op jit(solution)/shard_map/ppermute | solution.py:535
  2.9 0.0 copy-start.4
  2.9 0.0 copy-start.5
  2.9 2.9 %collective-permute-start.1 = (f32[2,2,8,128]{3,2,1,0:T(8,128)S(1)}, f32[2,2,8,128]{3,2,1,0:T(8,128)S(1)}, u32[]{:S(2)}, u32[]{:S(2)}) collective-permute-start(f32[2,2,8,128]{3,2,1,0:T(8,128)S(1)} %shard_map.128), channel_id=1, source_target_pairs={{1,8},{8,1},{9,16},{16,9},{17,24},{24,17},{0,2},{25,27},{3,10},{10... | collective-permute-start | bytes 49160 | tf_op jit(solution)/shard_map/ppermute | solution.py:536
  5.8 1.7 %collective-permute-done.1.direct_ref.xd_ref = f32[2,2,8,128]{3,2,1,0:T(8,128)S(1)} collective-permute-done((f32[2,2,8,128]{3,2,1,0:T(8,128)S(1)}, f32[2,2,8,128]{3,2,1,0:T(8,128)S(1)}, u32[]{:S(2)}, u32[]{:S(2)}) %collective-permute-start.1) | collective-permute-done | bytes 16416 | tf_op jit(solution)/shard_map/ppermute | solution.py:536
  7.5 0.0 collective-permute-start.2
  7.6 1.2 %collective-permute-done.2.passed_ref.xp_ref = f32[2,2,8,128]{3,2,1,0:T(8,128)S(1)} collective-permute-done((f32[2,2,8,128]{3,2,1,0:T(8,128)S(1)}, f32[2,2,8,128]{3,2,1,0:T(8,128)S(1)}, u32[]{:S(2)}, u32[]{:S(2)}) %collective-permute-start.2) | collective-permute-done | bytes 16416 | tf_op jit(solution)/shard_map/ppermute | solution.py:535
  8.7 0.0 copy-start.6
  8.7 2.1 %collective-permute-start.3 = (f32[6,8,128]{2,1,0:T(8,128)S(1)}, f32[6,8,128]{2,1,0:T(8,128)S(1)}, u32[]{:S(2)}, u32[]{:S(2)}) collective-permute-start(f32[6,8,128]{2,1,0:T(8,128)S(1)} %shard_map.129), channel_id=1, source_target_pairs={{1,2},{2,1},{3,4},{4,3},{5,6},{6,5},{0,8},{7,15},{9,10},{10,9},{11... | collective-permute-start | bytes 73736 | tf_op jit(solution)/shard_map/ppermute | solution.py:536
  10.9 1.8 %collective-permute-done.3.yd_ref = f32[6,8,128]{2,1,0:T(8,128)S(1)} collective-permute-done((f32[6,8,128]{2,1,0:T(8,128)S(1)}, f32[6,8,128]{2,1,0:T(8,128)S(1)}, u32[]{:S(2)}, u32[]{:S(2)}) %collective-permute-start.3) | collective-permute-done | bytes 24608 | tf_op jit(solution)/shard_map/ppermute | solution.py:536
  12.7 0.1 collective-permute-start.4
  12.8 0.0 copy-done
  12.8 0.0 copy-done.3
  12.8 0.0 copy-done.1
  12.8 0.0 copy-done.4
  12.8 0.0 copy-done.5
  12.8 0.0 copy-done.6
  12.8 1.2 %shard_map.130 = (f32[100,160]{1,0:T(8,128)S(1)}, f32[2,10,16,160]{3,2,1,0:T(8,128)S(1)}, f32[10,16,160]{2,1,0:T(8,128)S(1)}, bf16[2,256,160]{2,1,0:T(8,128)(2,1)S(1)}) custom-call(f32[300,1,16]{2,1,0:T(1,128)S(1)} %bitcast.2, f32[30,1,16]{2,1,0:T(1,128)S(1)} %bitcast.3, bf16[48,160]{1,0:T(8,128)(2,1)S(1)} %copy-done.4, f32[100,160]{1,0:T(8,128)S(1)} %copy-done.3, ...), custom_call_target="tpu_custom_call" | custom-call | bytes 866288 | tf_op jit(solution)/shard_map/pallas_call | solution.py:186
  14.0 0.0 collective-permute-done.4.yp_ref
  14.0 1.0 %shard_map.131.mine_ref = f32[10,16,256]{2,1,0:T(8,128)S(1)} custom-call(f32[8,8,128]{2,1,0:T(8,128)S(1)} %shard_map.127.own_ref.after_ref, f32[8,8,128]{2,1,0:T(8,128)S(1)} %collective-permute-done.partner_ref, f32[2,2,8,128]{3,2,1,0:T(8,128)S(1)} %collective-permute-done.1.direct_ref.xd_ref, f32[2,2,8,128]{3,2,1,0:T(8,128)S(1)} %collective-permute-done.2.passed_ref.xp_ref, ...), custom_call_target="tpu_custom_call" | custom-call | bytes 846336 | tf_op jit(solution)/shard_map/pallas_call | solution.py:186
  15.0 0.5 %collective-permute-start.5 = (f32[10,16,256]{2,1,0:T(8,128)S(1)}, f32[10,16,256]{2,1,0:T(8,128)S(1)}, u32[]{:S(2)}, u32[]{:S(2)}) collective-permute-start(f32[10,16,256]{2,1,0:T(8,128)S(1)} %shard_map.131.mine_ref), channel_id=1, source_target_pairs={{0,1},{1,0},{2,3},{3,2},{4,5},{5,4},{6,7},{7,6},{8,9},{9,8},{10,11... | collective-permute-start | bytes 491528 | tf_op jit(solution)/shard_map/ppermute | solution.py:535
  15.5 1.0 %collective-permute-done.5.other_ref = f32[10,16,256]{2,1,0:T(8,128)S(1)} collective-permute-done((f32[10,16,256]{2,1,0:T(8,128)S(1)}, f32[10,16,256]{2,1,0:T(8,128)S(1)}, u32[]{:S(2)}, u32[]{:S(2)}) %collective-permute-start.5) | collective-permute-done | bytes 163872 | tf_op jit(solution)/shard_map/ppermute | solution.py:535
  16.5 0.0 copy-start.2
  16.6 1.5 %collective-permute-start.6 = (f32[5,8,128]{2,1,0:T(8,128)S(1)}, f32[5,8,128]{2,1,0:T(8,128)S(1)}, u32[]{:S(2)}, u32[]{:S(2)}) collective-permute-start(f32[5,8,128]{2,1,0:T(8,128)S(1)} %shard_map.132.after_ref), channel_id=1, source_target_pairs={{1,8},{8,1},{9,16},{16,9},{17,24},{24,17},{0,2},{25,27},{3,10},{10... | collective-permute-start | bytes 61448 | tf_op jit(solution)/shard_map/ppermute | solution.py:536
  18.0 2.3 %collective-permute-done.6.direct_ref = f32[5,8,128]{2,1,0:T(8,128)S(1)} collective-permute-done((f32[5,8,128]{2,1,0:T(8,128)S(1)}, f32[5,8,128]{2,1,0:T(8,128)S(1)}, u32[]{:S(2)}, u32[]{:S(2)}) %collective-permute-start.6) | collective-permute-done | bytes 20512 | tf_op jit(solution)/shard_map/ppermute | solution.py:536
  20.4 0.1 collective-permute-start.7
  20.5 1.1 %collective-permute-done.7.passed_ref = f32[5,8,128]{2,1,0:T(8,128)S(1)} collective-permute-done((f32[5,8,128]{2,1,0:T(8,128)S(1)}, f32[5,8,128]{2,1,0:T(8,128)S(1)}, u32[]{:S(2)}, u32[]{:S(2)}) %collective-permute-start.7) | collective-permute-done | bytes 20512 | tf_op jit(solution)/shard_map/ppermute | solution.py:535
  21.6 0.0 copy-done.2
  21.6 2.5 %collective-permute-start.8 = (f32[4,8,128]{2,1,0:T(8,128)S(1)}, f32[4,8,128]{2,1,0:T(8,128)S(1)}, u32[]{:S(2)}, u32[]{:S(2)}) collective-permute-start(f32[4,8,128]{2,1,0:T(8,128)S(1)} %get-tuple-element.16), channel_id=1, source_target_pairs={{1,2},{2,1},{3,4},{4,3},{5,6},{6,5},{0,8},{7,15},{9,10},{10,9},{11... | collective-permute-start | bytes 49160 | tf_op jit(solution)/shard_map/ppermute | solution.py:536
  24.1 1.7 %collective-permute-done.8.direct_ref = f32[4,8,128]{2,1,0:T(8,128)S(1)} collective-permute-done((f32[4,8,128]{2,1,0:T(8,128)S(1)}, f32[4,8,128]{2,1,0:T(8,128)S(1)}, u32[]{:S(2)}, u32[]{:S(2)}) %collective-permute-start.8) | collective-permute-done | bytes 16416 | tf_op jit(solution)/shard_map/ppermute | solution.py:536
  25.8 0.0 collective-permute-start.9
  25.8 1.2 %collective-permute-done.9.passed_ref = f32[4,8,128]{2,1,0:T(8,128)S(1)} collective-permute-done((f32[4,8,128]{2,1,0:T(8,128)S(1)}, f32[4,8,128]{2,1,0:T(8,128)S(1)}, u32[]{:S(2)}, u32[]{:S(2)}) %collective-permute-start.9) | collective-permute-done | bytes 16416 | tf_op jit(solution)/shard_map/ppermute | solution.py:535
  27.0 0.6 %shard_map.135 = f32[8,8,128]{2,1,0:T(8,128)} custom-call(f32[8,8,128]{2,1,0:T(8,128)S(1)} %get-tuple-element.15.base_ref, f32[4,8,128]{2,1,0:T(8,128)S(1)} %collective-permute-done.8.direct_ref, f32[4,8,128]{2,1,0:T(8,128)S(1)} %collective-permute-done.9.passed_ref), custom_call_target="tpu_custom_call" | custom-call | bytes 98304 | tf_op jit(solution)/shard_map/pallas_call | solution.py:186
  (5 shorter events, 0.1 us)
Async XLA Ops:
  0.0 12.8 %copy-start = (bf16[320,300]{1,0:T(8,128)(2,1)S(1)}, bf16[320,300]{1,0:T(8,128)(2,1)}, u32[]{:S(2)}) copy-start(bf16[320,300]{1,0:T(8,128)(2,1)} %constant.23.clone.both) | copy-start | bytes 576004
  0.0 12.8 %copy-start.3 = (f32[100,160]{1,0:T(8,128)S(1)}, f32[100,160]{1,0:T(8,128)}, u32[]{:S(2)}) copy-start(f32[100,160]{1,0:T(8,128)} %constant.21.clone.mask) | copy-start | bytes 192004
  1.5 11.3 %copy-start.1 = (f32[3,10,10,1,1,16]{5,4,3,2,1,0:T(1,128)S(1)}, f32[3,10,10,1,1,16]{5,4,3,2,1,0:T(1,128)}, u32[]{:S(2)}) copy-start(f32[3,10,10,1,1,16]{5,4,3,2,1,0:T(1,128)} %param.16) | copy-start | bytes 57604
  1.5 1.4 %collective-permute-start = (f32[8,8,128]{2,1,0:T(8,128)S(1)}, f32[8,8,128]{2,1,0:T(8,128)S(1)}, u32[]{:S(2)}, u32[]{:S(2)}) collective-permute-start(f32[8,8,128]{2,1,0:T(8,128)S(1)} %shard_map.127.own_ref.after_ref), channel_id=1, source_target_pairs={{0,1},{1,0},{2,3},{3,2},{4,5},{5,4},{6,7},{7,6},{8,9},{9,8},{10,11... | collective-permute-start | bytes 98312 | tf_op jit(solution)/shard_map/ppermute | solution.py:535
  2.9 9.9 %copy-start.4 = (bf16[48,160]{1,0:T(8,128)(2,1)S(1)}, bf16[48,160]{1,0:T(8,128)(2,1)}, u32[]{:S(2)}) copy-start(bf16[48,160]{1,0:T(8,128)(2,1)} %constant.20.clone.repeat) | copy-start | bytes 46084
  2.9 9.9 %copy-start.5 = (f32[3,10,1,1,16]{4,3,2,1,0:T(1,128)S(1)}, f32[3,10,1,1,16]{4,3,2,1,0:T(1,128)}, u32[]{:S(2)}) copy-start(f32[3,10,1,1,16]{4,3,2,1,0:T(1,128)} %param.17) | copy-start | bytes 5764
  2.9 4.6 %collective-permute-start.1 = (f32[2,2,8,128]{3,2,1,0:T(8,128)S(1)}, f32[2,2,8,128]{3,2,1,0:T(8,128)S(1)}, u32[]{:S(2)}, u32[]{:S(2)}) collective-permute-start(f32[2,2,8,128]{3,2,1,0:T(8,128)S(1)} %shard_map.128), channel_id=1, source_target_pairs={{1,8},{8,1},{9,16},{16,9},{17,24},{24,17},{0,2},{25,27},{3,10},{10... | collective-permute-start | bytes 49160 | tf_op jit(solution)/shard_map/ppermute | solution.py:536
  7.5 1.2 %collective-permute-start.2 = (f32[2,2,8,128]{3,2,1,0:T(8,128)S(1)}, f32[2,2,8,128]{3,2,1,0:T(8,128)S(1)}, u32[]{:S(2)}, u32[]{:S(2)}) collective-permute-start(f32[2,2,8,128]{3,2,1,0:T(8,128)S(1)} %collective-permute-done.1.direct_ref.xd_ref), channel_id=1, source_target_pairs={{0,1},{1,0},{2,3},{3,2},{4,5},{5,4},{6,7},{7,6},{8,9},{9,8},{10,11... | collective-permute-start | bytes 49160 | tf_op jit(solution)/shard_map/ppermute | solution.py:535
  8.7 4.1 %copy-start.6 = (bf16[10,300]{1,0:T(8,128)(2,1)S(1)}, bf16[10,300]{1,0:T(8,128)(2,1)}, u32[]{:S(2)}) copy-start(bf16[10,300]{1,0:T(8,128)(2,1)} %constant.22.clone.gather) | copy-start | bytes 18004
  8.7 4.0 %collective-permute-start.3 = (f32[6,8,128]{2,1,0:T(8,128)S(1)}, f32[6,8,128]{2,1,0:T(8,128)S(1)}, u32[]{:S(2)}, u32[]{:S(2)}) collective-permute-start(f32[6,8,128]{2,1,0:T(8,128)S(1)} %shard_map.129), channel_id=1, source_target_pairs={{1,2},{2,1},{3,4},{4,3},{5,6},{6,5},{0,8},{7,15},{9,10},{10,9},{11... | collective-permute-start | bytes 73736 | tf_op jit(solution)/shard_map/ppermute | solution.py:536
  12.7 1.3 %collective-permute-start.4 = (f32[6,8,128]{2,1,0:T(8,128)S(1)}, f32[6,8,128]{2,1,0:T(8,128)S(1)}, u32[]{:S(2)}, u32[]{:S(2)}) collective-permute-start(f32[6,8,128]{2,1,0:T(8,128)S(1)} %collective-permute-done.3.yd_ref), channel_id=1, source_target_pairs={{0,1},{1,0},{2,3},{3,2},{4,5},{5,4},{6,7},{7,6},{8,9},{9,8},{10,11... | collective-permute-start | bytes 73736 | tf_op jit(solution)/shard_map/ppermute | solution.py:535
  15.0 1.5 %collective-permute-start.5 = (f32[10,16,256]{2,1,0:T(8,128)S(1)}, f32[10,16,256]{2,1,0:T(8,128)S(1)}, u32[]{:S(2)}, u32[]{:S(2)}) collective-permute-start(f32[10,16,256]{2,1,0:T(8,128)S(1)} %shard_map.131.mine_ref), channel_id=1, source_target_pairs={{0,1},{1,0},{2,3},{3,2},{4,5},{5,4},{6,7},{7,6},{8,9},{9,8},{10,11... | collective-permute-start | bytes 491528 | tf_op jit(solution)/shard_map/ppermute | solution.py:535
  16.5 5.0 %copy-start.2 = (f32[8,8,128]{2,1,0:T(8,128)S(1)}, f32[8,8,128]{2,1,0:T(8,128)}, u32[]{:S(2)}) copy-start(f32[8,8,128]{2,1,0:T(8,128)} %initial_ref.1) | copy-start | bytes 98308
  16.6 3.8 %collective-permute-start.6 = (f32[5,8,128]{2,1,0:T(8,128)S(1)}, f32[5,8,128]{2,1,0:T(8,128)S(1)}, u32[]{:S(2)}, u32[]{:S(2)}) collective-permute-start(f32[5,8,128]{2,1,0:T(8,128)S(1)} %shard_map.132.after_ref), channel_id=1, source_target_pairs={{1,8},{8,1},{9,16},{16,9},{17,24},{24,17},{0,2},{25,27},{3,10},{10... | collective-permute-start | bytes 61448 | tf_op jit(solution)/shard_map/ppermute | solution.py:536
  20.4 1.2 %collective-permute-start.7 = (f32[5,8,128]{2,1,0:T(8,128)S(1)}, f32[5,8,128]{2,1,0:T(8,128)S(1)}, u32[]{:S(2)}, u32[]{:S(2)}) collective-permute-start(f32[5,8,128]{2,1,0:T(8,128)S(1)} %collective-permute-done.6.direct_ref), channel_id=1, source_target_pairs={{0,1},{1,0},{2,3},{3,2},{4,5},{5,4},{6,7},{7,6},{8,9},{9,8},{10,11... | collective-permute-start | bytes 61448 | tf_op jit(solution)/shard_map/ppermute | solution.py:535
  21.6 4.2 %collective-permute-start.8 = (f32[4,8,128]{2,1,0:T(8,128)S(1)}, f32[4,8,128]{2,1,0:T(8,128)S(1)}, u32[]{:S(2)}, u32[]{:S(2)}) collective-permute-start(f32[4,8,128]{2,1,0:T(8,128)S(1)} %get-tuple-element.16), channel_id=1, source_target_pairs={{1,2},{2,1},{3,4},{4,3},{5,6},{6,5},{0,8},{7,15},{9,10},{10,9},{11... | collective-permute-start | bytes 49160 | tf_op jit(solution)/shard_map/ppermute | solution.py:536
  25.8 1.2 %collective-permute-start.9 = (f32[4,8,128]{2,1,0:T(8,128)S(1)}, f32[4,8,128]{2,1,0:T(8,128)S(1)}, u32[]{:S(2)}, u32[]{:S(2)}) collective-permute-start(f32[4,8,128]{2,1,0:T(8,128)S(1)} %collective-permute-done.8.direct_ref), channel_id=1, source_target_pairs={{0,1},{1,0},{2,3},{3,2},{4,5},{5,4},{6,7},{7,6},{8,9},{9,8},{10,11... | collective-permute-start | bytes 49160 | tf_op jit(solution)/shard_map/ppermute | solution.py:535

commit v4 on v0

--- a/solution.py
+++ b/solution.py
@@ -1,7 +1,11 @@
+import functools
+
 import jax
 import jax.numpy as jnp
 import numpy as np
 from jax import lax
+from jax.experimental import pallas as pl
+from jax.experimental.pallas import tpu as pltpu
 from jax.sharding import PartitionSpec as P
 
 gll_points = np.array(
@@ -155,7 +159,7 @@
     return jnp.moveaxis(summed.reshape((blocks * 8,) + trailing), 0, direction)
 
 
-def body(initial, source, metric, eigenvectors, eigenvalues):
+def general_body(initial, source, metric, eigenvectors, eigenvalues):
     solution = initial
     local_res = source - apply_operator(solution, metric)
     deeper = extended_2(local_res, (("gx", 0), ("gy", 1), ("gz", 2)), 2)
@@ -168,6 +172,486 @@
     return solution
 
 
+AXES = ("gx", "gy", "gz")
+VMEM = pl.BlockSpec(memory_space=pltpu.VMEM)
+HBM = pl.BlockSpec(memory_space=pltpu.HBM)
+VMEM_LIMIT = 16 * 2**20
+f32 = jnp.float32
+bf16 = jnp.bfloat16
+
+
+def call(kernel, outs, args, scratch=(), where=VMEM):
+    moved = sum(int(np.prod(a.shape)) * a.dtype.itemsize for a in (*args, *outs))
+    return pl.pallas_call(
+        kernel,
+        out_shape=outs,
+        in_specs=[where] * len(args),
+        out_specs=[VMEM] * len(outs),
+        scratch_shapes=scratch,
+        compiler_params=pltpu.CompilerParams(vmem_limit_bytes=VMEM_LIMIT),
+        cost_estimate=pl.CostEstimate(flops=0, bytes_accessed=moved, transcendentals=0),
+    )(*args)
+
+
+def shaped(shape, dtype=f32):
+    return jax.ShapeDtypeStruct(shape, dtype)
+
+
+def counted(shape, axis):
+    return lax.broadcasted_iota(jnp.int32, shape, axis)
+
+
+def split2(value):
+    high = value.astype(bf16)
+    return high, (value - high.astype(f32)).astype(bf16)
+
+
+def split3(value):
+    high = value.astype(bf16)
+    rest = value - high.astype(f32)
+    middle = rest.astype(bf16)
+    return high, middle, (rest - middle.astype(f32)).astype(bf16)
+
+
+def dot(left, right, transposed=False):
+    dims = (((1,), (1 if transposed else 0,)), ((), ()))
+    return lax.dot_general(left, right, dims, preferred_element_type=f32)
+
+
+def repeated_table(table, width):
+    nodes = table.shape[0]
+    row, column = counted((nodes, width), 0), counted((nodes, width), 1) % nodes
+    tile = jnp.zeros((nodes, width), f32)
+    for j in range(nodes):
+        values = jnp.zeros((nodes, width), f32)
+        for i in range(nodes):
+            values = jnp.where(row == i, float(table[i, j]), values)
+        tile = jnp.where(column == j, values, tile)
+    return tile
+
+
+def residual_kernel(u_hbm, source_hbm, metric_hbm, out_ref, u_ref, source_ref, metric_ref, sems):
+    copies = [pltpu.make_async_copy(u_hbm, u_ref, sems.at[0])]
+    copies += [
+        pltpu.make_async_copy(metric_hbm.at[d], metric_ref.at[d], sems.at[1 + d])
+        for d in range(metric_hbm.shape[0])
+    ]
+    copies.append(pltpu.make_async_copy(source_hbm, source_ref, sems.at[len(copies)]))
+    for copy in copies:
+        copy.start()
+    nodes, rows, width = u_ref.shape
+    flat_rows = nodes * rows
+    table = np.asarray(derivative_table(), np.float32)
+    along_y, along_z = [], []
+    for t in range(2):
+        tile = repeated_table(table if t == 0 else table.T, width)
+        high = tile.astype(bf16).astype(f32)
+        low = tile - high
+        group = counted((nodes, width), 1) // nodes
+        zero = jnp.zeros_like(tile)
+        for part in (high, low):
+            bands = [jnp.where(group == k, part, zero) for k in range(width // nodes)]
+            along_z.append(jnp.concatenate(bands, axis=0).astype(bf16))
+        group = group[:, 0 : 2 * flat_rows]
+        high, low, zero = (v[:, 0 : 2 * flat_rows] for v in (high, low, zero))
+        bands = [jnp.where(group % rows == k, high, zero) for k in range(nodes)]
+        bands += [jnp.where(group == k, low, zero) for k in range(nodes)]
+        along_y.append(jnp.concatenate(bands, axis=0).astype(bf16))
+
+    def by_y(value, t):
+        both = dot(along_y[t], jnp.concatenate(split2(value), axis=0))
+        return both[0:flat_rows] + both[flat_rows:]
+
+    def by_z(value, t):
+        high, low = split2(value)
+        both = dot(jnp.concatenate([high, low], axis=0), along_z[2 * t])
+        return both[0:flat_rows] + (both[flat_rows:] + dot(high, along_z[2 * t + 1]))
+
+    copies[0].wait()
+    flat = u_ref[...].reshape(flat_rows, width)
+    flux_y, flux_z = by_y(flat, 0), by_z(flat, 1)
+    layers = [u_ref[j] for j in range(nodes)]
+    flux_x = [sum(float(table[i, j]) * layers[j] for j in range(nodes)) for i in range(nodes)]
+    for copy in copies[1:]:
+        copy.wait()
+    total = by_y(flux_y * metric_ref[1].reshape(flat.shape), 1)
+    total = total + by_z(flux_z * metric_ref[2].reshape(flat.shape), 0)
+    total = total.reshape(nodes, rows, width)
+    flux_x = [metric_ref[0, i] * flux_x[i] for i in range(nodes)]
+    for j in range(nodes):
+        applied = sum(float(table[i, j]) * flux_x[i] for i in range(nodes))
+        out_ref[j] = source_ref[j] - (applied + total[j])
+
+
+def layers_kernel(own_ref, partner_ref, out_ref):
+    start = lax.axis_index("gz") * (own_ref.shape[0] - 2)
+    for half, ref in enumerate((partner_ref, own_ref)):
+        for layer in range(2):
+            out_ref[half, layer] = ref[start + layer]
+
+
+def spread(own_ref, partner_ref, first, count, ext):
+    blocks = own_ref.shape[2]
+    parts = []
+    for ref in (own_ref, partner_ref):
+        parts += split3(ref[first : first + count].reshape(count, blocks))
+    shape = (blocks, 2 * blocks * ext)
+    repeat = []
+    for half in range(2):
+        element = counted(shape, 1) // ext - half * blocks
+        repeat += [(element == counted(shape, 0)).astype(f32).astype(bf16)] * 3
+    return dot(jnp.concatenate(parts, axis=1), jnp.concatenate(repeat, axis=0))
+
+
+def gathered(choice, value):
+    choice = choice.astype(f32).astype(bf16)
+    high, middle, low = split3(value)
+    return dot(choice, high) + (dot(choice, middle) + dot(choice, low))
+
+
+def xy_coefficients_kernel(own_ref, partner_ref, after_ref, cx_ref, cy_ref):
+    square = cx_ref.shape[0]
+    ext, padded = cy_ref.shape[1:3]
+    cx_ref[...] = spread(own_ref, partner_ref, 0, square, ext)
+    along_y = spread(own_ref, partner_ref, square, square, ext)
+    shape = (ext * padded, square)
+    first, second, entry = counted(shape, 0) // padded, counted(shape, 0) % padded, counted(shape, 1)
+    forward = (second < ext) & (entry == first * ext + second)
+    position = jnp.where(second < ext - 2, second + 1, jnp.where(second == ext - 2, 0, ext - 1))
+    backward = (second < ext) & (entry == position * ext + first)
+    for k, choice in enumerate((forward, backward)):
+        cy_ref[k] = gathered(choice, along_y).reshape(cy_ref.shape[1:])
+
+
+def z_coefficients_kernel(
+    own_vec, partner_vec, own_val, partner_val, after_ref, rate_ref, mz_ref
+):
+    ext, padded, lanes = rate_ref.shape
+    square = ext * ext
+    half = lanes // 2
+    blocks = half // ext
+    nodes = ext - 2
+    core = lax.axis_index("gz")
+    shape = (square, lanes)
+    same = counted(shape, 0) % ext == counted(shape, 1) % ext
+    along_z = spread(own_vec, partner_vec, 2 * square, square, ext)
+    along_z = jnp.where(same, along_z, jnp.zeros_like(along_z))
+    shape = (ext, square)
+    along_z = gathered(counted(shape, 1) // ext == counted(shape, 0), along_z)
+
+    rates = spread(own_val, partner_val, 0, 3 * ext, ext)
+    rate_z = rates[2 * ext : 3 * ext]
+    rate_z = jnp.where(same[0:ext], rate_z, jnp.zeros_like(rate_z))
+    rate_z = jnp.sum(rate_z, axis=0, keepdims=True)
+    rate_y = jnp.concatenate([rates[ext : 2 * ext], jnp.ones((padded - ext, lanes), f32)], axis=0)
+    for p in range(ext):
+        rate_ref[p] = 1.0 / (rates[p : p + 1] + rate_y + rate_z)
+
+    zeros = jnp.zeros((nodes - 2, lanes), f32)
+    own = along_z[1 : nodes + 1]
+    below = jnp.concatenate([zeros, along_z[0:2]], axis=0)
+    above = jnp.concatenate([along_z[nodes : nodes + 2], zeros], axis=0)
+    lane = lax.broadcasted_iota(jnp.int32, (nodes, lanes), 1)
+    first_own = core * blocks
+    first_partner = blocks - first_own
+    element = jnp.where(
+        lane < half, lane // ext + first_own, (lane - half) // ext + first_partner
+    )
+    zero = jnp.zeros_like(own)
+    for place in range(0, 2 * blocks, 2):
+        first = place + first_own if place < blocks else place - blocks + first_partner
+        pair = []
+        for block in (first, first + 1):
+            value = jnp.where(element == block, own, zero)
+            value = value + jnp.where(element == block + 1, below, zero)
+            pair.append(value + jnp.where(element == block - 1, above, zero))
+        high, low = split2(jnp.concatenate(pair, axis=0))
+        mz_ref[0, place * nodes : (place + 2) * nodes, :] = high
+        mz_ref[1, place * nodes : (place + 2) * nodes, :] = low
+
+
+def both_sides(core, direct, passed):
+    low = [jnp.where(core == 0, direct[h], passed[1 - h]) for h in range(2)]
+    high = [jnp.where(core == 0, passed[1 - h], direct[h]) for h in range(2)]
+    return low, high
+
+
+def edges(axis):
+    place, size = lax.axis_index(axis), lax.axis_size(axis)
+    return place > 0, place < size - 1
+
+
+def x_layers(core, own_ref, partner_ref, direct_ref, passed_ref):
+    has_low, has_high = edges("gx")
+    length = own_ref.shape[0]
+
+    def at(layer):
+        if 2 <= layer < length + 2:
+            return own_ref[layer - 2], partner_ref[layer - 2]
+        slot = layer if layer < 2 else layer - length - 2
+        direct = [direct_ref[h, slot] for h in range(2)]
+        passed = [passed_ref[h, slot] for h in range(2)]
+        low, high = both_sides(core, direct, passed)
+        side, valid = (low, has_low) if layer < 2 else (high, has_high)
+        return [jnp.where(valid, v, jnp.zeros_like(v)) for v in side]
+
+    return at
+
+
+def rows_kernel(own_ref, partner_ref, direct_ref, passed_ref, after_x, after_z, out_ref):
+    core = lax.axis_index("gz")
+    length, rows, width = own_ref.shape
+    at = x_layers(core, own_ref, partner_ref, direct_ref, passed_ref)
+    for layer in range(length + 4):
+        own, partner = at(layer)
+        for half, value in enumerate((partner, own)):
+            out_ref[layer, :, half * width : (half + 1) * width] = jnp.where(
+                core == 0, value[0:2], value[rows - 2 : rows]
+            )
+
+
+def by_z(value, mz):
+    high, low = split2(value)
+    return dot(high, mz[0]) + (dot(low, mz[0]) + dot(high, mz[1]))
+
+
+def back_by_z(value, mz):
+    high, low = split2(value)
+    return dot(high, mz[0], True) + (dot(low, mz[0], True) + dot(high, mz[1], True))
+
+
+def by_x(along_z, cx, ext):
+    last = along_z.shape[0] - 1
+    block = [along_z[0], along_z[1] + along_z[2]]
+    block += [along_z[k] for k in range(3, last - 2)]
+    block += [along_z[last - 2] + along_z[last - 1], along_z[last]]
+    for p in range(ext):
+        yield sum(cx[a * ext + p : a * ext + p + 1, :] * block[a] for a in range(ext))
+
+
+def interior_solve_kernel(
+    own_ref, partner_ref, xd_ref, xp_ref, after_ref, cx, cy, mz, out_ref, grid
+):
+    core = lax.axis_index("gz")
+    length, rows, width = own_ref.shape
+    ext = out_ref.shape[0]
+    at = x_layers(core, own_ref, partner_ref, xd_ref, xp_ref)
+    for layer in range(length + 4):
+        for half, value in enumerate(at(layer)):
+            grid[layer, :, half * width : (half + 1) * width] = value
+    along_z = by_z(grid[...].reshape((length + 4) * rows, 2 * width), mz)
+    along_z = along_z.reshape(length + 4, rows, along_z.shape[1])
+    for p, value in enumerate(by_x(along_z, cx, ext)):
+        out_ref[p] = sum(cy[0, b + 1] * value[b : b + 1] for b in range(rows))
+
+
+def solve_kernel(yd_ref, yp_ref, part_ref, cx, cy, rate, mz, spectral, sent_ref, grid):
+    core = lax.axis_index("gz")
+    length, _, both = yd_ref.shape
+    width = both // 2
+    ext, padded, lanes = rate.shape
+    nodes = ext - 2
+    has_low, has_high = edges("gy")
+    use_direct = jnp.where(core == 0, has_low, has_high)
+    use_passed = jnp.where(core == 0, has_high, has_low)
+    nothing = jnp.zeros((nodes - 4, both), f32)
+    for layer in range(length):
+        direct = yd_ref[layer]
+        passed = jnp.concatenate([yp_ref[layer, :, width:], yp_ref[layer, :, 0:width]], axis=1)
+        direct = jnp.where(use_direct, direct, jnp.zeros_like(direct))
+        passed = jnp.where(use_passed, passed, jnp.zeros_like(passed))
+        grid[layer] = jnp.concatenate([direct, passed, nothing], axis=0)
+    along_z = by_z(grid[...].reshape(length * nodes, both), mz)
+    along_z = along_z.reshape(length, nodes, lanes)
+    places = [core * nodes, core * nodes + 1, (1 - core) * nodes, (1 - core) * nodes + 1]
+    coefficients = [cy[0, place] for place in places]
+    for p, value in enumerate(by_x(along_z, cx, ext)):
+        total = part_ref[p] + sum(coefficients[k] * value[k : k + 1] for k in range(4))
+        total = total * rate[p]
+        spectral[p] = sum(cy[1, q] * total[q : q + 1] for q in range(ext))
+    layers = []
+    for layer in range(2):
+        value = None
+        for p in range(ext):
+            row = layer * ext + p
+            coefficient = jnp.where(
+                core == 0, cx[row : row + 1, :], cx[row + nodes * ext : row + nodes * ext + 1, :]
+            )
+            term = coefficient * spectral[p]
+            value = term if value is None else value + term
+        layers.append(value)
+    result = back_by_z(jnp.concatenate(layers, axis=0), mz)
+    for layer in range(2):
+        for half in range(2):
+            lanes_at = slice((1 - half) * width, (2 - half) * width)
+            place = half * 2 + layer
+            value = result[layer * padded : layer * padded + nodes + 2, lanes_at]
+            sent_ref[place] = value[0:nodes]
+            sent_ref[4, 2 * place : 2 * place + 2, :] = value[nodes : nodes + 2]
+
+
+def interior_kernel(spectral, cx, mz, after_ref, out_ref):
+    ext, padded, lanes = spectral.shape
+    nodes, _, both = out_ref.shape
+    layers = []
+    for a in range(1, ext - 1):
+        layers.append(
+            sum(cx[a * ext + p : a * ext + p + 1, :] * spectral[p] for p in range(ext))
+        )
+    result = back_by_z(jnp.concatenate(layers, axis=0), mz)
+    out_ref[...] = result.reshape(nodes, padded, both)
+
+
+def return_rows_kernel(initial_ref, inner_ref, direct_ref, passed_ref, out_ref, base_ref):
+    core = lax.axis_index("gz")
+    has_low, has_high = edges("gx")
+    nodes, rows, width = initial_ref.shape
+    for layer in range(nodes):
+        lanes = [slice(0, width), slice(width, 2 * width)]
+        outer = [inner_ref[layer, rows : rows + 2, lanes[h]] for h in range(2)]
+        values = [inner_ref[layer, 0:rows, lanes[h]] for h in range(2)]
+        if layer < 2 or layer >= nodes - 2:
+            slot = layer if layer < 2 else layer - (nodes - 2)
+
+            def parts(ref, h, slot=slot):
+                place = 2 * h + slot
+                return ref[place], ref[4, 2 * place : 2 * place + 2, :]
+
+            direct = [parts(direct_ref, h) for h in range(2)]
+            passed = [parts(passed_ref, h) for h in range(2)]
+            side = 0 if layer < 2 else 1
+            valid = (has_low, has_high)[side]
+            for k, target in enumerate((values, outer)):
+                both = both_sides(core, [d[k] for d in direct], [d[k] for d in passed])[side]
+                for h in range(2):
+                    target[h] = target[h] + jnp.where(valid, both[h], jnp.zeros_like(both[h]))
+        base_ref[layer] = initial_ref[layer] + values[0]
+        for place, h in enumerate((1, 0)):
+            first = jnp.where(core == 0, outer[h][0:1], values[h][rows - 1 : rows])
+            second = jnp.where(core == 0, values[h][0:1], outer[h][1:2])
+            out_ref[layer, :, lanes[place]] = jnp.concatenate([first, second], axis=0)
+
+
+def result_kernel(base_ref, direct_ref, passed_ref, out_ref):
+    core = lax.axis_index("gz")
+    has_low, has_high = edges("gy")
+    nodes, rows, width = base_ref.shape
+    for layer in range(nodes):
+        direct = direct_ref[layer, :, 0:width]
+        passed = passed_ref[layer, :, width:]
+        low = jnp.where(core == 0, direct, passed)
+        high = jnp.where(core == 0, passed, direct)
+        low = jnp.where(has_low, low, jnp.zeros_like(low))
+        high = jnp.where(has_high, high, jnp.zeros_like(high))
+        between = jnp.zeros((rows - 4, low.shape[1]), f32)
+        out_ref[layer] = base_ref[layer] + jnp.concatenate([low, between, high], axis=0)
+
+
+def swap_pairs(axis):
+    sizes = [lax.axis_size(name) for name in AXES]
+    along, across = (0, 1) if axis == "gx" else (1, 0)
+
+    def number(place, other, core):
+        spot = (place, other) if along == 0 else (other, place)
+        return (spot[0] * sizes[1] + spot[1]) * 2 + core
+
+    pairs = []
+    for other in range(sizes[across]):
+        for place in range(sizes[along] - 1):
+            here, there = number(place, other, 1), number(place + 1, other, 0)
+            pairs += [(here, there), (there, here)]
+        if other ^ 1 < sizes[across]:
+            for place, core in ((0, 0), (sizes[along] - 1, 1)):
+                pairs.append((number(place, other, core), number(place, other ^ 1, core)))
+    return pairs
+
+
+def swap(value, axis):
+    if axis == "gz":
+        return lax.ppermute(value, "gz", [(0, 1), (1, 0)])
+    return lax.ppermute(value, AXES, swap_pairs(axis))
+
+
+def paired_body(initial, source, metric, eigenvectors, eigenvalues):
+    nodes, rows, width = initial.shape
+    ext = eigenvectors.shape[1]
+    blocks = width // nodes
+    lanes = 2 * blocks * ext
+    padded = 2 * rows
+    vectors = eigenvectors.reshape(3 * ext * ext, 1, blocks)
+    values = eigenvalues.reshape(3 * ext, 1, blocks)
+    inputs = [
+        pltpu.with_memory_space_constraint(value, pltpu.HBM)
+        for value in (initial, source, metric)
+    ]
+    own = call(
+        residual_kernel,
+        [shaped(initial.shape)],
+        inputs,
+        scratch=[
+            *(pltpu.VMEM(value.shape, value.dtype) for value in inputs),
+            pltpu.SemaphoreType.DMA((2 + metric.shape[0],)),
+        ],
+        where=HBM,
+    )[0]
+    partner = swap(own, "gz")
+    partner_vectors = swap(lax.optimization_barrier((vectors, own))[0], "gz")
+    sent = call(layers_kernel, [shaped((2, 2, rows, width))], [own, partner])[0]
+    x_direct = swap(sent, "gx")
+    partner_values = swap(lax.optimization_barrier((values, sent))[0], "gz")
+    cx, cy = call(
+        xy_coefficients_kernel,
+        [shaped((ext * ext, lanes)), shaped((2, ext, padded, lanes))],
+        [vectors, partner_vectors, sent],
+    )
+    x_direct, cx, partner_values = lax.optimization_barrier((x_direct, cx, partner_values))
+    x_passed = swap(x_direct, "gz")
+    rate, mz = call(
+        z_coefficients_kernel,
+        [shaped((ext, padded, lanes)), shaped((2, 2 * width, lanes), bf16)],
+        [vectors, partner_vectors, values, partner_values, x_direct],
+    )
+    sent = call(
+        rows_kernel,
+        [shaped((nodes + 4, 2, 2 * width))],
+        [own, partner, x_direct, x_passed, cx, mz],
+    )[0]
+    y_direct = swap(sent, "gy")
+    part = call(
+        interior_solve_kernel,
+        [shaped((ext, padded, lanes))],
+        [own, partner, x_direct, x_passed, sent, cx, cy, mz],
+        scratch=[pltpu.VMEM((nodes + 4, rows, 2 * width), f32)],
+    )[0]
+    y_passed = swap(y_direct, "gz")
+    spectral, sent = call(
+        solve_kernel,
+        [shaped((ext, padded, lanes)), shaped((5, rows, width))],
+        [y_direct, y_passed, part, cx, cy, rate, mz],
+        scratch=[pltpu.VMEM((nodes + 4, rows, 2 * width), f32)],
+    )
+
+    x_direct = swap(sent, "gx")
+    inner = call(interior_kernel, [shaped((nodes, padded, 2 * width))], [spectral, cx, mz, sent])[0]
+    x_passed = swap(x_direct, "gz")
+    sent, base = call(
+        return_rows_kernel,
+        [shaped((nodes, 2, 2 * width)), shaped(initial.shape)],
+        [initial, inner, x_direct, x_passed],
+    )
+    y_direct = swap(sent, "gy")
+    y_passed = swap(y_direct, "gz")
+    return call(result_kernel, [shaped(initial.shape)], [base, y_direct, y_passed])[0]
+
+
+def body(initial, source, metric, eigenvectors, eigenvalues):
+    nodes = gll_points.shape[0]
+    one_element = initial.shape[0] == nodes and initial.shape[1] == nodes
+    if lax.axis_size("gz") == 2 and one_element and initial.shape[2] % 128 == 0:
+        return paired_body(initial, source, metric, eigenvectors, eigenvalues)
+    return general_body(initial, source, metric, eigenvectors, eigenvalues)
+
+
 def solution(mesh):
     placed = (
         P("gx", "gy", "gz"),

time: 78.8 us -> 25.7 us (0.33)
  starting transfers between devices: 26.6 us -> 9.66 us
  matrix products: 14.5 us -> 0 us
  local copies, waits for them, and re-layouts: 14.4 us -> 0.01 us
  waiting for transfers between devices: 18.6 us -> 9.79 us
  Pallas kernels: 0 us -> 6 us
  other arithmetic: 3.36 us -> 0 us
    ppermute x12 -> x11, starting transfers between devices: 26.6 us -> 9.66 us  [the longest x4 8.69 us: swap(): return lax.ppermute(value, AXES, swap_pairs(axis))]
    dot_general x12 -> x0, matrix products: 14.5 us -> none  [the longest x6 3.32 us: apply_along(): jnp.tensordot(values.reshape(pieces_shape), matrix, axes=((direction + 1,...]
    ppermute x12 -> x11, waiting for transfers between devices: 18.6 us -> 9.79 us  [the longest x4 6.45 us: swap(): return lax.ppermute(value, AXES, swap_pairs(axis))]
    pallas_call x0 -> x10, Pallas kernels: none -> 6 us  [call(): pl.pallas_call(kernel, out_shape=outs, in_specs=[where] * len(args), out_...]
    reshape x13 -> x0, local copies, waits for them, and re-layouts: 3.8 us -> none  [the longest x1 1.05 us: apply_along(): values.reshape(pieces_shape)]
    another operation x3 -> x0, local copies, waits for them, and re-layouts: 3.76 us -> none
    slice x25 -> x0, local copies, waits for them, and re-layouts: 2.55 us -> none  [the longest x1 0.78 us: apply_operator(): metric[direction] * gradient]
    add x6 -> x0, other arithmetic: 2.14 us -> none  [the longest x1 0.75 us: fast_solve(): spectral = spectral / (rate_x + rate_y + rate_z)]
  transfers between devices with their start and end apart: 12 -> 11, of which waited for: 7 -> 8; matrix products, arithmetic and copies ran while one was open for 5% -> 0% of each run, Pallas kernels for 0% -> 13%
where the time goes in v4:
time: 25.7 us; the launch traced here: 25.5 us
  waiting for transfers between devices  9.79 us (38%)
  starting transfers between devices  9.66 us (38%)
  Pallas kernels  6 us (23%)
    ppermute x4, starting transfers between devices, swap(): return lax.ppermute(value, AXES, swap_pairs(axis))  8.69 us
    ppermute x4, waiting for transfers between devices, swap(): return lax.ppermute(value, AXES, swap_pairs(axis))  6.45 us
    pallas_call x10, Pallas kernels, call(): pl.pallas_call(kernel, out_shape=outs, in_specs=[where] * len(args), out_...  6 us
    ppermute x7, waiting for transfers between devices, swap(): return lax.ppermute(value, 'gz', [(0, 1), (1, 0)])  3.34 us
    ppermute x7, starting transfers between devices, swap(): return lax.ppermute(value, 'gz', [(0, 1), (1, 0)])  0.97 us
  transfers between devices with their start and end apart: 11, of which 8 were waited for; matrix products, arithmetic and copies ran while one was open for 0% of the time, Pallas kernels for 13%

profile of v4, /device:TPU:0, one launch (start us, length us, event | category | flops | bytes accessed | tf_op | source)
XLA Modules:
  0.0 25.5 jit_solution(6738256169175411644)
XLA Ops:
  0.0 0.0 copy-start
  0.0 1.2 %shard_map.55.own_ref = f32[8,8,128]{2,1,0:T(8,128)S(1)} custom-call(f32[8,8,128]{2,1,0:T(8,128)} %initial_ref.1, f32[8,8,128]{2,1,0:T(8,128)} %source_hbm.1, f32[3,8,8,128]{3,2,1,0:T(8,128)} %metric_hbm.1), custom_call_target="tpu_custom_call" | custom-call | bytes 196608 | tf_op jit(solution)/shard_map/pallas_call | solution.py:185
  1.2 0.5 %collective-permute-start = (f32[8,8,128]{2,1,0:T(8,128)S(1)}, f32[8,8,128]{2,1,0:T(8,128)S(1)}, u32[]{:S(2)}, u32[]{:S(2)}) collective-permute-start(f32[8,8,128]{2,1,0:T(8,128)S(1)} %shard_map.55.own_ref), channel_id=1, source_target_pairs={{0,1},{1,0},{2,3},{3,2},{4,5},{5,4},{6,7},{7,6},{8,9},{9,8},{10,11... | collective-permute-start | bytes 98312 | tf_op jit(solution)/shard_map/ppermute | solution.py:571
  1.7 0.0 copy-done
  1.7 0.0 copy-start.2
  1.7 0.1 collective-permute-start.2
  1.8 0.8 %collective-permute-done.partner_ref = f32[8,8,128]{2,1,0:T(8,128)S(1)} collective-permute-done((f32[8,8,128]{2,1,0:T(8,128)S(1)}, f32[8,8,128]{2,1,0:T(8,128)S(1)}, u32[]{:S(2)}, u32[]{:S(2)}) %collective-permute-start) | collective-permute-done | bytes 32800 | tf_op jit(solution)/shard_map/ppermute | solution.py:571
  2.6 2.9 %collective-permute-start.1 = (f32[2,2,8,128]{3,2,1,0:T(8,128)S(1)}, f32[2,2,8,128]{3,2,1,0:T(8,128)S(1)}, u32[]{:S(2)}, u32[]{:S(2)}) collective-permute-start(f32[2,2,8,128]{3,2,1,0:T(8,128)S(1)} %shard_map.56.after_ref), channel_id=1, source_target_pairs={{1,8},{8,1},{9,16},{16,9},{17,24},{24,17},{0,2},{25,27},{3,10},{10... | collective-permute-start | bytes 49160 | tf_op jit(solution)/shard_map/ppermute | solution.py:572
  5.5 0.0 copy-done.2
  5.5 0.0 collective-permute-start.3
  5.6 0.0 collective-permute-done.2.partner_ref.partner_vec
  5.6 1.3 %shard_map.57 = (f32[100,320]{1,0:T(8,128)S(1)}, f32[2,10,16,320]{3,2,1,0:T(8,128)S(1)}) custom-call(f32[300,1,16]{2,1,0:T(1,128)S(1)} %bitcast.3, f32[300,1,16]{2,1,0:T(1,128)S(1)} %collective-permute-done.2.partner_ref.partner_vec, f32[2,2,8,128]{3,2,1,0:T(8,128)S(1)} %shard_map.56.after_ref), custom_call_target="tpu_custom_call" | custom-call | bytes 592384 | tf_op jit(solution)/shard_map/pallas_call | solution.py:185
  6.9 0.0 collective-permute-done.3.partner_val
  6.9 0.3 %collective-permute-done.1.after_ref.direct_ref.xd_ref = f32[2,2,8,128]{3,2,1,0:T(8,128)S(1)} collective-permute-done((f32[2,2,8,128]{3,2,1,0:T(8,128)S(1)}, f32[2,2,8,128]{3,2,1,0:T(8,128)S(1)}, u32[]{:S(2)}, u32[]{:S(2)}) %collective-permute-start.1) | collective-permute-done | bytes 16416 | tf_op jit(solution)/shard_map/ppermute | solution.py:572
  7.2 0.2 collective-permute-start.4
  7.4 1.1 %shard_map.58 = (f32[10,16,320]{2,1,0:T(8,128)S(1)}, bf16[2,256,320]{2,1,0:T(8,128)(2,1)S(1)}) custom-call(f32[300,1,16]{2,1,0:T(1,128)S(1)} %bitcast.4, f32[300,1,16]{2,1,0:T(1,128)S(1)} %collective-permute-done.2.partner_ref.partner_vec, f32[30,1,16]{2,1,0:T(1,128)S(1)} %bitcast.6, f32[30,1,16]{2,1,0:T(1,128)S(1)} %collective-permute-done.3.partner_val, ...), custom_call_target="tpu_custom_call" | custom-call | bytes 591104 | tf_op jit(solution)/shard_map/pallas_call | solution.py:185
  8.5 0.0 collective-permute-done.4.passed_ref.xp_ref
  8.6 2.3 %collective-permute-start.5 = (f32[12,2,256]{2,1,0:T(2,128)S(1)}, f32[12,2,256]{2,1,0:T(2,128)S(1)}, u32[]{:S(2)}, u32[]{:S(2)}) collective-permute-start(f32[12,2,256]{2,1,0:T(2,128)S(1)} %shard_map.59.after_ref), channel_id=1, source_target_pairs={{1,2},{2,1},{3,4},{4,3},{5,6},{6,5},{0,8},{7,15},{9,10},{10,9},{11... | collective-permute-start | bytes 73736 | tf_op jit(solution)/shard_map/ppermute | solution.py:572
  10.9 1.8 %collective-permute-done.5.yd_ref = f32[12,2,256]{2,1,0:T(2,128)S(1)} collective-permute-done((f32[12,2,256]{2,1,0:T(2,128)S(1)}, f32[12,2,256]{2,1,0:T(2,128)S(1)}, u32[]{:S(2)}, u32[]{:S(2)}) %collective-permute-start.5) | collective-permute-done | bytes 24608 | tf_op jit(solution)/shard_map/ppermute | solution.py:572
  12.7 0.0 collective-permute-start.6
  12.7 0.5 %shard_map.60.part_ref = f32[10,16,320]{2,1,0:T(8,128)S(1)} custom-call(f32[8,8,128]{2,1,0:T(8,128)S(1)} %shard_map.55.own_ref, f32[8,8,128]{2,1,0:T(8,128)S(1)} %collective-permute-done.partner_ref, f32[2,2,8,128]{3,2,1,0:T(8,128)S(1)} %collective-permute-done.1.after_ref.direct_ref.xd_ref, f32[2,2,8,128]{3,2,1,0:T(8,128)S(1)} %collective-permute-done.4.passed_ref.xp_ref, ...), custom_call_target="tpu_custom_call" | custom-call | bytes 1192960 | tf_op jit(solution)/shard_map/pallas_call | solution.py:185
  13.2 0.7 %collective-permute-done.6.yp_ref = f32[12,2,256]{2,1,0:T(2,128)S(1)} collective-permute-done((f32[12,2,256]{2,1,0:T(2,128)S(1)}, f32[12,2,256]{2,1,0:T(2,128)S(1)}, u32[]{:S(2)}, u32[]{:S(2)}) %collective-permute-start.6) | collective-permute-done | bytes 24608 | tf_op jit(solution)/shard_map/ppermute | solution.py:571
  13.9 0.8 %shard_map.61 = (f32[10,16,320]{2,1,0:T(8,128)S(1)}, f32[5,8,128]{2,1,0:T(8,128)S(1)}) custom-call(f32[12,2,256]{2,1,0:T(2,128)S(1)} %collective-permute-done.5.yd_ref, f32[12,2,256]{2,1,0:T(2,128)S(1)} %collective-permute-done.6.yp_ref, f32[10,16,320]{2,1,0:T(8,128)S(1)} %shard_map.60.part_ref, f32[100,320]{1,0:T(8,128)S(1)} %get-tuple-element.22.after_x.cx, ...), custom_call_target="tpu_custom_call" | custom-call | bytes 1549312 | tf_op jit(solution)/shard_map/pallas_call | solution.py:185
  14.7 1.3 %collective-permute-start.7 = (f32[5,8,128]{2,1,0:T(8,128)S(1)}, f32[5,8,128]{2,1,0:T(8,128)S(1)}, u32[]{:S(2)}, u32[]{:S(2)}) collective-permute-start(f32[5,8,128]{2,1,0:T(8,128)S(1)} %get-tuple-element.28.after_ref), channel_id=1, source_target_pairs={{1,8},{8,1},{9,16},{16,9},{17,24},{24,17},{0,2},{25,27},{3,10},{10... | collective-permute-start | bytes 61448 | tf_op jit(solution)/shard_map/ppermute | solution.py:572
  16.0 2.6 %collective-permute-done.7.direct_ref = f32[5,8,128]{2,1,0:T(8,128)S(1)} collective-permute-done((f32[5,8,128]{2,1,0:T(8,128)S(1)}, f32[5,8,128]{2,1,0:T(8,128)S(1)}, u32[]{:S(2)}, u32[]{:S(2)}) %collective-permute-start.7) | collective-permute-done | bytes 20512 | tf_op jit(solution)/shard_map/ppermute | solution.py:572
  18.5 0.1 collective-permute-start.8
  18.7 0.0 copy-start.1
  18.7 0.4 %shard_map.62.inner_ref = f32[8,16,256]{2,1,0:T(8,128)S(1)} custom-call(f32[10,16,320]{2,1,0:T(8,128)S(1)} %get-tuple-element.27.spectral, f32[100,320]{1,0:T(8,128)S(1)} %get-tuple-element.22.after_x.cx, bf16[2,256,320]{2,1,0:T(8,128)(2,1)S(1)} %get-tuple-element.24.after_z.mz, f32[5,8,128]{2,1,0:T(8,128)S(1)} %get-tuple-element.28.after_ref), custom_call_target="tpu_custom_call" | custom-call | bytes 812032 | tf_op jit(solution)/shard_map/pallas_call | solution.py:185
  19.0 0.7 %collective-permute-done.8.passed_ref = f32[5,8,128]{2,1,0:T(8,128)S(1)} collective-permute-done((f32[5,8,128]{2,1,0:T(8,128)S(1)}, f32[5,8,128]{2,1,0:T(8,128)S(1)}, u32[]{:S(2)}, u32[]{:S(2)}) %collective-permute-start.8) | collective-permute-done | bytes 20512 | tf_op jit(solution)/shard_map/ppermute | solution.py:571
  19.7 0.0 copy-done.1
  19.8 2.2 %collective-permute-start.9 = (f32[8,2,256]{2,1,0:T(2,128)S(1)}, f32[8,2,256]{2,1,0:T(2,128)S(1)}, u32[]{:S(2)}, u32[]{:S(2)}) collective-permute-start(f32[8,2,256]{2,1,0:T(2,128)S(1)} %get-tuple-element.30), channel_id=1, source_target_pairs={{1,2},{2,1},{3,4},{4,3},{5,6},{6,5},{0,8},{7,15},{9,10},{10,9},{11... | collective-permute-start | bytes 49160 | tf_op jit(solution)/shard_map/ppermute | solution.py:572
  22.0 1.7 %collective-permute-done.9.direct_ref = f32[8,2,256]{2,1,0:T(2,128)S(1)} collective-permute-done((f32[8,2,256]{2,1,0:T(2,128)S(1)}, f32[8,2,256]{2,1,0:T(2,128)S(1)}, u32[]{:S(2)}, u32[]{:S(2)}) %collective-permute-start.9) | collective-permute-done | bytes 16416 | tf_op jit(solution)/shard_map/ppermute | solution.py:572
  23.7 0.0 collective-permute-start.10
  23.7 1.2 %collective-permute-done.10.passed_ref = f32[8,2,256]{2,1,0:T(2,128)S(1)} collective-permute-done((f32[8,2,256]{2,1,0:T(2,128)S(1)}, f32[8,2,256]{2,1,0:T(2,128)S(1)}, u32[]{:S(2)}, u32[]{:S(2)}) %collective-permute-start.10) | collective-permute-done | bytes 16416 | tf_op jit(solution)/shard_map/ppermute | solution.py:571
  24.9 0.6 %shard_map.64 = f32[8,8,128]{2,1,0:T(8,128)} custom-call(f32[8,8,128]{2,1,0:T(8,128)S(1)} %get-tuple-element.29.base_ref, f32[8,2,256]{2,1,0:T(2,128)S(1)} %collective-permute-done.9.direct_ref, f32[8,2,256]{2,1,0:T(2,128)S(1)} %collective-permute-done.10.passed_ref), custom_call_target="tpu_custom_call" | custom-call | bytes 98304 | tf_op jit(solution)/shard_map/pallas_call | solution.py:185
  (3 shorter events, 0.1 us)
Async XLA Ops:
  0.0 1.7 %copy-start = (f32[3,10,10,1,1,16]{5,4,3,2,1,0:T(1,128)S(1)}, f32[3,10,10,1,1,16]{5,4,3,2,1,0:T(1,128)}, u32[]{:S(2)}) copy-start(f32[3,10,10,1,1,16]{5,4,3,2,1,0:T(1,128)} %param.8) | copy-start | bytes 57604
  1.2 1.4 %collective-permute-start = (f32[8,8,128]{2,1,0:T(8,128)S(1)}, f32[8,8,128]{2,1,0:T(8,128)S(1)}, u32[]{:S(2)}, u32[]{:S(2)}) collective-permute-start(f32[8,8,128]{2,1,0:T(8,128)S(1)} %shard_map.55.own_ref), channel_id=1, source_target_pairs={{0,1},{1,0},{2,3},{3,2},{4,5},{5,4},{6,7},{7,6},{8,9},{9,8},{10,11... | collective-permute-start | bytes 98312 | tf_op jit(solution)/shard_map/ppermute | solution.py:571
  1.7 3.8 %copy-start.2 = (f32[3,10,1,1,16]{4,3,2,1,0:T(1,128)S(1)}, f32[3,10,1,1,16]{4,3,2,1,0:T(1,128)}, u32[]{:S(2)}) copy-start(f32[3,10,1,1,16]{4,3,2,1,0:T(1,128)} %param.9) | copy-start | bytes 5764
  1.7 3.8 %collective-permute-start.2 = (f32[300,1,16]{2,1,0:T(1,128)S(1)}, f32[300,1,16]{2,1,0:T(1,128)S(1)}, u32[]{:S(2)}, u32[]{:S(2)}) collective-permute-start(f32[300,1,16]{2,1,0:T(1,128)S(1)} %bitcast.2), channel_id=1, source_target_pairs={{0,1},{1,0},{2,3},{3,2},{4,5},{5,4},{6,7},{7,6},{8,9},{9,8},{10,11... | collective-permute-start | bytes 57608 | tf_op jit(solution)/shard_map/ppermute | solution.py:571
  2.6 4.6 %collective-permute-start.1 = (f32[2,2,8,128]{3,2,1,0:T(8,128)S(1)}, f32[2,2,8,128]{3,2,1,0:T(8,128)S(1)}, u32[]{:S(2)}, u32[]{:S(2)}) collective-permute-start(f32[2,2,8,128]{3,2,1,0:T(8,128)S(1)} %shard_map.56.after_ref), channel_id=1, source_target_pairs={{1,8},{8,1},{9,16},{16,9},{17,24},{24,17},{0,2},{25,27},{3,10},{10... | collective-permute-start | bytes 49160 | tf_op jit(solution)/shard_map/ppermute | solution.py:572
  5.5 1.4 %collective-permute-start.3 = (f32[30,1,16]{2,1,0:T(1,128)S(1)}, f32[30,1,16]{2,1,0:T(1,128)S(1)}, u32[]{:S(2)}, u32[]{:S(2)}) collective-permute-start(f32[30,1,16]{2,1,0:T(1,128)S(1)} %bitcast.5), channel_id=1, source_target_pairs={{0,1},{1,0},{2,3},{3,2},{4,5},{5,4},{6,7},{7,6},{8,9},{9,8},{10,11... | collective-permute-start | bytes 5768 | tf_op jit(solution)/shard_map/ppermute | solution.py:571
  7.2 1.3 %collective-permute-start.4 = (f32[2,2,8,128]{3,2,1,0:T(8,128)S(1)}, f32[2,2,8,128]{3,2,1,0:T(8,128)S(1)}, u32[]{:S(2)}, u32[]{:S(2)}) collective-permute-start(f32[2,2,8,128]{3,2,1,0:T(8,128)S(1)} %collective-permute-done.1.after_ref.direct_ref.xd_ref), channel_id=1, source_target_pairs={{0,1},{1,0},{2,3},{3,2},{4,5},{5,4},{6,7},{7,6},{8,9},{9,8},{10,11... | collective-permute-start | bytes 49160 | tf_op jit(solution)/shard_map/ppermute | solution.py:571
  8.6 4.1 %collective-permute-start.5 = (f32[12,2,256]{2,1,0:T(2,128)S(1)}, f32[12,2,256]{2,1,0:T(2,128)S(1)}, u32[]{:S(2)}, u32[]{:S(2)}) collective-permute-start(f32[12,2,256]{2,1,0:T(2,128)S(1)} %shard_map.59.after_ref), channel_id=1, source_target_pairs={{1,2},{2,1},{3,4},{4,3},{5,6},{6,5},{0,8},{7,15},{9,10},{10,9},{11... | collective-permute-start | bytes 73736 | tf_op jit(solution)/shard_map/ppermute | solution.py:572
  12.7 1.2 %collective-permute-start.6 = (f32[12,2,256]{2,1,0:T(2,128)S(1)}, f32[12,2,256]{2,1,0:T(2,128)S(1)}, u32[]{:S(2)}, u32[]{:S(2)}) collective-permute-start(f32[12,2,256]{2,1,0:T(2,128)S(1)} %collective-permute-done.5.yd_ref), channel_id=1, source_target_pairs={{0,1},{1,0},{2,3},{3,2},{4,5},{5,4},{6,7},{7,6},{8,9},{9,8},{10,11... | collective-permute-start | bytes 73736 | tf_op jit(solution)/shard_map/ppermute | solution.py:571
  14.7 3.8 %collective-permute-start.7 = (f32[5,8,128]{2,1,0:T(8,128)S(1)}, f32[5,8,128]{2,1,0:T(8,128)S(1)}, u32[]{:S(2)}, u32[]{:S(2)}) collective-permute-start(f32[5,8,128]{2,1,0:T(8,128)S(1)} %get-tuple-element.28.after_ref), channel_id=1, source_target_pairs={{1,8},{8,1},{9,16},{16,9},{17,24},{24,17},{0,2},{25,27},{3,10},{10... | collective-permute-start | bytes 61448 | tf_op jit(solution)/shard_map/ppermute | solution.py:572
  18.5 1.2 %collective-permute-start.8 = (f32[5,8,128]{2,1,0:T(8,128)S(1)}, f32[5,8,128]{2,1,0:T(8,128)S(1)}, u32[]{:S(2)}, u32[]{:S(2)}) collective-permute-start(f32[5,8,128]{2,1,0:T(8,128)S(1)} %collective-permute-done.7.direct_ref), channel_id=1, source_target_pairs={{0,1},{1,0},{2,3},{3,2},{4,5},{5,4},{6,7},{7,6},{8,9},{9,8},{10,11... | collective-permute-start | bytes 61448 | tf_op jit(solution)/shard_map/ppermute | solution.py:571
  18.7 1.1 %copy-start.1 = (f32[8,8,128]{2,1,0:T(8,128)S(1)}, f32[8,8,128]{2,1,0:T(8,128)}, u32[]{:S(2)}) copy-start(f32[8,8,128]{2,1,0:T(8,128)} %initial_ref.1) | copy-start | bytes 98308
  19.8 3.9 %collective-permute-start.9 = (f32[8,2,256]{2,1,0:T(2,128)S(1)}, f32[8,2,256]{2,1,0:T(2,128)S(1)}, u32[]{:S(2)}, u32[]{:S(2)}) collective-permute-start(f32[8,2,256]{2,1,0:T(2,128)S(1)} %get-tuple-element.30), channel_id=1, source_target_pairs={{1,2},{2,1},{3,4},{4,3},{5,6},{6,5},{0,8},{7,15},{9,10},{10,9},{11... | collective-permute-start | bytes 49160 | tf_op jit(solution)/shard_map/ppermute | solution.py:572
  23.7 1.2 %collective-permute-start.10 = (f32[8,2,256]{2,1,0:T(2,128)S(1)}, f32[8,2,256]{2,1,0:T(2,128)S(1)}, u32[]{:S(2)}, u32[]{:S(2)}) collective-permute-start(f32[8,2,256]{2,1,0:T(2,128)S(1)} %collective-permute-done.9.direct_ref), channel_id=1, source_target_pairs={{0,1},{1,0},{2,3},{3,2},{4,5},{5,4},{6,7},{7,6},{8,9},{9,8},{10,11... | collective-permute-start | bytes 49160 | tf_op jit(solution)/shard_map/ppermute | solution.py:571

commit v5 on v4

--- a/solution.py
+++ b/solution.py
@@ -230,13 +230,16 @@
     return tile
 
 
-def residual_kernel(u_hbm, source_hbm, metric_hbm, out_ref, u_ref, source_ref, metric_ref, sems):
+def residual_kernel(
+    u_hbm, source_hbm, metric_hbm, val_hbm, out_ref, u_ref, source_ref, metric_ref, val_ref, sems
+):
     copies = [pltpu.make_async_copy(u_hbm, u_ref, sems.at[0])]
     copies += [
         pltpu.make_async_copy(metric_hbm.at[d], metric_ref.at[d], sems.at[1 + d])
         for d in range(metric_hbm.shape[0])
     ]
     copies.append(pltpu.make_async_copy(source_hbm, source_ref, sems.at[len(copies)]))
+    copies.append(pltpu.make_async_copy(val_hbm, val_ref, sems.at[len(copies)]))
     for copy in copies:
         copy.start()
     nodes, rows, width = u_ref.shape
@@ -281,20 +284,27 @@
     for j in range(nodes):
         applied = sum(float(table[i, j]) * flux_x[i] for i in range(nodes))
         out_ref[j] = source_ref[j] - (applied + total[j])
+    count, _, blocks = val_ref.shape
+    values = val_ref[...].reshape(count, blocks)
+    for first in range(0, count, rows):
+        last = min(first + rows, count)
+        out_ref[nodes + first // rows, 0 : last - first, 0:blocks] = values[first:last]
 
 
 def layers_kernel(own_ref, partner_ref, out_ref):
-    start = lax.axis_index("gz") * (own_ref.shape[0] - 2)
+    start = lax.axis_index("gz") * (out_ref.shape[2] - 2)
     for half, ref in enumerate((partner_ref, own_ref)):
         for layer in range(2):
             out_ref[half, layer] = ref[start + layer]
 
 
-def spread(own_ref, partner_ref, first, count, ext):
-    blocks = own_ref.shape[2]
-    parts = []
-    for ref in (own_ref, partner_ref):
-        parts += split3(ref[first : first + count].reshape(count, blocks))
+def taken(ref, first, count):
+    return ref[first : first + count].reshape(count, ref.shape[2])
+
+
+def spread(own, partner, ext):
+    blocks = own.shape[1]
+    parts = [*split3(own), *split3(partner)]
     shape = (blocks, 2 * blocks * ext)
     repeat = []
     for half in range(2):
@@ -309,11 +319,37 @@
     return dot(choice, high) + (dot(choice, middle) + dot(choice, low))
 
 
-def xy_coefficients_kernel(own_ref, partner_ref, after_ref, cx_ref, cy_ref):
-    square = cx_ref.shape[0]
+def x_coefficients_kernel(
+    own_vec, partner_vec, own_ref, partner_ref, after_ref, cx_ref, cx_rows_ref, rate_ref
+):
+    ext, padded, lanes = rate_ref.shape
+    blocks = own_vec.shape[2]
+    nodes = ext - 2
+    square = ext * ext
+    along_x = spread(taken(own_vec, 0, square), taken(partner_vec, 0, square), ext)
+    cx_ref[...] = along_x
+    shape = (cx_rows_ref.shape[0], square)
+    place = counted(shape, 0) % (shape[0] // ext) // 2
+    choice = (place < ext) & (counted(shape, 1) == place * ext + counted(shape, 0) // (shape[0] // ext))
+    cx_rows_ref[...] = gathered(choice, along_x)
+    rates = []
+    for ref in (own_ref, partner_ref):
+        tiles = ref[nodes : ref.shape[0]]
+        rates.append(tiles.reshape(-1, tiles.shape[2])[0 : 3 * ext, 0:blocks])
+    rates = spread(*rates, ext)
+    shape = (ext, lanes)
+    rate_z = rates[2 * ext : 3 * ext]
+    same = counted(shape, 0) == counted(shape, 1) % ext
+    rate_z = jnp.sum(jnp.where(same, rate_z, jnp.zeros_like(rate_z)), axis=0, keepdims=True)
+    rate_y = jnp.concatenate([rates[ext : 2 * ext], jnp.ones((padded - ext, lanes), f32)], axis=0)
+    for p in range(ext):
+        rate_ref[p] = 1.0 / (rates[p : p + 1] + rate_y + rate_z)
+
+
+def y_coefficients_kernel(own_vec, partner_vec, after_ref, cy_ref):
     ext, padded = cy_ref.shape[1:3]
-    cx_ref[...] = spread(own_ref, partner_ref, 0, square, ext)
-    along_y = spread(own_ref, partner_ref, square, square, ext)
+    square = ext * ext
+    along_y = spread(taken(own_vec, square, square), taken(partner_vec, square, square), ext)
     shape = (ext * padded, square)
     first, second, entry = counted(shape, 0) // padded, counted(shape, 0) % padded, counted(shape, 1)
     forward = (second < ext) & (entry == first * ext + second)
@@ -323,40 +359,31 @@
         cy_ref[k] = gathered(choice, along_y).reshape(cy_ref.shape[1:])
 
 
-def z_coefficients_kernel(
-    own_vec, partner_vec, own_val, partner_val, after_ref, rate_ref, mz_ref
-):
-    ext, padded, lanes = rate_ref.shape
+def z_coefficients_kernel(own_vec, partner_vec, after_ref, mz_ref):
+    blocks = own_vec.shape[2]
+    lanes = mz_ref.shape[2]
+    half = lanes // 2
+    ext = half // blocks
     square = ext * ext
-    half = lanes // 2
-    blocks = half // ext
     nodes = ext - 2
     core = lax.axis_index("gz")
     shape = (square, lanes)
     same = counted(shape, 0) % ext == counted(shape, 1) % ext
-    along_z = spread(own_vec, partner_vec, 2 * square, square, ext)
+    along_z = spread(
+        taken(own_vec, 2 * square, square), taken(partner_vec, 2 * square, square), ext
+    )
     along_z = jnp.where(same, along_z, jnp.zeros_like(along_z))
     shape = (ext, square)
     along_z = gathered(counted(shape, 1) // ext == counted(shape, 0), along_z)
-
-    rates = spread(own_val, partner_val, 0, 3 * ext, ext)
-    rate_z = rates[2 * ext : 3 * ext]
-    rate_z = jnp.where(same[0:ext], rate_z, jnp.zeros_like(rate_z))
-    rate_z = jnp.sum(rate_z, axis=0, keepdims=True)
-    rate_y = jnp.concatenate([rates[ext : 2 * ext], jnp.ones((padded - ext, lanes), f32)], axis=0)
-    for p in range(ext):
-        rate_ref[p] = 1.0 / (rates[p : p + 1] + rate_y + rate_z)
 
     zeros = jnp.zeros((nodes - 2, lanes), f32)
     own = along_z[1 : nodes + 1]
     below = jnp.concatenate([zeros, along_z[0:2]], axis=0)
     above = jnp.concatenate([along_z[nodes : nodes + 2], zeros], axis=0)
-    lane = lax.broadcasted_iota(jnp.int32, (nodes, lanes), 1)
+    lane = counted((nodes, lanes), 1)
     first_own = core * blocks
     first_partner = blocks - first_own
-    element = jnp.where(
-        lane < half, lane // ext + first_own, (lane - half) // ext + first_partner
-    )
+    element = jnp.where(lane < half, lane // ext + first_own, (lane - half) // ext + first_partner)
     zero = jnp.zeros_like(own)
     for place in range(0, 2 * blocks, 2):
         first = place + first_own if place < blocks else place - blocks + first_partner
@@ -381,31 +408,37 @@
     return place > 0, place < size - 1
 
 
-def x_layers(core, own_ref, partner_ref, direct_ref, passed_ref):
+def x_positions(core, own_ref, partner_ref, direct_ref, passed_ref):
     has_low, has_high = edges("gx")
-    length = own_ref.shape[0]
-
-    def at(layer):
-        if 2 <= layer < length + 2:
-            return own_ref[layer - 2], partner_ref[layer - 2]
-        slot = layer if layer < 2 else layer - length - 2
+    length = own_ref.shape[1]
+    sides = []
+    for slot in range(2):
         direct = [direct_ref[h, slot] for h in range(2)]
         passed = [passed_ref[h, slot] for h in range(2)]
         low, high = both_sides(core, direct, passed)
-        side, valid = (low, has_low) if layer < 2 else (high, has_high)
-        return [jnp.where(valid, v, jnp.zeros_like(v)) for v in side]
-
-    return at
-
-
-def rows_kernel(own_ref, partner_ref, direct_ref, passed_ref, after_x, after_z, out_ref):
+        low = [jnp.where(has_low, v, jnp.zeros_like(v)) for v in low]
+        high = [jnp.where(has_high, v, jnp.zeros_like(v)) for v in high]
+        sides.append((low, high))
+    positions = [sides[0][0]]
+    for layer in range(length):
+        value = [own_ref[layer], partner_ref[layer]]
+        if layer == 0:
+            value = [v + w for v, w in zip(sides[1][0], value)]
+        if layer == length - 1:
+            value = [v + w for v, w in zip(value, sides[0][1])]
+        positions.append(value)
+    return positions + [sides[1][1]]
+
+
+def rows_kernel(own_ref, partner_ref, direct_ref, passed_ref, after_ref, out_ref):
     core = lax.axis_index("gz")
-    length, rows, width = own_ref.shape
-    at = x_layers(core, own_ref, partner_ref, direct_ref, passed_ref)
-    for layer in range(length + 4):
-        own, partner = at(layer)
+    _, rows, width = own_ref.shape
+    positions = x_positions(core, own_ref, partner_ref, direct_ref, passed_ref)
+    out_ref[out_ref.shape[0] - 1] = jnp.zeros(out_ref.shape[1:], f32)
+    for a, (own, partner) in enumerate(positions):
+        row = 2 * a % rows
         for half, value in enumerate((partner, own)):
-            out_ref[layer, :, half * width : (half + 1) * width] = jnp.where(
+            out_ref[2 * a // rows, row : row + 2, half * width : (half + 1) * width] = jnp.where(
                 core == 0, value[0:2], value[rows - 2 : rows]
             )
 
@@ -420,66 +453,73 @@
     return dot(high, mz[0], True) + (dot(low, mz[0], True) + dot(high, mz[1], True))
 
 
-def by_x(along_z, cx, ext):
-    last = along_z.shape[0] - 1
-    block = [along_z[0], along_z[1] + along_z[2]]
-    block += [along_z[k] for k in range(3, last - 2)]
-    block += [along_z[last - 2] + along_z[last - 1], along_z[last]]
+def from_rows(value, use, mz, cx_rows, ext):
+    count, rows, both = value.shape
+    value = jnp.where(use, value, jnp.zeros_like(value))
+    along_z = by_z(value.reshape(count * rows, both), mz)
     for p in range(ext):
-        yield sum(cx[a * ext + p : a * ext + p + 1, :] * block[a] for a in range(ext))
+        total = sum(
+            cx_rows[(p * count + t) * rows : (p * count + t + 1) * rows, :]
+            * along_z[t * rows : (t + 1) * rows]
+            for t in range(count)
+        )
+        shift = 2
+        while shift < rows:
+            total = total + pltpu.roll(total, shift, 0)
+            shift *= 2
+        yield total
 
 
 def interior_solve_kernel(
-    own_ref, partner_ref, xd_ref, xp_ref, after_ref, cx, cy, mz, out_ref, grid
+    own_ref, partner_ref, xd_ref, xp_ref, yd_ref, cx, cx_rows, cy, mz, out_ref, grid
 ):
     core = lax.axis_index("gz")
-    length, rows, width = own_ref.shape
-    ext = out_ref.shape[0]
-    at = x_layers(core, own_ref, partner_ref, xd_ref, xp_ref)
-    for layer in range(length + 4):
-        for half, value in enumerate(at(layer)):
-            grid[layer, :, half * width : (half + 1) * width] = value
-    along_z = by_z(grid[...].reshape((length + 4) * rows, 2 * width), mz)
-    along_z = along_z.reshape(length + 4, rows, along_z.shape[1])
-    for p, value in enumerate(by_x(along_z, cx, ext)):
-        out_ref[p] = sum(cy[0, b + 1] * value[b : b + 1] for b in range(rows))
-
-
-def solve_kernel(yd_ref, yp_ref, part_ref, cx, cy, rate, mz, spectral, sent_ref, grid):
+    _, rows, width = own_ref.shape
+    ext, padded, lanes = out_ref.shape
+    nodes = ext - 2
+    has_low, has_high = edges("gy")
+    positions = x_positions(core, own_ref, partner_ref, xd_ref, xp_ref)
+    for a, halves in enumerate(positions):
+        for half, value in enumerate(halves):
+            grid[a, :, half * width : (half + 1) * width] = value
+    along_z = by_z(grid[...].reshape(ext * rows, 2 * width), mz)
+    along_z = along_z.reshape(ext, rows, lanes)
+    use = jnp.where(core == 0, has_low, has_high)
+    outer = [cy[0, core * nodes + k] for k in range(2)]
+    for p, value in enumerate(from_rows(yd_ref[...], use, mz, cx_rows, ext)):
+        inner = sum(cx[a * ext + p : a * ext + p + 1, :] * along_z[a] for a in range(ext))
+        total = sum(cy[0, b + 1] * inner[b : b + 1] for b in range(rows))
+        out_ref[p] = total + sum(outer[k] * value[k : k + 1] for k in range(2))
+
+
+def back_by_x(spectral, coefficients):
+    return sum(c * spectral[p] for p, c in enumerate(coefficients))
+
+
+def back_by_y(value, cy, ext):
+    return sum(cy[1, q] * value[q : q + 1] for q in range(ext))
+
+
+def solve_kernel(yp_ref, part_ref, cx, cx_rows, cy, rate, mz, spectral, sent_ref):
     core = lax.axis_index("gz")
-    length, _, both = yd_ref.shape
-    width = both // 2
+    width = yp_ref.shape[2] // 2
     ext, padded, lanes = rate.shape
     nodes = ext - 2
     has_low, has_high = edges("gy")
-    use_direct = jnp.where(core == 0, has_low, has_high)
-    use_passed = jnp.where(core == 0, has_high, has_low)
-    nothing = jnp.zeros((nodes - 4, both), f32)
-    for layer in range(length):
-        direct = yd_ref[layer]
-        passed = jnp.concatenate([yp_ref[layer, :, width:], yp_ref[layer, :, 0:width]], axis=1)
-        direct = jnp.where(use_direct, direct, jnp.zeros_like(direct))
-        passed = jnp.where(use_passed, passed, jnp.zeros_like(passed))
-        grid[layer] = jnp.concatenate([direct, passed, nothing], axis=0)
-    along_z = by_z(grid[...].reshape(length * nodes, both), mz)
-    along_z = along_z.reshape(length, nodes, lanes)
-    places = [core * nodes, core * nodes + 1, (1 - core) * nodes, (1 - core) * nodes + 1]
-    coefficients = [cy[0, place] for place in places]
-    for p, value in enumerate(by_x(along_z, cx, ext)):
-        total = part_ref[p] + sum(coefficients[k] * value[k : k + 1] for k in range(4))
-        total = total * rate[p]
-        spectral[p] = sum(cy[1, q] * total[q : q + 1] for q in range(ext))
+    passed = jnp.concatenate([yp_ref[:, :, width:], yp_ref[:, :, 0:width]], axis=2)
+    use = jnp.where(core == 0, has_high, has_low)
+    outer = [cy[0, (1 - core) * nodes + k] for k in range(2)]
+    for p, value in enumerate(from_rows(passed, use, mz, cx_rows, ext)):
+        total = part_ref[p] + sum(outer[k] * value[k : k + 1] for k in range(2))
+        spectral[p] = total * rate[p]
     layers = []
     for layer in range(2):
-        value = None
-        for p in range(ext):
-            row = layer * ext + p
-            coefficient = jnp.where(
-                core == 0, cx[row : row + 1, :], cx[row + nodes * ext : row + nodes * ext + 1, :]
-            )
-            term = coefficient * spectral[p]
-            value = term if value is None else value + term
-        layers.append(value)
+        rows = [layer * ext + p for p in range(ext)]
+        last = [r + nodes * ext for r in rows]
+        coefficients = [
+            jnp.where(core == 0, cx[r : r + 1, :], cx[k : k + 1, :]) for r, k in zip(rows, last)
+        ]
+        layers.append(back_by_y(back_by_x(spectral, coefficients), cy, ext))
     result = back_by_z(jnp.concatenate(layers, axis=0), mz)
     for layer in range(2):
         for half in range(2):
@@ -490,14 +530,13 @@
             sent_ref[4, 2 * place : 2 * place + 2, :] = value[nodes : nodes + 2]
 
 
-def interior_kernel(spectral, cx, mz, after_ref, out_ref):
+def interior_kernel(spectral, cx, cy, mz, after_ref, out_ref):
     ext, padded, lanes = spectral.shape
     nodes, _, both = out_ref.shape
     layers = []
     for a in range(1, ext - 1):
-        layers.append(
-            sum(cx[a * ext + p : a * ext + p + 1, :] * spectral[p] for p in range(ext))
-        )
+        coefficients = [cx[a * ext + p : a * ext + p + 1, :] for p in range(ext)]
+        layers.append(back_by_y(back_by_x(spectral, coefficients), cy, ext))
     result = back_by_z(jnp.concatenate(layers, axis=0), mz)
     out_ref[...] = result.reshape(nodes, padded, both)
 
@@ -582,57 +621,67 @@
     values = eigenvalues.reshape(3 * ext, 1, blocks)
     inputs = [
         pltpu.with_memory_space_constraint(value, pltpu.HBM)
-        for value in (initial, source, metric)
+        for value in (initial, source, metric, values)
     ]
     own = call(
         residual_kernel,
-        [shaped(initial.shape)],
+        [shaped((nodes + -(-3 * ext // rows), rows, width))],
         inputs,
         scratch=[
             *(pltpu.VMEM(value.shape, value.dtype) for value in inputs),
-            pltpu.SemaphoreType.DMA((2 + metric.shape[0],)),
+            pltpu.SemaphoreType.DMA((3 + metric.shape[0],)),
         ],
         where=HBM,
     )[0]
     partner = swap(own, "gz")
-    partner_vectors = swap(lax.optimization_barrier((vectors, own))[0], "gz")
+    vectors, own = lax.optimization_barrier((vectors, own))
+    partner_vectors = swap(vectors, "gz")
     sent = call(layers_kernel, [shaped((2, 2, rows, width))], [own, partner])[0]
     x_direct = swap(sent, "gx")
-    partner_values = swap(lax.optimization_barrier((values, sent))[0], "gz")
-    cx, cy = call(
-        xy_coefficients_kernel,
-        [shaped((ext * ext, lanes)), shaped((2, ext, padded, lanes))],
-        [vectors, partner_vectors, sent],
-    )
-    x_direct, cx, partner_values = lax.optimization_barrier((x_direct, cx, partner_values))
+    tiles = -(-2 * ext // rows)
+    cx, cx_rows, rate = call(
+        x_coefficients_kernel,
+        [
+            shaped((ext * ext, lanes)),
+            shaped((ext * tiles * rows, lanes)),
+            shaped((ext, padded, lanes)),
+        ],
+        [vectors, partner_vectors, own, partner, sent],
+    )
+    x_direct, cx, rate = lax.optimization_barrier((x_direct, cx, rate))
     x_passed = swap(x_direct, "gz")
-    rate, mz = call(
+    mz = call(
         z_coefficients_kernel,
-        [shaped((ext, padded, lanes)), shaped((2, 2 * width, lanes), bf16)],
-        [vectors, partner_vectors, values, partner_values, x_direct],
-    )
+        [shaped((2, 2 * width, lanes), bf16)],
+        [vectors, partner_vectors, x_direct],
+    )[0]
     sent = call(
         rows_kernel,
-        [shaped((nodes + 4, 2, 2 * width))],
-        [own, partner, x_direct, x_passed, cx, mz],
+        [shaped((tiles, rows, 2 * width))],
+        [own, partner, x_direct, x_passed, mz],
     )[0]
     y_direct = swap(sent, "gy")
+    cy = call(
+        y_coefficients_kernel,
+        [shaped((2, ext, padded, lanes))],
+        [vectors, partner_vectors, sent],
+    )[0]
+    y_direct, cy = lax.optimization_barrier((y_direct, cy))
+    y_passed = swap(y_direct, "gz")
     part = call(
         interior_solve_kernel,
         [shaped((ext, padded, lanes))],
-        [own, partner, x_direct, x_passed, sent, cx, cy, mz],
-        scratch=[pltpu.VMEM((nodes + 4, rows, 2 * width), f32)],
+        [own, partner, x_direct, x_passed, y_direct, cx, cx_rows, cy, mz],
+        scratch=[pltpu.VMEM((ext, rows, 2 * width), f32)],
     )[0]
-    y_passed = swap(y_direct, "gz")
     spectral, sent = call(
         solve_kernel,
         [shaped((ext, padded, lanes)), shaped((5, rows, width))],
-        [y_direct, y_passed, part, cx, cy, rate, mz],
-        scratch=[pltpu.VMEM((nodes + 4, rows, 2 * width), f32)],
+        [y_passed, part, cx, cx_rows, cy, rate, mz],
     )
 
     x_direct = swap(sent, "gx")
-    inner = call(interior_kernel, [shaped((nodes, padded, 2 * width))], [spectral, cx, mz, sent])[0]
+    inner = call(interior_kernel, [shaped((nodes, padded, 2 * width))], [spectral, cx, cy, mz, sent])[0]
     x_passed = swap(x_direct, "gz")
     sent, base = call(
         return_rows_kernel,

time: 25.7 us -> 25.3 us (0.984)
  waiting for transfers between devices: 9.79 us -> 9.21 us
  Pallas kernels: 6 us -> 6.36 us
    ppermute x4, waiting for transfers between devices: 6.45 us -> 5.86 us  [swap(): return lax.ppermute(value, AXES, swap_pairs(axis))]
    pallas_call x10 -> x11, Pallas kernels: 6 us -> 6.36 us  [call(): pl.pallas_call(kernel, out_shape=outs, in_specs=[where] * len(args), out_...]
    ppermute x7 -> x6, starting transfers between devices: 0.97 us -> 0.75 us  [swap(): return lax.ppermute(value, 'gz', [(0, 1), (1, 0)])]
    ppermute x7 -> x6, waiting for transfers between devices: 3.34 us -> 3.35 us  [swap(): return lax.ppermute(value, 'gz', [(0, 1), (1, 0)])]
  transfers between devices with their start and end apart: 11 -> 10, of which waited for: 8 -> 9; matrix products, arithmetic and copies ran while one was open for 0% -> 0% of each run, Pallas kernels for 13% -> 16%
where the time goes in v5:
time: 25.3 us; the launch traced here: 25.1 us
  starting transfers between devices  9.5 us (38%)
  waiting for transfers between devices  9.21 us (36%)
  Pallas kernels  6.36 us (25%)
    ppermute x4, starting transfers between devices, swap(): return lax.ppermute(value, AXES, swap_pairs(axis))  8.74 us
    pallas_call x11, Pallas kernels, call(): pl.pallas_call(kernel, out_shape=outs, in_specs=[where] * len(args), out_...  6.36 us
    ppermute x4, waiting for transfers between devices, swap(): return lax.ppermute(value, AXES, swap_pairs(axis))  5.86 us
    ppermute x6, waiting for transfers between devices, swap(): return lax.ppermute(value, 'gz', [(0, 1), (1, 0)])  3.35 us
    ppermute x6, starting transfers between devices, swap(): return lax.ppermute(value, 'gz', [(0, 1), (1, 0)])  0.75 us
  transfers between devices with their start and end apart: 10, of which 9 were waited for; matrix products, arithmetic and copies ran while one was open for 0% of the time, Pallas kernels for 16%

profile of v5, /device:TPU:0, one launch (start us, length us, event | category | flops | bytes accessed | tf_op | source)
XLA Modules:
  0.0 25.1 jit_solution(883413264813093406)
XLA Ops:
  0.0 0.0 copy-start
  0.0 1.2 %shard_map.55.own_ref = f32[12,8,128]{2,1,0:T(8,128)S(1)} custom-call(f32[8,8,128]{2,1,0:T(8,128)} %initial_ref.1, f32[8,8,128]{2,1,0:T(8,128)} %source_hbm.1, f32[3,8,8,128]{3,2,1,0:T(8,128)} %metric_hbm.1, f32[30,1,16]{2,1,0:T(1,128)} %bitcast.6), custom_call_target="tpu_custom_call" | custom-call | bytes 214912 | tf_op jit(solution)/shard_map/pallas_call | solution.py:185
  1.2 0.5 %collective-permute-start = (f32[12,8,128]{2,1,0:T(8,128)S(1)}, f32[12,8,128]{2,1,0:T(8,128)S(1)}, u32[]{:S(2)}, u32[]{:S(2)}) collective-permute-start(f32[12,8,128]{2,1,0:T(8,128)S(1)} %shard_map.55.own_ref), channel_id=1, source_target_pairs={{0,1},{1,0},{2,3},{3,2},{4,5},{5,4},{6,7},{7,6},{8,9},{9,8},{10,11... | collective-permute-start | bytes 147464 | tf_op jit(solution)/shard_map/ppermute | solution.py:610
  1.8 0.0 copy-done
  1.8 0.1 collective-permute-start.2
  1.8 0.8 %collective-permute-done.partner_ref = f32[12,8,128]{2,1,0:T(8,128)S(1)} collective-permute-done((f32[12,8,128]{2,1,0:T(8,128)S(1)}, f32[12,8,128]{2,1,0:T(8,128)S(1)}, u32[]{:S(2)}, u32[]{:S(2)}) %collective-permute-start) | collective-permute-done | bytes 49184 | tf_op jit(solution)/shard_map/ppermute | solution.py:610
  2.6 2.9 %collective-permute-start.1 = (f32[2,2,8,128]{3,2,1,0:T(8,128)S(1)}, f32[2,2,8,128]{3,2,1,0:T(8,128)S(1)}, u32[]{:S(2)}, u32[]{:S(2)}) collective-permute-start(f32[2,2,8,128]{3,2,1,0:T(8,128)S(1)} %shard_map.56.after_ref), channel_id=1, source_target_pairs={{1,8},{8,1},{9,16},{16,9},{17,24},{24,17},{0,2},{25,27},{3,10},{10... | collective-permute-start | bytes 49160 | tf_op jit(solution)/shard_map/ppermute | solution.py:611
  5.6 0.0 collective-permute-done.2.partner_vec
  5.6 1.0 %shard_map.57 = (f32[100,320]{1,0:T(8,128)S(1)}, f32[240,320]{1,0:T(8,128)S(1)}, f32[10,16,320]{2,1,0:T(8,128)S(1)}) custom-call(f32[300,1,16]{2,1,0:T(1,128)S(1)} %bitcast.3, f32[300,1,16]{2,1,0:T(1,128)S(1)} %collective-permute-done.2.partner_vec, f32[12,8,128]{2,1,0:T(8,128)S(1)} %shard_map.55.own_ref, ...), custom_call_target="tpu_custom_call" | custom-call | bytes 793088 | tf_op jit(solution)/shard_map/pallas_call | solution.py:185
  6.6 0.7 %collective-permute-done.1.after_ref.direct_ref.xd_ref = f32[2,2,8,128]{3,2,1,0:T(8,128)S(1)} collective-permute-done((f32[2,2,8,128]{3,2,1,0:T(8,128)S(1)}, f32[2,2,8,128]{3,2,1,0:T(8,128)S(1)}, u32[]{:S(2)}, u32[]{:S(2)}) %collective-permute-start.1) | collective-permute-done | bytes 16416 | tf_op jit(solution)/shard_map/ppermute | solution.py:611
  7.3 0.0 collective-permute-start.3
  7.3 1.0 %shard_map.58.after_ref.mz = bf16[2,256,320]{2,1,0:T(8,128)(2,1)S(1)} custom-call(f32[300,1,16]{2,1,0:T(1,128)S(1)} %bitcast.4, f32[300,1,16]{2,1,0:T(1,128)S(1)} %collective-permute-done.2.partner_vec, f32[2,2,8,128]{3,2,1,0:T(8,128)S(1)} %collective-permute-done.1.after_ref.direct_ref.xd_ref), custom_call_target="tpu_custom_call" | custom-call | bytes 382464 | tf_op jit(solution)/shard_map/pallas_call | solution.py:185
  8.3 0.2 collective-permute-done.3.passed_ref.xp_ref
  8.5 2.3 %collective-permute-start.4 = (f32[3,8,256]{2,1,0:T(8,128)S(1)}, f32[3,8,256]{2,1,0:T(8,128)S(1)}, u32[]{:S(2)}, u32[]{:S(2)}) collective-permute-start(f32[3,8,256]{2,1,0:T(8,128)S(1)} %shard_map.59.after_ref), channel_id=1, source_target_pairs={{1,2},{2,1},{3,4},{4,3},{5,6},{6,5},{0,8},{7,15},{9,10},{10,9},{11... | collective-permute-start | bytes 73736 | tf_op jit(solution)/shard_map/ppermute | solution.py:611
  10.8 0.9 %shard_map.60.cy = f32[2,10,16,320]{3,2,1,0:T(8,128)S(1)} custom-call(f32[300,1,16]{2,1,0:T(1,128)S(1)} %bitcast.5, f32[300,1,16]{2,1,0:T(1,128)S(1)} %collective-permute-done.2.partner_vec, f32[3,8,256]{2,1,0:T(8,128)S(1)} %shard_map.59.after_ref), custom_call_target="tpu_custom_call" | custom-call | bytes 472576 | tf_op jit(solution)/shard_map/pallas_call | solution.py:185
  11.7 0.9 %collective-permute-done.4.yd_ref = f32[3,8,256]{2,1,0:T(8,128)S(1)} collective-permute-done((f32[3,8,256]{2,1,0:T(8,128)S(1)}, f32[3,8,256]{2,1,0:T(8,128)S(1)}, u32[]{:S(2)}, u32[]{:S(2)}) %collective-permute-start.4) | collective-permute-done | bytes 24608 | tf_op jit(solution)/shard_map/ppermute | solution.py:611
  12.6 0.0 collective-permute-start.5
  12.6 0.5 %shard_map.61.part_ref = f32[10,16,320]{2,1,0:T(8,128)S(1)} custom-call(f32[12,8,128]{2,1,0:T(8,128)S(1)} %shard_map.55.own_ref, f32[12,8,128]{2,1,0:T(8,128)S(1)} %collective-permute-done.partner_ref, f32[2,2,8,128]{3,2,1,0:T(8,128)S(1)} %collective-permute-done.1.after_ref.direct_ref.xd_ref, f32[2,2,8,128]{3,2,1,0:T(8,128)S(1)} %collective-permute-done.3.passed_ref.xp_ref, ...), custom_call_target="tpu_custom_call" | custom-call | bytes 1532928 | tf_op jit(solution)/shard_map/pallas_call | solution.py:185
  13.1 0.7 %collective-permute-done.5.yp_ref = f32[3,8,256]{2,1,0:T(8,128)S(1)} collective-permute-done((f32[3,8,256]{2,1,0:T(8,128)S(1)}, f32[3,8,256]{2,1,0:T(8,128)S(1)}, u32[]{:S(2)}, u32[]{:S(2)}) %collective-permute-start.5) | collective-permute-done | bytes 24608 | tf_op jit(solution)/shard_map/ppermute | solution.py:610
  13.8 0.5 %shard_map.62 = (f32[10,16,320]{2,1,0:T(8,128)S(1)}, f32[5,8,128]{2,1,0:T(8,128)S(1)}) custom-call(f32[3,8,256]{2,1,0:T(8,128)S(1)} %collective-permute-done.5.yp_ref, f32[10,16,320]{2,1,0:T(8,128)S(1)} %shard_map.61.part_ref, f32[100,320]{1,0:T(8,128)S(1)} %get-tuple-element.25.cx, f32[240,320]{1,0:T(8,128)S(1)} %get-tuple-element.26.cx_rows, ...), custom_call_target="tpu_custom_call" | custom-call | bytes 1831936 | tf_op jit(solution)/shard_map/pallas_call | solution.py:185
  14.3 1.3 %collective-permute-start.6 = (f32[5,8,128]{2,1,0:T(8,128)S(1)}, f32[5,8,128]{2,1,0:T(8,128)S(1)}, u32[]{:S(2)}, u32[]{:S(2)}) collective-permute-start(f32[5,8,128]{2,1,0:T(8,128)S(1)} %get-tuple-element.30.after_ref), channel_id=1, source_target_pairs={{1,8},{8,1},{9,16},{16,9},{17,24},{24,17},{0,2},{25,27},{3,10},{10... | collective-permute-start | bytes 61448 | tf_op jit(solution)/shard_map/ppermute | solution.py:611
  15.6 2.5 %collective-permute-done.6.direct_ref = f32[5,8,128]{2,1,0:T(8,128)S(1)} collective-permute-done((f32[5,8,128]{2,1,0:T(8,128)S(1)}, f32[5,8,128]{2,1,0:T(8,128)S(1)}, u32[]{:S(2)}, u32[]{:S(2)}) %collective-permute-start.6) | collective-permute-done | bytes 20512 | tf_op jit(solution)/shard_map/ppermute | solution.py:611
  18.1 0.1 collective-permute-start.7
  18.3 0.0 copy-start.1
  18.3 0.5 %shard_map.63.inner_ref = f32[8,16,256]{2,1,0:T(8,128)S(1)} custom-call(f32[10,16,320]{2,1,0:T(8,128)S(1)} %get-tuple-element.29.spectral, f32[100,320]{1,0:T(8,128)S(1)} %get-tuple-element.25.cx, f32[2,10,16,320]{3,2,1,0:T(8,128)S(1)} %shard_map.60.cy, bf16[2,256,320]{2,1,0:T(8,128)(2,1)S(1)} %shard_map.58.after_ref.mz, ...), custom_call_target="tpu_custom_call" | custom-call | bytes 1221632 | tf_op jit(solution)/shard_map/pallas_call | solution.py:185
  18.8 0.5 %collective-permute-done.7.passed_ref = f32[5,8,128]{2,1,0:T(8,128)S(1)} collective-permute-done((f32[5,8,128]{2,1,0:T(8,128)S(1)}, f32[5,8,128]{2,1,0:T(8,128)S(1)}, u32[]{:S(2)}, u32[]{:S(2)}) %collective-permute-start.7) | collective-permute-done | bytes 20512 | tf_op jit(solution)/shard_map/ppermute | solution.py:610
  19.3 0.0 copy-done.1
  19.4 2.2 %collective-permute-start.8 = (f32[8,2,256]{2,1,0:T(2,128)S(1)}, f32[8,2,256]{2,1,0:T(2,128)S(1)}, u32[]{:S(2)}, u32[]{:S(2)}) collective-permute-start(f32[8,2,256]{2,1,0:T(2,128)S(1)} %get-tuple-element.32), channel_id=1, source_target_pairs={{1,2},{2,1},{3,4},{4,3},{5,6},{6,5},{0,8},{7,15},{9,10},{10,9},{11... | collective-permute-start | bytes 49160 | tf_op jit(solution)/shard_map/ppermute | solution.py:611
  21.6 1.7 %collective-permute-done.8.direct_ref = f32[8,2,256]{2,1,0:T(2,128)S(1)} collective-permute-done((f32[8,2,256]{2,1,0:T(2,128)S(1)}, f32[8,2,256]{2,1,0:T(2,128)S(1)}, u32[]{:S(2)}, u32[]{:S(2)}) %collective-permute-start.8) | collective-permute-done | bytes 16416 | tf_op jit(solution)/shard_map/ppermute | solution.py:611
  23.3 0.0 collective-permute-start.9
  23.3 1.2 %collective-permute-done.9.passed_ref = f32[8,2,256]{2,1,0:T(2,128)S(1)} collective-permute-done((f32[8,2,256]{2,1,0:T(2,128)S(1)}, f32[8,2,256]{2,1,0:T(2,128)S(1)}, u32[]{:S(2)}, u32[]{:S(2)}) %collective-permute-start.9) | collective-permute-done | bytes 16416 | tf_op jit(solution)/shard_map/ppermute | solution.py:610
  24.5 0.6 %shard_map.65 = f32[8,8,128]{2,1,0:T(8,128)} custom-call(f32[8,8,128]{2,1,0:T(8,128)S(1)} %get-tuple-element.31.base_ref, f32[8,2,256]{2,1,0:T(2,128)S(1)} %collective-permute-done.8.direct_ref, f32[8,2,256]{2,1,0:T(2,128)S(1)} %collective-permute-done.9.passed_ref), custom_call_target="tpu_custom_call" | custom-call | bytes 98304 | tf_op jit(solution)/shard_map/pallas_call | solution.py:185
  (3 shorter events, 0.1 us)
Async XLA Ops:
  0.0 1.8 %copy-start = (f32[3,10,10,1,1,16]{5,4,3,2,1,0:T(1,128)S(1)}, f32[3,10,10,1,1,16]{5,4,3,2,1,0:T(1,128)}, u32[]{:S(2)}) copy-start(f32[3,10,10,1,1,16]{5,4,3,2,1,0:T(1,128)} %param.8) | copy-start | bytes 57604
  1.2 1.4 %collective-permute-start = (f32[12,8,128]{2,1,0:T(8,128)S(1)}, f32[12,8,128]{2,1,0:T(8,128)S(1)}, u32[]{:S(2)}, u32[]{:S(2)}) collective-permute-start(f32[12,8,128]{2,1,0:T(8,128)S(1)} %shard_map.55.own_ref), channel_id=1, source_target_pairs={{0,1},{1,0},{2,3},{3,2},{4,5},{5,4},{6,7},{7,6},{8,9},{9,8},{10,11... | collective-permute-start | bytes 147464 | tf_op jit(solution)/shard_map/ppermute | solution.py:610
  1.8 3.8 %collective-permute-start.2 = (f32[300,1,16]{2,1,0:T(1,128)S(1)}, f32[300,1,16]{2,1,0:T(1,128)S(1)}, u32[]{:S(2)}, u32[]{:S(2)}) collective-permute-start(f32[300,1,16]{2,1,0:T(1,128)S(1)} %bitcast.2), channel_id=1, source_target_pairs={{0,1},{1,0},{2,3},{3,2},{4,5},{5,4},{6,7},{7,6},{8,9},{9,8},{10,11... | collective-permute-start | bytes 57608 | tf_op jit(solution)/shard_map/ppermute | solution.py:610
  2.6 4.6 %collective-permute-start.1 = (f32[2,2,8,128]{3,2,1,0:T(8,128)S(1)}, f32[2,2,8,128]{3,2,1,0:T(8,128)S(1)}, u32[]{:S(2)}, u32[]{:S(2)}) collective-permute-start(f32[2,2,8,128]{3,2,1,0:T(8,128)S(1)} %shard_map.56.after_ref), channel_id=1, source_target_pairs={{1,8},{8,1},{9,16},{16,9},{17,24},{24,17},{0,2},{25,27},{3,10},{10... | collective-permute-start | bytes 49160 | tf_op jit(solution)/shard_map/ppermute | solution.py:611
  7.3 1.2 %collective-permute-start.3 = (f32[2,2,8,128]{3,2,1,0:T(8,128)S(1)}, f32[2,2,8,128]{3,2,1,0:T(8,128)S(1)}, u32[]{:S(2)}, u32[]{:S(2)}) collective-permute-start(f32[2,2,8,128]{3,2,1,0:T(8,128)S(1)} %collective-permute-done.1.after_ref.direct_ref.xd_ref), channel_id=1, source_target_pairs={{0,1},{1,0},{2,3},{3,2},{4,5},{5,4},{6,7},{7,6},{8,9},{9,8},{10,11... | collective-permute-start | bytes 49160 | tf_op jit(solution)/shard_map/ppermute | solution.py:610
  8.5 4.1 %collective-permute-start.4 = (f32[3,8,256]{2,1,0:T(8,128)S(1)}, f32[3,8,256]{2,1,0:T(8,128)S(1)}, u32[]{:S(2)}, u32[]{:S(2)}) collective-permute-start(f32[3,8,256]{2,1,0:T(8,128)S(1)} %shard_map.59.after_ref), channel_id=1, source_target_pairs={{1,2},{2,1},{3,4},{4,3},{5,6},{6,5},{0,8},{7,15},{9,10},{10,9},{11... | collective-permute-start | bytes 73736 | tf_op jit(solution)/shard_map/ppermute | solution.py:611
  12.6 1.2 %collective-permute-start.5 = (f32[3,8,256]{2,1,0:T(8,128)S(1)}, f32[3,8,256]{2,1,0:T(8,128)S(1)}, u32[]{:S(2)}, u32[]{:S(2)}) collective-permute-start(f32[3,8,256]{2,1,0:T(8,128)S(1)} %collective-permute-done.4.yd_ref), channel_id=1, source_target_pairs={{0,1},{1,0},{2,3},{3,2},{4,5},{5,4},{6,7},{7,6},{8,9},{9,8},{10,11... | collective-permute-start | bytes 73736 | tf_op jit(solution)/shard_map/ppermute | solution.py:610
  14.3 3.8 %collective-permute-start.6 = (f32[5,8,128]{2,1,0:T(8,128)S(1)}, f32[5,8,128]{2,1,0:T(8,128)S(1)}, u32[]{:S(2)}, u32[]{:S(2)}) collective-permute-start(f32[5,8,128]{2,1,0:T(8,128)S(1)} %get-tuple-element.30.after_ref), channel_id=1, source_target_pairs={{1,8},{8,1},{9,16},{16,9},{17,24},{24,17},{0,2},{25,27},{3,10},{10... | collective-permute-start | bytes 61448 | tf_op jit(solution)/shard_map/ppermute | solution.py:611
  18.1 1.2 %collective-permute-start.7 = (f32[5,8,128]{2,1,0:T(8,128)S(1)}, f32[5,8,128]{2,1,0:T(8,128)S(1)}, u32[]{:S(2)}, u32[]{:S(2)}) collective-permute-start(f32[5,8,128]{2,1,0:T(8,128)S(1)} %collective-permute-done.6.direct_ref), channel_id=1, source_target_pairs={{0,1},{1,0},{2,3},{3,2},{4,5},{5,4},{6,7},{7,6},{8,9},{9,8},{10,11... | collective-permute-start | bytes 61448 | tf_op jit(solution)/shard_map/ppermute | solution.py:610
  18.3 1.1 %copy-start.1 = (f32[8,8,128]{2,1,0:T(8,128)S(1)}, f32[8,8,128]{2,1,0:T(8,128)}, u32[]{:S(2)}) copy-start(f32[8,8,128]{2,1,0:T(8,128)} %initial_ref.1) | copy-start | bytes 98308
  19.4 3.9 %collective-permute-start.8 = (f32[8,2,256]{2,1,0:T(2,128)S(1)}, f32[8,2,256]{2,1,0:T(2,128)S(1)}, u32[]{:S(2)}, u32[]{:S(2)}) collective-permute-start(f32[8,2,256]{2,1,0:T(2,128)S(1)} %get-tuple-element.32), channel_id=1, source_target_pairs={{1,2},{2,1},{3,4},{4,3},{5,6},{6,5},{0,8},{7,15},{9,10},{10,9},{11... | collective-permute-start | bytes 49160 | tf_op jit(solution)/shard_map/ppermute | solution.py:611
  23.3 1.2 %collective-permute-start.9 = (f32[8,2,256]{2,1,0:T(2,128)S(1)}, f32[8,2,256]{2,1,0:T(2,128)S(1)}, u32[]{:S(2)}, u32[]{:S(2)}) collective-permute-start(f32[8,2,256]{2,1,0:T(2,128)S(1)} %collective-permute-done.8.direct_ref), channel_id=1, source_target_pairs={{0,1},{1,0},{2,3},{3,2},{4,5},{5,4},{6,7},{7,6},{8,9},{9,8},{10,11... | collective-permute-start | bytes 49160 | tf_op jit(solution)/shard_map/ppermute | solution.py:610

commit v6 on v5

--- a/solution.py
+++ b/solution.py
@@ -397,9 +397,18 @@
         mz_ref[1, place * nodes : (place + 2) * nodes, :] = low
 
 
-def both_sides(core, direct, passed):
-    low = [jnp.where(core == 0, direct[h], passed[1 - h]) for h in range(2)]
-    high = [jnp.where(core == 0, passed[1 - h], direct[h]) for h in range(2)]
+def trade_cores(axis, place):
+    return (place % 2, place % 2) if axis == "gx" else (0, 1)
+
+
+def trades_below(axis):
+    core, place = lax.axis_index("gz"), lax.axis_index(axis)
+    return core != place % 2 if axis == "gx" else core == 1
+
+
+def sides(below, direct, passed):
+    low = [jnp.where(below, direct[h], passed[1 - h]) for h in range(2)]
+    high = [jnp.where(below, passed[1 - h], direct[h]) for h in range(2)]
     return low, high
 
 
@@ -408,49 +417,66 @@
     return place > 0, place < size - 1
 
 
-def x_positions(core, own_ref, partner_ref, direct_ref, passed_ref):
+def layers_kernel(own_ref, partner_ref, out_ref):
+    start = jnp.where(trades_below("gx"), 0, out_ref.shape[2] - 2)
+    for half, ref in enumerate((own_ref, partner_ref)):
+        for layer in range(2):
+            out_ref[half, layer] = ref[start + layer]
+
+
+def x_positions(own_ref, partner_ref, direct_ref, passed_ref):
     has_low, has_high = edges("gx")
     length = own_ref.shape[1]
-    sides = []
+    below = trades_below("gx")
+    outer = []
     for slot in range(2):
         direct = [direct_ref[h, slot] for h in range(2)]
         passed = [passed_ref[h, slot] for h in range(2)]
-        low, high = both_sides(core, direct, passed)
+        low, high = sides(below, direct, passed)
         low = [jnp.where(has_low, v, jnp.zeros_like(v)) for v in low]
         high = [jnp.where(has_high, v, jnp.zeros_like(v)) for v in high]
-        sides.append((low, high))
-    positions = [sides[0][0]]
+        outer.append((low, high))
+    positions = [outer[0][0]]
     for layer in range(length):
         value = [own_ref[layer], partner_ref[layer]]
         if layer == 0:
-            value = [v + w for v, w in zip(sides[1][0], value)]
+            value = [v + w for v, w in zip(outer[1][0], value)]
         if layer == length - 1:
-            value = [v + w for v, w in zip(value, sides[0][1])]
+            value = [v + w for v, w in zip(value, outer[0][1])]
         positions.append(value)
-    return positions + [sides[1][1]]
+    return positions + [outer[1][1]]
 
 
 def rows_kernel(own_ref, partner_ref, direct_ref, passed_ref, after_ref, out_ref):
-    core = lax.axis_index("gz")
     _, rows, width = own_ref.shape
-    positions = x_positions(core, own_ref, partner_ref, direct_ref, passed_ref)
+    below = trades_below("gy")
+    positions = x_positions(own_ref, partner_ref, direct_ref, passed_ref)
     out_ref[out_ref.shape[0] - 1] = jnp.zeros(out_ref.shape[1:], f32)
     for a, (own, partner) in enumerate(positions):
         row = 2 * a % rows
         for half, value in enumerate((partner, own)):
             out_ref[2 * a // rows, row : row + 2, half * width : (half + 1) * width] = jnp.where(
-                core == 0, value[0:2], value[rows - 2 : rows]
+                below, value[0:2], value[rows - 2 : rows]
             )
 
 
+def by_parts(value, mz, transposed):
+    rows = value.shape[0]
+    spare = -rows % 16
+    if spare:
+        value = jnp.concatenate([value, jnp.zeros((spare, value.shape[1]), f32)], axis=0)
+    high, low = split2(value)
+    both = dot(jnp.concatenate([high, low], axis=0), mz[0], transposed)
+    total = both[0 : rows + spare] + (both[rows + spare :] + dot(high, mz[1], transposed))
+    return total[0:rows]
+
+
 def by_z(value, mz):
-    high, low = split2(value)
-    return dot(high, mz[0]) + (dot(low, mz[0]) + dot(high, mz[1]))
+    return by_parts(value, mz, False)
 
 
 def back_by_z(value, mz):
-    high, low = split2(value)
-    return dot(high, mz[0], True) + (dot(low, mz[0], True) + dot(high, mz[1], True))
+    return by_parts(value, mz, True)
 
 
 def from_rows(value, use, mz, cx_rows, ext):
@@ -473,19 +499,19 @@
 def interior_solve_kernel(
     own_ref, partner_ref, xd_ref, xp_ref, yd_ref, cx, cx_rows, cy, mz, out_ref, grid
 ):
-    core = lax.axis_index("gz")
     _, rows, width = own_ref.shape
     ext, padded, lanes = out_ref.shape
     nodes = ext - 2
     has_low, has_high = edges("gy")
-    positions = x_positions(core, own_ref, partner_ref, xd_ref, xp_ref)
+    positions = x_positions(own_ref, partner_ref, xd_ref, xp_ref)
     for a, halves in enumerate(positions):
         for half, value in enumerate(halves):
             grid[a, :, half * width : (half + 1) * width] = value
     along_z = by_z(grid[...].reshape(ext * rows, 2 * width), mz)
     along_z = along_z.reshape(ext, rows, lanes)
-    use = jnp.where(core == 0, has_low, has_high)
-    outer = [cy[0, core * nodes + k] for k in range(2)]
+    below = trades_below("gy")
+    use = jnp.where(below, has_low, has_high)
+    outer = [cy[0, jnp.where(below, 0, nodes) + k] for k in range(2)]
     for p, value in enumerate(from_rows(yd_ref[...], use, mz, cx_rows, ext)):
         inner = sum(cx[a * ext + p : a * ext + p + 1, :] * along_z[a] for a in range(ext))
         total = sum(cy[0, b + 1] * inner[b : b + 1] for b in range(rows))
@@ -501,14 +527,14 @@
 
 
 def solve_kernel(yp_ref, part_ref, cx, cx_rows, cy, rate, mz, spectral, sent_ref):
-    core = lax.axis_index("gz")
+    below = trades_below("gy")
     width = yp_ref.shape[2] // 2
     ext, padded, lanes = rate.shape
     nodes = ext - 2
     has_low, has_high = edges("gy")
     passed = jnp.concatenate([yp_ref[:, :, width:], yp_ref[:, :, 0:width]], axis=2)
-    use = jnp.where(core == 0, has_high, has_low)
-    outer = [cy[0, (1 - core) * nodes + k] for k in range(2)]
+    use = jnp.where(below, has_high, has_low)
+    outer = [cy[0, jnp.where(below, nodes, 0) + k] for k in range(2)]
     for p, value in enumerate(from_rows(passed, use, mz, cx_rows, ext)):
         total = part_ref[p] + sum(outer[k] * value[k : k + 1] for k in range(2))
         spectral[p] = total * rate[p]
@@ -517,13 +543,14 @@
         rows = [layer * ext + p for p in range(ext)]
         last = [r + nodes * ext for r in rows]
         coefficients = [
-            jnp.where(core == 0, cx[r : r + 1, :], cx[k : k + 1, :]) for r, k in zip(rows, last)
+            jnp.where(trades_below("gx"), cx[r : r + 1, :], cx[k : k + 1, :])
+            for r, k in zip(rows, last)
         ]
         layers.append(back_by_y(back_by_x(spectral, coefficients), cy, ext))
     result = back_by_z(jnp.concatenate(layers, axis=0), mz)
     for layer in range(2):
         for half in range(2):
-            lanes_at = slice((1 - half) * width, (2 - half) * width)
+            lanes_at = slice(half * width, (half + 1) * width)
             place = half * 2 + layer
             value = result[layer * padded : layer * padded + nodes + 2, lanes_at]
             sent_ref[place] = value[0:nodes]
@@ -542,8 +569,8 @@
 
 
 def return_rows_kernel(initial_ref, inner_ref, direct_ref, passed_ref, out_ref, base_ref):
-    core = lax.axis_index("gz")
     has_low, has_high = edges("gx")
+    below_x, below_y = trades_below("gx"), trades_below("gy")
     nodes, rows, width = initial_ref.shape
     for layer in range(nodes):
         lanes = [slice(0, width), slice(width, 2 * width)]
@@ -561,25 +588,25 @@
             side = 0 if layer < 2 else 1
             valid = (has_low, has_high)[side]
             for k, target in enumerate((values, outer)):
-                both = both_sides(core, [d[k] for d in direct], [d[k] for d in passed])[side]
+                both = sides(below_x, [d[k] for d in direct], [d[k] for d in passed])[side]
                 for h in range(2):
                     target[h] = target[h] + jnp.where(valid, both[h], jnp.zeros_like(both[h]))
         base_ref[layer] = initial_ref[layer] + values[0]
         for place, h in enumerate((1, 0)):
-            first = jnp.where(core == 0, outer[h][0:1], values[h][rows - 1 : rows])
-            second = jnp.where(core == 0, values[h][0:1], outer[h][1:2])
+            first = jnp.where(below_y, outer[h][0:1], values[h][rows - 1 : rows])
+            second = jnp.where(below_y, values[h][0:1], outer[h][1:2])
             out_ref[layer, :, lanes[place]] = jnp.concatenate([first, second], axis=0)
 
 
 def result_kernel(base_ref, direct_ref, passed_ref, out_ref):
-    core = lax.axis_index("gz")
+    below = trades_below("gy")
     has_low, has_high = edges("gy")
     nodes, rows, width = base_ref.shape
     for layer in range(nodes):
         direct = direct_ref[layer, :, 0:width]
         passed = passed_ref[layer, :, width:]
-        low = jnp.where(core == 0, direct, passed)
-        high = jnp.where(core == 0, passed, direct)
+        low = jnp.where(below, direct, passed)
+        high = jnp.where(below, passed, direct)
         low = jnp.where(has_low, low, jnp.zeros_like(low))
         high = jnp.where(has_high, high, jnp.zeros_like(high))
         between = jnp.zeros((rows - 4, low.shape[1]), f32)
@@ -595,12 +622,18 @@
         return (spot[0] * sizes[1] + spot[1]) * 2 + core
 
     pairs = []
+    last = sizes[along] - 1
     for other in range(sizes[across]):
-        for place in range(sizes[along] - 1):
-            here, there = number(place, other, 1), number(place + 1, other, 0)
+        for place in range(last):
+            here, there = trade_cores(axis, place)
+            here, there = number(place, other, here), number(place + 1, other, there)
             pairs += [(here, there), (there, here)]
         if other ^ 1 < sizes[across]:
-            for place, core in ((0, 0), (sizes[along] - 1, 1)):
+            idle = [(place, core) for place in {0, last} for core in range(2)]
+            if last > 0:
+                idle.remove((0, trade_cores(axis, 0)[0]))
+                idle.remove((last, trade_cores(axis, last - 1)[1]))
+            for place, core in sorted(idle):
                 pairs.append((number(place, other, core), number(place, other ^ 1, core)))
     return pairs
 

time: 25.3 us -> 24.4 us (0.964)
  the two profiles are of different devices: /device:TPU:0 before, /device:TPU:25 now
where the time goes in v6:
time: 24.4 us; the launch traced here: 24.2 us
  waiting for transfers between devices  11.8 us (48%)
  Pallas kernels  6.32 us (26%)
  starting transfers between devices  5.98 us (25%)
    ppermute x4, waiting for transfers between devices, swap(): return lax.ppermute(value, AXES, swap_pairs(axis))  9.23 us
    pallas_call x11, Pallas kernels, call(): pl.pallas_call(kernel, out_shape=outs, in_specs=[where] * len(args), out_...  6.32 us
    ppermute x6, starting transfers between devices, swap(): return lax.ppermute(value, 'gz', [(0, 1), (1, 0)])  5.34 us
    ppermute x6, waiting for transfers between devices, swap(): return lax.ppermute(value, 'gz', [(0, 1), (1, 0)])  2.6 us
    ppermute x4, starting transfers between devices, swap(): return lax.ppermute(value, AXES, swap_pairs(axis))  0.63 us
  transfers between devices with their start and end apart: 10, of which 9 were waited for; matrix products, arithmetic and copies ran while one was open for 0% of the time, Pallas kernels for 16%

profile of v6, /device:TPU:25, one launch (start us, length us, event | category | flops | bytes accessed | tf_op | source)
XLA Modules:
  0.0 24.2 jit_solution(11540630143164676240)
XLA Ops:
  0.0 0.0 copy-start
  0.0 1.2 %shard_map.55.own_ref = f32[12,8,128]{2,1,0:T(8,128)S(1)} custom-call(f32[8,8,128]{2,1,0:T(8,128)} %initial_ref.1, f32[8,8,128]{2,1,0:T(8,128)} %source_hbm.1, f32[3,8,8,128]{3,2,1,0:T(8,128)} %metric_hbm.1, f32[30,1,16]{2,1,0:T(1,128)} %bitcast.6), custom_call_target="tpu_custom_call" | custom-call | bytes 214912 | tf_op jit(solution)/shard_map/pallas_call | solution.py:185
  1.2 0.7 %collective-permute-start = (f32[12,8,128]{2,1,0:T(8,128)S(1)}, f32[12,8,128]{2,1,0:T(8,128)S(1)}, u32[]{:S(2)}, u32[]{:S(2)}) collective-permute-start(f32[12,8,128]{2,1,0:T(8,128)S(1)} %shard_map.55.own_ref), channel_id=1, source_target_pairs={{0,1},{1,0},{2,3},{3,2},{4,5},{5,4},{6,7},{7,6},{8,9},{9,8},{10,11... | collective-permute-start | bytes 147464 | tf_op jit(solution)/shard_map/ppermute | solution.py:643
  2.0 0.0 copy-done
  2.0 0.1 collective-permute-start.2
  2.1 0.8 %collective-permute-done.partner_ref = f32[12,8,128]{2,1,0:T(8,128)S(1)} collective-permute-done((f32[12,8,128]{2,1,0:T(8,128)S(1)}, f32[12,8,128]{2,1,0:T(8,128)S(1)}, u32[]{:S(2)}, u32[]{:S(2)}) %collective-permute-start) | collective-permute-done | bytes 49184 | tf_op jit(solution)/shard_map/ppermute | solution.py:643
  2.9 0.2 collective-permute-start.1
  3.0 0.3 %collective-permute-done.2.partner_vec = f32[300,1,16]{2,1,0:T(1,128)S(1)} collective-permute-done((f32[300,1,16]{2,1,0:T(1,128)S(1)}, f32[300,1,16]{2,1,0:T(1,128)S(1)}, u32[]{:S(2)}, u32[]{:S(2)}) %collective-permute-start.2) | collective-permute-done | bytes 19232 | tf_op jit(solution)/shard_map/ppermute | solution.py:643
  3.4 1.0 %shard_map.57 = (f32[100,320]{1,0:T(8,128)S(1)}, f32[240,320]{1,0:T(8,128)S(1)}, f32[10,16,320]{2,1,0:T(8,128)S(1)}) custom-call(f32[300,1,16]{2,1,0:T(1,128)S(1)} %bitcast.3, f32[300,1,16]{2,1,0:T(1,128)S(1)} %collective-permute-done.2.partner_vec, f32[12,8,128]{2,1,0:T(8,128)S(1)} %shard_map.55.own_ref, ...), custom_call_target="tpu_custom_call" | custom-call | bytes 793088 | tf_op jit(solution)/shard_map/pallas_call | solution.py:185
  4.4 1.1 %collective-permute-done.1.after_ref.direct_ref.xd_ref = f32[2,2,8,128]{3,2,1,0:T(8,128)S(1)} collective-permute-done((f32[2,2,8,128]{3,2,1,0:T(8,128)S(1)}, f32[2,2,8,128]{3,2,1,0:T(8,128)S(1)}, u32[]{:S(2)}, u32[]{:S(2)}) %collective-permute-start.1) | collective-permute-done | bytes 16416 | tf_op jit(solution)/shard_map/ppermute | solution.py:644
  5.5 1.5 %collective-permute-start.3 = (f32[2,2,8,128]{3,2,1,0:T(8,128)S(1)}, f32[2,2,8,128]{3,2,1,0:T(8,128)S(1)}, u32[]{:S(2)}, u32[]{:S(2)}) collective-permute-start(f32[2,2,8,128]{3,2,1,0:T(8,128)S(1)} %collective-permute-done.1.after_ref.direct_ref.xd_ref), channel_id=1, source_target_pairs={{0,1},{1,0},{2,3},{3,2},{4,5},{5,4},{6,7},{7,6},{8,9},{9,8},{10,11... | collective-permute-start | bytes 49160 | tf_op jit(solution)/shard_map/ppermute | solution.py:643
  7.0 1.0 %shard_map.58.after_ref.mz = bf16[2,256,320]{2,1,0:T(8,128)(2,1)S(1)} custom-call(f32[300,1,16]{2,1,0:T(1,128)S(1)} %bitcast.4, f32[300,1,16]{2,1,0:T(1,128)S(1)} %collective-permute-done.2.partner_vec, f32[2,2,8,128]{3,2,1,0:T(8,128)S(1)} %collective-permute-done.1.after_ref.direct_ref.xd_ref), custom_call_target="tpu_custom_call" | custom-call | bytes 382464 | tf_op jit(solution)/shard_map/pallas_call | solution.py:185
  7.9 0.0 collective-permute-done.3.passed_ref.xp_ref
  8.0 0.3 %collective-permute-start.4 = (f32[3,8,256]{2,1,0:T(8,128)S(1)}, f32[3,8,256]{2,1,0:T(8,128)S(1)}, u32[]{:S(2)}, u32[]{:S(2)}) collective-permute-start(f32[3,8,256]{2,1,0:T(8,128)S(1)} %shard_map.59.after_ref), channel_id=1, source_target_pairs={{0,3},{3,0},{2,5},{5,2},{4,7},{7,4},{1,9},{6,14},{8,11},{11,8},{10... | collective-permute-start | bytes 73736 | tf_op jit(solution)/shard_map/ppermute | solution.py:644
  8.3 0.9 %shard_map.60.cy = f32[2,10,16,320]{3,2,1,0:T(8,128)S(1)} custom-call(f32[300,1,16]{2,1,0:T(1,128)S(1)} %bitcast.5, f32[300,1,16]{2,1,0:T(1,128)S(1)} %collective-permute-done.2.partner_vec, f32[3,8,256]{2,1,0:T(8,128)S(1)} %shard_map.59.after_ref), custom_call_target="tpu_custom_call" | custom-call | bytes 472576 | tf_op jit(solution)/shard_map/pallas_call | solution.py:185
  9.2 2.4 %collective-permute-done.4.yd_ref = f32[3,8,256]{2,1,0:T(8,128)S(1)} collective-permute-done((f32[3,8,256]{2,1,0:T(8,128)S(1)}, f32[3,8,256]{2,1,0:T(8,128)S(1)}, u32[]{:S(2)}, u32[]{:S(2)}) %collective-permute-start.4) | collective-permute-done | bytes 24608 | tf_op jit(solution)/shard_map/ppermute | solution.py:644
  11.6 0.5 %collective-permute-start.5 = (f32[3,8,256]{2,1,0:T(8,128)S(1)}, f32[3,8,256]{2,1,0:T(8,128)S(1)}, u32[]{:S(2)}, u32[]{:S(2)}) collective-permute-start(f32[3,8,256]{2,1,0:T(8,128)S(1)} %collective-permute-done.4.yd_ref), channel_id=1, source_target_pairs={{0,1},{1,0},{2,3},{3,2},{4,5},{5,4},{6,7},{7,6},{8,9},{9,8},{10,11... | collective-permute-start | bytes 73736 | tf_op jit(solution)/shard_map/ppermute | solution.py:643
  12.1 0.5 %shard_map.61.part_ref = f32[10,16,320]{2,1,0:T(8,128)S(1)} custom-call(f32[12,8,128]{2,1,0:T(8,128)S(1)} %shard_map.55.own_ref, f32[12,8,128]{2,1,0:T(8,128)S(1)} %collective-permute-done.partner_ref, f32[2,2,8,128]{3,2,1,0:T(8,128)S(1)} %collective-permute-done.1.after_ref.direct_ref.xd_ref, f32[2,2,8,128]{3,2,1,0:T(8,128)S(1)} %collective-permute-done.3.passed_ref.xp_ref, ...), custom_call_target="tpu_custom_call" | custom-call | bytes 1532928 | tf_op jit(solution)/shard_map/pallas_call | solution.py:185
  12.6 0.3 %collective-permute-done.5.yp_ref = f32[3,8,256]{2,1,0:T(8,128)S(1)} collective-permute-done((f32[3,8,256]{2,1,0:T(8,128)S(1)}, f32[3,8,256]{2,1,0:T(8,128)S(1)}, u32[]{:S(2)}, u32[]{:S(2)}) %collective-permute-start.5) | collective-permute-done | bytes 24608 | tf_op jit(solution)/shard_map/ppermute | solution.py:643
  12.9 0.5 %shard_map.62 = (f32[10,16,320]{2,1,0:T(8,128)S(1)}, f32[5,8,128]{2,1,0:T(8,128)S(1)}) custom-call(f32[3,8,256]{2,1,0:T(8,128)S(1)} %collective-permute-done.5.yp_ref, f32[10,16,320]{2,1,0:T(8,128)S(1)} %shard_map.61.part_ref, f32[100,320]{1,0:T(8,128)S(1)} %get-tuple-element.25.cx, f32[240,320]{1,0:T(8,128)S(1)} %get-tuple-element.26.cx_rows, ...), custom_call_target="tpu_custom_call" | custom-call | bytes 1831936 | tf_op jit(solution)/shard_map/pallas_call | solution.py:185
  13.4 0.1 collective-permute-start.6
  13.5 2.6 %collective-permute-done.6.direct_ref = f32[5,8,128]{2,1,0:T(8,128)S(1)} collective-permute-done((f32[5,8,128]{2,1,0:T(8,128)S(1)}, f32[5,8,128]{2,1,0:T(8,128)S(1)}, u32[]{:S(2)}, u32[]{:S(2)}) %collective-permute-start.6) | collective-permute-done | bytes 20512 | tf_op jit(solution)/shard_map/ppermute | solution.py:644
  16.1 1.6 %collective-permute-start.7 = (f32[5,8,128]{2,1,0:T(8,128)S(1)}, f32[5,8,128]{2,1,0:T(8,128)S(1)}, u32[]{:S(2)}, u32[]{:S(2)}) collective-permute-start(f32[5,8,128]{2,1,0:T(8,128)S(1)} %collective-permute-done.6.direct_ref), channel_id=1, source_target_pairs={{0,1},{1,0},{2,3},{3,2},{4,5},{5,4},{6,7},{7,6},{8,9},{9,8},{10,11... | collective-permute-start | bytes 61448 | tf_op jit(solution)/shard_map/ppermute | solution.py:643
  17.7 0.0 copy-start.1
  17.7 0.5 %shard_map.63.inner_ref = f32[8,16,256]{2,1,0:T(8,128)S(1)} custom-call(f32[10,16,320]{2,1,0:T(8,128)S(1)} %get-tuple-element.29.spectral, f32[100,320]{1,0:T(8,128)S(1)} %get-tuple-element.25.cx, f32[2,10,16,320]{3,2,1,0:T(8,128)S(1)} %shard_map.60.cy, bf16[2,256,320]{2,1,0:T(8,128)(2,1)S(1)} %shard_map.58.after_ref.mz, ...), custom_call_target="tpu_custom_call" | custom-call | bytes 1221632 | tf_op jit(solution)/shard_map/pallas_call | solution.py:185
  18.3 0.3 %collective-permute-done.7.passed_ref = f32[5,8,128]{2,1,0:T(8,128)S(1)} collective-permute-done((f32[5,8,128]{2,1,0:T(8,128)S(1)}, f32[5,8,128]{2,1,0:T(8,128)S(1)}, u32[]{:S(2)}, u32[]{:S(2)}) %collective-permute-start.7) | collective-permute-done | bytes 20512 | tf_op jit(solution)/shard_map/ppermute | solution.py:643
  18.6 0.0 copy-done.1
  18.6 0.1 collective-permute-start.8
  18.7 3.2 %collective-permute-done.8.direct_ref = f32[8,2,256]{2,1,0:T(2,128)S(1)} collective-permute-done((f32[8,2,256]{2,1,0:T(2,128)S(1)}, f32[8,2,256]{2,1,0:T(2,128)S(1)}, u32[]{:S(2)}, u32[]{:S(2)}) %collective-permute-start.8) | collective-permute-done | bytes 16416 | tf_op jit(solution)/shard_map/ppermute | solution.py:644
  21.8 0.9 %collective-permute-start.9 = (f32[8,2,256]{2,1,0:T(2,128)S(1)}, f32[8,2,256]{2,1,0:T(2,128)S(1)}, u32[]{:S(2)}, u32[]{:S(2)}) collective-permute-start(f32[8,2,256]{2,1,0:T(2,128)S(1)} %collective-permute-done.8.direct_ref), channel_id=1, source_target_pairs={{0,1},{1,0},{2,3},{3,2},{4,5},{5,4},{6,7},{7,6},{8,9},{9,8},{10,11... | collective-permute-start | bytes 49160 | tf_op jit(solution)/shard_map/ppermute | solution.py:643
  22.8 0.8 %collective-permute-done.9.passed_ref = f32[8,2,256]{2,1,0:T(2,128)S(1)} collective-permute-done((f32[8,2,256]{2,1,0:T(2,128)S(1)}, f32[8,2,256]{2,1,0:T(2,128)S(1)}, u32[]{:S(2)}, u32[]{:S(2)}) %collective-permute-start.9) | collective-permute-done | bytes 16416 | tf_op jit(solution)/shard_map/ppermute | solution.py:643
  23.6 0.6 %shard_map.65 = f32[8,8,128]{2,1,0:T(8,128)} custom-call(f32[8,8,128]{2,1,0:T(8,128)S(1)} %get-tuple-element.31.base_ref, f32[8,2,256]{2,1,0:T(2,128)S(1)} %collective-permute-done.8.direct_ref, f32[8,2,256]{2,1,0:T(2,128)S(1)} %collective-permute-done.9.passed_ref), custom_call_target="tpu_custom_call" | custom-call | bytes 98304 | tf_op jit(solution)/shard_map/pallas_call | solution.py:185
  (3 shorter events, 0.1 us)
Async XLA Ops:
  0.0 2.0 %copy-start = (f32[3,10,10,1,1,16]{5,4,3,2,1,0:T(1,128)S(1)}, f32[3,10,10,1,1,16]{5,4,3,2,1,0:T(1,128)}, u32[]{:S(2)}) copy-start(f32[3,10,10,1,1,16]{5,4,3,2,1,0:T(1,128)} %param.8) | copy-start | bytes 57604
  1.2 1.6 %collective-permute-start = (f32[12,8,128]{2,1,0:T(8,128)S(1)}, f32[12,8,128]{2,1,0:T(8,128)S(1)}, u32[]{:S(2)}, u32[]{:S(2)}) collective-permute-start(f32[12,8,128]{2,1,0:T(8,128)S(1)} %shard_map.55.own_ref), channel_id=1, source_target_pairs={{0,1},{1,0},{2,3},{3,2},{4,5},{5,4},{6,7},{7,6},{8,9},{9,8},{10,11... | collective-permute-start | bytes 147464 | tf_op jit(solution)/shard_map/ppermute | solution.py:643
  2.0 1.4 %collective-permute-start.2 = (f32[300,1,16]{2,1,0:T(1,128)S(1)}, f32[300,1,16]{2,1,0:T(1,128)S(1)}, u32[]{:S(2)}, u32[]{:S(2)}) collective-permute-start(f32[300,1,16]{2,1,0:T(1,128)S(1)} %bitcast.2), channel_id=1, source_target_pairs={{0,1},{1,0},{2,3},{3,2},{4,5},{5,4},{6,7},{7,6},{8,9},{9,8},{10,11... | collective-permute-start | bytes 57608 | tf_op jit(solution)/shard_map/ppermute | solution.py:643
  2.9 2.6 %collective-permute-start.1 = (f32[2,2,8,128]{3,2,1,0:T(8,128)S(1)}, f32[2,2,8,128]{3,2,1,0:T(8,128)S(1)}, u32[]{:S(2)}, u32[]{:S(2)}) collective-permute-start(f32[2,2,8,128]{3,2,1,0:T(8,128)S(1)} %shard_map.56.after_ref), channel_id=1, source_target_pairs={{0,8},{8,0},{9,17},{17,9},{16,24},{24,16},{1,3},{25,27},{2,10},{10... | collective-permute-start | bytes 49160 | tf_op jit(solution)/shard_map/ppermute | solution.py:644
  5.5 2.5 %collective-permute-start.3 = (f32[2,2,8,128]{3,2,1,0:T(8,128)S(1)}, f32[2,2,8,128]{3,2,1,0:T(8,128)S(1)}, u32[]{:S(2)}, u32[]{:S(2)}) collective-permute-start(f32[2,2,8,128]{3,2,1,0:T(8,128)S(1)} %collective-permute-done.1.after_ref.direct_ref.xd_ref), channel_id=1, source_target_pairs={{0,1},{1,0},{2,3},{3,2},{4,5},{5,4},{6,7},{7,6},{8,9},{9,8},{10,11... | collective-permute-start | bytes 49160 | tf_op jit(solution)/shard_map/ppermute | solution.py:643
  8.0 3.6 %collective-permute-start.4 = (f32[3,8,256]{2,1,0:T(8,128)S(1)}, f32[3,8,256]{2,1,0:T(8,128)S(1)}, u32[]{:S(2)}, u32[]{:S(2)}) collective-permute-start(f32[3,8,256]{2,1,0:T(8,128)S(1)} %shard_map.59.after_ref), channel_id=1, source_target_pairs={{0,3},{3,0},{2,5},{5,2},{4,7},{7,4},{1,9},{6,14},{8,11},{11,8},{10... | collective-permute-start | bytes 73736 | tf_op jit(solution)/shard_map/ppermute | solution.py:644
  11.6 1.3 %collective-permute-start.5 = (f32[3,8,256]{2,1,0:T(8,128)S(1)}, f32[3,8,256]{2,1,0:T(8,128)S(1)}, u32[]{:S(2)}, u32[]{:S(2)}) collective-permute-start(f32[3,8,256]{2,1,0:T(8,128)S(1)} %collective-permute-done.4.yd_ref), channel_id=1, source_target_pairs={{0,1},{1,0},{2,3},{3,2},{4,5},{5,4},{6,7},{7,6},{8,9},{9,8},{10,11... | collective-permute-start | bytes 73736 | tf_op jit(solution)/shard_map/ppermute | solution.py:643
  13.4 2.7 %collective-permute-start.6 = (f32[5,8,128]{2,1,0:T(8,128)S(1)}, f32[5,8,128]{2,1,0:T(8,128)S(1)}, u32[]{:S(2)}, u32[]{:S(2)}) collective-permute-start(f32[5,8,128]{2,1,0:T(8,128)S(1)} %get-tuple-element.30.after_ref), channel_id=1, source_target_pairs={{0,8},{8,0},{9,17},{17,9},{16,24},{24,16},{1,3},{25,27},{2,10},{10... | collective-permute-start | bytes 61448 | tf_op jit(solution)/shard_map/ppermute | solution.py:644
  16.1 2.4 %collective-permute-start.7 = (f32[5,8,128]{2,1,0:T(8,128)S(1)}, f32[5,8,128]{2,1,0:T(8,128)S(1)}, u32[]{:S(2)}, u32[]{:S(2)}) collective-permute-start(f32[5,8,128]{2,1,0:T(8,128)S(1)} %collective-permute-done.6.direct_ref), channel_id=1, source_target_pairs={{0,1},{1,0},{2,3},{3,2},{4,5},{5,4},{6,7},{7,6},{8,9},{9,8},{10,11... | collective-permute-start | bytes 61448 | tf_op jit(solution)/shard_map/ppermute | solution.py:643
  17.7 0.8 %copy-start.1 = (f32[8,8,128]{2,1,0:T(8,128)S(1)}, f32[8,8,128]{2,1,0:T(8,128)}, u32[]{:S(2)}) copy-start(f32[8,8,128]{2,1,0:T(8,128)} %initial_ref.1) | copy-start | bytes 98308
  18.6 3.2 %collective-permute-start.8 = (f32[8,2,256]{2,1,0:T(2,128)S(1)}, f32[8,2,256]{2,1,0:T(2,128)S(1)}, u32[]{:S(2)}, u32[]{:S(2)}) collective-permute-start(f32[8,2,256]{2,1,0:T(2,128)S(1)} %get-tuple-element.32), channel_id=1, source_target_pairs={{0,3},{3,0},{2,5},{5,2},{4,7},{7,4},{1,9},{6,14},{8,11},{11,8},{10... | collective-permute-start | bytes 49160 | tf_op jit(solution)/shard_map/ppermute | solution.py:644
  21.8 1.8 %collective-permute-start.9 = (f32[8,2,256]{2,1,0:T(2,128)S(1)}, f32[8,2,256]{2,1,0:T(2,128)S(1)}, u32[]{:S(2)}, u32[]{:S(2)}) collective-permute-start(f32[8,2,256]{2,1,0:T(2,128)S(1)} %collective-permute-done.8.direct_ref), channel_id=1, source_target_pairs={{0,1},{1,0},{2,3},{3,2},{4,5},{5,4},{6,7},{7,6},{8,9},{9,8},{10,11... | collective-permute-start | bytes 49160 | tf_op jit(solution)/shard_map/ppermute | solution.py:643

commit v7 on v6

--- a/solution.py
+++ b/solution.py
@@ -397,13 +397,14 @@
         mz_ref[1, place * nodes : (place + 2) * nodes, :] = low
 
 
-def trade_cores(axis, place):
-    return (place % 2, place % 2) if axis == "gx" else (0, 1)
-
-
-def trades_below(axis):
-    core, place = lax.axis_index("gz"), lax.axis_index(axis)
-    return core != place % 2 if axis == "gx" else core == 1
+def trade_cores(axis, place, other):
+    if axis == "gx":
+        return (place % 2, place % 2)
+    return (0, 1) if other % 2 == 0 else (1, 0)
+
+
+def trades_below():
+    return lax.axis_index("gz") != lax.axis_index("gx") % 2
 
 
 def sides(below, direct, passed):
@@ -418,7 +419,7 @@
 
 
 def layers_kernel(own_ref, partner_ref, out_ref):
-    start = jnp.where(trades_below("gx"), 0, out_ref.shape[2] - 2)
+    start = jnp.where(trades_below(), 0, out_ref.shape[2] - 2)
     for half, ref in enumerate((own_ref, partner_ref)):
         for layer in range(2):
             out_ref[half, layer] = ref[start + layer]
@@ -427,7 +428,7 @@
 def x_positions(own_ref, partner_ref, direct_ref, passed_ref):
     has_low, has_high = edges("gx")
     length = own_ref.shape[1]
-    below = trades_below("gx")
+    below = trades_below()
     outer = []
     for slot in range(2):
         direct = [direct_ref[h, slot] for h in range(2)]
@@ -449,7 +450,7 @@
 
 def rows_kernel(own_ref, partner_ref, direct_ref, passed_ref, after_ref, out_ref):
     _, rows, width = own_ref.shape
-    below = trades_below("gy")
+    below = trades_below()
     positions = x_positions(own_ref, partner_ref, direct_ref, passed_ref)
     out_ref[out_ref.shape[0] - 1] = jnp.zeros(out_ref.shape[1:], f32)
     for a, (own, partner) in enumerate(positions):
@@ -509,7 +510,7 @@
             grid[a, :, half * width : (half + 1) * width] = value
     along_z = by_z(grid[...].reshape(ext * rows, 2 * width), mz)
     along_z = along_z.reshape(ext, rows, lanes)
-    below = trades_below("gy")
+    below = trades_below()
     use = jnp.where(below, has_low, has_high)
     outer = [cy[0, jnp.where(below, 0, nodes) + k] for k in range(2)]
     for p, value in enumerate(from_rows(yd_ref[...], use, mz, cx_rows, ext)):
@@ -527,7 +528,7 @@
 
 
 def solve_kernel(yp_ref, part_ref, cx, cx_rows, cy, rate, mz, spectral, sent_ref):
-    below = trades_below("gy")
+    below = trades_below()
     width = yp_ref.shape[2] // 2
     ext, padded, lanes = rate.shape
     nodes = ext - 2
@@ -543,7 +544,7 @@
         rows = [layer * ext + p for p in range(ext)]
         last = [r + nodes * ext for r in rows]
         coefficients = [
-            jnp.where(trades_below("gx"), cx[r : r + 1, :], cx[k : k + 1, :])
+            jnp.where(trades_below(), cx[r : r + 1, :], cx[k : k + 1, :])
             for r, k in zip(rows, last)
         ]
         layers.append(back_by_y(back_by_x(spectral, coefficients), cy, ext))
@@ -570,7 +571,7 @@
 
 def return_rows_kernel(initial_ref, inner_ref, direct_ref, passed_ref, out_ref, base_ref):
     has_low, has_high = edges("gx")
-    below_x, below_y = trades_below("gx"), trades_below("gy")
+    below_x, below_y = trades_below(), trades_below()
     nodes, rows, width = initial_ref.shape
     for layer in range(nodes):
         lanes = [slice(0, width), slice(width, 2 * width)]
@@ -599,7 +600,7 @@
 
 
 def result_kernel(base_ref, direct_ref, passed_ref, out_ref):
-    below = trades_below("gy")
+    below = trades_below()
     has_low, has_high = edges("gy")
     nodes, rows, width = base_ref.shape
     for layer in range(nodes):
@@ -621,20 +622,19 @@
         spot = (place, other) if along == 0 else (other, place)
         return (spot[0] * sizes[1] + spot[1]) * 2 + core
 
-    pairs = []
+    pairs, idle = [], []
     last = sizes[along] - 1
     for other in range(sizes[across]):
+        spare = {(place, core) for place in (0, last) for core in range(2)}
         for place in range(last):
-            here, there = trade_cores(axis, place)
+            here, there = trade_cores(axis, place, other)
+            spare -= {(place, here), (place + 1, there)}
             here, there = number(place, other, here), number(place + 1, other, there)
             pairs += [(here, there), (there, here)]
-        if other ^ 1 < sizes[across]:
-            idle = [(place, core) for place in {0, last} for core in range(2)]
-            if last > 0:
-                idle.remove((0, trade_cores(axis, 0)[0]))
-                idle.remove((last, trade_cores(axis, last - 1)[1]))
-            for place, core in sorted(idle):
-                pairs.append((number(place, other, core), number(place, other ^ 1, core)))
+        idle.append([number(place, other, core) for place, core in sorted(spare)])
+    for one, two in zip(idle[0::2], idle[1::2]):
+        for here, there in zip(one, two):
+            pairs += [(here, there), (there, here)]
     return pairs
 
 

time: 24.4 us -> 24 us (0.984)
  the two profiles are of different devices: /device:TPU:25 before, /device:TPU:0 now
where the time goes in v7:
time: 24 us; the launch traced here: 23.9 us
  starting transfers between devices  9.25 us (39%)
  waiting for transfers between devices  8.24 us (34%)
  Pallas kernels  6.3 us (26%)
    ppermute x4, starting transfers between devices, swap(): return lax.ppermute(value, AXES, swap_pairs(axis))  8.37 us
    pallas_call x11, Pallas kernels, call(): pl.pallas_call(kernel, out_shape=outs, in_specs=[where] * len(args), out_...  6.3 us
    ppermute x4, waiting for transfers between devices, swap(): return lax.ppermute(value, AXES, swap_pairs(axis))  4.98 us
    ppermute x6, waiting for transfers between devices, swap(): return lax.ppermute(value, 'gz', [(0, 1), (1, 0)])  3.26 us
    ppermute x6, starting transfers between devices, swap(): return lax.ppermute(value, 'gz', [(0, 1), (1, 0)])  0.88 us
  transfers between devices with their start and end apart: 10, of which 9 were waited for; matrix products, arithmetic and copies ran while one was open for 0% of the time, Pallas kernels for 16%

profile of v7, /device:TPU:0, one launch (start us, length us, event | category | flops | bytes accessed | tf_op | source)
XLA Modules:
  0.0 23.9 jit_solution(8024475754068799525)
XLA Ops:
  0.0 0.0 copy-start
  0.0 1.2 %shard_map.55.own_ref = f32[12,8,128]{2,1,0:T(8,128)S(1)} custom-call(f32[8,8,128]{2,1,0:T(8,128)} %initial_ref.1, f32[8,8,128]{2,1,0:T(8,128)} %source_hbm.1, f32[3,8,8,128]{3,2,1,0:T(8,128)} %metric_hbm.1, f32[30,1,16]{2,1,0:T(1,128)} %bitcast.6), custom_call_target="tpu_custom_call" | custom-call | bytes 214912 | tf_op jit(solution)/shard_map/pallas_call | solution.py:185
  1.2 0.5 %collective-permute-start = (f32[12,8,128]{2,1,0:T(8,128)S(1)}, f32[12,8,128]{2,1,0:T(8,128)S(1)}, u32[]{:S(2)}, u32[]{:S(2)}) collective-permute-start(f32[12,8,128]{2,1,0:T(8,128)S(1)} %shard_map.55.own_ref), channel_id=1, source_target_pairs={{0,1},{1,0},{2,3},{3,2},{4,5},{5,4},{6,7},{7,6},{8,9},{9,8},{10,11... | collective-permute-start | bytes 147464 | tf_op jit(solution)/shard_map/ppermute | solution.py:643
  1.8 0.0 copy-done
  1.8 0.1 collective-permute-start.2
  1.8 0.8 %collective-permute-done.partner_ref = f32[12,8,128]{2,1,0:T(8,128)S(1)} collective-permute-done((f32[12,8,128]{2,1,0:T(8,128)S(1)}, f32[12,8,128]{2,1,0:T(8,128)S(1)}, u32[]{:S(2)}, u32[]{:S(2)}) %collective-permute-start) | collective-permute-done | bytes 49184 | tf_op jit(solution)/shard_map/ppermute | solution.py:643
  2.6 2.8 %collective-permute-start.1 = (f32[2,2,8,128]{3,2,1,0:T(8,128)S(1)}, f32[2,2,8,128]{3,2,1,0:T(8,128)S(1)}, u32[]{:S(2)}, u32[]{:S(2)}) collective-permute-start(f32[2,2,8,128]{3,2,1,0:T(8,128)S(1)} %shard_map.56.after_ref), channel_id=1, source_target_pairs={{0,8},{8,0},{9,17},{17,9},{16,24},{24,16},{2,10},{10,2},{11,19},{1... | collective-permute-start | bytes 49160 | tf_op jit(solution)/shard_map/ppermute | solution.py:644
  5.5 0.0 collective-permute-done.2.partner_vec
  5.5 1.0 %shard_map.57 = (f32[100,320]{1,0:T(8,128)S(1)}, f32[240,320]{1,0:T(8,128)S(1)}, f32[10,16,320]{2,1,0:T(8,128)S(1)}) custom-call(f32[300,1,16]{2,1,0:T(1,128)S(1)} %bitcast.3, f32[300,1,16]{2,1,0:T(1,128)S(1)} %collective-permute-done.2.partner_vec, f32[12,8,128]{2,1,0:T(8,128)S(1)} %shard_map.55.own_ref, ...), custom_call_target="tpu_custom_call" | custom-call | bytes 793088 | tf_op jit(solution)/shard_map/pallas_call | solution.py:185
  6.5 0.7 %collective-permute-done.1.after_ref.direct_ref.xd_ref = f32[2,2,8,128]{3,2,1,0:T(8,128)S(1)} collective-permute-done((f32[2,2,8,128]{3,2,1,0:T(8,128)S(1)}, f32[2,2,8,128]{3,2,1,0:T(8,128)S(1)}, u32[]{:S(2)}, u32[]{:S(2)}) %collective-permute-start.1) | collective-permute-done | bytes 16416 | tf_op jit(solution)/shard_map/ppermute | solution.py:644
  7.2 0.0 collective-permute-start.3
  7.2 1.0 %shard_map.58.after_ref.mz = bf16[2,256,320]{2,1,0:T(8,128)(2,1)S(1)} custom-call(f32[300,1,16]{2,1,0:T(1,128)S(1)} %bitcast.4, f32[300,1,16]{2,1,0:T(1,128)S(1)} %collective-permute-done.2.partner_vec, f32[2,2,8,128]{3,2,1,0:T(8,128)S(1)} %collective-permute-done.1.after_ref.direct_ref.xd_ref), custom_call_target="tpu_custom_call" | custom-call | bytes 382464 | tf_op jit(solution)/shard_map/pallas_call | solution.py:185
  8.2 0.2 collective-permute-done.3.passed_ref.xp_ref
  8.4 2.1 %collective-permute-start.4 = (f32[3,8,256]{2,1,0:T(8,128)S(1)}, f32[3,8,256]{2,1,0:T(8,128)S(1)}, u32[]{:S(2)}, u32[]{:S(2)}) collective-permute-start(f32[3,8,256]{2,1,0:T(8,128)S(1)} %shard_map.59.after_ref), channel_id=1, source_target_pairs={{0,3},{3,0},{2,5},{5,2},{4,7},{7,4},{9,10},{10,9},{11,12},{12,11},... | collective-permute-start | bytes 73736 | tf_op jit(solution)/shard_map/ppermute | solution.py:644
  10.5 0.9 %shard_map.60.cy = f32[2,10,16,320]{3,2,1,0:T(8,128)S(1)} custom-call(f32[300,1,16]{2,1,0:T(1,128)S(1)} %bitcast.5, f32[300,1,16]{2,1,0:T(1,128)S(1)} %collective-permute-done.2.partner_vec, f32[3,8,256]{2,1,0:T(8,128)S(1)} %shard_map.59.after_ref), custom_call_target="tpu_custom_call" | custom-call | bytes 472576 | tf_op jit(solution)/shard_map/pallas_call | solution.py:185
  11.4 0.6 %collective-permute-done.4.yd_ref = f32[3,8,256]{2,1,0:T(8,128)S(1)} collective-permute-done((f32[3,8,256]{2,1,0:T(8,128)S(1)}, f32[3,8,256]{2,1,0:T(8,128)S(1)}, u32[]{:S(2)}, u32[]{:S(2)}) %collective-permute-start.4) | collective-permute-done | bytes 24608 | tf_op jit(solution)/shard_map/ppermute | solution.py:644
  12.0 0.1 collective-permute-start.5
  12.1 0.5 %shard_map.61.part_ref = f32[10,16,320]{2,1,0:T(8,128)S(1)} custom-call(f32[12,8,128]{2,1,0:T(8,128)S(1)} %shard_map.55.own_ref, f32[12,8,128]{2,1,0:T(8,128)S(1)} %collective-permute-done.partner_ref, f32[2,2,8,128]{3,2,1,0:T(8,128)S(1)} %collective-permute-done.1.after_ref.direct_ref.xd_ref, f32[2,2,8,128]{3,2,1,0:T(8,128)S(1)} %collective-permute-done.3.passed_ref.xp_ref, ...), custom_call_target="tpu_custom_call" | custom-call | bytes 1532928 | tf_op jit(solution)/shard_map/pallas_call | solution.py:185
  12.7 0.6 %collective-permute-done.5.yp_ref = f32[3,8,256]{2,1,0:T(8,128)S(1)} collective-permute-done((f32[3,8,256]{2,1,0:T(8,128)S(1)}, f32[3,8,256]{2,1,0:T(8,128)S(1)}, u32[]{:S(2)}, u32[]{:S(2)}) %collective-permute-start.5) | collective-permute-done | bytes 24608 | tf_op jit(solution)/shard_map/ppermute | solution.py:643
  13.2 0.5 %shard_map.62 = (f32[10,16,320]{2,1,0:T(8,128)S(1)}, f32[5,8,128]{2,1,0:T(8,128)S(1)}) custom-call(f32[3,8,256]{2,1,0:T(8,128)S(1)} %collective-permute-done.5.yp_ref, f32[10,16,320]{2,1,0:T(8,128)S(1)} %shard_map.61.part_ref, f32[100,320]{1,0:T(8,128)S(1)} %get-tuple-element.25.cx, f32[240,320]{1,0:T(8,128)S(1)} %get-tuple-element.26.cx_rows, ...), custom_call_target="tpu_custom_call" | custom-call | bytes 1831936 | tf_op jit(solution)/shard_map/pallas_call | solution.py:185
  13.7 1.8 %collective-permute-start.6 = (f32[5,8,128]{2,1,0:T(8,128)S(1)}, f32[5,8,128]{2,1,0:T(8,128)S(1)}, u32[]{:S(2)}, u32[]{:S(2)}) collective-permute-start(f32[5,8,128]{2,1,0:T(8,128)S(1)} %get-tuple-element.30.after_ref), channel_id=1, source_target_pairs={{0,8},{8,0},{9,17},{17,9},{16,24},{24,16},{2,10},{10,2},{11,19},{1... | collective-permute-start | bytes 61448 | tf_op jit(solution)/shard_map/ppermute | solution.py:644
  15.5 2.1 %collective-permute-done.6.direct_ref = f32[5,8,128]{2,1,0:T(8,128)S(1)} collective-permute-done((f32[5,8,128]{2,1,0:T(8,128)S(1)}, f32[5,8,128]{2,1,0:T(8,128)S(1)}, u32[]{:S(2)}, u32[]{:S(2)}) %collective-permute-start.6) | collective-permute-done | bytes 20512 | tf_op jit(solution)/shard_map/ppermute | solution.py:644
  17.6 0.0 collective-permute-start.7
  17.6 0.0 copy-start.1
  17.6 0.5 %shard_map.63.inner_ref = f32[8,16,256]{2,1,0:T(8,128)S(1)} custom-call(f32[10,16,320]{2,1,0:T(8,128)S(1)} %get-tuple-element.29.spectral, f32[100,320]{1,0:T(8,128)S(1)} %get-tuple-element.25.cx, f32[2,10,16,320]{3,2,1,0:T(8,128)S(1)} %shard_map.60.cy, bf16[2,256,320]{2,1,0:T(8,128)(2,1)S(1)} %shard_map.58.after_ref.mz, ...), custom_call_target="tpu_custom_call" | custom-call | bytes 1221632 | tf_op jit(solution)/shard_map/pallas_call | solution.py:185
  18.1 0.7 %collective-permute-done.7.passed_ref = f32[5,8,128]{2,1,0:T(8,128)S(1)} collective-permute-done((f32[5,8,128]{2,1,0:T(8,128)S(1)}, f32[5,8,128]{2,1,0:T(8,128)S(1)}, u32[]{:S(2)}, u32[]{:S(2)}) %collective-permute-start.7) | collective-permute-done | bytes 20512 | tf_op jit(solution)/shard_map/ppermute | solution.py:643
  18.8 0.0 copy-done.1
  18.8 1.6 %collective-permute-start.8 = (f32[8,2,256]{2,1,0:T(2,128)S(1)}, f32[8,2,256]{2,1,0:T(2,128)S(1)}, u32[]{:S(2)}, u32[]{:S(2)}) collective-permute-start(f32[8,2,256]{2,1,0:T(2,128)S(1)} %get-tuple-element.32), channel_id=1, source_target_pairs={{0,3},{3,0},{2,5},{5,2},{4,7},{7,4},{9,10},{10,9},{11,12},{12,11},... | collective-permute-start | bytes 49160 | tf_op jit(solution)/shard_map/ppermute | solution.py:644
  20.5 1.6 %collective-permute-done.8.direct_ref = f32[8,2,256]{2,1,0:T(2,128)S(1)} collective-permute-done((f32[8,2,256]{2,1,0:T(2,128)S(1)}, f32[8,2,256]{2,1,0:T(2,128)S(1)}, u32[]{:S(2)}, u32[]{:S(2)}) %collective-permute-start.8) | collective-permute-done | bytes 16416 | tf_op jit(solution)/shard_map/ppermute | solution.py:644
  22.1 0.2 collective-permute-start.9
  22.2 1.0 %collective-permute-done.9.passed_ref = f32[8,2,256]{2,1,0:T(2,128)S(1)} collective-permute-done((f32[8,2,256]{2,1,0:T(2,128)S(1)}, f32[8,2,256]{2,1,0:T(2,128)S(1)}, u32[]{:S(2)}, u32[]{:S(2)}) %collective-permute-start.9) | collective-permute-done | bytes 16416 | tf_op jit(solution)/shard_map/ppermute | solution.py:643
  23.2 0.6 %shard_map.65 = f32[8,8,128]{2,1,0:T(8,128)} custom-call(f32[8,8,128]{2,1,0:T(8,128)S(1)} %get-tuple-element.31.base_ref, f32[8,2,256]{2,1,0:T(2,128)S(1)} %collective-permute-done.8.direct_ref, f32[8,2,256]{2,1,0:T(2,128)S(1)} %collective-permute-done.9.passed_ref), custom_call_target="tpu_custom_call" | custom-call | bytes 98304 | tf_op jit(solution)/shard_map/pallas_call | solution.py:185
  (3 shorter events, 0.1 us)
Async XLA Ops:
  0.0 1.8 %copy-start = (f32[3,10,10,1,1,16]{5,4,3,2,1,0:T(1,128)S(1)}, f32[3,10,10,1,1,16]{5,4,3,2,1,0:T(1,128)}, u32[]{:S(2)}) copy-start(f32[3,10,10,1,1,16]{5,4,3,2,1,0:T(1,128)} %param.8) | copy-start | bytes 57604
  1.2 1.4 %collective-permute-start = (f32[12,8,128]{2,1,0:T(8,128)S(1)}, f32[12,8,128]{2,1,0:T(8,128)S(1)}, u32[]{:S(2)}, u32[]{:S(2)}) collective-permute-start(f32[12,8,128]{2,1,0:T(8,128)S(1)} %shard_map.55.own_ref), channel_id=1, source_target_pairs={{0,1},{1,0},{2,3},{3,2},{4,5},{5,4},{6,7},{7,6},{8,9},{9,8},{10,11... | collective-permute-start | bytes 147464 | tf_op jit(solution)/shard_map/ppermute | solution.py:643
  1.8 3.7 %collective-permute-start.2 = (f32[300,1,16]{2,1,0:T(1,128)S(1)}, f32[300,1,16]{2,1,0:T(1,128)S(1)}, u32[]{:S(2)}, u32[]{:S(2)}) collective-permute-start(f32[300,1,16]{2,1,0:T(1,128)S(1)} %bitcast.2), channel_id=1, source_target_pairs={{0,1},{1,0},{2,3},{3,2},{4,5},{5,4},{6,7},{7,6},{8,9},{9,8},{10,11... | collective-permute-start | bytes 57608 | tf_op jit(solution)/shard_map/ppermute | solution.py:643
  2.6 4.6 %collective-permute-start.1 = (f32[2,2,8,128]{3,2,1,0:T(8,128)S(1)}, f32[2,2,8,128]{3,2,1,0:T(8,128)S(1)}, u32[]{:S(2)}, u32[]{:S(2)}) collective-permute-start(f32[2,2,8,128]{3,2,1,0:T(8,128)S(1)} %shard_map.56.after_ref), channel_id=1, source_target_pairs={{0,8},{8,0},{9,17},{17,9},{16,24},{24,16},{2,10},{10,2},{11,19},{1... | collective-permute-start | bytes 49160 | tf_op jit(solution)/shard_map/ppermute | solution.py:644
  7.2 1.2 %collective-permute-start.3 = (f32[2,2,8,128]{3,2,1,0:T(8,128)S(1)}, f32[2,2,8,128]{3,2,1,0:T(8,128)S(1)}, u32[]{:S(2)}, u32[]{:S(2)}) collective-permute-start(f32[2,2,8,128]{3,2,1,0:T(8,128)S(1)} %collective-permute-done.1.after_ref.direct_ref.xd_ref), channel_id=1, source_target_pairs={{0,1},{1,0},{2,3},{3,2},{4,5},{5,4},{6,7},{7,6},{8,9},{9,8},{10,11... | collective-permute-start | bytes 49160 | tf_op jit(solution)/shard_map/ppermute | solution.py:643
  8.4 3.6 %collective-permute-start.4 = (f32[3,8,256]{2,1,0:T(8,128)S(1)}, f32[3,8,256]{2,1,0:T(8,128)S(1)}, u32[]{:S(2)}, u32[]{:S(2)}) collective-permute-start(f32[3,8,256]{2,1,0:T(8,128)S(1)} %shard_map.59.after_ref), channel_id=1, source_target_pairs={{0,3},{3,0},{2,5},{5,2},{4,7},{7,4},{9,10},{10,9},{11,12},{12,11},... | collective-permute-start | bytes 73736 | tf_op jit(solution)/shard_map/ppermute | solution.py:644
  12.0 1.2 %collective-permute-start.5 = (f32[3,8,256]{2,1,0:T(8,128)S(1)}, f32[3,8,256]{2,1,0:T(8,128)S(1)}, u32[]{:S(2)}, u32[]{:S(2)}) collective-permute-start(f32[3,8,256]{2,1,0:T(8,128)S(1)} %collective-permute-done.4.yd_ref), channel_id=1, source_target_pairs={{0,1},{1,0},{2,3},{3,2},{4,5},{5,4},{6,7},{7,6},{8,9},{9,8},{10,11... | collective-permute-start | bytes 73736 | tf_op jit(solution)/shard_map/ppermute | solution.py:643
  13.7 3.8 %collective-permute-start.6 = (f32[5,8,128]{2,1,0:T(8,128)S(1)}, f32[5,8,128]{2,1,0:T(8,128)S(1)}, u32[]{:S(2)}, u32[]{:S(2)}) collective-permute-start(f32[5,8,128]{2,1,0:T(8,128)S(1)} %get-tuple-element.30.after_ref), channel_id=1, source_target_pairs={{0,8},{8,0},{9,17},{17,9},{16,24},{24,16},{2,10},{10,2},{11,19},{1... | collective-permute-start | bytes 61448 | tf_op jit(solution)/shard_map/ppermute | solution.py:644
  17.6 1.2 %collective-permute-start.7 = (f32[5,8,128]{2,1,0:T(8,128)S(1)}, f32[5,8,128]{2,1,0:T(8,128)S(1)}, u32[]{:S(2)}, u32[]{:S(2)}) collective-permute-start(f32[5,8,128]{2,1,0:T(8,128)S(1)} %collective-permute-done.6.direct_ref), channel_id=1, source_target_pairs={{0,1},{1,0},{2,3},{3,2},{4,5},{5,4},{6,7},{7,6},{8,9},{9,8},{10,11... | collective-permute-start | bytes 61448 | tf_op jit(solution)/shard_map/ppermute | solution.py:643
  17.6 1.2 %copy-start.1 = (f32[8,8,128]{2,1,0:T(8,128)S(1)}, f32[8,8,128]{2,1,0:T(8,128)}, u32[]{:S(2)}) copy-start(f32[8,8,128]{2,1,0:T(8,128)} %initial_ref.1) | copy-start | bytes 98308
  18.8 3.2 %collective-permute-start.8 = (f32[8,2,256]{2,1,0:T(2,128)S(1)}, f32[8,2,256]{2,1,0:T(2,128)S(1)}, u32[]{:S(2)}, u32[]{:S(2)}) collective-permute-start(f32[8,2,256]{2,1,0:T(2,128)S(1)} %get-tuple-element.32), channel_id=1, source_target_pairs={{0,3},{3,0},{2,5},{5,2},{4,7},{7,4},{9,10},{10,9},{11,12},{12,11},... | collective-permute-start | bytes 49160 | tf_op jit(solution)/shard_map/ppermute | solution.py:644
  22.1 1.2 %collective-permute-start.9 = (f32[8,2,256]{2,1,0:T(2,128)S(1)}, f32[8,2,256]{2,1,0:T(2,128)S(1)}, u32[]{:S(2)}, u32[]{:S(2)}) collective-permute-start(f32[8,2,256]{2,1,0:T(2,128)S(1)} %collective-permute-done.8.direct_ref), channel_id=1, source_target_pairs={{0,1},{1,0},{2,3},{3,2},{4,5},{5,4},{6,7},{7,6},{8,9},{9,8},{10,11... | collective-permute-start | bytes 49160 | tf_op jit(solution)/shard_map/ppermute | solution.py:643

commit v8 on v7

--- a/solution.py
+++ b/solution.py
@@ -213,9 +213,8 @@
     return high, middle, (rest - middle.astype(f32)).astype(bf16)
 
 
-def dot(left, right, transposed=False):
-    dims = (((1,), (1 if transposed else 0,)), ((), ()))
-    return lax.dot_general(left, right, dims, preferred_element_type=f32)
+def dot(left, right):
+    return jnp.dot(left, right, preferred_element_type=f32)
 
 
 def repeated_table(table, width):
@@ -359,14 +358,9 @@
         cy_ref[k] = gathered(choice, along_y).reshape(cy_ref.shape[1:])
 
 
-def z_coefficients_kernel(own_vec, partner_vec, after_ref, mz_ref):
-    blocks = own_vec.shape[2]
-    lanes = mz_ref.shape[2]
-    half = lanes // 2
-    ext = half // blocks
+def z_coefficients_kernel(own_vec, partner_vec, after_ref, out_ref):
+    ext, lanes = out_ref.shape
     square = ext * ext
-    nodes = ext - 2
-    core = lax.axis_index("gz")
     shape = (square, lanes)
     same = counted(shape, 0) % ext == counted(shape, 1) % ext
     along_z = spread(
@@ -374,37 +368,53 @@
     )
     along_z = jnp.where(same, along_z, jnp.zeros_like(along_z))
     shape = (ext, square)
-    along_z = gathered(counted(shape, 1) // ext == counted(shape, 0), along_z)
-
+    out_ref[...] = gathered(counted(shape, 1) // ext == counted(shape, 0), along_z)
+
+
+def z_matrix_kernel(along_z, after_ref, mz_ref, back_ref):
+    ext, lanes = along_z.shape
+    half = lanes // 2
+    blocks = half // ext
+    nodes = ext - 2
+    core = lax.axis_index("gz")
     zeros = jnp.zeros((nodes - 2, lanes), f32)
-    own = along_z[1 : nodes + 1]
-    below = jnp.concatenate([zeros, along_z[0:2]], axis=0)
-    above = jnp.concatenate([along_z[nodes : nodes + 2], zeros], axis=0)
+    own = along_z[1 : nodes + 1, :]
+    below = jnp.concatenate([zeros, along_z[0:2, :]], axis=0)
+    above = jnp.concatenate([along_z[nodes : nodes + 2, :], zeros], axis=0)
     lane = counted((nodes, lanes), 1)
     first_own = core * blocks
     first_partner = blocks - first_own
     element = jnp.where(lane < half, lane // ext + first_own, (lane - half) // ext + first_partner)
     zero = jnp.zeros_like(own)
-    for place in range(0, 2 * blocks, 2):
-        first = place + first_own if place < blocks else place - blocks + first_partner
-        pair = []
-        for block in (first, first + 1):
-            value = jnp.where(element == block, own, zero)
-            value = value + jnp.where(element == block + 1, below, zero)
-            pair.append(value + jnp.where(element == block - 1, above, zero))
-        high, low = split2(jnp.concatenate(pair, axis=0))
-        mz_ref[0, place * nodes : (place + 2) * nodes, :] = high
-        mz_ref[1, place * nodes : (place + 2) * nodes, :] = low
-
-
-def trade_cores(axis, place, other):
-    if axis == "gx":
-        return (place % 2, place % 2)
-    return (0, 1) if other % 2 == 0 else (1, 0)
-
-
-def trades_below():
-    return lax.axis_index("gz") != lax.axis_index("gx") % 2
+    rows = []
+    for place in range(2 * blocks):
+        block = place + first_own if place < blocks else place - blocks + first_partner
+        value = jnp.where(element == block, own, zero)
+        value = value + jnp.where(element == block + 1, below, zero)
+        rows.append(value + jnp.where(element == block - 1, above, zero))
+    matrix = jnp.concatenate(rows, axis=0)
+    for ref, value in ((mz_ref, matrix), (back_ref, matrix.T)):
+        ref[0], ref[1] = split2(value)
+
+
+OUT_X, BACK_X, ALONG_Y = "out x", "back x", "along y"
+
+
+def upper_core(leg, x, y):
+    if leg == OUT_X:
+        return 1 - x // 2 % 2
+    return 0 if leg == BACK_X else x % 2
+
+
+def trades_below(leg):
+    x, y = lax.axis_index("gx"), lax.axis_index("gy")
+    return lax.axis_index("gz") != upper_core(leg, x, y)
+
+
+def meets_same(leg):
+    x, y = lax.axis_index("gx"), lax.axis_index("gy")
+    x = jnp.where(trades_below(leg), x - 1, x)
+    return upper_core(leg, x, y) + upper_core(leg, x + 1, y) == 1
 
 
 def sides(below, direct, passed):
@@ -419,16 +429,18 @@
 
 
 def layers_kernel(own_ref, partner_ref, out_ref):
-    start = jnp.where(trades_below(), 0, out_ref.shape[2] - 2)
-    for half, ref in enumerate((own_ref, partner_ref)):
-        for layer in range(2):
-            out_ref[half, layer] = ref[start + layer]
+    start = jnp.where(trades_below(OUT_X), 0, out_ref.shape[2] - 2)
+    same = meets_same(OUT_X)
+    for layer in range(2):
+        own, partner = own_ref[start + layer], partner_ref[start + layer]
+        out_ref[0, layer] = jnp.where(same, own, partner)
+        out_ref[1, layer] = jnp.where(same, partner, own)
 
 
 def x_positions(own_ref, partner_ref, direct_ref, passed_ref):
     has_low, has_high = edges("gx")
     length = own_ref.shape[1]
-    below = trades_below()
+    below = trades_below(OUT_X)
     outer = []
     for slot in range(2):
         direct = [direct_ref[h, slot] for h in range(2)]
@@ -450,7 +462,7 @@
 
 def rows_kernel(own_ref, partner_ref, direct_ref, passed_ref, after_ref, out_ref):
     _, rows, width = own_ref.shape
-    below = trades_below()
+    below = trades_below(ALONG_Y)
     positions = x_positions(own_ref, partner_ref, direct_ref, passed_ref)
     out_ref[out_ref.shape[0] - 1] = jnp.zeros(out_ref.shape[1:], f32)
     for a, (own, partner) in enumerate(positions):
@@ -461,23 +473,15 @@
             )
 
 
-def by_parts(value, mz, transposed):
+def by_z(value, matrix):
     rows = value.shape[0]
     spare = -rows % 16
     if spare:
         value = jnp.concatenate([value, jnp.zeros((spare, value.shape[1]), f32)], axis=0)
     high, low = split2(value)
-    both = dot(jnp.concatenate([high, low], axis=0), mz[0], transposed)
-    total = both[0 : rows + spare] + (both[rows + spare :] + dot(high, mz[1], transposed))
+    both = dot(jnp.concatenate([high, low], axis=0), matrix[0])
+    total = both[0 : rows + spare] + (both[rows + spare :] + dot(high, matrix[1]))
     return total[0:rows]
-
-
-def by_z(value, mz):
-    return by_parts(value, mz, False)
-
-
-def back_by_z(value, mz):
-    return by_parts(value, mz, True)
 
 
 def from_rows(value, use, mz, cx_rows, ext):
@@ -510,7 +514,7 @@
             grid[a, :, half * width : (half + 1) * width] = value
     along_z = by_z(grid[...].reshape(ext * rows, 2 * width), mz)
     along_z = along_z.reshape(ext, rows, lanes)
-    below = trades_below()
+    below = trades_below(ALONG_Y)
     use = jnp.where(below, has_low, has_high)
     outer = [cy[0, jnp.where(below, 0, nodes) + k] for k in range(2)]
     for p, value in enumerate(from_rows(yd_ref[...], use, mz, cx_rows, ext)):
@@ -527,8 +531,8 @@
     return sum(cy[1, q] * value[q : q + 1] for q in range(ext))
 
 
-def solve_kernel(yp_ref, part_ref, cx, cx_rows, cy, rate, mz, spectral, sent_ref):
-    below = trades_below()
+def solve_kernel(yp_ref, part_ref, cx, cx_rows, cy, rate, mz, mz_back, spectral, sent_ref):
+    below = trades_below(ALONG_Y)
     width = yp_ref.shape[2] // 2
     ext, padded, lanes = rate.shape
     nodes = ext - 2
@@ -539,39 +543,41 @@
     for p, value in enumerate(from_rows(passed, use, mz, cx_rows, ext)):
         total = part_ref[p] + sum(outer[k] * value[k : k + 1] for k in range(2))
         spectral[p] = total * rate[p]
+    same = meets_same(BACK_X)
     layers = []
     for layer in range(2):
         rows = [layer * ext + p for p in range(ext)]
         last = [r + nodes * ext for r in rows]
         coefficients = [
-            jnp.where(trades_below(), cx[r : r + 1, :], cx[k : k + 1, :])
+            jnp.where(trades_below(BACK_X), cx[r : r + 1, :], cx[k : k + 1, :])
             for r, k in zip(rows, last)
         ]
         layers.append(back_by_y(back_by_x(spectral, coefficients), cy, ext))
-    result = back_by_z(jnp.concatenate(layers, axis=0), mz)
+    result = by_z(jnp.concatenate(layers, axis=0), mz_back)
     for layer in range(2):
+        value = result[layer * padded : layer * padded + nodes + 2]
+        own, partner = value[:, 0:width], value[:, width:]
         for half in range(2):
-            lanes_at = slice(half * width, (half + 1) * width)
             place = half * 2 + layer
-            value = result[layer * padded : layer * padded + nodes + 2, lanes_at]
+            value = jnp.where(same, own, partner) if half == 0 else jnp.where(same, partner, own)
             sent_ref[place] = value[0:nodes]
             sent_ref[4, 2 * place : 2 * place + 2, :] = value[nodes : nodes + 2]
 
 
-def interior_kernel(spectral, cx, cy, mz, after_ref, out_ref):
+def interior_kernel(spectral, cx, cy, mz_back, after_ref, out_ref):
     ext, padded, lanes = spectral.shape
     nodes, _, both = out_ref.shape
     layers = []
     for a in range(1, ext - 1):
         coefficients = [cx[a * ext + p : a * ext + p + 1, :] for p in range(ext)]
         layers.append(back_by_y(back_by_x(spectral, coefficients), cy, ext))
-    result = back_by_z(jnp.concatenate(layers, axis=0), mz)
+    result = by_z(jnp.concatenate(layers, axis=0), mz_back)
     out_ref[...] = result.reshape(nodes, padded, both)
 
 
 def return_rows_kernel(initial_ref, inner_ref, direct_ref, passed_ref, out_ref, base_ref):
     has_low, has_high = edges("gx")
-    below_x, below_y = trades_below(), trades_below()
+    below_x, below_y = trades_below(BACK_X), trades_below(ALONG_Y)
     nodes, rows, width = initial_ref.shape
     for layer in range(nodes):
         lanes = [slice(0, width), slice(width, 2 * width)]
@@ -600,7 +606,7 @@
 
 
 def result_kernel(base_ref, direct_ref, passed_ref, out_ref):
-    below = trades_below()
+    below = trades_below(ALONG_Y)
     has_low, has_high = edges("gy")
     nodes, rows, width = base_ref.shape
     for layer in range(nodes):
@@ -614,34 +620,34 @@
         out_ref[layer] = base_ref[layer] + jnp.concatenate([low, between, high], axis=0)
 
 
-def swap_pairs(axis):
-    sizes = [lax.axis_size(name) for name in AXES]
-    along, across = (0, 1) if axis == "gx" else (1, 0)
-
-    def number(place, other, core):
-        spot = (place, other) if along == 0 else (other, place)
-        return (spot[0] * sizes[1] + spot[1]) * 2 + core
+def swap_pairs(leg):
+    count_x, count_y = (lax.axis_size(name) for name in AXES[:2])
+    last, others = (count_y - 1, count_x) if leg == ALONG_Y else (count_x - 1, count_y)
+
+    def cores(place, other):
+        x, y = (other, place) if leg == ALONG_Y else (place, other)
+        upper, first = upper_core(leg, x, y), (x * count_y + y) * 2
+        return first + upper, first + 1 - upper
 
     pairs, idle = [], []
-    last = sizes[along] - 1
-    for other in range(sizes[across]):
-        spare = {(place, core) for place in (0, last) for core in range(2)}
+    for other in range(others):
+        line = [cores(place, other) for place in range(last + 1)]
         for place in range(last):
-            here, there = trade_cores(axis, place, other)
-            spare -= {(place, here), (place + 1, there)}
-            here, there = number(place, other, here), number(place + 1, other, there)
+            here, there = line[place][0], line[place + 1][1]
             pairs += [(here, there), (there, here)]
-        idle.append([number(place, other, core) for place, core in sorted(spare)])
+        idle.append((line[0][1], line[last][0]))
     for one, two in zip(idle[0::2], idle[1::2]):
         for here, there in zip(one, two):
             pairs += [(here, there), (there, here)]
     return pairs
 
 
-def swap(value, axis):
-    if axis == "gz":
-        return lax.ppermute(value, "gz", [(0, 1), (1, 0)])
-    return lax.ppermute(value, AXES, swap_pairs(axis))
+def swap_cores(value):
+    return lax.ppermute(value, "gz", [(0, 1), (1, 0)])
+
+
+def swap_chips(value, leg):
+    return lax.ppermute(value, AXES, swap_pairs(leg))
 
 
 def paired_body(initial, source, metric, eigenvectors, eigenvalues):
@@ -666,11 +672,11 @@
         ],
         where=HBM,
     )[0]
-    partner = swap(own, "gz")
+    partner = swap_cores(own)
     vectors, own = lax.optimization_barrier((vectors, own))
-    partner_vectors = swap(vectors, "gz")
+    partner_vectors = swap_cores(vectors)
     sent = call(layers_kernel, [shaped((2, 2, rows, width))], [own, partner])[0]
-    x_direct = swap(sent, "gx")
+    x_direct = swap_chips(sent, OUT_X)
     tiles = -(-2 * ext // rows)
     cx, cx_rows, rate = call(
         x_coefficients_kernel,
@@ -682,25 +688,30 @@
         [vectors, partner_vectors, own, partner, sent],
     )
     x_direct, cx, rate = lax.optimization_barrier((x_direct, cx, rate))
-    x_passed = swap(x_direct, "gz")
-    mz = call(
+    x_passed = swap_cores(x_direct)
+    along_z = call(
         z_coefficients_kernel,
-        [shaped((2, 2 * width, lanes), bf16)],
+        [shaped((ext, lanes))],
         [vectors, partner_vectors, x_direct],
     )[0]
     sent = call(
         rows_kernel,
         [shaped((tiles, rows, 2 * width))],
-        [own, partner, x_direct, x_passed, mz],
+        [own, partner, x_direct, x_passed, along_z],
     )[0]
-    y_direct = swap(sent, "gy")
+    y_direct = swap_chips(sent, ALONG_Y)
     cy = call(
         y_coefficients_kernel,
         [shaped((2, ext, padded, lanes))],
         [vectors, partner_vectors, sent],
     )[0]
-    y_direct, cy = lax.optimization_barrier((y_direct, cy))
-    y_passed = swap(y_direct, "gz")
+    mz, mz_back = call(
+        z_matrix_kernel,
+        [shaped((2, 2 * width, lanes), bf16), shaped((2, lanes, 2 * width), bf16)],
+        [along_z, cy],
+    )
+    y_direct, cy, mz = lax.optimization_barrier((y_direct, cy, mz))
+    y_passed = swap_cores(y_direct)
     part = call(
         interior_solve_kernel,
         [shaped((ext, padded, lanes))],
@@ -710,19 +721,19 @@
     spectral, sent = call(
         solve_kernel,
         [shaped((ext, padded, lanes)), shaped((5, rows, width))],
-        [y_passed, part, cx, cx_rows, cy, rate, mz],
-    )
-
-    x_direct = swap(sent, "gx")
-    inner = call(interior_kernel, [shaped((nodes, padded, 2 * width))], [spectral, cx, cy, mz, sent])[0]
-    x_passed = swap(x_direct, "gz")
+        [y_passed, part, cx, cx_rows, cy, rate, mz, mz_back],
+    )
+
+    x_direct = swap_chips(sent, BACK_X)
+    inner = call(interior_kernel, [shaped((nodes, padded, 2 * width))], [spectral, cx, cy, mz_back, sent])[0]
+    x_passed = swap_cores(x_direct)
     sent, base = call(
         return_rows_kernel,
         [shaped((nodes, 2, 2 * width)), shaped(initial.shape)],
         [initial, inner, x_direct, x_passed],
     )
-    y_direct = swap(sent, "gy")
-    y_passed = swap(y_direct, "gz")
+    y_direct = swap_chips(sent, ALONG_Y)
+    y_passed = swap_cores(y_direct)
     return call(result_kernel, [shaped(initial.shape)], [base, y_direct, y_passed])[0]
 
 

time: 24 us -> 23.7 us (0.987)
  waiting for transfers between devices: 8.24 us -> 7.44 us
  starting transfers between devices: 9.25 us -> 9.58 us
    ppermute x10, waiting for transfers between devices: 8.24 us -> 7.44 us  [the longest x4 4.27 us: swap_chips(): return lax.ppermute(value, AXES, swap_pairs(leg))]
    ppermute x10, starting transfers between devices: 9.25 us -> 9.58 us  [the longest x4 8.03 us: swap_chips(): return lax.ppermute(value, AXES, swap_pairs(leg))]
    pallas_call x11 -> x12, Pallas kernels: 6.3 us -> 6.4 us  [call(): pl.pallas_call(kernel, out_shape=outs, in_specs=[where] * len(args), out_...]
  transfers between devices with their start and end apart: 10 -> 10, of which waited for: 9 -> 9; matrix products, arithmetic and copies ran while one was open for 0% -> 0% of each run, Pallas kernels for 16% -> 17%
where the time goes in v8:
time: 23.7 us; the launch traced here: 23.5 us
  starting transfers between devices  9.58 us (40%)
  waiting for transfers between devices  7.44 us (31%)
  Pallas kernels  6.4 us (27%)
    ppermute x4, starting transfers between devices, swap_chips(): return lax.ppermute(value, AXES, swap_pairs(leg))  8.03 us
    pallas_call x12, Pallas kernels, call(): pl.pallas_call(kernel, out_shape=outs, in_specs=[where] * len(args), out_...  6.4 us
    ppermute x4, waiting for transfers between devices, swap_chips(): return lax.ppermute(value, AXES, swap_pairs(leg))  4.27 us
    ppermute x6, waiting for transfers between devices, swap_cores(): return lax.ppermute(value, 'gz', [(0, 1), (1, 0)])  3.17 us
    ppermute x6, starting transfers between devices, swap_cores(): return lax.ppermute(value, 'gz', [(0, 1), (1, 0)])  1.55 us
  transfers between devices with their start and end apart: 10, of which 9 were waited for; matrix products, arithmetic and copies ran while one was open for 0% of the time, Pallas kernels for 17%

profile of v8, /device:TPU:0, one launch (start us, length us, event | category | flops | bytes accessed | tf_op | source)
XLA Modules:
  0.0 23.5 jit_solution(18068635887071323298)
XLA Ops:
  0.0 0.0 copy-start
  0.0 1.2 %shard_map.55.own_ref = f32[12,8,128]{2,1,0:T(8,128)S(1)} custom-call(f32[8,8,128]{2,1,0:T(8,128)} %initial_ref.1, f32[8,8,128]{2,1,0:T(8,128)} %source_hbm.1, f32[3,8,8,128]{3,2,1,0:T(8,128)} %metric_hbm.1, f32[30,1,16]{2,1,0:T(1,128)} %bitcast.6), custom_call_target="tpu_custom_call" | custom-call | bytes 214912 | tf_op jit(solution)/shard_map/pallas_call | solution.py:185
  1.2 0.5 %collective-permute-start = (f32[12,8,128]{2,1,0:T(8,128)S(1)}, f32[12,8,128]{2,1,0:T(8,128)S(1)}, u32[]{:S(2)}, u32[]{:S(2)}) collective-permute-start(f32[12,8,128]{2,1,0:T(8,128)S(1)} %shard_map.55.own_ref), channel_id=1, source_target_pairs={{0,1},{1,0},{2,3},{3,2},{4,5},{5,4},{6,7},{7,6},{8,9},{9,8},{10,11... | collective-permute-start | bytes 147464 | tf_op jit(solution)/shard_map/ppermute | solution.py:646
  1.8 0.0 copy-done
  1.8 0.1 collective-permute-start.2
  1.8 0.8 %collective-permute-done.partner_ref = f32[12,8,128]{2,1,0:T(8,128)S(1)} collective-permute-done((f32[12,8,128]{2,1,0:T(8,128)S(1)}, f32[12,8,128]{2,1,0:T(8,128)S(1)}, u32[]{:S(2)}, u32[]{:S(2)}) %collective-permute-start) | collective-permute-done | bytes 49184 | tf_op jit(solution)/shard_map/ppermute | solution.py:646
  2.6 2.9 %collective-permute-start.1 = (f32[2,2,8,128]{3,2,1,0:T(8,128)S(1)}, f32[2,2,8,128]{3,2,1,0:T(8,128)S(1)}, u32[]{:S(2)}, u32[]{:S(2)}) collective-permute-start(f32[2,2,8,128]{3,2,1,0:T(8,128)S(1)} %shard_map.56.after_ref), channel_id=1, source_target_pairs={{1,8},{8,1},{9,17},{17,9},{16,25},{25,16},{3,10},{10,3},{11,19},{1... | collective-permute-start | bytes 49160 | tf_op jit(solution)/shard_map/ppermute | solution.py:650
  5.6 0.0 collective-permute-done.2.partner_vec
  5.6 1.0 %shard_map.57 = (f32[100,320]{1,0:T(8,128)S(1)}, f32[240,320]{1,0:T(8,128)S(1)}, f32[10,16,320]{2,1,0:T(8,128)S(1)}) custom-call(f32[300,1,16]{2,1,0:T(1,128)S(1)} %bitcast.3, f32[300,1,16]{2,1,0:T(1,128)S(1)} %collective-permute-done.2.partner_vec, f32[12,8,128]{2,1,0:T(8,128)S(1)} %shard_map.55.own_ref, ...), custom_call_target="tpu_custom_call" | custom-call | bytes 793088 | tf_op jit(solution)/shard_map/pallas_call | solution.py:185
  6.6 0.7 %collective-permute-done.1.after_ref.direct_ref.xd_ref = f32[2,2,8,128]{3,2,1,0:T(8,128)S(1)} collective-permute-done((f32[2,2,8,128]{3,2,1,0:T(8,128)S(1)}, f32[2,2,8,128]{3,2,1,0:T(8,128)S(1)}, u32[]{:S(2)}, u32[]{:S(2)}) %collective-permute-start.1) | collective-permute-done | bytes 16416 | tf_op jit(solution)/shard_map/ppermute | solution.py:650
  7.3 0.0 collective-permute-start.3
  7.3 0.7 %shard_map.58.after_ref.along_z = f32[10,320]{1,0:T(8,128)S(1)} custom-call(f32[300,1,16]{2,1,0:T(1,128)S(1)} %bitcast.4, f32[300,1,16]{2,1,0:T(1,128)S(1)} %collective-permute-done.2.partner_vec, f32[2,2,8,128]{3,2,1,0:T(8,128)S(1)} %collective-permute-done.1.after_ref.direct_ref.xd_ref), custom_call_target="tpu_custom_call" | custom-call | bytes 67584 | tf_op jit(solution)/shard_map/pallas_call | solution.py:185
  8.0 0.4 %collective-permute-done.3.passed_ref.xp_ref = f32[2,2,8,128]{3,2,1,0:T(8,128)S(1)} collective-permute-done((f32[2,2,8,128]{3,2,1,0:T(8,128)S(1)}, f32[2,2,8,128]{3,2,1,0:T(8,128)S(1)}, u32[]{:S(2)}, u32[]{:S(2)}) %collective-permute-start.3) | collective-permute-done | bytes 16416 | tf_op jit(solution)/shard_map/ppermute | solution.py:646
  8.5 1.9 %collective-permute-start.4 = (f32[3,8,256]{2,1,0:T(8,128)S(1)}, f32[3,8,256]{2,1,0:T(8,128)S(1)}, u32[]{:S(2)}, u32[]{:S(2)}) collective-permute-start(f32[3,8,256]{2,1,0:T(8,128)S(1)} %shard_map.59.after_ref), channel_id=1, source_target_pairs={{0,3},{3,0},{2,5},{5,2},{4,7},{7,4},{9,10},{10,9},{11,12},{12,11},... | collective-permute-start | bytes 73736 | tf_op jit(solution)/shard_map/ppermute | solution.py:650
  10.3 0.9 %shard_map.60.after_ref.cy = f32[2,10,16,320]{3,2,1,0:T(8,128)S(1)} custom-call(f32[300,1,16]{2,1,0:T(1,128)S(1)} %bitcast.5, f32[300,1,16]{2,1,0:T(1,128)S(1)} %collective-permute-done.2.partner_vec, f32[3,8,256]{2,1,0:T(8,128)S(1)} %shard_map.59.after_ref), custom_call_target="tpu_custom_call" | custom-call | bytes 472576 | tf_op jit(solution)/shard_map/pallas_call | solution.py:185
  11.3 0.3 %shard_map.61 = (bf16[2,256,320]{2,1,0:T(8,128)(2,1)S(1)}, bf16[2,320,256]{2,1,0:T(8,128)(2,1)S(1)}) custom-call(f32[10,320]{1,0:T(8,128)S(1)} %shard_map.58.after_ref.along_z, f32[2,10,16,320]{3,2,1,0:T(8,128)S(1)} %shard_map.60.after_ref.cy), custom_call_target="tpu_custom_call" | custom-call | bytes 1077760 | tf_op jit(solution)/shard_map/pallas_call | solution.py:185
  11.6 0.3 %collective-permute-done.4.yd_ref = f32[3,8,256]{2,1,0:T(8,128)S(1)} collective-permute-done((f32[3,8,256]{2,1,0:T(8,128)S(1)}, f32[3,8,256]{2,1,0:T(8,128)S(1)}, u32[]{:S(2)}, u32[]{:S(2)}) %collective-permute-start.4) | collective-permute-done | bytes 24608 | tf_op jit(solution)/shard_map/ppermute | solution.py:650
  11.9 0.1 collective-permute-start.5
  12.0 0.5 %shard_map.62.part_ref = f32[10,16,320]{2,1,0:T(8,128)S(1)} custom-call(f32[12,8,128]{2,1,0:T(8,128)S(1)} %shard_map.55.own_ref, f32[12,8,128]{2,1,0:T(8,128)S(1)} %collective-permute-done.partner_ref, f32[2,2,8,128]{3,2,1,0:T(8,128)S(1)} %collective-permute-done.1.after_ref.direct_ref.xd_ref, f32[2,2,8,128]{3,2,1,0:T(8,128)S(1)} %collective-permute-done.3.passed_ref.xp_ref, ...), custom_call_target="tpu_custom_call" | custom-call | bytes 1532928 | tf_op jit(solution)/shard_map/pallas_call | solution.py:185
  12.5 0.6 %collective-permute-done.5.yp_ref = f32[3,8,256]{2,1,0:T(8,128)S(1)} collective-permute-done((f32[3,8,256]{2,1,0:T(8,128)S(1)}, f32[3,8,256]{2,1,0:T(8,128)S(1)}, u32[]{:S(2)}, u32[]{:S(2)}) %collective-permute-start.5) | collective-permute-done | bytes 24608 | tf_op jit(solution)/shard_map/ppermute | solution.py:646
  13.1 0.5 %shard_map.63 = (f32[10,16,320]{2,1,0:T(8,128)S(1)}, f32[5,8,128]{2,1,0:T(8,128)S(1)}) custom-call(f32[3,8,256]{2,1,0:T(8,128)S(1)} %collective-permute-done.5.yp_ref, f32[10,16,320]{2,1,0:T(8,128)S(1)} %shard_map.62.part_ref, f32[100,320]{1,0:T(8,128)S(1)} %get-tuple-element.29.cx, f32[240,320]{1,0:T(8,128)S(1)} %get-tuple-element.30.cx_rows, ...), custom_call_target="tpu_custom_call" | custom-call | bytes 2159616 | tf_op jit(solution)/shard_map/pallas_call | solution.py:185
  13.6 1.5 %collective-permute-start.6 = (f32[5,8,128]{2,1,0:T(8,128)S(1)}, f32[5,8,128]{2,1,0:T(8,128)S(1)}, u32[]{:S(2)}, u32[]{:S(2)}) collective-permute-start(f32[5,8,128]{2,1,0:T(8,128)S(1)} %get-tuple-element.36.after_ref), channel_id=1, source_target_pairs={{0,9},{9,0},{8,17},{17,8},{16,25},{25,16},{2,11},{11,2},{10,19},{1... | collective-permute-start | bytes 61448 | tf_op jit(solution)/shard_map/ppermute | solution.py:650
  15.0 1.8 %collective-permute-done.6.direct_ref = f32[5,8,128]{2,1,0:T(8,128)S(1)} collective-permute-done((f32[5,8,128]{2,1,0:T(8,128)S(1)}, f32[5,8,128]{2,1,0:T(8,128)S(1)}, u32[]{:S(2)}, u32[]{:S(2)}) %collective-permute-start.6) | collective-permute-done | bytes 20512 | tf_op jit(solution)/shard_map/ppermute | solution.py:650
  16.9 0.1 collective-permute-start.7
  17.0 0.0 copy-start.1
  17.0 0.5 %shard_map.64.inner_ref = f32[8,16,256]{2,1,0:T(8,128)S(1)} custom-call(f32[10,16,320]{2,1,0:T(8,128)S(1)} %get-tuple-element.35.spectral, f32[100,320]{1,0:T(8,128)S(1)} %get-tuple-element.29.cx, f32[2,10,16,320]{3,2,1,0:T(8,128)S(1)} %shard_map.60.after_ref.cy, bf16[2,320,256]{2,1,0:T(8,128)(2,1)S(1)} %get-tuple-element.34.mz_back, ...), custom_call_target="tpu_custom_call" | custom-call | bytes 1221632 | tf_op jit(solution)/shard_map/pallas_call | solution.py:185
  17.5 0.6 %collective-permute-done.7.passed_ref = f32[5,8,128]{2,1,0:T(8,128)S(1)} collective-permute-done((f32[5,8,128]{2,1,0:T(8,128)S(1)}, f32[5,8,128]{2,1,0:T(8,128)S(1)}, u32[]{:S(2)}, u32[]{:S(2)}) %collective-permute-start.7) | collective-permute-done | bytes 20512 | tf_op jit(solution)/shard_map/ppermute | solution.py:646
  18.0 0.0 copy-done.1
  18.1 1.8 %collective-permute-start.8 = (f32[8,2,256]{2,1,0:T(2,128)S(1)}, f32[8,2,256]{2,1,0:T(2,128)S(1)}, u32[]{:S(2)}, u32[]{:S(2)}) collective-permute-start(f32[8,2,256]{2,1,0:T(2,128)S(1)} %get-tuple-element.38), channel_id=1, source_target_pairs={{0,3},{3,0},{2,5},{5,2},{4,7},{7,4},{9,10},{10,9},{11,12},{12,11},... | collective-permute-start | bytes 49160 | tf_op jit(solution)/shard_map/ppermute | solution.py:650
  19.9 1.4 %collective-permute-done.8.direct_ref = f32[8,2,256]{2,1,0:T(2,128)S(1)} collective-permute-done((f32[8,2,256]{2,1,0:T(2,128)S(1)}, f32[8,2,256]{2,1,0:T(2,128)S(1)}, u32[]{:S(2)}, u32[]{:S(2)}) %collective-permute-start.8) | collective-permute-done | bytes 16416 | tf_op jit(solution)/shard_map/ppermute | solution.py:650
  21.3 0.7 %collective-permute-start.9 = (f32[8,2,256]{2,1,0:T(2,128)S(1)}, f32[8,2,256]{2,1,0:T(2,128)S(1)}, u32[]{:S(2)}, u32[]{:S(2)}) collective-permute-start(f32[8,2,256]{2,1,0:T(2,128)S(1)} %collective-permute-done.8.direct_ref), channel_id=1, source_target_pairs={{0,1},{1,0},{2,3},{3,2},{4,5},{5,4},{6,7},{7,6},{8,9},{9,8},{10,11... | collective-permute-start | bytes 49160 | tf_op jit(solution)/shard_map/ppermute | solution.py:646
  22.0 0.8 %collective-permute-done.9.passed_ref = f32[8,2,256]{2,1,0:T(2,128)S(1)} collective-permute-done((f32[8,2,256]{2,1,0:T(2,128)S(1)}, f32[8,2,256]{2,1,0:T(2,128)S(1)}, u32[]{:S(2)}, u32[]{:S(2)}) %collective-permute-start.9) | collective-permute-done | bytes 16416 | tf_op jit(solution)/shard_map/ppermute | solution.py:646
  22.9 0.6 %shard_map.66 = f32[8,8,128]{2,1,0:T(8,128)} custom-call(f32[8,8,128]{2,1,0:T(8,128)S(1)} %get-tuple-element.37.base_ref, f32[8,2,256]{2,1,0:T(2,128)S(1)} %collective-permute-done.8.direct_ref, f32[8,2,256]{2,1,0:T(2,128)S(1)} %collective-permute-done.9.passed_ref), custom_call_target="tpu_custom_call" | custom-call | bytes 98304 | tf_op jit(solution)/shard_map/pallas_call | solution.py:185
  (3 shorter events, 0.1 us)
Async XLA Ops:
  0.0 1.8 %copy-start = (f32[3,10,10,1,1,16]{5,4,3,2,1,0:T(1,128)S(1)}, f32[3,10,10,1,1,16]{5,4,3,2,1,0:T(1,128)}, u32[]{:S(2)}) copy-start(f32[3,10,10,1,1,16]{5,4,3,2,1,0:T(1,128)} %param.8) | copy-start | bytes 57604
  1.2 1.4 %collective-permute-start = (f32[12,8,128]{2,1,0:T(8,128)S(1)}, f32[12,8,128]{2,1,0:T(8,128)S(1)}, u32[]{:S(2)}, u32[]{:S(2)}) collective-permute-start(f32[12,8,128]{2,1,0:T(8,128)S(1)} %shard_map.55.own_ref), channel_id=1, source_target_pairs={{0,1},{1,0},{2,3},{3,2},{4,5},{5,4},{6,7},{7,6},{8,9},{9,8},{10,11... | collective-permute-start | bytes 147464 | tf_op jit(solution)/shard_map/ppermute | solution.py:646
  1.8 3.8 %collective-permute-start.2 = (f32[300,1,16]{2,1,0:T(1,128)S(1)}, f32[300,1,16]{2,1,0:T(1,128)S(1)}, u32[]{:S(2)}, u32[]{:S(2)}) collective-permute-start(f32[300,1,16]{2,1,0:T(1,128)S(1)} %bitcast.2), channel_id=1, source_target_pairs={{0,1},{1,0},{2,3},{3,2},{4,5},{5,4},{6,7},{7,6},{8,9},{9,8},{10,11... | collective-permute-start | bytes 57608 | tf_op jit(solution)/shard_map/ppermute | solution.py:646
  2.6 4.6 %collective-permute-start.1 = (f32[2,2,8,128]{3,2,1,0:T(8,128)S(1)}, f32[2,2,8,128]{3,2,1,0:T(8,128)S(1)}, u32[]{:S(2)}, u32[]{:S(2)}) collective-permute-start(f32[2,2,8,128]{3,2,1,0:T(8,128)S(1)} %shard_map.56.after_ref), channel_id=1, source_target_pairs={{1,8},{8,1},{9,17},{17,9},{16,25},{25,16},{3,10},{10,3},{11,19},{1... | collective-permute-start | bytes 49160 | tf_op jit(solution)/shard_map/ppermute | solution.py:650
  7.3 1.2 %collective-permute-start.3 = (f32[2,2,8,128]{3,2,1,0:T(8,128)S(1)}, f32[2,2,8,128]{3,2,1,0:T(8,128)S(1)}, u32[]{:S(2)}, u32[]{:S(2)}) collective-permute-start(f32[2,2,8,128]{3,2,1,0:T(8,128)S(1)} %collective-permute-done.1.after_ref.direct_ref.xd_ref), channel_id=1, source_target_pairs={{0,1},{1,0},{2,3},{3,2},{4,5},{5,4},{6,7},{7,6},{8,9},{9,8},{10,11... | collective-permute-start | bytes 49160 | tf_op jit(solution)/shard_map/ppermute | solution.py:646
  8.5 3.4 %collective-permute-start.4 = (f32[3,8,256]{2,1,0:T(8,128)S(1)}, f32[3,8,256]{2,1,0:T(8,128)S(1)}, u32[]{:S(2)}, u32[]{:S(2)}) collective-permute-start(f32[3,8,256]{2,1,0:T(8,128)S(1)} %shard_map.59.after_ref), channel_id=1, source_target_pairs={{0,3},{3,0},{2,5},{5,2},{4,7},{7,4},{9,10},{10,9},{11,12},{12,11},... | collective-permute-start | bytes 73736 | tf_op jit(solution)/shard_map/ppermute | solution.py:650
  11.9 1.2 %collective-permute-start.5 = (f32[3,8,256]{2,1,0:T(8,128)S(1)}, f32[3,8,256]{2,1,0:T(8,128)S(1)}, u32[]{:S(2)}, u32[]{:S(2)}) collective-permute-start(f32[3,8,256]{2,1,0:T(8,128)S(1)} %collective-permute-done.4.yd_ref), channel_id=1, source_target_pairs={{0,1},{1,0},{2,3},{3,2},{4,5},{5,4},{6,7},{7,6},{8,9},{9,8},{10,11... | collective-permute-start | bytes 73736 | tf_op jit(solution)/shard_map/ppermute | solution.py:646
  13.6 3.3 %collective-permute-start.6 = (f32[5,8,128]{2,1,0:T(8,128)S(1)}, f32[5,8,128]{2,1,0:T(8,128)S(1)}, u32[]{:S(2)}, u32[]{:S(2)}) collective-permute-start(f32[5,8,128]{2,1,0:T(8,128)S(1)} %get-tuple-element.36.after_ref), channel_id=1, source_target_pairs={{0,9},{9,0},{8,17},{17,8},{16,25},{25,16},{2,11},{11,2},{10,19},{1... | collective-permute-start | bytes 61448 | tf_op jit(solution)/shard_map/ppermute | solution.py:650
  16.9 1.2 %collective-permute-start.7 = (f32[5,8,128]{2,1,0:T(8,128)S(1)}, f32[5,8,128]{2,1,0:T(8,128)S(1)}, u32[]{:S(2)}, u32[]{:S(2)}) collective-permute-start(f32[5,8,128]{2,1,0:T(8,128)S(1)} %collective-permute-done.6.direct_ref), channel_id=1, source_target_pairs={{0,1},{1,0},{2,3},{3,2},{4,5},{5,4},{6,7},{7,6},{8,9},{9,8},{10,11... | collective-permute-start | bytes 61448 | tf_op jit(solution)/shard_map/ppermute | solution.py:646
  17.0 1.1 %copy-start.1 = (f32[8,8,128]{2,1,0:T(8,128)S(1)}, f32[8,8,128]{2,1,0:T(8,128)}, u32[]{:S(2)}) copy-start(f32[8,8,128]{2,1,0:T(8,128)} %initial_ref.1) | copy-start | bytes 98308
  18.1 3.2 %collective-permute-start.8 = (f32[8,2,256]{2,1,0:T(2,128)S(1)}, f32[8,2,256]{2,1,0:T(2,128)S(1)}, u32[]{:S(2)}, u32[]{:S(2)}) collective-permute-start(f32[8,2,256]{2,1,0:T(2,128)S(1)} %get-tuple-element.38), channel_id=1, source_target_pairs={{0,3},{3,0},{2,5},{5,2},{4,7},{7,4},{9,10},{10,9},{11,12},{12,11},... | collective-permute-start | bytes 49160 | tf_op jit(solution)/shard_map/ppermute | solution.py:650
  21.3 1.5 %collective-permute-start.9 = (f32[8,2,256]{2,1,0:T(2,128)S(1)}, f32[8,2,256]{2,1,0:T(2,128)S(1)}, u32[]{:S(2)}, u32[]{:S(2)}) collective-permute-start(f32[8,2,256]{2,1,0:T(2,128)S(1)} %collective-permute-done.8.direct_ref), channel_id=1, source_target_pairs={{0,1},{1,0},{2,3},{3,2},{4,5},{5,4},{6,7},{7,6},{8,9},{9,8},{10,11... | collective-permute-start | bytes 49160 | tf_op jit(solution)/shard_map/ppermute | solution.py:646

commit v9 on v8

--- a/solution.py
+++ b/solution.py
@@ -397,13 +397,15 @@
         ref[0], ref[1] = split2(value)
 
 
-OUT_X, BACK_X, ALONG_Y = "out x", "back x", "along y"
+OUT_X, BACK_X, OUT_Y, BACK_Y = "out x", "back x", "out y", "back y"
 
 
 def upper_core(leg, x, y):
     if leg == OUT_X:
         return 1 - x // 2 % 2
-    return 0 if leg == BACK_X else x % 2
+    if leg == BACK_X:
+        return 0
+    return x % 2 if leg == OUT_Y else (x + 1) // 2 % 2
 
 
 def trades_below(leg):
@@ -462,7 +464,7 @@
 
 def rows_kernel(own_ref, partner_ref, direct_ref, passed_ref, after_ref, out_ref):
     _, rows, width = own_ref.shape
-    below = trades_below(ALONG_Y)
+    below = trades_below(OUT_Y)
     positions = x_positions(own_ref, partner_ref, direct_ref, passed_ref)
     out_ref[out_ref.shape[0] - 1] = jnp.zeros(out_ref.shape[1:], f32)
     for a, (own, partner) in enumerate(positions):
@@ -514,7 +516,7 @@
             grid[a, :, half * width : (half + 1) * width] = value
     along_z = by_z(grid[...].reshape(ext * rows, 2 * width), mz)
     along_z = along_z.reshape(ext, rows, lanes)
-    below = trades_below(ALONG_Y)
+    below = trades_below(OUT_Y)
     use = jnp.where(below, has_low, has_high)
     outer = [cy[0, jnp.where(below, 0, nodes) + k] for k in range(2)]
     for p, value in enumerate(from_rows(yd_ref[...], use, mz, cx_rows, ext)):
@@ -532,7 +534,7 @@
 
 
 def solve_kernel(yp_ref, part_ref, cx, cx_rows, cy, rate, mz, mz_back, spectral, sent_ref):
-    below = trades_below(ALONG_Y)
+    below = trades_below(OUT_Y)
     width = yp_ref.shape[2] // 2
     ext, padded, lanes = rate.shape
     nodes = ext - 2
@@ -577,7 +579,7 @@
 
 def return_rows_kernel(initial_ref, inner_ref, direct_ref, passed_ref, out_ref, base_ref):
     has_low, has_high = edges("gx")
-    below_x, below_y = trades_below(BACK_X), trades_below(ALONG_Y)
+    below_x, below_y = trades_below(BACK_X), trades_below(BACK_Y)
     nodes, rows, width = initial_ref.shape
     for layer in range(nodes):
         lanes = [slice(0, width), slice(width, 2 * width)]
@@ -606,7 +608,7 @@
 
 
 def result_kernel(base_ref, direct_ref, passed_ref, out_ref):
-    below = trades_below(ALONG_Y)
+    below = trades_below(BACK_Y)
     has_low, has_high = edges("gy")
     nodes, rows, width = base_ref.shape
     for layer in range(nodes):
@@ -622,10 +624,11 @@
 
 def swap_pairs(leg):
     count_x, count_y = (lax.axis_size(name) for name in AXES[:2])
-    last, others = (count_y - 1, count_x) if leg == ALONG_Y else (count_x - 1, count_y)
+    by_y = leg in (OUT_Y, BACK_Y)
+    last, others = (count_y - 1, count_x) if by_y else (count_x - 1, count_y)
 
     def cores(place, other):
-        x, y = (other, place) if leg == ALONG_Y else (place, other)
+        x, y = (other, place) if by_y else (place, other)
         upper, first = upper_core(leg, x, y), (x * count_y + y) * 2
         return first + upper, first + 1 - upper
 
@@ -636,9 +639,11 @@
             here, there = line[place][0], line[place + 1][1]
             pairs += [(here, there), (there, here)]
         idle.append((line[0][1], line[last][0]))
-    for one, two in zip(idle[0::2], idle[1::2]):
-        for here, there in zip(one, two):
-            pairs += [(here, there), (there, here)]
+    step = 2 if leg == BACK_Y and others % 4 == 0 else 1
+    for other in range(others - step):
+        if other // step % 2 == 0:
+            for here, there in zip(idle[other], idle[other + step]):
+                pairs += [(here, there), (there, here)]
     return pairs
 
 
@@ -699,7 +704,7 @@
         [shaped((tiles, rows, 2 * width))],
         [own, partner, x_direct, x_passed, along_z],
     )[0]
-    y_direct = swap_chips(sent, ALONG_Y)
+    y_direct = swap_chips(sent, OUT_Y)
     cy = call(
         y_coefficients_kernel,
         [shaped((2, ext, padded, lanes))],
@@ -732,7 +737,7 @@
         [shaped((nodes, 2, 2 * width)), shaped(initial.shape)],
         [initial, inner, x_direct, x_passed],
     )
-    y_direct = swap_chips(sent, ALONG_Y)
+    y_direct = swap_chips(sent, BACK_Y)
     y_passed = swap_cores(y_direct)
     return call(result_kernel, [shaped(initial.shape)], [base, y_direct, y_passed])[0]
 

time: 23.7 us -> 23.7 us (level)
  no operation moved by 1% of the time
where the time goes in v9:
time: 23.7 us; the launch traced here: 23.5 us
  starting transfers between devices  9.61 us (41%)
  waiting for transfers between devices  7.44 us (31%)
  Pallas kernels  6.4 us (27%)
    ppermute x4, starting transfers between devices, swap_chips(): return lax.ppermute(value, AXES, swap_pairs(leg))  8.03 us
    pallas_call x12, Pallas kernels, call(): pl.pallas_call(kernel, out_shape=outs, in_specs=[where] * len(args), out_...  6.4 us
    ppermute x4, waiting for transfers between devices, swap_chips(): return lax.ppermute(value, AXES, swap_pairs(leg))  4.27 us
    ppermute x6, waiting for transfers between devices, swap_cores(): return lax.ppermute(value, 'gz', [(0, 1), (1, 0)])  3.17 us
    ppermute x6, starting transfers between devices, swap_cores(): return lax.ppermute(value, 'gz', [(0, 1), (1, 0)])  1.58 us
  transfers between devices with their start and end apart: 10, of which 9 were waited for; matrix products, arithmetic and copies ran while one was open for 0% of the time, Pallas kernels for 17%

profile of v9, /device:TPU:0, one launch (start us, length us, event | category | flops | bytes accessed | tf_op | source)
XLA Modules:
  0.0 23.5 jit_solution(17351958564339499585)
XLA Ops:
  0.0 0.0 copy-start
  0.0 1.2 %shard_map.55.own_ref = f32[12,8,128]{2,1,0:T(8,128)S(1)} custom-call(f32[8,8,128]{2,1,0:T(8,128)} %initial_ref.1, f32[8,8,128]{2,1,0:T(8,128)} %source_hbm.1, f32[3,8,8,128]{3,2,1,0:T(8,128)} %metric_hbm.1, f32[30,1,16]{2,1,0:T(1,128)} %bitcast.6), custom_call_target="tpu_custom_call" | custom-call | bytes 214912 | tf_op jit(solution)/shard_map/pallas_call | solution.py:185
  1.2 0.5 %collective-permute-start = (f32[12,8,128]{2,1,0:T(8,128)S(1)}, f32[12,8,128]{2,1,0:T(8,128)S(1)}, u32[]{:S(2)}, u32[]{:S(2)}) collective-permute-start(f32[12,8,128]{2,1,0:T(8,128)S(1)} %shard_map.55.own_ref), channel_id=1, source_target_pairs={{0,1},{1,0},{2,3},{3,2},{4,5},{5,4},{6,7},{7,6},{8,9},{9,8},{10,11... | collective-permute-start | bytes 147464 | tf_op jit(solution)/shard_map/ppermute | solution.py:651
  1.8 0.0 copy-done
  1.8 0.1 collective-permute-start.2
  1.8 0.8 %collective-permute-done.partner_ref = f32[12,8,128]{2,1,0:T(8,128)S(1)} collective-permute-done((f32[12,8,128]{2,1,0:T(8,128)S(1)}, f32[12,8,128]{2,1,0:T(8,128)S(1)}, u32[]{:S(2)}, u32[]{:S(2)}) %collective-permute-start) | collective-permute-done | bytes 49184 | tf_op jit(solution)/shard_map/ppermute | solution.py:651
  2.6 2.9 %collective-permute-start.1 = (f32[2,2,8,128]{3,2,1,0:T(8,128)S(1)}, f32[2,2,8,128]{3,2,1,0:T(8,128)S(1)}, u32[]{:S(2)}, u32[]{:S(2)}) collective-permute-start(f32[2,2,8,128]{3,2,1,0:T(8,128)S(1)} %shard_map.56.after_ref), channel_id=1, source_target_pairs={{1,8},{8,1},{9,17},{17,9},{16,25},{25,16},{3,10},{10,3},{11,19},{1... | collective-permute-start | bytes 49160 | tf_op jit(solution)/shard_map/ppermute | solution.py:655
  5.6 0.0 collective-permute-done.2.partner_vec
  5.6 1.0 %shard_map.57 = (f32[100,320]{1,0:T(8,128)S(1)}, f32[240,320]{1,0:T(8,128)S(1)}, f32[10,16,320]{2,1,0:T(8,128)S(1)}) custom-call(f32[300,1,16]{2,1,0:T(1,128)S(1)} %bitcast.3, f32[300,1,16]{2,1,0:T(1,128)S(1)} %collective-permute-done.2.partner_vec, f32[12,8,128]{2,1,0:T(8,128)S(1)} %shard_map.55.own_ref, ...), custom_call_target="tpu_custom_call" | custom-call | bytes 793088 | tf_op jit(solution)/shard_map/pallas_call | solution.py:185
  6.6 0.7 %collective-permute-done.1.after_ref.direct_ref.xd_ref = f32[2,2,8,128]{3,2,1,0:T(8,128)S(1)} collective-permute-done((f32[2,2,8,128]{3,2,1,0:T(8,128)S(1)}, f32[2,2,8,128]{3,2,1,0:T(8,128)S(1)}, u32[]{:S(2)}, u32[]{:S(2)}) %collective-permute-start.1) | collective-permute-done | bytes 16416 | tf_op jit(solution)/shard_map/ppermute | solution.py:655
  7.3 0.0 collective-permute-start.3
  7.3 0.7 %shard_map.58.after_ref.along_z = f32[10,320]{1,0:T(8,128)S(1)} custom-call(f32[300,1,16]{2,1,0:T(1,128)S(1)} %bitcast.4, f32[300,1,16]{2,1,0:T(1,128)S(1)} %collective-permute-done.2.partner_vec, f32[2,2,8,128]{3,2,1,0:T(8,128)S(1)} %collective-permute-done.1.after_ref.direct_ref.xd_ref), custom_call_target="tpu_custom_call" | custom-call | bytes 67584 | tf_op jit(solution)/shard_map/pallas_call | solution.py:185
  8.0 0.4 %collective-permute-done.3.passed_ref.xp_ref = f32[2,2,8,128]{3,2,1,0:T(8,128)S(1)} collective-permute-done((f32[2,2,8,128]{3,2,1,0:T(8,128)S(1)}, f32[2,2,8,128]{3,2,1,0:T(8,128)S(1)}, u32[]{:S(2)}, u32[]{:S(2)}) %collective-permute-start.3) | collective-permute-done | bytes 16416 | tf_op jit(solution)/shard_map/ppermute | solution.py:651
  8.5 1.9 %collective-permute-start.4 = (f32[3,8,256]{2,1,0:T(8,128)S(1)}, f32[3,8,256]{2,1,0:T(8,128)S(1)}, u32[]{:S(2)}, u32[]{:S(2)}) collective-permute-start(f32[3,8,256]{2,1,0:T(8,128)S(1)} %shard_map.59.after_ref), channel_id=1, source_target_pairs={{0,3},{3,0},{2,5},{5,2},{4,7},{7,4},{9,10},{10,9},{11,12},{12,11},... | collective-permute-start | bytes 73736 | tf_op jit(solution)/shard_map/ppermute | solution.py:655
  10.3 0.9 %shard_map.60.after_ref.cy = f32[2,10,16,320]{3,2,1,0:T(8,128)S(1)} custom-call(f32[300,1,16]{2,1,0:T(1,128)S(1)} %bitcast.5, f32[300,1,16]{2,1,0:T(1,128)S(1)} %collective-permute-done.2.partner_vec, f32[3,8,256]{2,1,0:T(8,128)S(1)} %shard_map.59.after_ref), custom_call_target="tpu_custom_call" | custom-call | bytes 472576 | tf_op jit(solution)/shard_map/pallas_call | solution.py:185
  11.3 0.3 %shard_map.61 = (bf16[2,256,320]{2,1,0:T(8,128)(2,1)S(1)}, bf16[2,320,256]{2,1,0:T(8,128)(2,1)S(1)}) custom-call(f32[10,320]{1,0:T(8,128)S(1)} %shard_map.58.after_ref.along_z, f32[2,10,16,320]{3,2,1,0:T(8,128)S(1)} %shard_map.60.after_ref.cy), custom_call_target="tpu_custom_call" | custom-call | bytes 1077760 | tf_op jit(solution)/shard_map/pallas_call | solution.py:185
  11.6 0.3 %collective-permute-done.4.yd_ref = f32[3,8,256]{2,1,0:T(8,128)S(1)} collective-permute-done((f32[3,8,256]{2,1,0:T(8,128)S(1)}, f32[3,8,256]{2,1,0:T(8,128)S(1)}, u32[]{:S(2)}, u32[]{:S(2)}) %collective-permute-start.4) | collective-permute-done | bytes 24608 | tf_op jit(solution)/shard_map/ppermute | solution.py:655
  11.9 0.1 collective-permute-start.5
  12.0 0.5 %shard_map.62.part_ref = f32[10,16,320]{2,1,0:T(8,128)S(1)} custom-call(f32[12,8,128]{2,1,0:T(8,128)S(1)} %shard_map.55.own_ref, f32[12,8,128]{2,1,0:T(8,128)S(1)} %collective-permute-done.partner_ref, f32[2,2,8,128]{3,2,1,0:T(8,128)S(1)} %collective-permute-done.1.after_ref.direct_ref.xd_ref, f32[2,2,8,128]{3,2,1,0:T(8,128)S(1)} %collective-permute-done.3.passed_ref.xp_ref, ...), custom_call_target="tpu_custom_call" | custom-call | bytes 1532928 | tf_op jit(solution)/shard_map/pallas_call | solution.py:185
  12.5 0.6 %collective-permute-done.5.yp_ref = f32[3,8,256]{2,1,0:T(8,128)S(1)} collective-permute-done((f32[3,8,256]{2,1,0:T(8,128)S(1)}, f32[3,8,256]{2,1,0:T(8,128)S(1)}, u32[]{:S(2)}, u32[]{:S(2)}) %collective-permute-start.5) | collective-permute-done | bytes 24608 | tf_op jit(solution)/shard_map/ppermute | solution.py:651
  13.1 0.5 %shard_map.63 = (f32[10,16,320]{2,1,0:T(8,128)S(1)}, f32[5,8,128]{2,1,0:T(8,128)S(1)}) custom-call(f32[3,8,256]{2,1,0:T(8,128)S(1)} %collective-permute-done.5.yp_ref, f32[10,16,320]{2,1,0:T(8,128)S(1)} %shard_map.62.part_ref, f32[100,320]{1,0:T(8,128)S(1)} %get-tuple-element.29.cx, f32[240,320]{1,0:T(8,128)S(1)} %get-tuple-element.30.cx_rows, ...), custom_call_target="tpu_custom_call" | custom-call | bytes 2159616 | tf_op jit(solution)/shard_map/pallas_call | solution.py:185
  13.6 1.5 %collective-permute-start.6 = (f32[5,8,128]{2,1,0:T(8,128)S(1)}, f32[5,8,128]{2,1,0:T(8,128)S(1)}, u32[]{:S(2)}, u32[]{:S(2)}) collective-permute-start(f32[5,8,128]{2,1,0:T(8,128)S(1)} %get-tuple-element.36.after_ref), channel_id=1, source_target_pairs={{0,9},{9,0},{8,17},{17,8},{16,25},{25,16},{2,11},{11,2},{10,19},{1... | collective-permute-start | bytes 61448 | tf_op jit(solution)/shard_map/ppermute | solution.py:655
  15.0 1.8 %collective-permute-done.6.direct_ref = f32[5,8,128]{2,1,0:T(8,128)S(1)} collective-permute-done((f32[5,8,128]{2,1,0:T(8,128)S(1)}, f32[5,8,128]{2,1,0:T(8,128)S(1)}, u32[]{:S(2)}, u32[]{:S(2)}) %collective-permute-start.6) | collective-permute-done | bytes 20512 | tf_op jit(solution)/shard_map/ppermute | solution.py:655
  16.9 0.1 collective-permute-start.7
  17.0 0.0 copy-start.1
  17.0 0.5 %shard_map.64.inner_ref = f32[8,16,256]{2,1,0:T(8,128)S(1)} custom-call(f32[10,16,320]{2,1,0:T(8,128)S(1)} %get-tuple-element.35.spectral, f32[100,320]{1,0:T(8,128)S(1)} %get-tuple-element.29.cx, f32[2,10,16,320]{3,2,1,0:T(8,128)S(1)} %shard_map.60.after_ref.cy, bf16[2,320,256]{2,1,0:T(8,128)(2,1)S(1)} %get-tuple-element.34.mz_back, ...), custom_call_target="tpu_custom_call" | custom-call | bytes 1221632 | tf_op jit(solution)/shard_map/pallas_call | solution.py:185
  17.5 0.6 %collective-permute-done.7.passed_ref = f32[5,8,128]{2,1,0:T(8,128)S(1)} collective-permute-done((f32[5,8,128]{2,1,0:T(8,128)S(1)}, f32[5,8,128]{2,1,0:T(8,128)S(1)}, u32[]{:S(2)}, u32[]{:S(2)}) %collective-permute-start.7) | collective-permute-done | bytes 20512 | tf_op jit(solution)/shard_map/ppermute | solution.py:651
  18.0 0.0 copy-done.1
  18.1 1.8 %collective-permute-start.8 = (f32[8,2,256]{2,1,0:T(2,128)S(1)}, f32[8,2,256]{2,1,0:T(2,128)S(1)}, u32[]{:S(2)}, u32[]{:S(2)}) collective-permute-start(f32[8,2,256]{2,1,0:T(2,128)S(1)} %get-tuple-element.38), channel_id=1, source_target_pairs={{0,3},{3,0},{2,5},{5,2},{4,7},{7,4},{9,10},{10,9},{11,12},{12,11},... | collective-permute-start | bytes 49160 | tf_op jit(solution)/shard_map/ppermute | solution.py:655
  19.9 1.4 %collective-permute-done.8.direct_ref = f32[8,2,256]{2,1,0:T(2,128)S(1)} collective-permute-done((f32[8,2,256]{2,1,0:T(2,128)S(1)}, f32[8,2,256]{2,1,0:T(2,128)S(1)}, u32[]{:S(2)}, u32[]{:S(2)}) %collective-permute-start.8) | collective-permute-done | bytes 16416 | tf_op jit(solution)/shard_map/ppermute | solution.py:655
  21.3 0.7 %collective-permute-start.9 = (f32[8,2,256]{2,1,0:T(2,128)S(1)}, f32[8,2,256]{2,1,0:T(2,128)S(1)}, u32[]{:S(2)}, u32[]{:S(2)}) collective-permute-start(f32[8,2,256]{2,1,0:T(2,128)S(1)} %collective-permute-done.8.direct_ref), channel_id=1, source_target_pairs={{0,1},{1,0},{2,3},{3,2},{4,5},{5,4},{6,7},{7,6},{8,9},{9,8},{10,11... | collective-permute-start | bytes 49160 | tf_op jit(solution)/shard_map/ppermute | solution.py:651
  22.1 0.8 %collective-permute-done.9.passed_ref = f32[8,2,256]{2,1,0:T(2,128)S(1)} collective-permute-done((f32[8,2,256]{2,1,0:T(2,128)S(1)}, f32[8,2,256]{2,1,0:T(2,128)S(1)}, u32[]{:S(2)}, u32[]{:S(2)}) %collective-permute-start.9) | collective-permute-done | bytes 16416 | tf_op jit(solution)/shard_map/ppermute | solution.py:651
  22.9 0.6 %shard_map.66 = f32[8,8,128]{2,1,0:T(8,128)} custom-call(f32[8,8,128]{2,1,0:T(8,128)S(1)} %get-tuple-element.37.base_ref, f32[8,2,256]{2,1,0:T(2,128)S(1)} %collective-permute-done.8.direct_ref, f32[8,2,256]{2,1,0:T(2,128)S(1)} %collective-permute-done.9.passed_ref), custom_call_target="tpu_custom_call" | custom-call | bytes 98304 | tf_op jit(solution)/shard_map/pallas_call | solution.py:185
  (3 shorter events, 0.1 us)
Async XLA Ops:
  0.0 1.8 %copy-start = (f32[3,10,10,1,1,16]{5,4,3,2,1,0:T(1,128)S(1)}, f32[3,10,10,1,1,16]{5,4,3,2,1,0:T(1,128)}, u32[]{:S(2)}) copy-start(f32[3,10,10,1,1,16]{5,4,3,2,1,0:T(1,128)} %param.8) | copy-start | bytes 57604
  1.2 1.4 %collective-permute-start = (f32[12,8,128]{2,1,0:T(8,128)S(1)}, f32[12,8,128]{2,1,0:T(8,128)S(1)}, u32[]{:S(2)}, u32[]{:S(2)}) collective-permute-start(f32[12,8,128]{2,1,0:T(8,128)S(1)} %shard_map.55.own_ref), channel_id=1, source_target_pairs={{0,1},{1,0},{2,3},{3,2},{4,5},{5,4},{6,7},{7,6},{8,9},{9,8},{10,11... | collective-permute-start | bytes 147464 | tf_op jit(solution)/shard_map/ppermute | solution.py:651
  1.8 3.8 %collective-permute-start.2 = (f32[300,1,16]{2,1,0:T(1,128)S(1)}, f32[300,1,16]{2,1,0:T(1,128)S(1)}, u32[]{:S(2)}, u32[]{:S(2)}) collective-permute-start(f32[300,1,16]{2,1,0:T(1,128)S(1)} %bitcast.2), channel_id=1, source_target_pairs={{0,1},{1,0},{2,3},{3,2},{4,5},{5,4},{6,7},{7,6},{8,9},{9,8},{10,11... | collective-permute-start | bytes 57608 | tf_op jit(solution)/shard_map/ppermute | solution.py:651
  2.6 4.6 %collective-permute-start.1 = (f32[2,2,8,128]{3,2,1,0:T(8,128)S(1)}, f32[2,2,8,128]{3,2,1,0:T(8,128)S(1)}, u32[]{:S(2)}, u32[]{:S(2)}) collective-permute-start(f32[2,2,8,128]{3,2,1,0:T(8,128)S(1)} %shard_map.56.after_ref), channel_id=1, source_target_pairs={{1,8},{8,1},{9,17},{17,9},{16,25},{25,16},{3,10},{10,3},{11,19},{1... | collective-permute-start | bytes 49160 | tf_op jit(solution)/shard_map/ppermute | solution.py:655
  7.3 1.2 %collective-permute-start.3 = (f32[2,2,8,128]{3,2,1,0:T(8,128)S(1)}, f32[2,2,8,128]{3,2,1,0:T(8,128)S(1)}, u32[]{:S(2)}, u32[]{:S(2)}) collective-permute-start(f32[2,2,8,128]{3,2,1,0:T(8,128)S(1)} %collective-permute-done.1.after_ref.direct_ref.xd_ref), channel_id=1, source_target_pairs={{0,1},{1,0},{2,3},{3,2},{4,5},{5,4},{6,7},{7,6},{8,9},{9,8},{10,11... | collective-permute-start | bytes 49160 | tf_op jit(solution)/shard_map/ppermute | solution.py:651
  8.5 3.4 %collective-permute-start.4 = (f32[3,8,256]{2,1,0:T(8,128)S(1)}, f32[3,8,256]{2,1,0:T(8,128)S(1)}, u32[]{:S(2)}, u32[]{:S(2)}) collective-permute-start(f32[3,8,256]{2,1,0:T(8,128)S(1)} %shard_map.59.after_ref), channel_id=1, source_target_pairs={{0,3},{3,0},{2,5},{5,2},{4,7},{7,4},{9,10},{10,9},{11,12},{12,11},... | collective-permute-start | bytes 73736 | tf_op jit(solution)/shard_map/ppermute | solution.py:655
  11.9 1.2 %collective-permute-start.5 = (f32[3,8,256]{2,1,0:T(8,128)S(1)}, f32[3,8,256]{2,1,0:T(8,128)S(1)}, u32[]{:S(2)}, u32[]{:S(2)}) collective-permute-start(f32[3,8,256]{2,1,0:T(8,128)S(1)} %collective-permute-done.4.yd_ref), channel_id=1, source_target_pairs={{0,1},{1,0},{2,3},{3,2},{4,5},{5,4},{6,7},{7,6},{8,9},{9,8},{10,11... | collective-permute-start | bytes 73736 | tf_op jit(solution)/shard_map/ppermute | solution.py:651
  13.6 3.3 %collective-permute-start.6 = (f32[5,8,128]{2,1,0:T(8,128)S(1)}, f32[5,8,128]{2,1,0:T(8,128)S(1)}, u32[]{:S(2)}, u32[]{:S(2)}) collective-permute-start(f32[5,8,128]{2,1,0:T(8,128)S(1)} %get-tuple-element.36.after_ref), channel_id=1, source_target_pairs={{0,9},{9,0},{8,17},{17,8},{16,25},{25,16},{2,11},{11,2},{10,19},{1... | collective-permute-start | bytes 61448 | tf_op jit(solution)/shard_map/ppermute | solution.py:655
  16.9 1.2 %collective-permute-start.7 = (f32[5,8,128]{2,1,0:T(8,128)S(1)}, f32[5,8,128]{2,1,0:T(8,128)S(1)}, u32[]{:S(2)}, u32[]{:S(2)}) collective-permute-start(f32[5,8,128]{2,1,0:T(8,128)S(1)} %collective-permute-done.6.direct_ref), channel_id=1, source_target_pairs={{0,1},{1,0},{2,3},{3,2},{4,5},{5,4},{6,7},{7,6},{8,9},{9,8},{10,11... | collective-permute-start | bytes 61448 | tf_op jit(solution)/shard_map/ppermute | solution.py:651
  17.0 1.1 %copy-start.1 = (f32[8,8,128]{2,1,0:T(8,128)S(1)}, f32[8,8,128]{2,1,0:T(8,128)}, u32[]{:S(2)}) copy-start(f32[8,8,128]{2,1,0:T(8,128)} %initial_ref.1) | copy-start | bytes 98308
  18.1 3.2 %collective-permute-start.8 = (f32[8,2,256]{2,1,0:T(2,128)S(1)}, f32[8,2,256]{2,1,0:T(2,128)S(1)}, u32[]{:S(2)}, u32[]{:S(2)}) collective-permute-start(f32[8,2,256]{2,1,0:T(2,128)S(1)} %get-tuple-element.38), channel_id=1, source_target_pairs={{0,3},{3,0},{2,5},{5,2},{4,7},{7,4},{9,10},{10,9},{11,12},{12,11},... | collective-permute-start | bytes 49160 | tf_op jit(solution)/shard_map/ppermute | solution.py:655
  21.3 1.6 %collective-permute-start.9 = (f32[8,2,256]{2,1,0:T(2,128)S(1)}, f32[8,2,256]{2,1,0:T(2,128)S(1)}, u32[]{:S(2)}, u32[]{:S(2)}) collective-permute-start(f32[8,2,256]{2,1,0:T(2,128)S(1)} %collective-permute-done.8.direct_ref), channel_id=1, source_target_pairs={{0,1},{1,0},{2,3},{3,2},{4,5},{5,4},{6,7},{7,6},{8,9},{9,8},{10,11... | collective-permute-start | bytes 49160 | tf_op jit(solution)/shard_map/ppermute | solution.py:651

commit v10 on v8

--- a/solution.py
+++ b/solution.py
@@ -611,7 +611,7 @@
     nodes, rows, width = base_ref.shape
     for layer in range(nodes):
         direct = direct_ref[layer, :, 0:width]
-        passed = passed_ref[layer, :, width:]
+        passed = passed_ref[layer]
         low = jnp.where(below, direct, passed)
         high = jnp.where(below, passed, direct)
         low = jnp.where(has_low, low, jnp.zeros_like(low))
@@ -733,7 +733,7 @@
         [initial, inner, x_direct, x_passed],
     )
     y_direct = swap_chips(sent, ALONG_Y)
-    y_passed = swap_cores(y_direct)
+    y_passed = swap_cores(y_direct[:, :, width:])
     return call(result_kernel, [shaped(initial.shape)], [base, y_direct, y_passed])[0]
 
 

time: 23.7 us -> 23.7 us (level)
  no operation moved by 1% of the time
where the time goes in v10:
time: 23.7 us; the launch traced here: 23.5 us
  starting transfers between devices  9.58 us (40%)
  waiting for transfers between devices  7.43 us (31%)
  Pallas kernels  6.4 us (27%)
    ppermute x4, starting transfers between devices, swap_chips(): return lax.ppermute(value, AXES, swap_pairs(leg))  8.03 us
    pallas_call x12, Pallas kernels, call(): pl.pallas_call(kernel, out_shape=outs, in_specs=[where] * len(args), out_...  6.4 us
    ppermute x4, waiting for transfers between devices, swap_chips(): return lax.ppermute(value, AXES, swap_pairs(leg))  4.27 us
    ppermute x6, waiting for transfers between devices, swap_cores(): return lax.ppermute(value, 'gz', [(0, 1), (1, 0)])  3.16 us
    ppermute x6, starting transfers between devices, swap_cores(): return lax.ppermute(value, 'gz', [(0, 1), (1, 0)])  1.55 us
  transfers between devices with their start and end apart: 10, of which 9 were waited for; matrix products, arithmetic and copies ran while one was open for 0% of the time, Pallas kernels for 17%

profile of v10, /device:TPU:0, one launch (start us, length us, event | category | flops | bytes accessed | tf_op | source)
XLA Modules:
  0.0 23.5 jit_solution(9773177656486377857)
XLA Ops:
  0.0 0.0 copy-start
  0.0 1.2 %shard_map.55.own_ref = f32[12,8,128]{2,1,0:T(8,128)S(1)} custom-call(f32[8,8,128]{2,1,0:T(8,128)} %initial_ref.1, f32[8,8,128]{2,1,0:T(8,128)} %source_hbm.1, f32[3,8,8,128]{3,2,1,0:T(8,128)} %metric_hbm.1, f32[30,1,16]{2,1,0:T(1,128)} %bitcast.6), custom_call_target="tpu_custom_call" | custom-call | bytes 214912 | tf_op jit(solution)/shard_map/pallas_call | solution.py:185
  1.2 0.5 %collective-permute-start = (f32[12,8,128]{2,1,0:T(8,128)S(1)}, f32[12,8,128]{2,1,0:T(8,128)S(1)}, u32[]{:S(2)}, u32[]{:S(2)}) collective-permute-start(f32[12,8,128]{2,1,0:T(8,128)S(1)} %shard_map.55.own_ref), channel_id=1, source_target_pairs={{0,1},{1,0},{2,3},{3,2},{4,5},{5,4},{6,7},{7,6},{8,9},{9,8},{10,11... | collective-permute-start | bytes 147464 | tf_op jit(solution)/shard_map/ppermute | solution.py:646
  1.8 0.0 copy-done
  1.8 0.1 collective-permute-start.2
  1.8 0.8 %collective-permute-done.partner_ref = f32[12,8,128]{2,1,0:T(8,128)S(1)} collective-permute-done((f32[12,8,128]{2,1,0:T(8,128)S(1)}, f32[12,8,128]{2,1,0:T(8,128)S(1)}, u32[]{:S(2)}, u32[]{:S(2)}) %collective-permute-start) | collective-permute-done | bytes 49184 | tf_op jit(solution)/shard_map/ppermute | solution.py:646
  2.6 2.9 %collective-permute-start.1 = (f32[2,2,8,128]{3,2,1,0:T(8,128)S(1)}, f32[2,2,8,128]{3,2,1,0:T(8,128)S(1)}, u32[]{:S(2)}, u32[]{:S(2)}) collective-permute-start(f32[2,2,8,128]{3,2,1,0:T(8,128)S(1)} %shard_map.56.after_ref), channel_id=1, source_target_pairs={{1,8},{8,1},{9,17},{17,9},{16,25},{25,16},{3,10},{10,3},{11,19},{1... | collective-permute-start | bytes 49160 | tf_op jit(solution)/shard_map/ppermute | solution.py:650
  5.6 0.0 collective-permute-done.2.partner_vec
  5.6 1.0 %shard_map.57 = (f32[100,320]{1,0:T(8,128)S(1)}, f32[240,320]{1,0:T(8,128)S(1)}, f32[10,16,320]{2,1,0:T(8,128)S(1)}) custom-call(f32[300,1,16]{2,1,0:T(1,128)S(1)} %bitcast.3, f32[300,1,16]{2,1,0:T(1,128)S(1)} %collective-permute-done.2.partner_vec, f32[12,8,128]{2,1,0:T(8,128)S(1)} %shard_map.55.own_ref, ...), custom_call_target="tpu_custom_call" | custom-call | bytes 793088 | tf_op jit(solution)/shard_map/pallas_call | solution.py:185
  6.6 0.7 %collective-permute-done.1.after_ref.direct_ref.xd_ref = f32[2,2,8,128]{3,2,1,0:T(8,128)S(1)} collective-permute-done((f32[2,2,8,128]{3,2,1,0:T(8,128)S(1)}, f32[2,2,8,128]{3,2,1,0:T(8,128)S(1)}, u32[]{:S(2)}, u32[]{:S(2)}) %collective-permute-start.1) | collective-permute-done | bytes 16416 | tf_op jit(solution)/shard_map/ppermute | solution.py:650
  7.3 0.0 collective-permute-start.3
  7.3 0.7 %shard_map.58.after_ref.along_z = f32[10,320]{1,0:T(8,128)S(1)} custom-call(f32[300,1,16]{2,1,0:T(1,128)S(1)} %bitcast.4, f32[300,1,16]{2,1,0:T(1,128)S(1)} %collective-permute-done.2.partner_vec, f32[2,2,8,128]{3,2,1,0:T(8,128)S(1)} %collective-permute-done.1.after_ref.direct_ref.xd_ref), custom_call_target="tpu_custom_call" | custom-call | bytes 67584 | tf_op jit(solution)/shard_map/pallas_call | solution.py:185
  8.0 0.4 %collective-permute-done.3.passed_ref.xp_ref = f32[2,2,8,128]{3,2,1,0:T(8,128)S(1)} collective-permute-done((f32[2,2,8,128]{3,2,1,0:T(8,128)S(1)}, f32[2,2,8,128]{3,2,1,0:T(8,128)S(1)}, u32[]{:S(2)}, u32[]{:S(2)}) %collective-permute-start.3) | collective-permute-done | bytes 16416 | tf_op jit(solution)/shard_map/ppermute | solution.py:646
  8.5 1.9 %collective-permute-start.4 = (f32[3,8,256]{2,1,0:T(8,128)S(1)}, f32[3,8,256]{2,1,0:T(8,128)S(1)}, u32[]{:S(2)}, u32[]{:S(2)}) collective-permute-start(f32[3,8,256]{2,1,0:T(8,128)S(1)} %shard_map.59.after_ref), channel_id=1, source_target_pairs={{0,3},{3,0},{2,5},{5,2},{4,7},{7,4},{9,10},{10,9},{11,12},{12,11},... | collective-permute-start | bytes 73736 | tf_op jit(solution)/shard_map/ppermute | solution.py:650
  10.3 0.9 %shard_map.60.after_ref.cy = f32[2,10,16,320]{3,2,1,0:T(8,128)S(1)} custom-call(f32[300,1,16]{2,1,0:T(1,128)S(1)} %bitcast.5, f32[300,1,16]{2,1,0:T(1,128)S(1)} %collective-permute-done.2.partner_vec, f32[3,8,256]{2,1,0:T(8,128)S(1)} %shard_map.59.after_ref), custom_call_target="tpu_custom_call" | custom-call | bytes 472576 | tf_op jit(solution)/shard_map/pallas_call | solution.py:185
  11.3 0.3 %shard_map.61 = (bf16[2,256,320]{2,1,0:T(8,128)(2,1)S(1)}, bf16[2,320,256]{2,1,0:T(8,128)(2,1)S(1)}) custom-call(f32[10,320]{1,0:T(8,128)S(1)} %shard_map.58.after_ref.along_z, f32[2,10,16,320]{3,2,1,0:T(8,128)S(1)} %shard_map.60.after_ref.cy), custom_call_target="tpu_custom_call" | custom-call | bytes 1077760 | tf_op jit(solution)/shard_map/pallas_call | solution.py:185
  11.6 0.3 %collective-permute-done.4.yd_ref = f32[3,8,256]{2,1,0:T(8,128)S(1)} collective-permute-done((f32[3,8,256]{2,1,0:T(8,128)S(1)}, f32[3,8,256]{2,1,0:T(8,128)S(1)}, u32[]{:S(2)}, u32[]{:S(2)}) %collective-permute-start.4) | collective-permute-done | bytes 24608 | tf_op jit(solution)/shard_map/ppermute | solution.py:650
  11.9 0.1 collective-permute-start.5
  12.0 0.5 %shard_map.62.part_ref = f32[10,16,320]{2,1,0:T(8,128)S(1)} custom-call(f32[12,8,128]{2,1,0:T(8,128)S(1)} %shard_map.55.own_ref, f32[12,8,128]{2,1,0:T(8,128)S(1)} %collective-permute-done.partner_ref, f32[2,2,8,128]{3,2,1,0:T(8,128)S(1)} %collective-permute-done.1.after_ref.direct_ref.xd_ref, f32[2,2,8,128]{3,2,1,0:T(8,128)S(1)} %collective-permute-done.3.passed_ref.xp_ref, ...), custom_call_target="tpu_custom_call" | custom-call | bytes 1532928 | tf_op jit(solution)/shard_map/pallas_call | solution.py:185
  12.5 0.6 %collective-permute-done.5.yp_ref = f32[3,8,256]{2,1,0:T(8,128)S(1)} collective-permute-done((f32[3,8,256]{2,1,0:T(8,128)S(1)}, f32[3,8,256]{2,1,0:T(8,128)S(1)}, u32[]{:S(2)}, u32[]{:S(2)}) %collective-permute-start.5) | collective-permute-done | bytes 24608 | tf_op jit(solution)/shard_map/ppermute | solution.py:646
  13.1 0.5 %shard_map.63 = (f32[10,16,320]{2,1,0:T(8,128)S(1)}, f32[5,8,128]{2,1,0:T(8,128)S(1)}) custom-call(f32[3,8,256]{2,1,0:T(8,128)S(1)} %collective-permute-done.5.yp_ref, f32[10,16,320]{2,1,0:T(8,128)S(1)} %shard_map.62.part_ref, f32[100,320]{1,0:T(8,128)S(1)} %get-tuple-element.29.cx, f32[240,320]{1,0:T(8,128)S(1)} %get-tuple-element.30.cx_rows, ...), custom_call_target="tpu_custom_call" | custom-call | bytes 2159616 | tf_op jit(solution)/shard_map/pallas_call | solution.py:185
  13.6 1.5 %collective-permute-start.6 = (f32[5,8,128]{2,1,0:T(8,128)S(1)}, f32[5,8,128]{2,1,0:T(8,128)S(1)}, u32[]{:S(2)}, u32[]{:S(2)}) collective-permute-start(f32[5,8,128]{2,1,0:T(8,128)S(1)} %get-tuple-element.36.after_ref), channel_id=1, source_target_pairs={{0,9},{9,0},{8,17},{17,8},{16,25},{25,16},{2,11},{11,2},{10,19},{1... | collective-permute-start | bytes 61448 | tf_op jit(solution)/shard_map/ppermute | solution.py:650
  15.0 1.8 %collective-permute-done.6.direct_ref = f32[5,8,128]{2,1,0:T(8,128)S(1)} collective-permute-done((f32[5,8,128]{2,1,0:T(8,128)S(1)}, f32[5,8,128]{2,1,0:T(8,128)S(1)}, u32[]{:S(2)}, u32[]{:S(2)}) %collective-permute-start.6) | collective-permute-done | bytes 20512 | tf_op jit(solution)/shard_map/ppermute | solution.py:650
  16.9 0.1 collective-permute-start.7
  17.0 0.0 copy-start.1
  17.0 0.5 %shard_map.64.inner_ref = f32[8,16,256]{2,1,0:T(8,128)S(1)} custom-call(f32[10,16,320]{2,1,0:T(8,128)S(1)} %get-tuple-element.35.spectral, f32[100,320]{1,0:T(8,128)S(1)} %get-tuple-element.29.cx, f32[2,10,16,320]{3,2,1,0:T(8,128)S(1)} %shard_map.60.after_ref.cy, bf16[2,320,256]{2,1,0:T(8,128)(2,1)S(1)} %get-tuple-element.34.mz_back, ...), custom_call_target="tpu_custom_call" | custom-call | bytes 1221632 | tf_op jit(solution)/shard_map/pallas_call | solution.py:185
  17.5 0.6 %collective-permute-done.7.passed_ref = f32[5,8,128]{2,1,0:T(8,128)S(1)} collective-permute-done((f32[5,8,128]{2,1,0:T(8,128)S(1)}, f32[5,8,128]{2,1,0:T(8,128)S(1)}, u32[]{:S(2)}, u32[]{:S(2)}) %collective-permute-start.7) | collective-permute-done | bytes 20512 | tf_op jit(solution)/shard_map/ppermute | solution.py:646
  18.0 0.0 copy-done.1
  18.1 1.8 %collective-permute-start.8 = (f32[8,2,256]{2,1,0:T(2,128)S(1)}, f32[8,2,256]{2,1,0:T(2,128)S(1)}, u32[]{:S(2)}, u32[]{:S(2)}) collective-permute-start(f32[8,2,256]{2,1,0:T(2,128)S(1)} %get-tuple-element.38), channel_id=1, source_target_pairs={{0,3},{3,0},{2,5},{5,2},{4,7},{7,4},{9,10},{10,9},{11,12},{12,11},... | collective-permute-start | bytes 49160 | tf_op jit(solution)/shard_map/ppermute | solution.py:650
  19.9 1.4 %collective-permute-done.8.direct_ref = f32[8,2,256]{2,1,0:T(2,128)S(1)} collective-permute-done((f32[8,2,256]{2,1,0:T(2,128)S(1)}, f32[8,2,256]{2,1,0:T(2,128)S(1)}, u32[]{:S(2)}, u32[]{:S(2)}) %collective-permute-start.8) | collective-permute-done | bytes 16416 | tf_op jit(solution)/shard_map/ppermute | solution.py:650
  21.3 0.7 %collective-permute-start.9 = (f32[8,2,128]{2,1,0:T(2,128)S(1)}, f32[8,2,128]{2,1,0:T(2,128)S(1)}, u32[]{:S(2)}, u32[]{:S(2)}) collective-permute-start(f32[8,2,128]{2,1,0:T(2,128)S(1)} %slice.4), channel_id=1, source_target_pairs={{0,1},{1,0},{2,3},{3,2},{4,5},{5,4},{6,7},{7,6},{8,9},{9,8},{10,11... | collective-permute-start | bytes 24584 | tf_op jit(solution)/shard_map/ppermute | solution.py:646
  22.0 0.8 %collective-permute-done.9.passed_ref = f32[8,2,128]{2,1,0:T(2,128)S(1)} collective-permute-done((f32[8,2,128]{2,1,0:T(2,128)S(1)}, f32[8,2,128]{2,1,0:T(2,128)S(1)}, u32[]{:S(2)}, u32[]{:S(2)}) %collective-permute-start.9) | collective-permute-done | bytes 8224 | tf_op jit(solution)/shard_map/ppermute | solution.py:646
  22.9 0.6 %shard_map.66 = f32[8,8,128]{2,1,0:T(8,128)} custom-call(f32[8,8,128]{2,1,0:T(8,128)S(1)} %get-tuple-element.37.base_ref, f32[8,2,256]{2,1,0:T(2,128)S(1)} %collective-permute-done.8.direct_ref, f32[8,2,128]{2,1,0:T(2,128)S(1)} %collective-permute-done.9.passed_ref), custom_call_target="tpu_custom_call" | custom-call | bytes 90112 | tf_op jit(solution)/shard_map/pallas_call | solution.py:185
  (4 shorter events, 0.1 us)
Async XLA Ops:
  0.0 1.8 %copy-start = (f32[3,10,10,1,1,16]{5,4,3,2,1,0:T(1,128)S(1)}, f32[3,10,10,1,1,16]{5,4,3,2,1,0:T(1,128)}, u32[]{:S(2)}) copy-start(f32[3,10,10,1,1,16]{5,4,3,2,1,0:T(1,128)} %param.8) | copy-start | bytes 57604
  1.2 1.4 %collective-permute-start = (f32[12,8,128]{2,1,0:T(8,128)S(1)}, f32[12,8,128]{2,1,0:T(8,128)S(1)}, u32[]{:S(2)}, u32[]{:S(2)}) collective-permute-start(f32[12,8,128]{2,1,0:T(8,128)S(1)} %shard_map.55.own_ref), channel_id=1, source_target_pairs={{0,1},{1,0},{2,3},{3,2},{4,5},{5,4},{6,7},{7,6},{8,9},{9,8},{10,11... | collective-permute-start | bytes 147464 | tf_op jit(solution)/shard_map/ppermute | solution.py:646
  1.8 3.8 %collective-permute-start.2 = (f32[300,1,16]{2,1,0:T(1,128)S(1)}, f32[300,1,16]{2,1,0:T(1,128)S(1)}, u32[]{:S(2)}, u32[]{:S(2)}) collective-permute-start(f32[300,1,16]{2,1,0:T(1,128)S(1)} %bitcast.2), channel_id=1, source_target_pairs={{0,1},{1,0},{2,3},{3,2},{4,5},{5,4},{6,7},{7,6},{8,9},{9,8},{10,11... | collective-permute-start | bytes 57608 | tf_op jit(solution)/shard_map/ppermute | solution.py:646
  2.6 4.6 %collective-permute-start.1 = (f32[2,2,8,128]{3,2,1,0:T(8,128)S(1)}, f32[2,2,8,128]{3,2,1,0:T(8,128)S(1)}, u32[]{:S(2)}, u32[]{:S(2)}) collective-permute-start(f32[2,2,8,128]{3,2,1,0:T(8,128)S(1)} %shard_map.56.after_ref), channel_id=1, source_target_pairs={{1,8},{8,1},{9,17},{17,9},{16,25},{25,16},{3,10},{10,3},{11,19},{1... | collective-permute-start | bytes 49160 | tf_op jit(solution)/shard_map/ppermute | solution.py:650
  7.3 1.2 %collective-permute-start.3 = (f32[2,2,8,128]{3,2,1,0:T(8,128)S(1)}, f32[2,2,8,128]{3,2,1,0:T(8,128)S(1)}, u32[]{:S(2)}, u32[]{:S(2)}) collective-permute-start(f32[2,2,8,128]{3,2,1,0:T(8,128)S(1)} %collective-permute-done.1.after_ref.direct_ref.xd_ref), channel_id=1, source_target_pairs={{0,1},{1,0},{2,3},{3,2},{4,5},{5,4},{6,7},{7,6},{8,9},{9,8},{10,11... | collective-permute-start | bytes 49160 | tf_op jit(solution)/shard_map/ppermute | solution.py:646
  8.5 3.4 %collective-permute-start.4 = (f32[3,8,256]{2,1,0:T(8,128)S(1)}, f32[3,8,256]{2,1,0:T(8,128)S(1)}, u32[]{:S(2)}, u32[]{:S(2)}) collective-permute-start(f32[3,8,256]{2,1,0:T(8,128)S(1)} %shard_map.59.after_ref), channel_id=1, source_target_pairs={{0,3},{3,0},{2,5},{5,2},{4,7},{7,4},{9,10},{10,9},{11,12},{12,11},... | collective-permute-start | bytes 73736 | tf_op jit(solution)/shard_map/ppermute | solution.py:650
  11.9 1.2 %collective-permute-start.5 = (f32[3,8,256]{2,1,0:T(8,128)S(1)}, f32[3,8,256]{2,1,0:T(8,128)S(1)}, u32[]{:S(2)}, u32[]{:S(2)}) collective-permute-start(f32[3,8,256]{2,1,0:T(8,128)S(1)} %collective-permute-done.4.yd_ref), channel_id=1, source_target_pairs={{0,1},{1,0},{2,3},{3,2},{4,5},{5,4},{6,7},{7,6},{8,9},{9,8},{10,11... | collective-permute-start | bytes 73736 | tf_op jit(solution)/shard_map/ppermute | solution.py:646
  13.6 3.3 %collective-permute-start.6 = (f32[5,8,128]{2,1,0:T(8,128)S(1)}, f32[5,8,128]{2,1,0:T(8,128)S(1)}, u32[]{:S(2)}, u32[]{:S(2)}) collective-permute-start(f32[5,8,128]{2,1,0:T(8,128)S(1)} %get-tuple-element.36.after_ref), channel_id=1, source_target_pairs={{0,9},{9,0},{8,17},{17,8},{16,25},{25,16},{2,11},{11,2},{10,19},{1... | collective-permute-start | bytes 61448 | tf_op jit(solution)/shard_map/ppermute | solution.py:650
  16.9 1.2 %collective-permute-start.7 = (f32[5,8,128]{2,1,0:T(8,128)S(1)}, f32[5,8,128]{2,1,0:T(8,128)S(1)}, u32[]{:S(2)}, u32[]{:S(2)}) collective-permute-start(f32[5,8,128]{2,1,0:T(8,128)S(1)} %collective-permute-done.6.direct_ref), channel_id=1, source_target_pairs={{0,1},{1,0},{2,3},{3,2},{4,5},{5,4},{6,7},{7,6},{8,9},{9,8},{10,11... | collective-permute-start | bytes 61448 | tf_op jit(solution)/shard_map/ppermute | solution.py:646
  17.0 1.1 %copy-start.1 = (f32[8,8,128]{2,1,0:T(8,128)S(1)}, f32[8,8,128]{2,1,0:T(8,128)}, u32[]{:S(2)}) copy-start(f32[8,8,128]{2,1,0:T(8,128)} %initial_ref.1) | copy-start | bytes 98308
  18.1 3.2 %collective-permute-start.8 = (f32[8,2,256]{2,1,0:T(2,128)S(1)}, f32[8,2,256]{2,1,0:T(2,128)S(1)}, u32[]{:S(2)}, u32[]{:S(2)}) collective-permute-start(f32[8,2,256]{2,1,0:T(2,128)S(1)} %get-tuple-element.38), channel_id=1, source_target_pairs={{0,3},{3,0},{2,5},{5,2},{4,7},{7,4},{9,10},{10,9},{11,12},{12,11},... | collective-permute-start | bytes 49160 | tf_op jit(solution)/shard_map/ppermute | solution.py:650
  21.3 1.5 %collective-permute-start.9 = (f32[8,2,128]{2,1,0:T(2,128)S(1)}, f32[8,2,128]{2,1,0:T(2,128)S(1)}, u32[]{:S(2)}, u32[]{:S(2)}) collective-permute-start(f32[8,2,128]{2,1,0:T(2,128)S(1)} %slice.4), channel_id=1, source_target_pairs={{0,1},{1,0},{2,3},{3,2},{4,5},{5,4},{6,7},{7,6},{8,9},{9,8},{10,11... | collective-permute-start | bytes 24584 | tf_op jit(solution)/shard_map/ppermute | solution.py:646

commit v11 on v9

--- a/solution.py
+++ b/solution.py
@@ -613,7 +613,7 @@
     nodes, rows, width = base_ref.shape
     for layer in range(nodes):
         direct = direct_ref[layer, :, 0:width]
-        passed = passed_ref[layer, :, width:]
+        passed = passed_ref[layer]
         low = jnp.where(below, direct, passed)
         high = jnp.where(below, passed, direct)
         low = jnp.where(has_low, low, jnp.zeros_like(low))
@@ -738,7 +738,7 @@
         [initial, inner, x_direct, x_passed],
     )
     y_direct = swap_chips(sent, BACK_Y)
-    y_passed = swap_cores(y_direct)
+    y_passed = swap_cores(y_direct[:, :, width:])
     return call(result_kernel, [shaped(initial.shape)], [base, y_direct, y_passed])[0]
 
 

time: 23.7 us -> 23.7 us (level)
  no operation moved by 1% of the time
where the time goes in v11:
time: 23.7 us; the launch traced here: 23.5 us
  starting transfers between devices  9.61 us (41%)
  waiting for transfers between devices  7.43 us (31%)
  Pallas kernels  6.4 us (27%)
    ppermute x4, starting transfers between devices, swap_chips(): return lax.ppermute(value, AXES, swap_pairs(leg))  8.03 us
    pallas_call x12, Pallas kernels, call(): pl.pallas_call(kernel, out_shape=outs, in_specs=[where] * len(args), out_...  6.4 us
    ppermute x4, waiting for transfers between devices, swap_chips(): return lax.ppermute(value, AXES, swap_pairs(leg))  4.27 us
    ppermute x6, waiting for transfers between devices, swap_cores(): return lax.ppermute(value, 'gz', [(0, 1), (1, 0)])  3.16 us
    ppermute x6, starting transfers between devices, swap_cores(): return lax.ppermute(value, 'gz', [(0, 1), (1, 0)])  1.58 us
  transfers between devices with their start and end apart: 10, of which 9 were waited for; matrix products, arithmetic and copies ran while one was open for 0% of the time, Pallas kernels for 17%

profile of v11, /device:TPU:0, one launch (start us, length us, event | category | flops | bytes accessed | tf_op | source)
XLA Modules:
  0.0 23.5 jit_solution(9576376254848452427)
XLA Ops:
  0.0 0.0 copy-start
  0.0 1.2 %shard_map.55.own_ref = f32[12,8,128]{2,1,0:T(8,128)S(1)} custom-call(f32[8,8,128]{2,1,0:T(8,128)} %initial_ref.1, f32[8,8,128]{2,1,0:T(8,128)} %source_hbm.1, f32[3,8,8,128]{3,2,1,0:T(8,128)} %metric_hbm.1, f32[30,1,16]{2,1,0:T(1,128)} %bitcast.6), custom_call_target="tpu_custom_call" | custom-call | bytes 214912 | tf_op jit(solution)/shard_map/pallas_call | solution.py:185
  1.2 0.5 %collective-permute-start = (f32[12,8,128]{2,1,0:T(8,128)S(1)}, f32[12,8,128]{2,1,0:T(8,128)S(1)}, u32[]{:S(2)}, u32[]{:S(2)}) collective-permute-start(f32[12,8,128]{2,1,0:T(8,128)S(1)} %shard_map.55.own_ref), channel_id=1, source_target_pairs={{0,1},{1,0},{2,3},{3,2},{4,5},{5,4},{6,7},{7,6},{8,9},{9,8},{10,11... | collective-permute-start | bytes 147464 | tf_op jit(solution)/shard_map/ppermute | solution.py:651
  1.8 0.0 copy-done
  1.8 0.1 collective-permute-start.2
  1.8 0.8 %collective-permute-done.partner_ref = f32[12,8,128]{2,1,0:T(8,128)S(1)} collective-permute-done((f32[12,8,128]{2,1,0:T(8,128)S(1)}, f32[12,8,128]{2,1,0:T(8,128)S(1)}, u32[]{:S(2)}, u32[]{:S(2)}) %collective-permute-start) | collective-permute-done | bytes 49184 | tf_op jit(solution)/shard_map/ppermute | solution.py:651
  2.6 2.9 %collective-permute-start.1 = (f32[2,2,8,128]{3,2,1,0:T(8,128)S(1)}, f32[2,2,8,128]{3,2,1,0:T(8,128)S(1)}, u32[]{:S(2)}, u32[]{:S(2)}) collective-permute-start(f32[2,2,8,128]{3,2,1,0:T(8,128)S(1)} %shard_map.56.after_ref), channel_id=1, source_target_pairs={{1,8},{8,1},{9,17},{17,9},{16,25},{25,16},{3,10},{10,3},{11,19},{1... | collective-permute-start | bytes 49160 | tf_op jit(solution)/shard_map/ppermute | solution.py:655
  5.6 0.0 collective-permute-done.2.partner_vec
  5.6 1.0 %shard_map.57 = (f32[100,320]{1,0:T(8,128)S(1)}, f32[240,320]{1,0:T(8,128)S(1)}, f32[10,16,320]{2,1,0:T(8,128)S(1)}) custom-call(f32[300,1,16]{2,1,0:T(1,128)S(1)} %bitcast.3, f32[300,1,16]{2,1,0:T(1,128)S(1)} %collective-permute-done.2.partner_vec, f32[12,8,128]{2,1,0:T(8,128)S(1)} %shard_map.55.own_ref, ...), custom_call_target="tpu_custom_call" | custom-call | bytes 793088 | tf_op jit(solution)/shard_map/pallas_call | solution.py:185
  6.6 0.7 %collective-permute-done.1.after_ref.direct_ref.xd_ref = f32[2,2,8,128]{3,2,1,0:T(8,128)S(1)} collective-permute-done((f32[2,2,8,128]{3,2,1,0:T(8,128)S(1)}, f32[2,2,8,128]{3,2,1,0:T(8,128)S(1)}, u32[]{:S(2)}, u32[]{:S(2)}) %collective-permute-start.1) | collective-permute-done | bytes 16416 | tf_op jit(solution)/shard_map/ppermute | solution.py:655
  7.3 0.0 collective-permute-start.3
  7.3 0.7 %shard_map.58.after_ref.along_z = f32[10,320]{1,0:T(8,128)S(1)} custom-call(f32[300,1,16]{2,1,0:T(1,128)S(1)} %bitcast.4, f32[300,1,16]{2,1,0:T(1,128)S(1)} %collective-permute-done.2.partner_vec, f32[2,2,8,128]{3,2,1,0:T(8,128)S(1)} %collective-permute-done.1.after_ref.direct_ref.xd_ref), custom_call_target="tpu_custom_call" | custom-call | bytes 67584 | tf_op jit(solution)/shard_map/pallas_call | solution.py:185
  8.0 0.4 %collective-permute-done.3.passed_ref.xp_ref = f32[2,2,8,128]{3,2,1,0:T(8,128)S(1)} collective-permute-done((f32[2,2,8,128]{3,2,1,0:T(8,128)S(1)}, f32[2,2,8,128]{3,2,1,0:T(8,128)S(1)}, u32[]{:S(2)}, u32[]{:S(2)}) %collective-permute-start.3) | collective-permute-done | bytes 16416 | tf_op jit(solution)/shard_map/ppermute | solution.py:651
  8.5 1.9 %collective-permute-start.4 = (f32[3,8,256]{2,1,0:T(8,128)S(1)}, f32[3,8,256]{2,1,0:T(8,128)S(1)}, u32[]{:S(2)}, u32[]{:S(2)}) collective-permute-start(f32[3,8,256]{2,1,0:T(8,128)S(1)} %shard_map.59.after_ref), channel_id=1, source_target_pairs={{0,3},{3,0},{2,5},{5,2},{4,7},{7,4},{9,10},{10,9},{11,12},{12,11},... | collective-permute-start | bytes 73736 | tf_op jit(solution)/shard_map/ppermute | solution.py:655
  10.3 0.9 %shard_map.60.after_ref.cy = f32[2,10,16,320]{3,2,1,0:T(8,128)S(1)} custom-call(f32[300,1,16]{2,1,0:T(1,128)S(1)} %bitcast.5, f32[300,1,16]{2,1,0:T(1,128)S(1)} %collective-permute-done.2.partner_vec, f32[3,8,256]{2,1,0:T(8,128)S(1)} %shard_map.59.after_ref), custom_call_target="tpu_custom_call" | custom-call | bytes 472576 | tf_op jit(solution)/shard_map/pallas_call | solution.py:185
  11.3 0.3 %shard_map.61 = (bf16[2,256,320]{2,1,0:T(8,128)(2,1)S(1)}, bf16[2,320,256]{2,1,0:T(8,128)(2,1)S(1)}) custom-call(f32[10,320]{1,0:T(8,128)S(1)} %shard_map.58.after_ref.along_z, f32[2,10,16,320]{3,2,1,0:T(8,128)S(1)} %shard_map.60.after_ref.cy), custom_call_target="tpu_custom_call" | custom-call | bytes 1077760 | tf_op jit(solution)/shard_map/pallas_call | solution.py:185
  11.6 0.3 %collective-permute-done.4.yd_ref = f32[3,8,256]{2,1,0:T(8,128)S(1)} collective-permute-done((f32[3,8,256]{2,1,0:T(8,128)S(1)}, f32[3,8,256]{2,1,0:T(8,128)S(1)}, u32[]{:S(2)}, u32[]{:S(2)}) %collective-permute-start.4) | collective-permute-done | bytes 24608 | tf_op jit(solution)/shard_map/ppermute | solution.py:655
  11.9 0.1 collective-permute-start.5
  12.0 0.5 %shard_map.62.part_ref = f32[10,16,320]{2,1,0:T(8,128)S(1)} custom-call(f32[12,8,128]{2,1,0:T(8,128)S(1)} %shard_map.55.own_ref, f32[12,8,128]{2,1,0:T(8,128)S(1)} %collective-permute-done.partner_ref, f32[2,2,8,128]{3,2,1,0:T(8,128)S(1)} %collective-permute-done.1.after_ref.direct_ref.xd_ref, f32[2,2,8,128]{3,2,1,0:T(8,128)S(1)} %collective-permute-done.3.passed_ref.xp_ref, ...), custom_call_target="tpu_custom_call" | custom-call | bytes 1532928 | tf_op jit(solution)/shard_map/pallas_call | solution.py:185
  12.5 0.6 %collective-permute-done.5.yp_ref = f32[3,8,256]{2,1,0:T(8,128)S(1)} collective-permute-done((f32[3,8,256]{2,1,0:T(8,128)S(1)}, f32[3,8,256]{2,1,0:T(8,128)S(1)}, u32[]{:S(2)}, u32[]{:S(2)}) %collective-permute-start.5) | collective-permute-done | bytes 24608 | tf_op jit(solution)/shard_map/ppermute | solution.py:651
  13.1 0.5 %shard_map.63 = (f32[10,16,320]{2,1,0:T(8,128)S(1)}, f32[5,8,128]{2,1,0:T(8,128)S(1)}) custom-call(f32[3,8,256]{2,1,0:T(8,128)S(1)} %collective-permute-done.5.yp_ref, f32[10,16,320]{2,1,0:T(8,128)S(1)} %shard_map.62.part_ref, f32[100,320]{1,0:T(8,128)S(1)} %get-tuple-element.29.cx, f32[240,320]{1,0:T(8,128)S(1)} %get-tuple-element.30.cx_rows, ...), custom_call_target="tpu_custom_call" | custom-call | bytes 2159616 | tf_op jit(solution)/shard_map/pallas_call | solution.py:185
  13.6 1.5 %collective-permute-start.6 = (f32[5,8,128]{2,1,0:T(8,128)S(1)}, f32[5,8,128]{2,1,0:T(8,128)S(1)}, u32[]{:S(2)}, u32[]{:S(2)}) collective-permute-start(f32[5,8,128]{2,1,0:T(8,128)S(1)} %get-tuple-element.36.after_ref), channel_id=1, source_target_pairs={{0,9},{9,0},{8,17},{17,8},{16,25},{25,16},{2,11},{11,2},{10,19},{1... | collective-permute-start | bytes 61448 | tf_op jit(solution)/shard_map/ppermute | solution.py:655
  15.0 1.8 %collective-permute-done.6.direct_ref = f32[5,8,128]{2,1,0:T(8,128)S(1)} collective-permute-done((f32[5,8,128]{2,1,0:T(8,128)S(1)}, f32[5,8,128]{2,1,0:T(8,128)S(1)}, u32[]{:S(2)}, u32[]{:S(2)}) %collective-permute-start.6) | collective-permute-done | bytes 20512 | tf_op jit(solution)/shard_map/ppermute | solution.py:655
  16.9 0.1 collective-permute-start.7
  17.0 0.0 copy-start.1
  17.0 0.5 %shard_map.64.inner_ref = f32[8,16,256]{2,1,0:T(8,128)S(1)} custom-call(f32[10,16,320]{2,1,0:T(8,128)S(1)} %get-tuple-element.35.spectral, f32[100,320]{1,0:T(8,128)S(1)} %get-tuple-element.29.cx, f32[2,10,16,320]{3,2,1,0:T(8,128)S(1)} %shard_map.60.after_ref.cy, bf16[2,320,256]{2,1,0:T(8,128)(2,1)S(1)} %get-tuple-element.34.mz_back, ...), custom_call_target="tpu_custom_call" | custom-call | bytes 1221632 | tf_op jit(solution)/shard_map/pallas_call | solution.py:185
  17.5 0.6 %collective-permute-done.7.passed_ref = f32[5,8,128]{2,1,0:T(8,128)S(1)} collective-permute-done((f32[5,8,128]{2,1,0:T(8,128)S(1)}, f32[5,8,128]{2,1,0:T(8,128)S(1)}, u32[]{:S(2)}, u32[]{:S(2)}) %collective-permute-start.7) | collective-permute-done | bytes 20512 | tf_op jit(solution)/shard_map/ppermute | solution.py:651
  18.0 0.0 copy-done.1
  18.1 1.8 %collective-permute-start.8 = (f32[8,2,256]{2,1,0:T(2,128)S(1)}, f32[8,2,256]{2,1,0:T(2,128)S(1)}, u32[]{:S(2)}, u32[]{:S(2)}) collective-permute-start(f32[8,2,256]{2,1,0:T(2,128)S(1)} %get-tuple-element.38), channel_id=1, source_target_pairs={{0,3},{3,0},{2,5},{5,2},{4,7},{7,4},{9,10},{10,9},{11,12},{12,11},... | collective-permute-start | bytes 49160 | tf_op jit(solution)/shard_map/ppermute | solution.py:655
  19.9 1.4 %collective-permute-done.8.direct_ref = f32[8,2,256]{2,1,0:T(2,128)S(1)} collective-permute-done((f32[8,2,256]{2,1,0:T(2,128)S(1)}, f32[8,2,256]{2,1,0:T(2,128)S(1)}, u32[]{:S(2)}, u32[]{:S(2)}) %collective-permute-start.8) | collective-permute-done | bytes 16416 | tf_op jit(solution)/shard_map/ppermute | solution.py:655
  21.3 0.7 %collective-permute-start.9 = (f32[8,2,128]{2,1,0:T(2,128)S(1)}, f32[8,2,128]{2,1,0:T(2,128)S(1)}, u32[]{:S(2)}, u32[]{:S(2)}) collective-permute-start(f32[8,2,128]{2,1,0:T(2,128)S(1)} %slice.4), channel_id=1, source_target_pairs={{0,1},{1,0},{2,3},{3,2},{4,5},{5,4},{6,7},{7,6},{8,9},{9,8},{10,11... | collective-permute-start | bytes 24584 | tf_op jit(solution)/shard_map/ppermute | solution.py:651
  22.1 0.8 %collective-permute-done.9.passed_ref = f32[8,2,128]{2,1,0:T(2,128)S(1)} collective-permute-done((f32[8,2,128]{2,1,0:T(2,128)S(1)}, f32[8,2,128]{2,1,0:T(2,128)S(1)}, u32[]{:S(2)}, u32[]{:S(2)}) %collective-permute-start.9) | collective-permute-done | bytes 8224 | tf_op jit(solution)/shard_map/ppermute | solution.py:651
  22.9 0.6 %shard_map.66 = f32[8,8,128]{2,1,0:T(8,128)} custom-call(f32[8,8,128]{2,1,0:T(8,128)S(1)} %get-tuple-element.37.base_ref, f32[8,2,256]{2,1,0:T(2,128)S(1)} %collective-permute-done.8.direct_ref, f32[8,2,128]{2,1,0:T(2,128)S(1)} %collective-permute-done.9.passed_ref), custom_call_target="tpu_custom_call" | custom-call | bytes 90112 | tf_op jit(solution)/shard_map/pallas_call | solution.py:185
  (4 shorter events, 0.1 us)
Async XLA Ops:
  0.0 1.8 %copy-start = (f32[3,10,10,1,1,16]{5,4,3,2,1,0:T(1,128)S(1)}, f32[3,10,10,1,1,16]{5,4,3,2,1,0:T(1,128)}, u32[]{:S(2)}) copy-start(f32[3,10,10,1,1,16]{5,4,3,2,1,0:T(1,128)} %param.8) | copy-start | bytes 57604
  1.2 1.4 %collective-permute-start = (f32[12,8,128]{2,1,0:T(8,128)S(1)}, f32[12,8,128]{2,1,0:T(8,128)S(1)}, u32[]{:S(2)}, u32[]{:S(2)}) collective-permute-start(f32[12,8,128]{2,1,0:T(8,128)S(1)} %shard_map.55.own_ref), channel_id=1, source_target_pairs={{0,1},{1,0},{2,3},{3,2},{4,5},{5,4},{6,7},{7,6},{8,9},{9,8},{10,11... | collective-permute-start | bytes 147464 | tf_op jit(solution)/shard_map/ppermute | solution.py:651
  1.8 3.8 %collective-permute-start.2 = (f32[300,1,16]{2,1,0:T(1,128)S(1)}, f32[300,1,16]{2,1,0:T(1,128)S(1)}, u32[]{:S(2)}, u32[]{:S(2)}) collective-permute-start(f32[300,1,16]{2,1,0:T(1,128)S(1)} %bitcast.2), channel_id=1, source_target_pairs={{0,1},{1,0},{2,3},{3,2},{4,5},{5,4},{6,7},{7,6},{8,9},{9,8},{10,11... | collective-permute-start | bytes 57608 | tf_op jit(solution)/shard_map/ppermute | solution.py:651
  2.6 4.6 %collective-permute-start.1 = (f32[2,2,8,128]{3,2,1,0:T(8,128)S(1)}, f32[2,2,8,128]{3,2,1,0:T(8,128)S(1)}, u32[]{:S(2)}, u32[]{:S(2)}) collective-permute-start(f32[2,2,8,128]{3,2,1,0:T(8,128)S(1)} %shard_map.56.after_ref), channel_id=1, source_target_pairs={{1,8},{8,1},{9,17},{17,9},{16,25},{25,16},{3,10},{10,3},{11,19},{1... | collective-permute-start | bytes 49160 | tf_op jit(solution)/shard_map/ppermute | solution.py:655
  7.3 1.2 %collective-permute-start.3 = (f32[2,2,8,128]{3,2,1,0:T(8,128)S(1)}, f32[2,2,8,128]{3,2,1,0:T(8,128)S(1)}, u32[]{:S(2)}, u32[]{:S(2)}) collective-permute-start(f32[2,2,8,128]{3,2,1,0:T(8,128)S(1)} %collective-permute-done.1.after_ref.direct_ref.xd_ref), channel_id=1, source_target_pairs={{0,1},{1,0},{2,3},{3,2},{4,5},{5,4},{6,7},{7,6},{8,9},{9,8},{10,11... | collective-permute-start | bytes 49160 | tf_op jit(solution)/shard_map/ppermute | solution.py:651
  8.5 3.4 %collective-permute-start.4 = (f32[3,8,256]{2,1,0:T(8,128)S(1)}, f32[3,8,256]{2,1,0:T(8,128)S(1)}, u32[]{:S(2)}, u32[]{:S(2)}) collective-permute-start(f32[3,8,256]{2,1,0:T(8,128)S(1)} %shard_map.59.after_ref), channel_id=1, source_target_pairs={{0,3},{3,0},{2,5},{5,2},{4,7},{7,4},{9,10},{10,9},{11,12},{12,11},... | collective-permute-start | bytes 73736 | tf_op jit(solution)/shard_map/ppermute | solution.py:655
  11.9 1.2 %collective-permute-start.5 = (f32[3,8,256]{2,1,0:T(8,128)S(1)}, f32[3,8,256]{2,1,0:T(8,128)S(1)}, u32[]{:S(2)}, u32[]{:S(2)}) collective-permute-start(f32[3,8,256]{2,1,0:T(8,128)S(1)} %collective-permute-done.4.yd_ref), channel_id=1, source_target_pairs={{0,1},{1,0},{2,3},{3,2},{4,5},{5,4},{6,7},{7,6},{8,9},{9,8},{10,11... | collective-permute-start | bytes 73736 | tf_op jit(solution)/shard_map/ppermute | solution.py:651
  13.6 3.3 %collective-permute-start.6 = (f32[5,8,128]{2,1,0:T(8,128)S(1)}, f32[5,8,128]{2,1,0:T(8,128)S(1)}, u32[]{:S(2)}, u32[]{:S(2)}) collective-permute-start(f32[5,8,128]{2,1,0:T(8,128)S(1)} %get-tuple-element.36.after_ref), channel_id=1, source_target_pairs={{0,9},{9,0},{8,17},{17,8},{16,25},{25,16},{2,11},{11,2},{10,19},{1... | collective-permute-start | bytes 61448 | tf_op jit(solution)/shard_map/ppermute | solution.py:655
  16.9 1.2 %collective-permute-start.7 = (f32[5,8,128]{2,1,0:T(8,128)S(1)}, f32[5,8,128]{2,1,0:T(8,128)S(1)}, u32[]{:S(2)}, u32[]{:S(2)}) collective-permute-start(f32[5,8,128]{2,1,0:T(8,128)S(1)} %collective-permute-done.6.direct_ref), channel_id=1, source_target_pairs={{0,1},{1,0},{2,3},{3,2},{4,5},{5,4},{6,7},{7,6},{8,9},{9,8},{10,11... | collective-permute-start | bytes 61448 | tf_op jit(solution)/shard_map/ppermute | solution.py:651
  17.0 1.1 %copy-start.1 = (f32[8,8,128]{2,1,0:T(8,128)S(1)}, f32[8,8,128]{2,1,0:T(8,128)}, u32[]{:S(2)}) copy-start(f32[8,8,128]{2,1,0:T(8,128)} %initial_ref.1) | copy-start | bytes 98308
  18.1 3.2 %collective-permute-start.8 = (f32[8,2,256]{2,1,0:T(2,128)S(1)}, f32[8,2,256]{2,1,0:T(2,128)S(1)}, u32[]{:S(2)}, u32[]{:S(2)}) collective-permute-start(f32[8,2,256]{2,1,0:T(2,128)S(1)} %get-tuple-element.38), channel_id=1, source_target_pairs={{0,3},{3,0},{2,5},{5,2},{4,7},{7,4},{9,10},{10,9},{11,12},{12,11},... | collective-permute-start | bytes 49160 | tf_op jit(solution)/shard_map/ppermute | solution.py:655
  21.3 1.6 %collective-permute-start.9 = (f32[8,2,128]{2,1,0:T(2,128)S(1)}, f32[8,2,128]{2,1,0:T(2,128)S(1)}, u32[]{:S(2)}, u32[]{:S(2)}) collective-permute-start(f32[8,2,128]{2,1,0:T(2,128)S(1)} %slice.4), channel_id=1, source_target_pairs={{0,1},{1,0},{2,3},{3,2},{4,5},{5,4},{6,7},{7,6},{8,9},{9,8},{10,11... | collective-permute-start | bytes 24584 | tf_op jit(solution)/shard_map/ppermute | solution.py:651
